TPU v7x, 512 devices: a whole 4x4x16 slice. The times are simulated.
512 devices in a mesh: dp: 16 (over x_hi, y, core), ctx: 32 (over z, x_lo).
Axes of the slice: x: 4 (x_hi: 2, x_lo: 2; x = x_hi * 2 + x_lo), y: 4, z: 16, core: 2. Of those that a mesh axis runs over, the one named last changes fastest.
Arguments:
- series: bfloat16 [16, 4096, 512], P('dp', 'ctx'), may hold values from -40 to 40
- norm_gain: float32 [512], replicated, may hold values from 0.5 to 1.5
- query_kernel: bfloat16 [3, 512, 512], P(None, 'dp'), may hold values from -6.251302 to 6.251302
- key_kernel: bfloat16 [3, 512, 512], P(None, 'dp'), may hold values from -0.104613624 to 0.104613624
- value_weight: bfloat16 [512, 512], P('dp'), may hold values from -0.25 to 0.25
- out_weight: bfloat16 [512, 512], P('dp'), may hold values from -0.25 to 0.25
- block_links: int32 [16, 32, 8, 4], P('dp', 'ctx'), may hold values 0 or 1
- grad_out: bfloat16 [16, 4096, 512], P('dp', 'ctx'), may hold values from -36 to 36
Outputs:
- mixed: bfloat16 [16, 4096, 512], P('dp', 'ctx')
- grad_series: bfloat16 [16, 4096, 512], P('dp', 'ctx')
- grad_gain: float32 [512], replicated
- grad_query_kernel: float32 [3, 512, 512], P(None, 'dp')
- grad_key_kernel: float32 [3, 512, 512], P(None, 'dp')
- grad_value_weight: float32 [512, 512], P('dp')
- grad_out_weight: float32 [512, 512], P('dp')
All inputs are finite; a program needn't handle non-finite values. No bound on the sum of `block_links` on one device may be relied on, other than what follows from the above.
Results may differ from a plain program's by a relative error of at most 0.039.
The roundings to bfloat16 on the way count: a program that leaves them out, or rounds other values in their place, can miss the bound.
Values may be sent and summed in bfloat16 or wider, within the bound.
No kernel may reach another device: no remote copies, remote signals or barrier semaphores. Data moves between devices by JAX's collectives and lax.ppermute only.
A program may use at most 64 MiB of HBM per device.

v0:
```python
import jax
import jax.numpy as jnp
from jax import lax
from jax.sharding import PartitionSpec as P

block_offsets = (1, 2, 4, 8)
epsilon = 1e-06
heads_together = 2


def from_behind(shard, axis, by):
    devices = lax.axis_size(axis)
    pairs = [(i, i + by) for i in range(devices) if 0 <= i + by < devices]
    return lax.ppermute(shard, axis, pairs)


def normalize(values, norm_gain):
    scale = lax.rsqrt(jnp.mean(values * values, axis=-1, keepdims=True) + epsilon)
    return values * scale * norm_gain


def product(left, right):
    return jnp.dot(left, right, preferred_element_type=jnp.float32)


def product_right_t(left, right):
    return lax.dot_general(
        left, right, (((1,), (1,)), ((), ())), preferred_element_type=jnp.float32
    )


def product_left_t(left, right):
    return lax.dot_general(
        left, right, (((0,), (0,)), ((), ())), preferred_element_type=jnp.float32
    )


def convolve(window, kernel, count):
    result = product(window[2 : 2 + count], kernel[0])
    result = result + product(window[1 : 1 + count], kernel[1])
    return result + product(window[0:count], kernel[2])


def visibility(count, total, allowed):
    column = jnp.arange(total)
    source = column // count
    inside = column % count
    causal = (source[None, :] > 0) | (inside[None, :] <= jnp.arange(count)[:, None])
    linked = jnp.repeat(allowed, count, axis=1)
    return causal[None, :, :] & linked[:, None, :]


def pair_probabilities(query, keys, allowed, head_width):
    count = query.shape[0]
    total = keys.shape[0]
    query_heads = query.reshape(count, heads_together, head_width)
    key_heads = keys.reshape(total, heads_together, head_width)
    scores = jnp.einsum(
        "thd,uhd->htu", query_heads, key_heads, preferred_element_type=jnp.float32
    ) * head_width ** (-0.5)
    visible = visibility(count, total, allowed)
    scores = jnp.where(visible, scores, -1e30)
    highest = jnp.max(scores, axis=-1, keepdims=True)
    weights = jnp.where(visible, jnp.exp(scores - highest), 0.0)
    return weights / jnp.sum(weights, axis=-1, keepdims=True)


def pair_slices(arrays, allowed, pair, head_width):
    span = heads_together * head_width
    pieces = [lax.dynamic_slice_in_dim(array, pair * span, span, 1) for array in arrays]
    return (pieces, lax.dynamic_slice_in_dim(allowed, pair * heads_together, heads_together, 0))


def regroup(stacked):
    pairs, count, span = stacked.shape
    return jnp.transpose(stacked, (1, 0, 2)).reshape(count, pairs * span)


def attend(query, keys, values, allowed, head_width):
    count = query.shape[0]
    pairs = allowed.shape[0] // heads_together

    def one_pair(pair):
        pieces, local = pair_slices((query, keys, values), allowed, pair, head_width)
        probs = pair_probabilities(pieces[0], pieces[1], local, head_width).astype(jnp.bfloat16)
        value_heads = pieces[2].reshape(-1, heads_together, head_width)
        result = jnp.einsum("htu,uhd->thd", probs, value_heads, preferred_element_type=jnp.float32)
        return result.reshape(count, heads_together * head_width)

    return regroup(lax.map(one_pair, jnp.arange(pairs)))


def attend_back(query, keys, values, allowed, upstream, head_width):
    count = query.shape[0]
    total = keys.shape[0]
    pairs = allowed.shape[0] // heads_together
    span = heads_together * head_width

    def one_pair(pair):
        pieces, local = pair_slices((query, keys, values, upstream), allowed, pair, head_width)
        probs = pair_probabilities(pieces[0], pieces[1], local, head_width)
        query_heads = pieces[0].reshape(count, heads_together, head_width)
        key_heads = pieces[1].reshape(total, heads_together, head_width)
        value_heads = pieces[2].reshape(total, heads_together, head_width)
        upper_heads = pieces[3].reshape(count, heads_together, head_width)
        d_prob = jnp.einsum(
            "thd,uhd->htu", upper_heads, value_heads, preferred_element_type=jnp.float32
        )
        centre = jnp.sum(probs * d_prob, axis=-1, keepdims=True)
        d_score = (probs * (d_prob - centre) * head_width ** (-0.5)).astype(jnp.bfloat16)
        d_query = jnp.einsum("htu,uhd->thd", d_score, key_heads, preferred_element_type=jnp.float32)
        d_key = jnp.einsum("htu,thd->uhd", d_score, query_heads, preferred_element_type=jnp.float32)
        d_value = jnp.einsum(
            "htu,thd->uhd",
            probs.astype(jnp.bfloat16),
            upper_heads,
            preferred_element_type=jnp.float32,
        )
        return (
            d_query.reshape(count, span),
            d_key.reshape(total, span),
            d_value.reshape(total, span),
        )

    parts = lax.map(one_pair, jnp.arange(pairs))
    return (regroup(parts[0]), regroup(parts[1]), regroup(parts[2]))


def body(
    series, norm_gain, query_kernel, key_kernel, value_weight, out_weight, block_links, grad_out
):
    full_query, full_key, full_value, full_out = (
        lax.all_gather(query_kernel, "dp", axis=1, tiled=True),
        lax.all_gather(key_kernel, "dp", axis=1, tiled=True),
        lax.all_gather(value_weight, "dp", axis=0, tiled=True),
        lax.all_gather(out_weight, "dp", axis=0, tiled=True),
    )
    heads = block_links.shape[2]
    features = full_value.shape[1]
    head_width = features // heads
    values = series[0].astype(jnp.float32)
    count = values.shape[0]
    cotangent = grad_out[0]
    normed = normalize(values, norm_gain).astype(jnp.bfloat16)
    previous = from_behind(normed[count - 2 :], "ctx", 1)
    window = jnp.concatenate([previous, normed], axis=0)
    query = convolve(window, full_query, count).astype(jnp.bfloat16)
    keyed = convolve(window, full_key, count).astype(jnp.bfloat16)
    value = product(normed, full_value).astype(jnp.bfloat16)
    payload = jnp.concatenate([keyed, value], axis=1)
    remote = [from_behind(payload, "ctx", offset) for offset in block_offsets]
    key_sources = jnp.concatenate([keyed] + [piece[:, :features] for piece in remote], axis=0)
    value_sources = jnp.concatenate([value] + [piece[:, features:] for piece in remote], axis=0)
    block = lax.axis_index("ctx")
    offsets = jnp.array(block_offsets, dtype=jnp.int32)
    reach = (block_links[0, 0] > 0) & (block >= offsets)[None, :]
    allowed = jnp.concatenate([jnp.ones((heads, 1), jnp.bool_), reach], axis=1)
    attn = attend(query, key_sources, value_sources, allowed, head_width).astype(jnp.bfloat16)
    mixed = (values + product(attn, full_out)).astype(jnp.bfloat16)
    out_term = product_left_t(attn, cotangent)
    upstream = product_right_t(cotangent, full_out).astype(jnp.bfloat16)
    d_query, key_terms, value_terms = attend_back(
        query, key_sources, value_sources, allowed, upstream, head_width
    )
    returned = [
        jnp.concatenate(
            [
                key_terms[slot * count : (slot + 1) * count],
                value_terms[slot * count : (slot + 1) * count],
            ],
            axis=1,
        )
        for slot in range(5)
    ]
    collected = returned[0]
    for slot, offset in enumerate(block_offsets):
        collected = collected + from_behind(
            returned[slot + 1].astype(jnp.bfloat16), "ctx", -offset
        ).astype(jnp.float32)
    d_query = d_query.astype(jnp.bfloat16)
    d_key = collected[:, :features].astype(jnp.bfloat16)
    d_value = collected[:, features:].astype(jnp.bfloat16)
    leading = from_behind(jnp.concatenate([d_query[:2], d_key[:2]], axis=1), "ctx", -1)
    after_query = jnp.concatenate([d_query, leading[:, :features]], axis=0)
    after_key = jnp.concatenate([d_key, leading[:, features:]], axis=0)
    d_normed = product_right_t(d_value, full_value)
    for tap in range(3):
        d_normed = d_normed + product_right_t(after_query[tap : tap + count], full_query[tap])
        d_normed = d_normed + product_right_t(after_key[tap : tap + count], full_key[tap])
    unused, pull = jax.vjp(normalize, values, norm_gain)
    d_values, d_gain = pull(d_normed)
    grad_series = (cotangent.astype(jnp.float32) + d_values).astype(jnp.bfloat16)
    query_terms = [product_left_t(window[2 - tap : 2 - tap + count], d_query) for tap in range(3)]
    key_grads = [product_left_t(window[2 - tap : 2 - tap + count], d_key) for tap in range(3)]
    value_term = product_left_t(normed, d_value)
    shares = (
        lax.psum_scatter(
            query_terms[0].astype(jnp.bfloat16), "dp", scatter_dimension=0, tiled=True
        ).astype(jnp.float32),
        lax.psum_scatter(
            query_terms[1].astype(jnp.bfloat16), "dp", scatter_dimension=0, tiled=True
        ).astype(jnp.float32),
        lax.psum_scatter(
            query_terms[2].astype(jnp.bfloat16), "dp", scatter_dimension=0, tiled=True
        ).astype(jnp.float32),
        lax.psum_scatter(
            key_grads[0].astype(jnp.bfloat16), "dp", scatter_dimension=0, tiled=True
        ).astype(jnp.float32),
        lax.psum_scatter(
            key_grads[1].astype(jnp.bfloat16), "dp", scatter_dimension=0, tiled=True
        ).astype(jnp.float32),
        lax.psum_scatter(
            key_grads[2].astype(jnp.bfloat16), "dp", scatter_dimension=0, tiled=True
        ).astype(jnp.float32),
        lax.psum_scatter(
            value_term.astype(jnp.bfloat16), "dp", scatter_dimension=0, tiled=True
        ).astype(jnp.float32),
        lax.psum_scatter(
            out_term.astype(jnp.bfloat16), "dp", scatter_dimension=0, tiled=True
        ).astype(jnp.float32),
    )
    sums = (
        lax.psum(shares[0].astype(jnp.bfloat16), "ctx").astype(jnp.float32),
        lax.psum(shares[1].astype(jnp.bfloat16), "ctx").astype(jnp.float32),
        lax.psum(shares[2].astype(jnp.bfloat16), "ctx").astype(jnp.float32),
        lax.psum(shares[3].astype(jnp.bfloat16), "ctx").astype(jnp.float32),
        lax.psum(shares[4].astype(jnp.bfloat16), "ctx").astype(jnp.float32),
        lax.psum(shares[5].astype(jnp.bfloat16), "ctx").astype(jnp.float32),
        lax.psum(shares[6].astype(jnp.bfloat16), "ctx").astype(jnp.float32),
        lax.psum(shares[7].astype(jnp.bfloat16), "ctx").astype(jnp.float32),
    )
    gain_total = lax.psum(d_gain, ("dp", "ctx"))
    return (
        mixed[None],
        grad_series[None],
        gain_total,
        jnp.stack(sums[0:3]),
        jnp.stack(sums[3:6]),
        sums[6],
        sums[7],
    )


def solution(mesh):
    placed = (
        P("dp", "ctx", None),
        P(),
        P(None, "dp", None),
        P(None, "dp", None),
        P("dp", None),
        P("dp", None),
        P("dp", "ctx", None, None),
        P("dp", "ctx", None),
    )
    return jax.shard_map(
        body,
        mesh=mesh,
        in_specs=placed,
        out_specs=(
            P("dp", "ctx", None),
            P("dp", "ctx", None),
            P(),
            P(None, "dp", None),
            P(None, "dp", None),
            P("dp", None),
            P("dp", None),
        ),
        check_vma=False,
    )
```

profile of v0, /device:TPU:24, one launch (start us, length us, event | category | flops | bytes accessed | tf_op | source)
XLA Modules:
  0.0 1181.7 jit_solution(14111861011539160384)
XLA Ops:
  11.3 3.5 collective-permute-start
  15.5 19.8 %all_gather.15 = bf16[512,512]{1,0:T(8,128)(2,1)S(1)} all-gather(bf16[32,512]{1,0:T(8,128)(2,1)} %param.18), channel_id=1, replica_groups=mesh['dp'=16,'ctx'=32] {'dp'}, dimensions={0}, use_global_device_ids=true | all-gather | bytes 557056 | tf_op jit(solution)/shard_map/all_gather | solution.py:136
  37.4 23.5 %all_gather.12 = bf16[512,512]{1,0:T(8,128)(2,1)S(1)} all-gather(bf16[32,512]{1,0:T(8,128)(2,1)S(1)} %copy-done.13), channel_id=1, replica_groups=mesh['dp'=16,'ctx'=32] {'dp'}, dimensions={0}, use_global_device_ids=true | all-gather | bytes 557056 | tf_op jit(solution)/shard_map/all_gather | solution.py:135
  61.4 15.5 %all-gather.3.cloned.1.call-done = bf16[3,512,512]{2,1,0:T(8,128)(2,1)} async-done(((bf16[3,32,512]{2,1,0:T(8,128)(2,1)}), bf16[3,512,512]{2,1,0:T(8,128)(2,1)}) %all-gather.3.cloned.1.call-update) | async-done | bytes 1572880 | tf_op jit(solution)/shard_map/all_gather | solution.py:134
  76.9 1.3 fusion.63
  79.5 2.0 constant_dynamic-update-slice_fusion.5
  81.5 7.8 collective-permute-start.4
  89.3 4.5 collective-permute-start.3
  93.8 4.2 collective-permute-start.2
  97.9 3.5 collective-permute-start.1
  101.5 39.4 %all-gather.5.cloned.1.call-done = bf16[3,512,512]{2,1,0:T(8,128)(2,1)} async-done(((bf16[3,32,512]{2,1,0:T(8,128)(2,1)}), bf16[3,512,512]{2,1,0:T(8,128)(2,1)}) %all-gather.5.cloned.1.call-update) | async-done | bytes 1572880 | tf_op jit(solution)/shard_map/all_gather | solution.py:133
  140.8 1.3 fusion.65
  147.6 14.7 %while.28 = (s32[]{:T(128)}, bf16[4,128,128]{1,2,0:T(8,128)(2,1)S(1)}, s32[4]{0:T(128)S(1)}, bf16[640,512]{0,1:T(8,128)(2,1)S(1)}, pred[8,5]{1,0:T(8,128)(4,1)S(...) while((s32[]{:T(128)}, ...), condition=%wide.region_4.5_spmd, body=%wide.region_1.4_spmd.sunk | while | flops 65547144 | bytes 3031067 | solution.py:90
  163.4 41.8 %while.29 = (s32[]{:T(128)}, bf16[4,128,128]{1,2,0:T(8,128)(2,1)S(1)}, f32[4,640,128]{1,2,0:T(8,128)}, f32[4,640,128]{1,2,0:T(8,128)}, s32[4]{0:T(128)S(1)}, /*i...) while((s32[]{:T(128)}, ...), condition=%wide.region_9.10_spmd, body=%wide.region_5.9_spmd.sunk | while | flops 130757248 | bytes 8979319 | solution.py:125
  166.1 1.4 fusion.203
  167.5 2.3 fusion.204
  169.8 2.5 fusion.206
  176.5 1.4 fusion.203
  177.9 2.3 fusion.204
  180.3 2.5 fusion.206
  187.0 1.4 fusion.203
  188.4 2.3 fusion.204
  190.7 2.5 fusion.206
  197.4 1.4 fusion.203
  198.8 2.3 fusion.204
  201.2 2.5 fusion.206
  206.7 1.5 bitcast_convert_fusion
  212.9 1.3 collective-permute-start.6
  223.6 13.0 %collective-permute-done.7 = bf16[128,1024]{1,0:T(8,128)(2,1)S(1)} collective-permute-done((bf16[128,1024]{1,0:T(8,128)(2,1)}, bf16[128,1024]{1,0:T(8,128)(2,1)S(1)}, u32[]{:S(2)}, u32[]{:S(2)}) %collective-permute-start.7) | collective-permute-done | bytes 262176 | tf_op jit(solution)/shard_map/ppermute | solution.py:14
  236.6 25.4 %collective-permute-done.8 = bf16[128,1024]{1,0:T(8,128)(2,1)S(1)} collective-permute-done((bf16[128,1024]{1,0:T(8,128)(2,1)}, bf16[128,1024]{1,0:T(8,128)(2,1)S(1)}, u32[]{:S(2)}, u32[]{:S(2)}) %collective-permute-start.8) | collective-permute-done | bytes 262176 | tf_op jit(solution)/shard_map/ppermute | solution.py:14
  269.0 1.3 collective-permute-start.9
  272.7 1.3 convolution_add_fusion.4
  274.1 3.7 collective-permute-done.9
  278.4 1.4 convolution_add_fusion.2
  280.3 1.5 fusion.73
  281.8 67.3 %reduce-scatter.13.cloned.1.call-done = bf16[32,512]{1,0:T(8,128)(2,1)} async-done(((bf16[512,512]{1,0:T(8,128)(2,1)}), bf16[32,512]{1,0:T(8,128)(2,1)}) %reduce-scatter.13.cloned.1.call-update) | async-done | bytes 32784 | tf_op jit(solution)/shard_map/reduce_scatter | solution.py:203
  349.0 92.1 %reduce-scatter.11.cloned.1.call-done = bf16[32,512]{1,0:T(8,128)(2,1)} async-done(((bf16[512,512]{1,0:T(8,128)(2,1)}), bf16[32,512]{1,0:T(8,128)(2,1)}) %reduce-scatter.11.cloned.1.call-update) | async-done | bytes 32784 | tf_op jit(solution)/shard_map/reduce_scatter | solution.py:200
  441.2 92.9 %reduce-scatter.9.cloned.1.call-done = bf16[32,512]{1,0:T(8,128)(2,1)} async-done(((bf16[512,512]{1,0:T(8,128)(2,1)}), bf16[32,512]{1,0:T(8,128)(2,1)}) %reduce-scatter.9.cloned.1.call-update) | async-done | bytes 32784 | tf_op jit(solution)/shard_map/reduce_scatter | solution.py:197
  534.1 92.3 %reduce-scatter.17.cloned.1.call-done = bf16[32,512]{1,0:T(8,128)(2,1)} async-done(((bf16[512,512]{1,0:T(8,128)(2,1)}), bf16[32,512]{1,0:T(8,128)(2,1)}) %reduce-scatter.17.cloned.1.call-update) | async-done | bytes 32784 | tf_op jit(solution)/shard_map/reduce_scatter | solution.py:209
  626.4 93.0 %reduce-scatter.19.cloned.1.call-done = bf16[32,512]{1,0:T(8,128)(2,1)} async-done(((bf16[512,512]{1,0:T(8,128)(2,1)}), bf16[32,512]{1,0:T(8,128)(2,1)}) %reduce-scatter.19.cloned.1.call-update) | async-done | bytes 32784 | tf_op jit(solution)/shard_map/reduce_scatter | solution.py:212
  719.3 92.3 %reduce-scatter.15.cloned.1.call-done = bf16[32,512]{1,0:T(8,128)(2,1)} async-done(((bf16[512,512]{1,0:T(8,128)(2,1)}), bf16[32,512]{1,0:T(8,128)(2,1)}) %reduce-scatter.15.cloned.1.call-update) | async-done | bytes 32784 | tf_op jit(solution)/shard_map/reduce_scatter | solution.py:206
  811.6 92.9 %reduce-scatter.21.cloned.1.call-done = bf16[32,512]{1,0:T(8,128)(2,1)} async-done(((bf16[512,512]{1,0:T(8,128)(2,1)}), bf16[32,512]{1,0:T(8,128)(2,1)}) %reduce-scatter.21.cloned.1.call-update) | async-done | bytes 32784 | tf_op jit(solution)/shard_map/reduce_scatter | solution.py:215
  904.5 102.1 %psum.63 = f32[512]{0:T(512)} all-reduce(f32[512]{0:T(512)S(1)} %get-tuple-element.267), channel_id=1, replica_groups=mesh['dp'=16,'ctx'=32] {'dp','ctx'}, use_global_device_ids=true, to_apply=%region_12.13 | all-reduce | flops 512 | bytes 4096 | tf_op jit(solution)/shard_map/psum | solution.py:232
  1007.5 161.9 %all-reduce.4.cloned.1.call-done = (bf16[1,32,512]{2,1,0:T(8,128)(2,1)}, bf16[1,32,512]{2,1,0:T(8,128)(2,1)}, bf16[1,32,512]{2,1,0:T(8,128)(2,1)}, bf16[1,32,512...) async-done(((bf16[1,32,512]{2,1,0:T(8,128)(2,1)}, ...) | async-done | bytes 262160 | tf_op jit(solution)/shard_map/psum | solution.py:225
  1169.4 1.4 convert_element_type.183
  1170.8 1.4 convert_element_type.185
  1172.2 1.5 maximum_convert_fusion
  1173.6 1.5 maximum_convert_fusion.1
  (263 shorter events, 62.1 us)
Async XLA Ops:
  7.2 30.2 %copy-start.13 = (bf16[32,512]{1,0:T(8,128)(2,1)S(1)}, bf16[32,512]{1,0:T(8,128)(2,1)}, u32[]{:S(2)}) copy-start(bf16[32,512]{1,0:T(8,128)(2,1)} %param.17) | copy-start | bytes 98308
  7.2 69.7 %all-gather.3.cloned.1.call-start = ((), (), s32[]{:S(2)}) async-start(), calls=%async_computation.8 | async-start | bytes 1671168 | tf_op jit(solution)/shard_map/all_gather | solution.py:134
  7.9 132.9 %all-gather.5.cloned.1.call-start = ((), (), s32[]{:S(2)}) async-start(), calls=%async_computation.9 | async-start | bytes 1671168 | tf_op jit(solution)/shard_map/all_gather | solution.py:133
  8.7 273.1 %reduce-scatter.23.cloned.1.call-start = ((), (), s32[]{:S(2)}) async-start(), calls=%async_computation.17 | async-start | bytes 557056 | tf_op jit(solution)/shard_map/reduce_scatter | solution.py:218
  9.7 0.5 copy-start.15
  9.7 51.4 %copy-start.14 = (s32[1,1,8,4]{2,3,1,0:T(4,128)S(1)}, s32[1,1,8,4]{2,3,1,0:T(4,128)}, u32[]{:S(2)}) copy-start(s32[1,1,8,4]{2,3,1,0:T(4,128)} %param.19) | copy-start | bytes 388
  11.2 65.7 %copy-start = (bf16[1,128,512]{2,1,0:T(8,128)(2,1)S(1)}, bf16[1,128,512]{2,1,0:T(8,128)(2,1)}, u32[]{:S(2)}) copy-start(bf16[1,128,512]{2,1,0:T(8,128)(2,1)} %param.13) | copy-start | bytes 393220
  11.3 65.6 %copy-start.12 = (f32[512]{0:T(512)S(1)}, f32[512]{0:T(512)}, u32[]{:S(2)}) copy-start(f32[512]{0:T(512)} %param.14) | copy-start | bytes 6148
  11.3 50.1 %collective-permute-start = (bf16[2,512]{1,0:T(2,128)(2,1)S(1)}, bf16[2,512]{1,0:T(2,128)(2,1)S(1)}, u32[]{:S(2)}, u32[]{:S(2)}) collective-permute-start(bf16[2,512]{1,0:T(2,128)(2,1)S(1)} %slice.216), channel_id=1, source_target_pairs={{0,1},{1,2},{2,3},{3,4},{4,5},{5,6},{6,7},{7,8},{8,9},{9,10},{10,1... | collective-permute-start | bytes 6152 | tf_op jit(solution)/shard_map/ppermute | solution.py:14
  35.3 0.8 copy-start.4
  60.9 18.6 %copy-start.2 = (bf16[512,512]{1,0:T(8,128)(2,1)}, bf16[512,512]{1,0:T(8,128)(2,1)S(1)}, u32[]{:S(2)}) copy-start(bf16[512,512]{1,0:T(8,128)(2,1)S(1)} %all_gather.12) | copy-start | bytes 1572868
  81.5 63.4 %copy-start.9 = (bf16[640,512]{1,0:T(8,128)(2,1)S(1)}, bf16[640,512]{1,0:T(8,128)(2,1)}, u32[]{:S(2)}) copy-start(bf16[640,512]{1,0:T(8,128)(2,1)} %get-tuple-element.335) | copy-start | bytes 1966084
  81.5 65.4 %collective-permute-start.4 = (bf16[128,1024]{1,0:T(8,128)(2,1)S(1)}, bf16[128,1024]{1,0:T(8,128)(2,1)S(1)}, u32[]{:S(2)}, u32[]{:S(2)}) collective-permute-start(bf16[128,1024]{1,0:T(8,128)(2,1)S(1)} %pad_maximum_fusion), channel_id=1, source_target_pairs={{0,8},{1,9},{2,10},{3,11},{4,12},{5,13},{6,14},{7,15},{8,16},{9,17... | collective-permute-start | bytes 786440 | tf_op jit(solution)/shard_map/ppermute | solution.py:14
  89.3 57.6 %collective-permute-start.3 = (bf16[128,1024]{1,0:T(8,128)(2,1)S(1)}, bf16[128,1024]{1,0:T(8,128)(2,1)S(1)}, u32[]{:S(2)}, u32[]{:S(2)}) collective-permute-start(bf16[128,1024]{1,0:T(8,128)(2,1)S(1)} %pad_maximum_fusion), channel_id=1, source_target_pairs={{0,4},{1,5},{2,6},{3,7},{4,8},{5,9},{6,10},{7,11},{8,12},{9,13},{1... | collective-permute-start | bytes 786440 | tf_op jit(solution)/shard_map/ppermute | solution.py:14
  93.8 52.1 %collective-permute-start.2 = (bf16[128,1024]{1,0:T(8,128)(2,1)S(1)}, bf16[128,1024]{1,0:T(8,128)(2,1)}, u32[]{:S(2)}, u32[]{:S(2)}) collective-permute-start(bf16[128,1024]{1,0:T(8,128)(2,1)S(1)} %pad_maximum_fusion), channel_id=1, source_target_pairs={{0,2},{1,3},{2,4},{3,5},{4,6},{5,7},{6,8},{7,9},{8,10},{9,11},{10,... | collective-permute-start | bytes 786440 | tf_op jit(solution)/shard_map/ppermute | solution.py:14
  97.9 46.9 %collective-permute-start.1 = (bf16[128,1024]{1,0:T(8,128)(2,1)S(1)}, bf16[128,1024]{1,0:T(8,128)(2,1)}, u32[]{:S(2)}, u32[]{:S(2)}) collective-permute-start(bf16[128,1024]{1,0:T(8,128)(2,1)S(1)} %pad_maximum_fusion), channel_id=1, source_target_pairs={{0,1},{1,2},{2,3},{3,4},{4,5},{5,6},{6,7},{7,8},{8,9},{9,10},{10,1... | collective-permute-start | bytes 786440 | tf_op jit(solution)/shard_map/ppermute | solution.py:14
  147.6 14.7 %copy-start.7 = (bf16[1,128,512]{2,1,0:T(8,128)(2,1)S(1)}, bf16[1,128,512]{2,1,0:T(8,128)(2,1)}, u32[]{:S(2)}) copy-start(bf16[1,128,512]{2,1,0:T(8,128)(2,1)} %param.20) | copy-start | bytes 393220
  163.3 185.7 %reduce-scatter.13.cloned.1.call-start = ((), (), s32[]{:S(2)}) async-start(), calls=%async_computation.12 | async-start | bytes 557056 | tf_op jit(solution)/shard_map/reduce_scatter | solution.py:203
  163.4 2.3 copy-start.10
  172.3 1.6 copy-start.11
  173.9 2.3 copy-start.10
  182.7 1.6 copy-start.11
  184.4 2.3 copy-start.10
  193.2 1.6 copy-start.11
  194.8 2.3 copy-start.10
  203.6 1.6 copy-start.11
  205.3 1.4 copy-start.6
  206.4 234.8 %reduce-scatter.11.cloned.1.call-start = ((), (), s32[]{:S(2)}) async-start(), calls=%async_computation.11 | async-start | bytes 557056 | tf_op jit(solution)/shard_map/reduce_scatter | solution.py:200
  209.9 324.1 %reduce-scatter.9.cloned.1.call-start = ((), (), s32[]{:S(2)}) async-start(), calls=%async_computation.10 | async-start | bytes 557056 | tf_op jit(solution)/shard_map/reduce_scatter | solution.py:197
  212.9 10.7 collective-permute-start.6
  214.9 21.7 %collective-permute-start.7 = (bf16[128,1024]{1,0:T(8,128)(2,1)}, bf16[128,1024]{1,0:T(8,128)(2,1)S(1)}, u32[]{:S(2)}, u32[]{:S(2)}) collective-permute-start(bf16[128,1024]{1,0:T(8,128)(2,1)} %pad_maximum_fusion.3), channel_id=1, source_target_pairs={{4,0},{5,1},{6,2},{7,3},{8,4},{9,5},{10,6},{11,7},{12,8},{13,9},{1... | collective-permute-start | bytes 786440 | tf_op jit(solution)/shard_map/ppermute | solution.py:14
  217.0 45.0 %collective-permute-start.8 = (bf16[128,1024]{1,0:T(8,128)(2,1)}, bf16[128,1024]{1,0:T(8,128)(2,1)S(1)}, u32[]{:S(2)}, u32[]{:S(2)}) collective-permute-start(bf16[128,1024]{1,0:T(8,128)(2,1)} %pad_maximum_fusion.4), channel_id=1, source_target_pairs={{8,0},{9,1},{10,2},{11,3},{12,4},{13,5},{14,6},{15,7},{16,8},{17,9... | collective-permute-start | bytes 786440 | tf_op jit(solution)/shard_map/ppermute | solution.py:14
  219.5 406.9 %reduce-scatter.17.cloned.1.call-start = ((), (), s32[]{:S(2)}) async-start(), calls=%async_computation.14 | async-start | bytes 557056 | tf_op jit(solution)/shard_map/reduce_scatter | solution.py:209
  220.3 41.8 %collective-permute-start.5 = (bf16[128,1024]{1,0:T(8,128)(2,1)}, bf16[128,1024]{1,0:T(8,128)(2,1)S(1)}, u32[]{:S(2)}, u32[]{:S(2)}) collective-permute-start(bf16[128,1024]{1,0:T(8,128)(2,1)} %pad_maximum_fusion.1), channel_id=1, source_target_pairs={{1,0},{2,1},{3,2},{4,3},{5,4},{6,5},{7,6},{8,7},{9,8},{10,9},{11,1... | collective-permute-start | bytes 786440 | tf_op jit(solution)/shard_map/ppermute | solution.py:14
  264.3 2.5 copy-start.1
  264.3 455.0 %reduce-scatter.19.cloned.1.call-start = ((), (), s32[]{:S(2)}) async-start(), calls=%async_computation.15 | async-start | bytes 557056 | tf_op jit(solution)/shard_map/reduce_scatter | solution.py:212
  265.5 2.5 copy-start.5
  265.5 546.1 %reduce-scatter.15.cloned.1.call-start = ((), (), s32[]{:S(2)}) async-start(), calls=%async_computation.13 | async-start | bytes 557056 | tf_op jit(solution)/shard_map/reduce_scatter | solution.py:206
  266.8 4.6 copy-start.3
  266.8 637.7 %reduce-scatter.21.cloned.1.call-start = ((), (), s32[]{:S(2)}) async-start(), calls=%async_computation.16 | async-start | bytes 557056 | tf_op jit(solution)/shard_map/reduce_scatter | solution.py:215
  269.0 8.8 collective-permute-start.9
  272.7 896.7 %all-reduce.4.cloned.1.call-start = ((), (), s32[]{:S(2)}) async-start(), calls=%async_computation.18 | async-start | bytes 524288 | tf_op jit(solution)/shard_map/psum | solution.py:225
  279.8 624.7 %copy-start.16 = (f32[128]{0:T(128)S(1)}, f32[128]{0:T(128)}, u32[]{:S(2)}) copy-start(f32[128]{0:T(128)} %copy-done.15) | copy-start | bytes 1540
  279.8 726.8 %copy-start.8 = (bf16[1,128,512]{2,1,0:T(8,128)(2,1)S(1)}, bf16[1,128,512]{2,1,0:T(8,128)(2,1)}, u32[]{:S(2)}) copy-start(bf16[1,128,512]{2,1,0:T(8,128)(2,1)} %param.20) | copy-start | bytes 393220
Sparse Core Ops, SparseCore 0:
  11.4 65.4 all-gather.2
  80.3 60.5 all-gather.4
  163.5 92.6 reduce-scatter.22
  261.3 87.7 reduce-scatter.12
  353.5 87.6 reduce-scatter.10
  446.3 87.7 reduce-scatter.8
  538.6 87.6 reduce-scatter.16
  631.6 87.6 reduce-scatter.18
  723.9 87.6 reduce-scatter.14
  816.7 87.7 reduce-scatter.20
  908.0 261.3 all-reduce.3
where the time goes:
time: 1180 us
  waiting for transfers between devices  884 us (75%)
  blocking collectives  145 us (12%)
  matrix products  61.7 us (5%)
  starting transfers between devices  30.3 us (3%)
  local copies, waits for them, and re-layouts  18.9 us (2%)
  other arithmetic  15.6 us (1%)
  between operations  14.5 us (1%)
    psum x1, waiting for transfers between devices, body(): lax.psum(shares[2].astype(jnp.bfloat16), 'ctx').astype(jnp.float32)  162 us
    psum x1, blocking collectives, body(): gain_total = lax.psum(d_gain, ('dp', 'ctx'))  102 us
    reduce_scatter x1, waiting for transfers between devices, body(): lax.psum_scatter(key_grads[2].astype(jnp.bfloat16), 'dp', scatter_dimensi...  93 us
    reduce_scatter x1, waiting for transfers between devices, body(): lax.psum_scatter(query_terms[0].astype(jnp.bfloat16), 'dp', scatter_dimen...  92.9 us
    reduce_scatter x1, waiting for transfers between devices, body(): lax.psum_scatter(value_term.astype(jnp.bfloat16), 'dp', scatter_dimension...  92.9 us
    reduce_scatter x1, waiting for transfers between devices, body(): lax.psum_scatter(key_grads[1].astype(jnp.bfloat16), 'dp', scatter_dimensi...  92.3 us
    reduce_scatter x1, waiting for transfers between devices, body(): lax.psum_scatter(key_grads[0].astype(jnp.bfloat16), 'dp', scatter_dimensi...  92.3 us
    reduce_scatter x1, waiting for transfers between devices, body(): lax.psum_scatter(query_terms[1].astype(jnp.bfloat16), 'dp', scatter_dimen...  92.1 us
  transfers between devices with their start and end apart: 21, of which 14 were waited for; matrix products, arithmetic and copies ran while one was open for 7% of the time, Pallas kernels for 0%

commit v1 on v0

v1 whole, which is shorter than its diff:
```python
import jax
import jax.numpy as jnp
from jax import lax
from jax.sharding import PartitionSpec as P

block_offsets = (1, 2, 4, 8)
epsilon = 1e-06
f32 = jnp.float32
bf16 = jnp.bfloat16


def shift_ctx(shard, by):
    devices = lax.axis_size("ctx")
    pairs = [(i, i + by) for i in range(devices) if 0 <= i + by < devices]
    return lax.ppermute(shard, "ctx", pairs)


def dp_to(shard, dx, dy, dc):
    def target(i):
        x, y, c = i // 8, (i // 2) % 4, i % 2
        return ((x + dx) % 2) * 8 + ((y + dy) % 4) * 2 + (c + dc) % 2

    return lax.ppermute(shard, "dp", [(i, target(i)) for i in range(16)])


def normalize(values, norm_gain):
    scale = lax.rsqrt(jnp.mean(values * values, axis=-1, keepdims=True) + epsilon)
    return values * scale * norm_gain


def product(left, right):
    return jnp.dot(left, right, preferred_element_type=f32)


def product_right_t(left, right):
    return lax.dot_general(left, right, (((1,), (1,)), ((), ())), preferred_element_type=f32)


def product_left_t(left, right):
    return lax.dot_general(left, right, (((0,), (0,)), ((), ())), preferred_element_type=f32)


def take(array, index, axis):
    return lax.dynamic_index_in_dim(array, index, axis, keepdims=False)


def in_place(mine, other, place, axis):
    return jnp.where(
        place == 0, jnp.stack([mine, other], axis), jnp.stack([other, mine], axis)
    )


def unroll_y(pieces, y, axis):
    order = [pieces[0], pieces[3], pieces[2], pieces[1]]
    twice = jnp.stack(order + order, axis)
    return lax.dynamic_slice_in_dim(twice, (4 - y) % 4, 4, axis)


def gather_weights(shard, x, y, core):
    first, second = shard[:4], shard[4:]
    second_y = [second] + [dp_to(second, 0, r, 0) for r in (1, 2, 3)]
    first_x = in_place(first, dp_to(first, 1, 0, 0), x, 0)
    first_xy = unroll_y([first_x] + [dp_to(first_x, 0, r, 0) for r in (1, 2, 3)], y, 1)
    second_yy = unroll_y(second_y, y, 0)
    second_xy = in_place(second_yy, dp_to(second_yy, 1, 0, 0), x, 0)
    result = []
    for part in (first_xy, second_xy):
        whole = in_place(part, dp_to(part, 0, 0, 1), core, 2)
        whole = jnp.transpose(whole, (3, 0, 1, 2, 4, 5))
        result.append(whole.reshape(4, 512, 512))
    return result


def total(parts):
    result = parts[0].astype(f32)
    for part in parts[1:]:
        result = result + part.astype(f32)
    return result.astype(bf16)


def spread(array, x_or_y, axis):
    return [take(array, (x_or_y + r) % 4, axis) for r in range(4)]


def scatter_partials(terms, x, y, core):
    kept = take(terms, core, 2)
    half = total([kept, dp_to(take(terms, 1 - core, 2), 0, 0, 1)])
    first, second = half[:, :, :128], half[:, :, 128:]
    out_y = spread(second, y, 1)
    second = total([out_y[0]] + [dp_to(out_y[r], 0, r, 0) for r in (1, 2, 3)])
    first = total([take(first, x, 0), dp_to(take(first, 1 - x, 0), 1, 0, 0)])
    out_y = spread(first, y, 0)
    first = total([out_y[0]] + [dp_to(out_y[r], 0, r, 0) for r in (1, 2, 3)])
    second = total([take(second, x, 0), dp_to(take(second, 1 - x, 0), 1, 0, 0)])
    return jnp.concatenate([first, second], axis=0)


def heads_of(array, heads):
    return array.reshape(array.shape[:-1] + (heads, array.shape[-1] // heads))


def body(
    series, norm_gain, query_kernel, key_kernel, value_weight, out_weight, block_links, grad_out
):
    place = lax.axis_index("dp")
    x, y, core = place // 8, (place // 2) % 4, place % 2
    block = lax.axis_index("ctx")
    heads = block_links.shape[2]
    own = series[0]
    cotangent = grad_out[0]
    count, features = own.shape
    width = features // heads
    scaling = width ** (-0.5)

    halo = shift_ctx(own[count - 2 :], 1)
    window = jnp.concatenate([halo, own], axis=0)
    carried = jnp.concatenate([window, cotangent], axis=0)
    shard = jnp.concatenate(
        [key_kernel, value_weight[None], query_kernel, out_weight[None]], axis=0
    )
    early, late = gather_weights(shard, x, y, core)
    full_key, full_value, full_query, full_out = early[:3], early[3], late[:3], late[3]
    before = [shift_ctx(window, offset) for offset in block_offsets]
    after = [shift_ctx(carried, -offset) for offset in block_offsets]

    key_windows = normalize(jnp.stack([window] + before).astype(f32), norm_gain).astype(bf16)
    query_windows = normalize(
        jnp.stack([window] + [piece[: count + 2] for piece in after]).astype(f32), norm_gain
    ).astype(bf16)
    uppers = jnp.stack([cotangent] + [piece[count + 2 :] for piece in after])

    def convolve(windows, kernel):
        result = product(windows[:, 2 : 2 + count], kernel[0])
        result = result + product(windows[:, 1 : 1 + count], kernel[1])
        return (result + product(windows[:, 0:count], kernel[2])).astype(bf16)

    keys = heads_of(convolve(key_windows, full_key), heads)
    values = heads_of(product(key_windows[:, 2:], full_value).astype(bf16), heads)
    queries = heads_of(convolve(query_windows, full_query), heads)
    upstream = heads_of(
        lax.dot_general(
            uppers, full_out, (((2,), (1,)), ((), ())), preferred_element_type=f32
        ).astype(bf16),
        heads,
    )

    offsets = jnp.array(block_offsets, dtype=jnp.int32)
    reach = (block_links[0, 0] > 0) & (block >= offsets)[None, :]
    allowed = jnp.concatenate([jnp.ones((heads, 1), jnp.bool_), reach], axis=1)
    row = lax.broadcasted_iota(jnp.int32, (count, 5, count), 0)
    slot = lax.broadcasted_iota(jnp.int32, (count, 5, count), 1)
    column = lax.broadcasted_iota(jnp.int32, (count, 5, count), 2)
    visible = ((slot > 0) | (column <= row))[None] & allowed[:, None, :, None]

    query, upper = queries[0], upstream[0]
    scores = jnp.einsum("thd,kuhd->htku", query, keys, preferred_element_type=f32) * scaling
    scores = jnp.where(visible, scores, -1e30)
    highest = jnp.max(scores, axis=(2, 3), keepdims=True)
    weights = jnp.where(visible, jnp.exp(scores - highest), 0.0)
    inverse = 1.0 / jnp.sum(weights, axis=(2, 3), keepdims=True)
    probs = weights * inverse
    probs_low = probs.astype(bf16)
    d_prob = jnp.einsum("thd,kuhd->htku", upper, values, preferred_element_type=f32)
    centre = jnp.sum(probs * d_prob, axis=(2, 3), keepdims=True)
    statistics = [
        jnp.concatenate(
            [
                jnp.where(reach[:, i][:, None], highest[:, :, 0, 0], 1e30),
                inverse[:, :, 0, 0],
                centre[:, :, 0, 0],
            ],
            axis=0,
        )
        for i in range(4)
    ]
    returned = [shift_ctx(statistics[i], -block_offsets[i]) for i in range(4)]
    attn = jnp.einsum("htku,kuhd->thd", probs_low, values, preferred_element_type=f32)
    attn = attn.reshape(count, features).astype(bf16)
    mixed = (own.astype(f32) + product(attn, full_out)).astype(bf16)
    d_score = (probs * (d_prob - centre) * scaling).astype(bf16)
    d_query = jnp.einsum("htku,kuhd->thd", d_score, keys, preferred_element_type=f32)
    d_query = d_query.reshape(count, features).astype(bf16)
    d_key = jnp.einsum("htu,thd->uhd", d_score[:, :, 0], query, preferred_element_type=f32)
    d_value = jnp.einsum("htu,thd->uhd", probs_low[:, :, 0], upper, preferred_element_type=f32)

    stacked = jnp.stack(returned).reshape(4, 3, heads, count)
    scores = jnp.einsum("kthd,uhd->khtu", queries[1:], keys[0], preferred_element_type=f32)
    probs = jnp.exp(scores * scaling - stacked[:, 0][..., None]) * stacked[:, 1][..., None]
    d_prob = jnp.einsum("kthd,uhd->khtu", upstream[1:], values[0], preferred_element_type=f32)
    d_score = (probs * (d_prob - stacked[:, 2][..., None]) * scaling).astype(bf16)
    d_key = d_key + jnp.einsum("khtu,kthd->uhd", d_score, queries[1:], preferred_element_type=f32)
    d_value = d_value + jnp.einsum(
        "khtu,kthd->uhd", probs.astype(bf16), upstream[1:], preferred_element_type=f32
    )
    d_key = d_key.reshape(count, features).astype(bf16)
    d_value = d_value.reshape(count, features).astype(bf16)

    leading = shift_ctx(jnp.concatenate([d_query[:2], d_key[:2]], axis=1), -1)
    base = key_windows[0]
    terms = [product_left_t(base[2 - tap : 2 - tap + count], d_key) for tap in range(3)]
    terms = terms + [product_left_t(base[2:], d_value)]
    terms = terms + [product_left_t(base[2 - tap : 2 - tap + count], d_query) for tap in range(3)]
    terms = terms + [product_left_t(attn, cotangent)]
    terms = jnp.stack([term.astype(bf16).reshape(16, 32, features) for term in terms], axis=1)
    rows = scatter_partials(terms.reshape(2, 4, 2, 256, features), x, y, core)

    after_query = jnp.concatenate([d_query, leading[:, :features]], axis=0)
    after_key = jnp.concatenate([d_key, leading[:, features:]], axis=0)
    d_normed = product_right_t(d_value, full_value)
    for tap in range(3):
        d_normed = d_normed + product_right_t(after_query[tap : tap + count], full_query[tap])
        d_normed = d_normed + product_right_t(after_key[tap : tap + count], full_key[tap])
    unused, pull = jax.vjp(normalize, own.astype(f32), norm_gain)
    d_values, d_gain = pull(d_normed)
    grad_series = (cotangent.astype(f32) + d_values).astype(bf16)
    for step in ((0, 0, 1), (0, 2, 0), (1, 0, 0)):
        d_gain = d_gain + dp_to(d_gain, *step)
    d_gain = d_gain + lax.ppermute(d_gain, "dp", [(i, i ^ 2) for i in range(16)])

    top = d_gain.astype(bf16)
    middle = (d_gain - top.astype(f32)).astype(bf16)
    low = (d_gain - top.astype(f32) - middle.astype(f32)).astype(bf16)
    extra = jnp.concatenate(
        [jnp.stack([top, middle, low]), jnp.zeros((5, features), bf16)], axis=0
    )
    payload = jnp.concatenate(
        [rows.reshape(32, 8, features), jnp.broadcast_to(extra[None], (32, 8, features))], axis=1
    )
    arrived = lax.all_to_all(payload, "ctx", 0, 0, tiled=True).astype(f32)
    gain_total = jnp.sum(arrived[:, 8:11], axis=(0, 1))
    summed = jnp.sum(arrived[:, :8], axis=0).astype(bf16)
    final = lax.all_to_all(
        jnp.broadcast_to(summed[None], (32, 8, features)), "ctx", 0, 0, tiled=True
    )
    final = final.reshape(8, 32, features).astype(f32)
    return (mixed[None], grad_series[None], gain_total, final[4:7], final[:3], final[3], final[7])


def solution(mesh):
    placed = (
        P("dp", "ctx", None),
        P(),
        P(None, "dp", None),
        P(None, "dp", None),
        P("dp", None),
        P("dp", None),
        P("dp", "ctx", None, None),
        P("dp", "ctx", None),
    )
    return jax.shard_map(
        body,
        mesh=mesh,
        in_specs=placed,
        out_specs=(
            P("dp", "ctx", None),
            P("dp", "ctx", None),
            P(),
            P(None, "dp", None),
            P(None, "dp", None),
            P("dp", None),
            P("dp", None),
        ),
        check_vma=False,
    )
```

time: 1180 us -> 335 us (0.28)
  waiting for transfers between devices: 884 us -> 90.3 us
  blocking collectives: 145 us -> 39.8 us
  starting transfers between devices: 30.3 us -> 116 us
  matrix products: 61.7 us -> 26.1 us
  local copies, waits for them, and re-layouts: 18.9 us -> 33.7 us
  between operations: 14.5 us -> 2.66 us
    reduce_scatter x8 -> x0, waiting for transfers between devices: 623 us -> none  [the longest x1 93 us: body(): lax.psum_scatter(key_grads[2].astype(jnp.bfloat16), 'dp', scatter_dimensi...]
    psum x1 -> x0, waiting for transfers between devices: 162 us -> none  [body(): lax.psum(shares[2].astype(jnp.bfloat16), 'ctx').astype(jnp.float32)]
    psum x1 -> x0, blocking collectives: 102 us -> none  [body(): gain_total = lax.psum(d_gain, ('dp', 'ctx'))]
    ppermute x10 -> x37, starting transfers between devices: 29.9 us -> 112 us  [the longest x22 72.2 us: dp_to(): return lax.ppermute(shard, 'dp', [(i, target(i)) for i in range(16)])]
    all_gather x2 -> x0, waiting for transfers between devices: 54.9 us -> none  [the longest x1 39.4 us: body(): lax.all_gather(query_kernel, 'dp', axis=1, tiled=True)]
    all_gather x2 -> x0, blocking collectives: 43.3 us -> none  [the longest x1 23.5 us: body(): lax.all_gather(value_weight, 'dp', axis=0, tiled=True)]
    all_to_all x0 -> x1, blocking collectives: none -> 39.8 us  [body(): arrived = lax.all_to_all(payload, 'ctx', 0, 0, tiled=True).astype(f32)]
    ppermute x10 -> x37, waiting for transfers between devices: 42.9 us -> 75 us  [the longest x14 50 us: shift_ctx(): return lax.ppermute(shard, 'ctx', pairs)]
  transfers between devices with their start and end apart: 21 -> 38, of which waited for: 14 -> 16; matrix products, arithmetic and copies ran while one was open for 7% -> 13% of each run, Pallas kernels for 0% -> 0%
where the time goes in v1:
time: 335 us; the launch traced here: 329 us
  starting transfers between devices  116 us (35%)
  waiting for transfers between devices  90.3 us (27%)
  blocking collectives  39.8 us (12%)
  local copies, waits for them, and re-layouts  33.7 us (10%)
  matrix products  26.1 us (8%)
  other arithmetic  20.6 us (6%)
    ppermute x22, starting transfers between devices, dp_to(): return lax.ppermute(shard, 'dp', [(i, target(i)) for i in range(16)])  72.2 us
    ppermute x14, waiting for transfers between devices, shift_ctx(): return lax.ppermute(shard, 'ctx', pairs)  50 us
    all_to_all x1, blocking collectives, body(): arrived = lax.all_to_all(payload, 'ctx', 0, 0, tiled=True).astype(f32)  39.8 us
    ppermute x14, starting transfers between devices, shift_ctx(): return lax.ppermute(shard, 'ctx', pairs)  36.4 us
    ppermute x22, waiting for transfers between devices, dp_to(): return lax.ppermute(shard, 'dp', [(i, target(i)) for i in range(16)])  23.3 us
    all_to_all x1, waiting for transfers between devices, body(): lax.all_to_all(jnp.broadcast_to(summed[None], (32, 8, features)), 'ctx',...  15.3 us
    unnamed x124, local copies, waits for them, and re-layouts  9.59 us
    dot_general x8, matrix products, product_left_t(): lax.dot_general(left, right, (((0,), (0,)), ((), ())), preferred_element_...  7.6 us
  transfers between devices with their start and end apart: 38, of which 16 were waited for; matrix products, arithmetic and copies ran while one was open for 13% of the time, Pallas kernels for 0%

profile of v1, /device:TPU:24, one launch (start us, length us, event | category | flops | bytes accessed | tf_op | source)
XLA Modules:
  0.0 329.2 jit_solution(11897891580920025618)
XLA Ops:
  1.6 3.1 collective-permute-start.15
  4.8 7.1 %collective-permute-start.14 = (bf16[4,32,512]{2,1,0:T(8,128)(2,1)S(1)}, bf16[4,32,512]{2,1,0:T(8,128)(2,1)S(1)}, u32[]{:S(2)}, u32[]{:S(2)}) collective-permute-start(bf16[4,32,512]{2,1,0:T(8,128)(2,1)S(1)} %pad_maximum_fusion.10), channel_id=1, source_target_pairs={{0,192},{32,224},{64,0},{96,32},{128,64},{160,96},{192,128},{224,1... | collective-permute-start | bytes 393224 | tf_op jit(solution)/shard_map/ppermute | solution.py:23
  11.9 1.9 collective-permute-start.16
  16.9 4.8 %collective-permute-start.5 = (bf16[4,32,512]{2,1,0:T(8,128)(2,1)S(1)}, bf16[4,32,512]{2,1,0:T(8,128)(2,1)S(1)}, u32[]{:S(2)}, u32[]{:S(2)}) collective-permute-start(bf16[4,32,512]{2,1,0:T(8,128)(2,1)S(1)} %get-tuple-element.35), channel_id=1, source_target_pairs={{0,256},{32,288},{64,320},{96,352},{128,384},{160,416},{192,448},{... | collective-permute-start | bytes 393224 | tf_op jit(solution)/shard_map/ppermute | solution.py:23
  29.1 5.2 %collective-permute-start.3 = (bf16[130,512]{1,0:T(8,128)(2,1)S(1)}, bf16[130,512]{1,0:T(8,128)(2,1)S(1)}, u32[]{:S(2)}, u32[]{:S(2)}) collective-permute-start(bf16[130,512]{1,0:T(8,128)(2,1)S(1)} %pad_maximum_fusion.4), channel_id=1, source_target_pairs={{0,4},{1,5},{2,6},{3,7},{4,8},{5,9},{6,10},{7,11},{8,12},{9,13},{1... | collective-permute-start | bytes 399368 | tf_op jit(solution)/shard_map/ppermute | solution.py:15
  35.3 3.8 %collective-permute-start.2 = (bf16[130,512]{1,0:T(8,128)(2,1)S(1)}, bf16[130,512]{1,0:T(8,128)(2,1)S(1)}, u32[]{:S(2)}, u32[]{:S(2)}) collective-permute-start(bf16[130,512]{1,0:T(8,128)(2,1)S(1)} %pad_maximum_fusion.4), channel_id=1, source_target_pairs={{0,2},{1,3},{2,4},{3,5},{4,6},{5,7},{6,8},{7,9},{8,10},{9,11},{10,... | collective-permute-start | bytes 399368 | tf_op jit(solution)/shard_map/ppermute | solution.py:15
  39.2 4.7 %collective-permute-start.1 = (bf16[130,512]{1,0:T(8,128)(2,1)S(1)}, bf16[130,512]{1,0:T(8,128)(2,1)S(1)}, u32[]{:S(2)}, u32[]{:S(2)}) collective-permute-start(bf16[130,512]{1,0:T(8,128)(2,1)S(1)} %pad_maximum_fusion.4), channel_id=1, source_target_pairs={{0,1},{1,2},{2,3},{3,4},{4,5},{5,6},{6,7},{7,8},{8,9},{9,10},{10,1... | collective-permute-start | bytes 399368 | tf_op jit(solution)/shard_map/ppermute | solution.py:15
  43.9 9.1 %collective-permute-start.4 = (bf16[130,512]{1,0:T(8,128)(2,1)S(1)}, bf16[130,512]{1,0:T(8,128)(2,1)S(1)}, u32[]{:S(2)}, u32[]{:S(2)}) collective-permute-start(bf16[130,512]{1,0:T(8,128)(2,1)S(1)} %pad_maximum_fusion.4), channel_id=1, source_target_pairs={{0,8},{1,9},{2,10},{3,11},{4,12},{5,13},{6,14},{7,15},{8,16},{9,17... | collective-permute-start | bytes 399368 | tf_op jit(solution)/shard_map/ppermute | solution.py:15
  59.0 2.9 collective-permute-start.8
  62.2 3.8 %collective-permute-done.10 = bf16[258,512]{1,0:T(8,128)(2,1)S(1)} collective-permute-done((bf16[258,512]{1,0:T(8,128)(2,1)S(1)}, bf16[258,512]{1,0:T(8,128)(2,1)S(1)}, u32[]{:S(2)}, u32[]{:S(2)}) %collective-permute-start.10) | collective-permute-done | bytes 264224 | tf_op jit(solution)/shard_map/ppermute | solution.py:15
  66.0 3.0 collective-permute-start.7
  69.1 2.7 collective-permute-start.6
  71.9 5.5 %collective-permute-done.12 = bf16[258,512]{1,0:T(8,128)(2,1)S(1)} collective-permute-done((bf16[258,512]{1,0:T(8,128)(2,1)S(1)}, bf16[258,512]{1,0:T(8,128)(2,1)S(1)}, u32[]{:S(2)}, u32[]{:S(2)}) %collective-permute-start.12) | collective-permute-done | bytes 264224 | tf_op jit(solution)/shard_map/ppermute | solution.py:15
  77.4 3.6 %collective-permute-start.17 = (bf16[4,4,32,512]{3,2,1,0:T(8,128)(2,1)S(1)}, bf16[4,4,32,512]{3,2,1,0:T(8,128)(2,1)S(1)}, u32[]{:S(2)}, u32[]{:S(2)}) collective-permute-start(bf16[4,4,32,512]{3,2,1,0:T(8,128)(2,1)S(1)} %constant_dynamic-slice_fusion), channel_id=1, source_target_pairs={{0,256},{32,288},{64,320},{96,352},{128,384},{160,416},{192,448},{... | collective-permute-start | bytes 1572872 | tf_op jit(solution)/shard_map/ppermute | solution.py:23
  81.1 3.4 %collective-permute-done.13 = bf16[258,512]{1,0:T(8,128)(2,1)S(1)} collective-permute-done((bf16[258,512]{1,0:T(8,128)(2,1)S(1)}, bf16[258,512]{1,0:T(8,128)(2,1)S(1)}, u32[]{:S(2)}, u32[]{:S(2)}) %collective-permute-start.13) | collective-permute-done | bytes 264224 | tf_op jit(solution)/shard_map/ppermute | solution.py:15
  85.5 1.9 collective-permute-start.9
  87.9 4.4 %collective-permute-done.17 = bf16[4,4,32,512]{3,2,1,0:T(8,128)(2,1)S(1)} collective-permute-done((bf16[4,4,32,512]{3,2,1,0:T(8,128)(2,1)S(1)}, bf16[4,4,32,512]{3,2,1,0:T(8,128)(2,1)S(1)}, u32[]{:S(2)}, u32[]{:S(2)}) %collective-permute-start.17) | collective-permute-done | bytes 524320 | tf_op jit(solution)/shard_map/ppermute | solution.py:23
  93.4 2.1 collective-permute-start.18
  98.8 2.2 copy.94
  105.7 2.2 copy.105
  109.4 1.9 fusion.3
  119.6 2.1 fusion.1
  141.0 7.7 %collective-permute-done.20 = f32[24,128]{1,0:T(8,128)S(1)} collective-permute-done((f32[24,128]{1,0:T(8,128)S(1)}, f32[24,128]{1,0:T(8,128)S(1)}, u32[]{:S(2)}, u32[]{:S(2)}) %collective-permute-start.20) | collective-permute-done | bytes 12320 | tf_op jit(solution)/shard_map/ppermute | solution.py:15
  148.7 13.3 %collective-permute-done.21 = f32[24,128]{1,0:T(8,128)S(1)} collective-permute-done((f32[24,128]{1,0:T(8,128)S(1)}, f32[24,128]{1,0:T(8,128)S(1)}, u32[]{:S(2)}, u32[]{:S(2)}) %collective-permute-start.21) | collective-permute-done | bytes 12320 | tf_op jit(solution)/shard_map/ppermute | solution.py:15
  162.0 16.2 %collective-permute-done.22 = f32[24,128]{1,0:T(8,128)S(1)} collective-permute-done((f32[24,128]{1,0:T(8,128)S(1)}, f32[24,128]{1,0:T(8,128)S(1)}, u32[]{:S(2)}, u32[]{:S(2)}) %collective-permute-start.22) | collective-permute-done | bytes 12320 | tf_op jit(solution)/shard_map/ppermute | solution.py:15
  194.4 2.0 collective-permute-start.24
  199.8 2.4 collective-permute-start.33
  203.0 3.9 %collective-permute-start.34 = (f32[512]{0:T(512)S(1)}, f32[512]{0:T(512)S(1)}, u32[]{:S(2)}, u32[]{:S(2)}) collective-permute-start(f32[512]{0:T(512)S(1)} %add.240), channel_id=1, source_target_pairs={{0,128},{32,160},{64,192},{96,224},{128,0},{160,32},{192,64},{224,... | collective-permute-start | bytes 6152 | tf_op jit(solution)/shard_map/ppermute | solution.py:23
  206.9 3.1 collective-permute-done.34
  210.0 3.6 %collective-permute-start.35 = (f32[512]{0:T(512)S(1)}, f32[512]{0:T(512)S(1)}, u32[]{:S(2)}, u32[]{:S(2)}) collective-permute-start(f32[512]{0:T(512)S(1)} %add.241), channel_id=1, source_target_pairs={{0,256},{32,288},{64,320},{96,352},{128,384},{160,416},{192,448},{... | collective-permute-start | bytes 6152 | tf_op jit(solution)/shard_map/ppermute | solution.py:23
  213.7 3.3 %collective-permute-done.35 = f32[512]{0:T(512)S(1)} collective-permute-done((f32[512]{0:T(512)S(1)}, f32[512]{0:T(512)S(1)}, u32[]{:S(2)}, u32[]{:S(2)}) %collective-permute-start.35) | collective-permute-done | bytes 2080 | tf_op jit(solution)/shard_map/ppermute | solution.py:23
  217.0 3.6 %collective-permute-start.36 = (f32[512]{0:T(512)S(1)}, f32[512]{0:T(512)S(1)}, u32[]{:S(2)}, u32[]{:S(2)}) collective-permute-start(f32[512]{0:T(512)S(1)} %add.242), channel_id=1, source_target_pairs={{0,64},{32,96},{64,0},{96,32},{128,192},{160,224},{192,128},{224,1... | collective-permute-start | bytes 6152 | tf_op jit(solution)/shard_map/ppermute | solution.py:218
  222.5 2.9 fusion
  225.7 4.4 %collective-permute-start.29 = (bf16[2,128,512]{2,1,0:T(8,128)(2,1)S(1)}, bf16[2,128,512]{2,1,0:T(8,128)(2,1)S(1)}, u32[]{:S(2)}, u32[]{:S(2)}) collective-permute-start(bf16[2,128,512]{2,1,0:T(8,128)(2,1)S(1)} %get-tuple-element.21), channel_id=1, source_target_pairs={{0,64},{32,96},{64,128},{96,160},{128,192},{160,224},{192,0},{224,... | collective-permute-start | bytes 786440 | tf_op jit(solution)/shard_map/ppermute | solution.py:23
  230.1 1.9 collective-permute-start.31
  232.0 3.4 %collective-permute-start.30 = (bf16[2,128,512]{2,1,0:T(8,128)(2,1)S(1)}, bf16[2,128,512]{2,1,0:T(8,128)(2,1)S(1)}, u32[]{:S(2)}, u32[]{:S(2)}) collective-permute-start(bf16[2,128,512]{2,1,0:T(8,128)(2,1)S(1)} %get-tuple-element.23), channel_id=1, source_target_pairs={{0,128},{32,160},{64,192},{96,224},{128,0},{160,32},{192,64},{224,... | collective-permute-start | bytes 786440 | tf_op jit(solution)/shard_map/ppermute | solution.py:23
  235.5 3.6 %collective-permute-start.25 = (bf16[4,128,512]{2,1,0:T(8,128)(2,1)S(1)}, bf16[4,128,512]{2,1,0:T(8,128)(2,1)S(1)}, u32[]{:S(2)}, u32[]{:S(2)}) collective-permute-start(bf16[4,128,512]{2,1,0:T(8,128)(2,1)S(1)} %dynamic-slice_bitcast_fusion.1), channel_id=1, source_target_pairs={{0,256},{32,288},{64,320},{96,352},{128,384},{160,416},{192,448},{... | collective-permute-start | bytes 1572872 | tf_op jit(solution)/shard_map/ppermute | solution.py:23
  239.2 4.7 %collective-permute-done.31 = bf16[2,128,512]{2,1,0:T(8,128)(2,1)S(1)} collective-permute-done((bf16[2,128,512]{2,1,0:T(8,128)(2,1)S(1)}, bf16[2,128,512]{2,1,0:T(8,128)(2,1)S(1)}, u32[]{:S(2)}, u32[]{:S(2)}) %collective-permute-start.31) | collective-permute-done | bytes 262176 | tf_op jit(solution)/shard_map/ppermute | solution.py:23
  244.1 3.6 %collective-permute-start.32 = (bf16[128,512]{1,0:T(8,128)(2,1)S(1)}, bf16[128,512]{1,0:T(8,128)(2,1)S(1)}, u32[]{:S(2)}, u32[]{:S(2)}) collective-permute-start(bf16[128,512]{1,0:T(8,128)(2,1)S(1)} %dynamic-slice_bitcast_fusion.5), channel_id=1, source_target_pairs={{0,256},{32,288},{64,320},{96,352},{128,384},{160,416},{192,448},{... | collective-permute-start | bytes 393224 | tf_op jit(solution)/shard_map/ppermute | solution.py:23
  247.7 2.7 collective-permute-done.25
  250.6 4.0 %collective-permute-start.26 = (bf16[128,512]{1,0:T(8,128)(2,1)S(1)}, bf16[128,512]{1,0:T(8,128)(2,1)S(1)}, u32[]{:S(2)}, u32[]{:S(2)}) collective-permute-start(bf16[128,512]{1,0:T(8,128)(2,1)S(1)} %get-tuple-element.28), channel_id=1, source_target_pairs={{0,64},{32,96},{64,128},{96,160},{128,192},{160,224},{192,0},{224,... | collective-permute-start | bytes 393224 | tf_op jit(solution)/shard_map/ppermute | solution.py:23
  254.6 2.2 collective-permute-start.28
  256.8 4.0 %collective-permute-start.27 = (bf16[128,512]{1,0:T(8,128)(2,1)S(1)}, bf16[128,512]{1,0:T(8,128)(2,1)S(1)}, u32[]{:S(2)}, u32[]{:S(2)}) collective-permute-start(bf16[128,512]{1,0:T(8,128)(2,1)S(1)} %get-tuple-element.30), channel_id=1, source_target_pairs={{0,128},{32,160},{64,192},{96,224},{128,0},{160,32},{192,64},{224,... | collective-permute-start | bytes 393224 | tf_op jit(solution)/shard_map/ppermute | solution.py:23
  260.8 1.9 collective-permute-done.28
  262.7 2.5 collective-permute-done.27
  265.4 39.8 %all_to_all.10 = bf16[32,16,512]{2,1,0:T(8,128)(2,1)S(1)} all-to-all(bf16[32,16,512]{2,1,0:T(8,128)(2,1)S(1)} %pad_maximum_fusion.2), channel_id=1, replica_groups=mesh['dp'=16,'ctx'=32] {'ctx'}, dimensions={0} | all-to-all | bytes 1048576 | tf_op jit(solution)/shard_map/all_to_all | solution.py:229
  306.1 3.9 %all-to-all-start.1 = ((bf16[32,8,512]{2,1,0:T(8,128)(2,1)}), bf16[32,8,512]{2,1,0:T(8,128)(2,1)S(1)}, u32[]{:S(2)}, u32[]{:S(2)}) async-start(bf16[32,8,512]{2,1,0:T(8,128)(2,1)} %broadcast_in_dim.105), calls=%async_computation.1 | async-start | bytes 524288 | tf_op jit(solution)/shard_map/all_to_all | solution.py:232
  312.4 15.3 %all-to-all-done.1 = bf16[32,8,512]{2,1,0:T(8,128)(2,1)S(1)} async-done(((bf16[32,8,512]{2,1,0:T(8,128)(2,1)}), bf16[32,8,512]{2,1,0:T(8,128)(2,1)S(1)}, u32[]{:S(2)}, u32[]{:S(2)}) %all-to-all-start.1) | async-done | bytes 262176 | tf_op jit(solution)/shard_map/all_to_all | solution.py:232
  (297 shorter events, 85.5 us)
Async XLA Ops:
  0.6 34.6 %copy-start.3 = (bf16[1,128,512]{2,1,0:T(8,128)(2,1)S(1)}, bf16[1,128,512]{2,1,0:T(8,128)(2,1)}, u32[]{:S(2)}) copy-start(bf16[1,128,512]{2,1,0:T(8,128)(2,1)} %param.9) | copy-start | bytes 393220
  0.6 34.6 %copy-start.23 = (bf16[1,128,512]{2,1,0:T(8,128)(2,1)S(1)}, bf16[1,128,512]{2,1,0:T(8,128)(2,1)}, u32[]{:S(2)}) copy-start(bf16[1,128,512]{2,1,0:T(8,128)(2,1)} %param.16) | copy-start | bytes 393220
  1.6 37.6 %collective-permute-start.15 = (bf16[4,32,512]{2,1,0:T(8,128)(2,1)S(1)}, bf16[4,32,512]{2,1,0:T(8,128)(2,1)S(1)}, u32[]{:S(2)}, u32[]{:S(2)}) collective-permute-start(bf16[4,32,512]{2,1,0:T(8,128)(2,1)S(1)} %pad_maximum_fusion.10), channel_id=1, source_target_pairs={{0,128},{32,160},{64,192},{96,224},{128,0},{160,32},{192,64},{224,... | collective-permute-start | bytes 393224 | tf_op jit(solution)/shard_map/ppermute | solution.py:23
  4.8 30.5 %collective-permute-start.14 = (bf16[4,32,512]{2,1,0:T(8,128)(2,1)S(1)}, bf16[4,32,512]{2,1,0:T(8,128)(2,1)S(1)}, u32[]{:S(2)}, u32[]{:S(2)}) collective-permute-start(bf16[4,32,512]{2,1,0:T(8,128)(2,1)S(1)} %pad_maximum_fusion.10), channel_id=1, source_target_pairs={{0,192},{32,224},{64,0},{96,32},{128,64},{160,96},{192,128},{224,1... | collective-permute-start | bytes 393224 | tf_op jit(solution)/shard_map/ppermute | solution.py:23
  11.9 32.0 %collective-permute-start.16 = (bf16[4,32,512]{2,1,0:T(8,128)(2,1)S(1)}, bf16[4,32,512]{2,1,0:T(8,128)(2,1)S(1)}, u32[]{:S(2)}, u32[]{:S(2)}) collective-permute-start(bf16[4,32,512]{2,1,0:T(8,128)(2,1)S(1)} %pad_maximum_fusion.10), channel_id=1, source_target_pairs={{0,64},{32,96},{64,128},{96,160},{128,192},{160,224},{192,0},{224,... | collective-permute-start | bytes 393224 | tf_op jit(solution)/shard_map/ppermute | solution.py:23
  14.5 13.6 %collective-permute-start = (bf16[2,512]{1,0:T(2,128)(2,1)S(1)}, bf16[2,512]{1,0:T(2,128)(2,1)S(1)}, u32[]{:S(2)}, u32[]{:S(2)}) collective-permute-start(bf16[2,512]{1,0:T(2,128)(2,1)S(1)} %slice_bitcast_fusion.27), channel_id=1, source_target_pairs={{0,1},{1,2},{2,3},{3,4},{4,5},{5,6},{6,7},{7,8},{8,9},{9,10},{10,1... | collective-permute-start | bytes 6152 | tf_op jit(solution)/shard_map/ppermute | solution.py:15
  16.9 36.2 %copy-start.28 = (bf16[3,32,512]{2,1,0:T(8,128)(2,1)S(1)}, bf16[3,32,512]{2,1,0:T(8,128)(2,1)}, u32[]{:S(2)}) copy-start(bf16[3,32,512]{2,1,0:T(8,128)(2,1)} %param.11) | copy-start | bytes 294916
  16.9 36.2 %copy-start.40 = (bf16[32,512]{1,0:T(8,128)(2,1)S(1)}, bf16[32,512]{1,0:T(8,128)(2,1)}, u32[]{:S(2)}) copy-start(bf16[32,512]{1,0:T(8,128)(2,1)} %param.14) | copy-start | bytes 98308
  16.9 36.4 %collective-permute-start.5 = (bf16[4,32,512]{2,1,0:T(8,128)(2,1)S(1)}, bf16[4,32,512]{2,1,0:T(8,128)(2,1)S(1)}, u32[]{:S(2)}, u32[]{:S(2)}) collective-permute-start(bf16[4,32,512]{2,1,0:T(8,128)(2,1)S(1)} %get-tuple-element.35), channel_id=1, source_target_pairs={{0,256},{32,288},{64,320},{96,352},{128,384},{160,416},{192,448},{... | collective-permute-start | bytes 393224 | tf_op jit(solution)/shard_map/ppermute | solution.py:23
  29.1 28.6 %collective-permute-start.3 = (bf16[130,512]{1,0:T(8,128)(2,1)S(1)}, bf16[130,512]{1,0:T(8,128)(2,1)S(1)}, u32[]{:S(2)}, u32[]{:S(2)}) collective-permute-start(bf16[130,512]{1,0:T(8,128)(2,1)S(1)} %pad_maximum_fusion.4), channel_id=1, source_target_pairs={{0,4},{1,5},{2,6},{3,7},{4,8},{5,9},{6,10},{7,11},{8,12},{9,13},{1... | collective-permute-start | bytes 399368 | tf_op jit(solution)/shard_map/ppermute | solution.py:15
  35.2 18.0 %copy-start = (bf16[5,130,512]{2,1,0:T(8,128)(2,1)}, bf16[5,130,512]{2,1,0:T(8,128)(2,1)S(1)}, u32[]{:S(2)}) copy-start(bf16[5,130,512]{2,1,0:T(8,128)(2,1)S(1)} %bitcast_dynamic-update-slice_fusion.11) | copy-start | bytes 1996804
  35.3 21.0 %collective-permute-start.2 = (bf16[130,512]{1,0:T(8,128)(2,1)S(1)}, bf16[130,512]{1,0:T(8,128)(2,1)S(1)}, u32[]{:S(2)}, u32[]{:S(2)}) collective-permute-start(bf16[130,512]{1,0:T(8,128)(2,1)S(1)} %pad_maximum_fusion.4), channel_id=1, source_target_pairs={{0,2},{1,3},{2,4},{3,5},{4,6},{5,7},{6,8},{7,9},{8,10},{9,11},{10,... | collective-permute-start | bytes 399368 | tf_op jit(solution)/shard_map/ppermute | solution.py:15
  39.2 15.7 %collective-permute-start.1 = (bf16[130,512]{1,0:T(8,128)(2,1)S(1)}, bf16[130,512]{1,0:T(8,128)(2,1)S(1)}, u32[]{:S(2)}, u32[]{:S(2)}) collective-permute-start(bf16[130,512]{1,0:T(8,128)(2,1)S(1)} %pad_maximum_fusion.4), channel_id=1, source_target_pairs={{0,1},{1,2},{2,3},{3,4},{4,5},{5,6},{6,7},{7,8},{8,9},{9,10},{10,1... | collective-permute-start | bytes 399368 | tf_op jit(solution)/shard_map/ppermute | solution.py:15
  43.9 15.1 %collective-permute-start.4 = (bf16[130,512]{1,0:T(8,128)(2,1)S(1)}, bf16[130,512]{1,0:T(8,128)(2,1)S(1)}, u32[]{:S(2)}, u32[]{:S(2)}) collective-permute-start(bf16[130,512]{1,0:T(8,128)(2,1)S(1)} %pad_maximum_fusion.4), channel_id=1, source_target_pairs={{0,8},{1,9},{2,10},{3,11},{4,12},{5,13},{6,14},{7,15},{8,16},{9,17... | collective-permute-start | bytes 399368 | tf_op jit(solution)/shard_map/ppermute | solution.py:15
  53.3 15.8 %copy-start.41 = (bf16[5,128,512]{2,1,0:T(8,128)(2,1)S(1)}, bf16[5,128,512]{2,1,0:T(8,128)(2,1)}, u32[]{:S(2)}) copy-start(bf16[5,128,512]{2,1,0:T(8,128)(2,1)} %constant_dynamic-update-slice_fusion.2) | copy-start | bytes 1966084
  53.3 31.2 %collective-permute-start.13 = (bf16[258,512]{1,0:T(8,128)(2,1)S(1)}, bf16[258,512]{1,0:T(8,128)(2,1)S(1)}, u32[]{:S(2)}, u32[]{:S(2)}) collective-permute-start(bf16[258,512]{1,0:T(8,128)(2,1)S(1)} %pad_maximum_fusion.3), channel_id=1, source_target_pairs={{8,0},{9,1},{10,2},{11,3},{12,4},{13,5},{14,6},{15,7},{16,8},{17,9... | collective-permute-start | bytes 792584 | tf_op jit(solution)/shard_map/ppermute | solution.py:15
  54.7 14.4 %copy-start.1 = (bf16[5,130,512]{2,1,0:T(8,128)(2,1)S(1)}, bf16[5,130,512]{2,1,0:T(8,128)(2,1)}, u32[]{:S(2)}) copy-start(bf16[5,130,512]{2,1,0:T(8,128)(2,1)} %copy-done) | copy-start | bytes 1996804
  54.9 22.5 %collective-permute-start.12 = (bf16[258,512]{1,0:T(8,128)(2,1)S(1)}, bf16[258,512]{1,0:T(8,128)(2,1)S(1)}, u32[]{:S(2)}, u32[]{:S(2)}) collective-permute-start(bf16[258,512]{1,0:T(8,128)(2,1)S(1)} %pad_maximum_fusion.3), channel_id=1, source_target_pairs={{4,0},{5,1},{6,2},{7,3},{8,4},{9,5},{10,6},{11,7},{12,8},{13,9},{1... | collective-permute-start | bytes 792584 | tf_op jit(solution)/shard_map/ppermute | solution.py:15
  56.4 12.8 %collective-permute-start.11 = (bf16[258,512]{1,0:T(8,128)(2,1)S(1)}, bf16[258,512]{1,0:T(8,128)(2,1)S(1)}, u32[]{:S(2)}, u32[]{:S(2)}) collective-permute-start(bf16[258,512]{1,0:T(8,128)(2,1)S(1)} %pad_maximum_fusion.3), channel_id=1, source_target_pairs={{2,0},{3,1},{4,2},{5,3},{6,4},{7,5},{8,6},{9,7},{10,8},{11,9},{12,... | collective-permute-start | bytes 792584 | tf_op jit(solution)/shard_map/ppermute | solution.py:15
  57.7 8.4 %collective-permute-start.10 = (bf16[258,512]{1,0:T(8,128)(2,1)S(1)}, bf16[258,512]{1,0:T(8,128)(2,1)S(1)}, u32[]{:S(2)}, u32[]{:S(2)}) collective-permute-start(bf16[258,512]{1,0:T(8,128)(2,1)S(1)} %pad_maximum_fusion.3), channel_id=1, source_target_pairs={{1,0},{2,1},{3,2},{4,3},{5,4},{6,5},{7,6},{8,7},{9,8},{10,9},{11,1... | collective-permute-start | bytes 792584 | tf_op jit(solution)/shard_map/ppermute | solution.py:15
  59.0 25.8 %collective-permute-start.8 = (bf16[2,4,32,512]{3,2,1,0:T(8,128)(2,1)S(1)}, bf16[2,4,32,512]{3,2,1,0:T(8,128)(2,1)S(1)}, u32[]{:S(2)}, u32[]{:S(2)}) collective-permute-start(bf16[2,4,32,512]{3,2,1,0:T(8,128)(2,1)S(1)} %maximum_select_fusion.4), channel_id=1, source_target_pairs={{0,64},{32,96},{64,128},{96,160},{128,192},{160,224},{192,0},{224,... | collective-permute-start | bytes 786440 | tf_op jit(solution)/shard_map/ppermute | solution.py:23
  66.0 18.8 %collective-permute-start.7 = (bf16[2,4,32,512]{3,2,1,0:T(8,128)(2,1)S(1)}, bf16[2,4,32,512]{3,2,1,0:T(8,128)(2,1)S(1)}, u32[]{:S(2)}, u32[]{:S(2)}) collective-permute-start(bf16[2,4,32,512]{3,2,1,0:T(8,128)(2,1)S(1)} %maximum_select_fusion.4), channel_id=1, source_target_pairs={{0,128},{32,160},{64,192},{96,224},{128,0},{160,32},{192,64},{224,... | collective-permute-start | bytes 786440 | tf_op jit(solution)/shard_map/ppermute | solution.py:23
  69.1 15.7 %collective-permute-start.6 = (bf16[2,4,32,512]{3,2,1,0:T(8,128)(2,1)S(1)}, bf16[2,4,32,512]{3,2,1,0:T(8,128)(2,1)S(1)}, u32[]{:S(2)}, u32[]{:S(2)}) collective-permute-start(bf16[2,4,32,512]{3,2,1,0:T(8,128)(2,1)S(1)} %maximum_select_fusion.4), channel_id=1, source_target_pairs={{0,192},{32,224},{64,0},{96,32},{128,64},{160,96},{192,128},{224,1... | collective-permute-start | bytes 786440 | tf_op jit(solution)/shard_map/ppermute | solution.py:23
  77.4 14.9 %collective-permute-start.17 = (bf16[4,4,32,512]{3,2,1,0:T(8,128)(2,1)S(1)}, bf16[4,4,32,512]{3,2,1,0:T(8,128)(2,1)S(1)}, u32[]{:S(2)}, u32[]{:S(2)}) collective-permute-start(bf16[4,4,32,512]{3,2,1,0:T(8,128)(2,1)S(1)} %constant_dynamic-slice_fusion), channel_id=1, source_target_pairs={{0,256},{32,288},{64,320},{96,352},{128,384},{160,416},{192,448},{... | collective-permute-start | bytes 1572872 | tf_op jit(solution)/shard_map/ppermute | solution.py:23
  85.5 10.3 %collective-permute-start.9 = (bf16[2,4,4,32,512]{4,3,2,0,1:T(8,128)(2,1)S(1)}, bf16[2,4,4,32,512]{4,3,2,0,1:T(8,128)(2,1)S(1)}, u32[]{:S(2)}, u32[]{:S(2)}) collective-permute-start(bf16[2,4,4,32,512]{4,3,2,0,1:T(8,128)(2,1)S(1)} %constant_dynamic-slice_fusion.1), channel_id=1, source_target_pairs={{0,32},{32,0},{64,96},{96,64},{128,160},{160,128},{192,224},{224,1... | collective-permute-start | bytes 3145736 | tf_op jit(solution)/shard_map/ppermute | solution.py:23
  93.4 16.0 %collective-permute-start.18 = (bf16[2,4,4,32,512]{4,3,2,0,1:T(8,128)(2,1)}, bf16[2,4,4,32,512]{4,3,2,0,1:T(8,128)(2,1)}, u32[]{:S(2)}, u32[]{:S(2)}) collective-permute-start(bf16[2,4,4,32,512]{4,3,2,0,1:T(8,128)(2,1)} %maximum_select_fusion.2), channel_id=1, source_target_pairs={{0,32},{32,0},{64,96},{96,64},{128,160},{160,128},{192,224},{224,1... | collective-permute-start | bytes 3145736 | tf_op jit(solution)/shard_map/ppermute | solution.py:23
  130.0 11.0 %collective-permute-start.19 = (f32[24,128]{1,0:T(8,128)S(1)}, f32[24,128]{1,0:T(8,128)S(1)}, u32[]{:S(2)}, u32[]{:S(2)}) collective-permute-start(f32[24,128]{1,0:T(8,128)S(1)} %get-tuple-element.39), channel_id=1, source_target_pairs={{1,0},{2,1},{3,2},{4,3},{5,4},{6,5},{7,6},{8,7},{9,8},{10,9},{11,1... | collective-permute-start | bytes 36872 | tf_op jit(solution)/shard_map/ppermute | solution.py:15
  131.3 17.4 %collective-permute-start.20 = (f32[24,128]{1,0:T(8,128)S(1)}, f32[24,128]{1,0:T(8,128)S(1)}, u32[]{:S(2)}, u32[]{:S(2)}) collective-permute-start(f32[24,128]{1,0:T(8,128)S(1)} %get-tuple-element.40), channel_id=1, source_target_pairs={{2,0},{3,1},{4,2},{5,3},{6,4},{7,5},{8,6},{9,7},{10,8},{11,9},{12,... | collective-permute-start | bytes 36872 | tf_op jit(solution)/shard_map/ppermute | solution.py:15
  132.6 29.3 %collective-permute-start.21 = (f32[24,128]{1,0:T(8,128)S(1)}, f32[24,128]{1,0:T(8,128)S(1)}, u32[]{:S(2)}, u32[]{:S(2)}) collective-permute-start(f32[24,128]{1,0:T(8,128)S(1)} %get-tuple-element.41), channel_id=1, source_target_pairs={{4,0},{5,1},{6,2},{7,3},{8,4},{9,5},{10,6},{11,7},{12,8},{13,9},{1... | collective-permute-start | bytes 36872 | tf_op jit(solution)/shard_map/ppermute | solution.py:15
  133.9 44.3 %collective-permute-start.22 = (f32[24,128]{1,0:T(8,128)S(1)}, f32[24,128]{1,0:T(8,128)S(1)}, u32[]{:S(2)}, u32[]{:S(2)}) collective-permute-start(f32[24,128]{1,0:T(8,128)S(1)} %get-tuple-element.42), channel_id=1, source_target_pairs={{8,0},{9,1},{10,2},{11,3},{12,4},{13,5},{14,6},{15,7},{16,8},{17,9... | collective-permute-start | bytes 36872 | tf_op jit(solution)/shard_map/ppermute | solution.py:15
  140.9 39.0 %copy-start.39 = (bf16[1,128,512]{1,2,0:T(8,128)(2,1)S(1)}, bf16[1,128,512]{1,2,0:T(8,128)(2,1)}, u32[]{:S(2)}) copy-start(bf16[1,128,512]{1,2,0:T(8,128)(2,1)} %copy.123) | copy-start | bytes 393220
  186.0 11.4 %collective-permute-start.23 = (bf16[2,1024]{1,0:T(2,128)(2,1)S(1)}, bf16[2,1024]{1,0:T(2,128)(2,1)S(1)}, u32[]{:S(2)}, u32[]{:S(2)}) collective-permute-start(bf16[2,1024]{1,0:T(2,128)(2,1)S(1)} %pad_maximum_fusion.20), channel_id=1, source_target_pairs={{1,0},{2,1},{3,2},{4,3},{5,4},{6,5},{7,6},{8,7},{9,8},{10,9},{11,1... | collective-permute-start | bytes 12296 | tf_op jit(solution)/shard_map/ppermute | solution.py:15
  194.4 28.1 %collective-permute-start.24 = (bf16[2,4,256,512]{3,2,1,0:T(8,128)(2,1)}, bf16[2,4,256,512]{3,2,1,0:T(8,128)(2,1)}, u32[]{:S(2)}, u32[]{:S(2)}) collective-permute-start(bf16[2,4,256,512]{3,2,1,0:T(8,128)(2,1)} %dynamic-slice_bitcast_fusion), channel_id=1, source_target_pairs={{0,32},{32,0},{64,96},{96,64},{128,160},{160,128},{192,224},{224,1... | collective-permute-start | bytes 6291464 | tf_op jit(solution)/shard_map/ppermute | solution.py:23
  199.8 3.2 collective-permute-start.33
  203.0 7.0 %collective-permute-start.34 = (f32[512]{0:T(512)S(1)}, f32[512]{0:T(512)S(1)}, u32[]{:S(2)}, u32[]{:S(2)}) collective-permute-start(f32[512]{0:T(512)S(1)} %add.240), channel_id=1, source_target_pairs={{0,128},{32,160},{64,192},{96,224},{128,0},{160,32},{192,64},{224,... | collective-permute-start | bytes 6152 | tf_op jit(solution)/shard_map/ppermute | solution.py:23
  210.0 7.0 %collective-permute-start.35 = (f32[512]{0:T(512)S(1)}, f32[512]{0:T(512)S(1)}, u32[]{:S(2)}, u32[]{:S(2)}) collective-permute-start(f32[512]{0:T(512)S(1)} %add.241), channel_id=1, source_target_pairs={{0,256},{32,288},{64,320},{96,352},{128,384},{160,416},{192,448},{... | collective-permute-start | bytes 6152 | tf_op jit(solution)/shard_map/ppermute | solution.py:23
  217.0 5.5 %collective-permute-start.36 = (f32[512]{0:T(512)S(1)}, f32[512]{0:T(512)S(1)}, u32[]{:S(2)}, u32[]{:S(2)}) collective-permute-start(f32[512]{0:T(512)S(1)} %add.242), channel_id=1, source_target_pairs={{0,64},{32,96},{64,0},{96,32},{128,192},{160,224},{192,128},{224,1... | collective-permute-start | bytes 6152 | tf_op jit(solution)/shard_map/ppermute | solution.py:218
  225.7 13.5 %collective-permute-start.29 = (bf16[2,128,512]{2,1,0:T(8,128)(2,1)S(1)}, bf16[2,128,512]{2,1,0:T(8,128)(2,1)S(1)}, u32[]{:S(2)}, u32[]{:S(2)}) collective-permute-start(bf16[2,128,512]{2,1,0:T(8,128)(2,1)S(1)} %get-tuple-element.21), channel_id=1, source_target_pairs={{0,64},{32,96},{64,128},{96,160},{128,192},{160,224},{192,0},{224,... | collective-permute-start | bytes 786440 | tf_op jit(solution)/shard_map/ppermute | solution.py:23
  230.1 13.9 %collective-permute-start.31 = (bf16[2,128,512]{2,1,0:T(8,128)(2,1)S(1)}, bf16[2,128,512]{2,1,0:T(8,128)(2,1)S(1)}, u32[]{:S(2)}, u32[]{:S(2)}) collective-permute-start(bf16[2,128,512]{2,1,0:T(8,128)(2,1)S(1)} %get-tuple-element.22), channel_id=1, source_target_pairs={{0,192},{32,224},{64,0},{96,32},{128,64},{160,96},{192,128},{224,1... | collective-permute-start | bytes 786440 | tf_op jit(solution)/shard_map/ppermute | solution.py:23
  232.0 11.9 %collective-permute-start.30 = (bf16[2,128,512]{2,1,0:T(8,128)(2,1)S(1)}, bf16[2,128,512]{2,1,0:T(8,128)(2,1)S(1)}, u32[]{:S(2)}, u32[]{:S(2)}) collective-permute-start(bf16[2,128,512]{2,1,0:T(8,128)(2,1)S(1)} %get-tuple-element.23), channel_id=1, source_target_pairs={{0,128},{32,160},{64,192},{96,224},{128,0},{160,32},{192,64},{224,... | collective-permute-start | bytes 786440 | tf_op jit(solution)/shard_map/ppermute | solution.py:23
  235.5 14.9 %collective-permute-start.25 = (bf16[4,128,512]{2,1,0:T(8,128)(2,1)S(1)}, bf16[4,128,512]{2,1,0:T(8,128)(2,1)S(1)}, u32[]{:S(2)}, u32[]{:S(2)}) collective-permute-start(bf16[4,128,512]{2,1,0:T(8,128)(2,1)S(1)} %dynamic-slice_bitcast_fusion.1), channel_id=1, source_target_pairs={{0,256},{32,288},{64,320},{96,352},{128,384},{160,416},{192,448},{... | collective-permute-start | bytes 1572872 | tf_op jit(solution)/shard_map/ppermute | solution.py:23
  244.1 16.6 %collective-permute-start.32 = (bf16[128,512]{1,0:T(8,128)(2,1)S(1)}, bf16[128,512]{1,0:T(8,128)(2,1)S(1)}, u32[]{:S(2)}, u32[]{:S(2)}) collective-permute-start(bf16[128,512]{1,0:T(8,128)(2,1)S(1)} %dynamic-slice_bitcast_fusion.5), channel_id=1, source_target_pairs={{0,256},{32,288},{64,320},{96,352},{128,384},{160,416},{192,448},{... | collective-permute-start | bytes 393224 | tf_op jit(solution)/shard_map/ppermute | solution.py:23
  250.6 10.2 %collective-permute-start.26 = (bf16[128,512]{1,0:T(8,128)(2,1)S(1)}, bf16[128,512]{1,0:T(8,128)(2,1)S(1)}, u32[]{:S(2)}, u32[]{:S(2)}) collective-permute-start(bf16[128,512]{1,0:T(8,128)(2,1)S(1)} %get-tuple-element.28), channel_id=1, source_target_pairs={{0,64},{32,96},{64,128},{96,160},{128,192},{160,224},{192,0},{224,... | collective-permute-start | bytes 393224 | tf_op jit(solution)/shard_map/ppermute | solution.py:23
  254.6 8.1 %collective-permute-start.28 = (bf16[128,512]{1,0:T(8,128)(2,1)S(1)}, bf16[128,512]{1,0:T(8,128)(2,1)S(1)}, u32[]{:S(2)}, u32[]{:S(2)}) collective-permute-start(bf16[128,512]{1,0:T(8,128)(2,1)S(1)} %get-tuple-element.29), channel_id=1, source_target_pairs={{0,192},{32,224},{64,0},{96,32},{128,64},{160,96},{192,128},{224,1... | collective-permute-start | bytes 393224 | tf_op jit(solution)/shard_map/ppermute | solution.py:23
  256.8 8.4 %collective-permute-start.27 = (bf16[128,512]{1,0:T(8,128)(2,1)S(1)}, bf16[128,512]{1,0:T(8,128)(2,1)S(1)}, u32[]{:S(2)}, u32[]{:S(2)}) collective-permute-start(bf16[128,512]{1,0:T(8,128)(2,1)S(1)} %get-tuple-element.30), channel_id=1, source_target_pairs={{0,128},{32,160},{64,192},{96,224},{128,0},{160,32},{192,64},{224,... | collective-permute-start | bytes 393224 | tf_op jit(solution)/shard_map/ppermute | solution.py:23
  265.3 44.6 %copy-start.11 = (bf16[1,2,4,2,32,512]{5,4,3,2,1,0:T(8,128)(2,1)S(1)}, bf16[1,2,4,2,32,512]{5,4,3,2,1,0:T(8,128)(2,1)}, u32[]{:S(2)}) copy-start(bf16[1,2,4,2,32,512]{5,4,3,2,1,0:T(8,128)(2,1)} %copy-done.10) | copy-start | bytes 1572868
  265.4 44.6 %copy-start.35 = (bf16[8,64,128]{2,1,0:T(8,128)(2,1)S(1)}, bf16[8,64,128]{2,1,0:T(8,128)(2,1)}, u32[]{:S(2)}) copy-start(bf16[8,64,128]{2,1,0:T(8,128)(2,1)} %copy-done.34) | copy-start | bytes 393220
  306.1 21.6 %all-to-all-start.1 = ((bf16[32,8,512]{2,1,0:T(8,128)(2,1)}), bf16[32,8,512]{2,1,0:T(8,128)(2,1)S(1)}, u32[]{:S(2)}, u32[]{:S(2)}) async-start(bf16[32,8,512]{2,1,0:T(8,128)(2,1)} %broadcast_in_dim.105), calls=%async_computation.1 | async-start | bytes 524288 | tf_op jit(solution)/shard_map/all_to_all | solution.py:232
  (39 other events, 99.4 us)

commit v2 on v1

v2 whole, which is shorter than its diff:
```python
import jax
import jax.numpy as jnp
from jax import lax
from jax.experimental import pallas as pl
from jax.experimental.pallas import tpu as pltpu
from jax.sharding import PartitionSpec as P

block_offsets = (1, 2, 4, 8)
epsilon = 1e-06
hidden = -1e30
f32 = jnp.float32
bf16 = jnp.bfloat16
edge = 16
chip_groups = [[2 * i + c for i in range(8)] for c in range(2)]


def shift_ctx(shard, by):
    devices = lax.axis_size("ctx")
    pairs = [(i, i + by) for i in range(devices) if 0 <= i + by < devices]
    return lax.ppermute(shard, "ctx", pairs)


def other_core(shard):
    return lax.ppermute(shard, "dp", [(i, i ^ 1) for i in range(16)])


def over_chips(stacked):
    return lax.all_to_all(stacked, "dp", 0, 0, axis_index_groups=chip_groups, tiled=True)


def product(left, right):
    return jnp.dot(left, right, preferred_element_type=f32)


def product_right_t(left, right):
    return lax.dot_general(left, right, (((1,), (1,)), ((), ())), preferred_element_type=f32)


def product_left_t(left, right):
    return lax.dot_general(left, right, (((0,), (0,)), ((), ())), preferred_element_type=f32)


def inverse_rms(values):
    return lax.rsqrt(jnp.mean(values * values, axis=-1, keepdims=True) + epsilon)


def normed_taps(window, gain):
    values = window.astype(f32)
    normed = values * inverse_rms(values) * gain
    count = window.shape[0] - edge
    return [normed[edge - tap : edge - tap + count].astype(bf16) for tap in range(3)]


def call(kernel, outs, scratch=(), smem=0, inputs=0):
    return pl.pallas_call(
        kernel,
        out_shape=[jax.ShapeDtypeStruct(shape, kind) for shape, kind in outs],
        in_specs=[pl.BlockSpec(memory_space=pltpu.SMEM)] * smem
        + [pl.BlockSpec(memory_space=pltpu.VMEM)] * (inputs - smem),
        out_specs=[pl.BlockSpec(memory_space=pltpu.VMEM)] * len(outs),
        scratch_shapes=list(scratch),
        compiler_params=pltpu.CompilerParams(vmem_limit_bytes=50 * 1024 * 1024),
    )


def split_heads(pair, first):
    wide = pair.astype(f32)
    return jnp.concatenate(
        [jnp.where(first, wide, 0.0), jnp.where(first, 0.0, wide)], axis=0
    ).astype(bf16)


def join_heads(stacked, first):
    count = stacked.shape[0] // 2
    return jnp.where(first, stacked[:count], stacked[count:])


def rows_kernel(
    core_ref, links_ref, mine_ref, other_ref, window_ref, one_ref, two_ref, four_ref, eight_ref,
    upstream_ref, gain_ref, barred_ref,
    weights_ref, mixed_ref, attn_ref, d_query_ref, query_ref, upper_ref, key_ref, value_ref,
    taps_ref, own_stats_ref, stats_ref,
    lines_ref, keys_ref, values_ref,
):
    even = core_ref[0] == 0
    for chip in range(8):
        for matrix in range(8):
            mine, other = mine_ref[chip, matrix], other_ref[chip, matrix]
            weights_ref[matrix, chip * 64 : chip * 64 + 32] = jnp.where(even, mine, other)
            weights_ref[matrix, chip * 64 + 32 : chip * 64 + 64] = jnp.where(even, other, mine)
    gain = gain_ref[...]
    count = one_ref.shape[0]
    one = jnp.concatenate([two_ref[count:], one_ref[...]], axis=0)
    for slot, window in enumerate(
        (window_ref[...], one, two_ref[...], four_ref[...], eight_ref[...])
    ):
        for tap, part in enumerate(normed_taps(window, gain)):
            lines_ref[tap, slot * count : (slot + 1) * count] = part
    for tap in range(3):
        taps_ref[tap] = lines_ref[tap, :count]
    keys = product(lines_ref[0], weights_ref[0])
    keys = keys + product(lines_ref[1], weights_ref[1])
    keys_ref[...] = (keys + product(lines_ref[2], weights_ref[2])).astype(bf16)
    values_ref[...] = product(lines_ref[0], weights_ref[3]).astype(bf16)
    query = product(taps_ref[0], weights_ref[4])
    query = query + product(taps_ref[1], weights_ref[5])
    query_ref[...] = (query + product(taps_ref[2], weights_ref[6])).astype(bf16)
    upper_ref[...] = product_right_t(upstream_ref[...], weights_ref[7]).astype(bf16)
    key_ref[...] = keys_ref[:count]
    value_ref[...] = values_ref[:count]

    lane = lax.broadcasted_iota(jnp.int32, (count, 128), 1)
    row = lax.broadcasted_iota(jnp.int32, (count, 128), 0)
    first = lane < 64
    causal = jnp.where(lane <= row, 0.0, hidden)
    table = jnp.zeros((count, 128), f32)
    scaling = 64 ** (-0.5)
    for pair in range(4):
        span = slice(pair * 128, (pair + 1) * 128)
        query = split_heads(query_ref[:, span], first)
        upper = split_heads(upper_ref[:, span], first)
        key, value = keys_ref[:, span], values_ref[:, span]
        scores = product_right_t(query, key) * scaling
        d_prob = product_right_t(upper, value)
        probs_low, d_score = [], []
        for inner in range(2):
            head = pair * 2 + inner
            mine = scores[inner * count : (inner + 1) * count]
            parts = [mine[:, :count] + causal]
            for i in range(4):
                bias = jnp.where(links_ref[head, i] > 0, 0.0, hidden)
                parts.append(mine[:, (i + 1) * count : (i + 2) * count] + bias)
            mine = jnp.concatenate(parts, axis=1)
            highest = jnp.max(mine, axis=1, keepdims=True)
            weight = jnp.exp(mine - highest)
            inverse = 1.0 / jnp.sum(weight, axis=1, keepdims=True)
            probs = weight * inverse
            slope = d_prob[inner * count : (inner + 1) * count]
            centre = jnp.sum(probs * slope, axis=1, keepdims=True)
            probs_low.append(probs.astype(bf16))
            d_score.append((probs * (slope - centre) * scaling).astype(bf16))
            table = jnp.where(lane == head, highest, table)
            table = jnp.where(lane == 8 + head, inverse, table)
            table = jnp.where(lane == 16 + head, centre, table)
        attn = product(jnp.concatenate(probs_low, axis=0), value)
        attn_ref[:, span] = join_heads(attn, first).astype(bf16)
        d_query = product(jnp.concatenate(d_score, axis=0), key)
        d_query_ref[:, span] = join_heads(d_query, first).astype(bf16)
    across = jnp.transpose(table)
    own_stats_ref[...] = across[:24]
    for i in range(4):
        stats_ref[i, :8] = jnp.maximum(across[:8], barred_ref[i])
        stats_ref[i, 8:] = across[8:24]
    mixed = window_ref[edge:].astype(f32) + product(attn_ref[...], weights_ref[7])
    mixed_ref[...] = mixed.astype(bf16)


def later_kernel(
    own_ref, one_ref, two_ref, four_ref, eight_ref, gain_ref, weights_ref,
    queries_ref, uppers_ref,
    lines_ref, cots_ref,
):
    gain = gain_ref[...]
    count = own_ref.shape[0]
    one = jnp.concatenate([own_ref[count - edge :], one_ref[:count]], axis=0)
    size = count + edge
    windows = (one, two_ref[:size], four_ref[:size], eight_ref[:size])
    cots = (one_ref[count:], two_ref[size:], four_ref[size:], eight_ref[size:])
    for slot in range(4):
        rows = slice(slot * count, (slot + 1) * count)
        cots_ref[rows] = cots[slot]
        for tap, part in enumerate(normed_taps(windows[slot], gain)):
            lines_ref[tap, rows] = part
    queries = product(lines_ref[0], weights_ref[4])
    queries = queries + product(lines_ref[1], weights_ref[5])
    queries_ref[...] = (queries + product(lines_ref[2], weights_ref[6])).astype(bf16)
    uppers_ref[...] = product_right_t(cots_ref[...], weights_ref[7]).astype(bf16)


def store_partials(even, term, keep_ref, send_ref, matrix):
    term = term.astype(bf16)
    for chip in range(8):
        low = term[chip * 64 : chip * 64 + 32]
        high = term[chip * 64 + 32 : chip * 64 + 64]
        keep_ref[chip, matrix] = jnp.where(even, low, high)
        send_ref[chip, matrix] = jnp.where(even, high, low)


def partials_kernel(core_ref, taps_ref, d_query_ref, attn_ref, upstream_ref, keep_ref, send_ref):
    even = core_ref[0] == 0
    for tap in range(3):
        term = product_left_t(taps_ref[tap], d_query_ref[...])
        store_partials(even, term, keep_ref, send_ref, tap)
    term = product_left_t(attn_ref[...], upstream_ref[...])
    store_partials(even, term, keep_ref, send_ref, 3)


def columns_kernel(
    core_ref, key_ref, value_ref, query_ref, upper_ref, queries_ref, uppers_ref, taps_ref,
    own_ref, one_ref, two_ref, four_ref, eight_ref,
    d_key_ref, d_value_ref, keep_ref, send_ref,
):
    even = core_ref[0] == 0
    count = key_ref.shape[0]
    lane = lax.broadcasted_iota(jnp.int32, (count, 128), 1)
    row = lax.broadcasted_iota(jnp.int32, (count, 128), 0)
    first = lane < 64
    causal = jnp.concatenate([row <= lane] * 2, axis=1)
    scaling = 64 ** (-0.5)
    all_stats = [own_ref[...], one_ref[...], two_ref[...], four_ref[...], eight_ref[...]]
    all_stats = [
        (jnp.where(stats[8:16] > 0.0, stats[:8], 1e30), stats[8:16], stats[16:24])
        for stats in all_stats
    ]
    for pair in range(4):
        span = slice(pair * 128, (pair + 1) * 128)
        key, value = key_ref[:, span], value_ref[:, span]
        d_key = jnp.zeros((count, 128), f32)
        d_value = jnp.zeros((count, 128), f32)
        for slot in range(5):
            if slot == 0:
                query, upper = query_ref[:, span], upper_ref[:, span]
            else:
                rows = slice((slot - 1) * count, slot * count)
                query, upper = queries_ref[rows, span], uppers_ref[rows, span]
            query, upper = split_heads(query, first), split_heads(upper, first)
            highest, inverse, centre = [
                jnp.concatenate([part[pair * 2 : pair * 2 + 1], part[pair * 2 + 1 : pair * 2 + 2]], axis=1)
                for part in all_stats[slot]
            ]
            scores = product_right_t(key, query) * scaling
            probs = jnp.exp(scores - highest) * inverse
            if slot == 0:
                probs = jnp.where(causal, probs, 0.0)
            d_prob = product_right_t(value, upper)
            d_score = (probs * (d_prob - centre) * scaling).astype(bf16)
            d_key = d_key + product(d_score, query)
            d_value = d_value + product(probs.astype(bf16), upper)
        d_key_ref[:, span] = d_key.astype(bf16)
        d_value_ref[:, span] = d_value.astype(bf16)
    for tap in range(3):
        term = product_left_t(taps_ref[tap], d_key_ref[...])
        store_partials(even, term, keep_ref, send_ref, tap)
    store_partials(even, product_left_t(taps_ref[0], d_value_ref[...]), keep_ref, send_ref, 3)


def series_kernel(
    d_query_ref, d_key_ref, d_value_ref, leading_ref, weights_ref, own_ref, upstream_ref, gain_ref,
    grad_ref, d_gain_ref,
):
    count, features = own_ref.shape
    d_normed = product_right_t(d_value_ref[...], weights_ref[3])
    for which, (ref, base) in enumerate(((d_query_ref, 4), (d_key_ref, 0))):
        after = leading_ref[:, which * features : (which + 1) * features]
        window = jnp.concatenate([ref[...], after], axis=0).astype(f32)
        for tap in range(3):
            part = window[tap : tap + count].astype(bf16)
            d_normed = d_normed + product_right_t(part, weights_ref[base + tap])
    values = own_ref[...].astype(f32)
    scale = inverse_rms(values)
    d_gain_ref[...] = jnp.sum(d_normed * values * scale, axis=0, keepdims=True)
    slope = d_normed * gain_ref[...]
    along = jnp.mean(slope * values, axis=-1, keepdims=True)
    d_values = scale * slope - values * (scale * scale * scale * along)
    grad_ref[...] = (upstream_ref[...].astype(f32) + d_values).astype(bf16)


def reduce_rows(keep, send):
    half = (keep.astype(f32) + other_core(send).astype(f32)).astype(bf16)
    return jnp.sum(over_chips(half).astype(f32), axis=0).astype(bf16)


def body(
    series, norm_gain, query_kernel, key_kernel, value_weight, out_weight, block_links, grad_out
):
    core = (lax.axis_index("dp") % 2).reshape(1)
    block = lax.axis_index("ctx")
    heads = block_links.shape[2]
    own, cotangent = series[0], grad_out[0]
    count, features = own.shape
    gain = norm_gain.reshape(1, features)
    shard = jnp.concatenate(
        [key_kernel, value_weight[None], query_kernel, out_weight[None]], axis=0
    )
    mine = over_chips(jnp.broadcast_to(shard[None], (8,) + shard.shape))

    before_one = shift_ctx(own, 1)
    after_one = shift_ctx(jnp.concatenate([own, cotangent], axis=0), -1)
    window = jnp.concatenate([before_one[count - edge :], own], axis=0)
    before_two = shift_ctx(window, 2)
    after_two = shift_ctx(jnp.concatenate([window, cotangent], axis=0), -2)
    before_four = shift_ctx(before_two, 2)
    after_four = shift_ctx(after_two, -2)
    before_eight = shift_ctx(before_four, 4)
    after_eight = shift_ctx(after_four, -4)
    other = other_core(mine)

    offsets = jnp.array(block_offsets, dtype=jnp.int32)
    reach = (block_links[0, 0] > 0) & (block >= offsets)[None, :]
    barred = jnp.where(reach.T[:, :, None], -3e38, 1e30).astype(f32)
    barred = jnp.broadcast_to(barred, (4, heads, 128))

    half = ((count, features), bf16)
    (
        weights, mixed, attn, d_query, query, upper, key, value, taps, own_stats, stats
    ) = call(
        rows_kernel,
        [((8, features, features), bf16)] + [half] * 7
        + [((3, count, features), bf16), ((24, count), f32), ((4, 24, count), f32)],
        [
            pltpu.VMEM((3, 5 * count, features), bf16),
            pltpu.VMEM((5 * count, features), bf16),
            pltpu.VMEM((5 * count, features), bf16),
        ],
        smem=2,
        inputs=12,
    )(
        core, reach.astype(jnp.int32), mine, other, window, before_one, before_two, before_four,
        before_eight, cotangent, gain, barred,
    )
    returned = [shift_ctx(stats[i], -block_offsets[i]) for i in range(4)]
    parts = ((8, 4, 32, features), bf16)
    keep, send = call(partials_kernel, [parts, parts], smem=1, inputs=5)(
        core, taps, d_query, attn, cotangent
    )
    queries, uppers = call(
        later_kernel,
        [((4 * count, features), bf16)] * 2,
        [pltpu.VMEM((3, 4 * count, features), bf16), pltpu.VMEM((4 * count, features), bf16)],
        inputs=7,
    )(own, after_one, after_two, after_four, after_eight, gain, weights)
    rows_query = reduce_rows(keep, send)
    d_key, d_value, keep, send = call(
        columns_kernel, [half, half, parts, parts], smem=1, inputs=13
    )(core, key, value, query, upper, queries, uppers, taps, own_stats, *returned)
    leading = shift_ctx(jnp.concatenate([d_query[:edge], d_key[:edge]], axis=1), -1)
    rows_key = reduce_rows(keep, send)
    grad_series, d_gain = call(
        series_kernel, [half, ((1, features), f32)], inputs=8
    )(d_query, d_key, d_value, leading, weights, own, cotangent, gain)

    d_gain = jnp.broadcast_to(d_gain.reshape(1, 4, 128), (16, 4, 128))
    d_gain = jnp.sum(lax.all_to_all(d_gain, "dp", 0, 0, tiled=True), axis=0)
    top = d_gain.astype(bf16)
    rest = (d_gain - top.astype(f32)).astype(bf16)
    extra = jnp.broadcast_to(jnp.concatenate([top, rest], axis=0)[None], (32, 8, 128))
    rows = jnp.concatenate([rows_query, rows_key], axis=0).reshape(32, 8, features)
    payload = jnp.concatenate([rows, extra], axis=2)
    arrived = lax.all_to_all(payload, "ctx", 0, 0, tiled=True).astype(f32)
    summed = jnp.sum(arrived, axis=0)
    gain_total = (summed[:4, features:] + summed[4:, features:]).reshape(features)
    summed = summed[:, :features].astype(bf16)
    final = lax.all_to_all(
        jnp.broadcast_to(summed[None], (32, 8, features)), "ctx", 0, 0, tiled=True
    )
    final = final.reshape(8, 32, features).astype(f32)
    return (mixed[None], grad_series[None], gain_total, final[:3], final[4:7], final[7], final[3])


def solution(mesh):
    placed = (
        P("dp", "ctx", None),
        P(),
        P(None, "dp", None),
        P(None, "dp", None),
        P("dp", None),
        P("dp", None),
        P("dp", "ctx", None, None),
        P("dp", "ctx", None),
    )
    return jax.shard_map(
        body,
        mesh=mesh,
        in_specs=placed,
        out_specs=(
            P("dp", "ctx", None),
            P("dp", "ctx", None),
            P(),
            P(None, "dp", None),
            P(None, "dp", None),
            P("dp", None),
            P("dp", None),
        ),
        check_vma=False,
    )
```

time: 335 us -> 271 us (0.81)
  starting transfers between devices: 116 us -> 58.5 us
  blocking collectives: 39.8 us -> 74.4 us
  local copies, waits for them, and re-layouts: 33.7 us -> 3.34 us
  matrix products: 26.1 us -> 0 us
  Pallas kernels: 0 us -> 22.7 us
  other arithmetic: 20.6 us -> 7.38 us
  waiting for transfers between devices: 90.3 us -> 100 us
    ppermute x23 -> x3, starting transfers between devices: 75.7 us -> 5.74 us  [other_core(): return lax.ppermute(shard, 'dp', [(i, i ^ 1) for i in range(16)])]
    all_to_all x0 -> x1, blocking collectives: none -> 33.1 us  [over_chips(): lax.all_to_all(stacked, 'dp', 0, 0, axis_index_groups=chip_groups, tiled=...]
    all_to_all x0 -> x3, waiting for transfers between devices: none -> 30.3 us  [the longest x2 27.2 us: over_chips(): lax.all_to_all(stacked, 'dp', 0, 0, axis_index_groups=chip_groups, tiled=...]
    dot_general x34 -> x0, matrix products: 26.1 us -> none  [the longest x8 7.6 us: product_left_t(): lax.dot_general(left, right, (((0,), (0,)), ((), ())), preferred_element_...]
    ppermute x23 -> x3, waiting for transfers between devices: 25 us -> 0.01 us  [other_core(): return lax.ppermute(shard, 'dp', [(i, i ^ 1) for i in range(16)])]
    pallas_call x0 -> x5, Pallas kernels: none -> 22.7 us  [the longest x1 9.09 us: body(): call(rows_kernel, [((8, features, features), bf16)] + [half] * 7 + [((3,...]
    all_to_all x0 -> x3, starting transfers between devices: none -> 16.6 us  [the longest x2 10.8 us: over_chips(): lax.all_to_all(stacked, 'dp', 0, 0, axis_index_groups=chip_groups, tiled=...]
    slice x31 -> x5, local copies, waits for them, and re-layouts: 15.9 us -> 0.8 us  [the longest x1 0.78 us: body(): final[4:7]]
  transfers between devices with their start and end apart: 38 -> 20, of which waited for: 16 -> 14; matrix products, arithmetic and copies ran while one was open for 13% -> 3% of each run, Pallas kernels for 0% -> 8%
where the time goes in v2:
time: 271 us; the launch traced here: 268 us
  waiting for transfers between devices  100 us (37%)
  blocking collectives  74.4 us (27%)
  starting transfers between devices  58.5 us (22%)
  Pallas kernels  22.7 us (8%)
  other arithmetic  7.38 us (3%)
  local copies, waits for them, and re-layouts  3.34 us (1%)
    ppermute x13, waiting for transfers between devices, shift_ctx(): return lax.ppermute(shard, 'ctx', pairs)  50.5 us
    all_to_all x1, blocking collectives, body(): arrived = lax.all_to_all(payload, 'ctx', 0, 0, tiled=True).astype(f32)  41.3 us
    all_to_all x1, blocking collectives, over_chips(): lax.all_to_all(stacked, 'dp', 0, 0, axis_index_groups=chip_groups, tiled=...  33.1 us
    ppermute x13, starting transfers between devices, shift_ctx(): return lax.ppermute(shard, 'ctx', pairs)  32.3 us
    all_to_all x2, waiting for transfers between devices, over_chips(): lax.all_to_all(stacked, 'dp', 0, 0, axis_index_groups=chip_groups, tiled=...  27.2 us
    all_to_all x1, waiting for transfers between devices, body(): lax.all_to_all(jnp.broadcast_to(summed[None], (32, 8, features)), 'ctx',...  19.6 us
    all_to_all x2, starting transfers between devices, over_chips(): lax.all_to_all(stacked, 'dp', 0, 0, axis_index_groups=chip_groups, tiled=...  10.8 us
    pallas_call x1, Pallas kernels, body(): call(rows_kernel, [((8, features, features), bf16)] + [half] * 7 + [((3,...  9.09 us
  transfers between devices with their start and end apart: 20, of which 14 were waited for; matrix products, arithmetic and copies ran while one was open for 3% of the time, Pallas kernels for 8%

profile of v2, /device:TPU:24, one launch (start us, length us, event | category | flops | bytes accessed | tf_op | source)
XLA Modules:
  0.0 267.7 jit_solution(15791917481044797064)
XLA Ops:
  0.6 1.0 pad_maximum_fusion.2
  2.0 33.1 %all_to_all.30.mine_ref = bf16[8,8,32,512]{3,2,1,0:T(8,128)(2,1)} all-to-all(bf16[8,8,32,512]{3,2,1,0:T(8,128)(2,1)S(1)} %broadcast_in_dim.54), channel_id=1, replica_groups={{0,64,128,192,256,320,384,448},{32,96,160,224,288,352,416,480},{1,65,12..., dimensions={0} | all-to-all | bytes 4194304 | tf_op jit(solution)/shard_map/all_to_all | solution.py:28
  35.1 1.9 collective-permute-start
  37.0 2.8 %collective-permute-start.1 = (bf16[128,512]{1,0:T(8,128)(2,1)S(1)}, bf16[128,512]{1,0:T(8,128)(2,1)S(1)}, u32[]{:S(2)}, u32[]{:S(2)}) collective-permute-start(bf16[128,512]{1,0:T(8,128)(2,1)S(1)} %bitcast.30), channel_id=1, source_target_pairs={{0,1},{1,2},{2,3},{3,4},{4,5},{5,6},{6,7},{7,8},{8,9},{9,10},{10,1... | collective-permute-start | bytes 393224 | tf_op jit(solution)/shard_map/ppermute | solution.py:20
  39.9 3.3 %collective-permute-done.1.one_ref = bf16[128,512]{1,0:T(8,128)(2,1)S(1)} collective-permute-done((bf16[128,512]{1,0:T(8,128)(2,1)S(1)}, bf16[128,512]{1,0:T(8,128)(2,1)S(1)}, u32[]{:S(2)}, u32[]{:S(2)}) %collective-permute-start.1) | collective-permute-done | bytes 131104 | tf_op jit(solution)/shard_map/ppermute | solution.py:20
  43.2 6.4 %collective-permute-start.2 = (bf16[144,512]{1,0:T(8,128)(2,1)S(1)}, bf16[144,512]{1,0:T(8,128)(2,1)S(1)}, u32[]{:S(2)}, u32[]{:S(2)}) collective-permute-start(bf16[144,512]{1,0:T(8,128)(2,1)S(1)} %pad_maximum_fusion.5.window_ref), channel_id=1, source_target_pairs={{0,2},{1,3},{2,4},{3,5},{4,6},{5,7},{6,8},{7,9},{8,10},{9,11},{10,... | collective-permute-start | bytes 442376 | tf_op jit(solution)/shard_map/ppermute | solution.py:20
  49.6 2.9 %collective-permute-done.2.two_ref = bf16[144,512]{1,0:T(8,128)(2,1)S(1)} collective-permute-done((bf16[144,512]{1,0:T(8,128)(2,1)S(1)}, bf16[144,512]{1,0:T(8,128)(2,1)S(1)}, u32[]{:S(2)}, u32[]{:S(2)}) %collective-permute-start.2) | collective-permute-done | bytes 147488 | tf_op jit(solution)/shard_map/ppermute | solution.py:20
  52.6 4.4 %collective-permute-start.3 = (bf16[144,512]{1,0:T(8,128)(2,1)S(1)}, bf16[144,512]{1,0:T(8,128)(2,1)S(1)}, u32[]{:S(2)}, u32[]{:S(2)}) collective-permute-start(bf16[144,512]{1,0:T(8,128)(2,1)S(1)} %collective-permute-done.2.two_ref), channel_id=1, source_target_pairs={{0,2},{1,3},{2,4},{3,5},{4,6},{5,7},{6,8},{7,9},{8,10},{9,11},{10,... | collective-permute-start | bytes 442376 | tf_op jit(solution)/shard_map/ppermute | solution.py:20
  57.0 1.3 collective-permute-start.6
  58.3 1.3 collective-permute-done.3.four_ref
  59.6 7.0 %collective-permute-start.4 = (bf16[144,512]{1,0:T(8,128)(2,1)S(1)}, bf16[144,512]{1,0:T(8,128)(2,1)S(1)}, u32[]{:S(2)}, u32[]{:S(2)}) collective-permute-start(bf16[144,512]{1,0:T(8,128)(2,1)S(1)} %collective-permute-done.3.four_ref), channel_id=1, source_target_pairs={{0,4},{1,5},{2,6},{3,7},{4,8},{5,9},{6,10},{7,11},{8,12},{9,13},{1... | collective-permute-start | bytes 442376 | tf_op jit(solution)/shard_map/ppermute | solution.py:20
  66.7 2.6 collective-permute-done.4.eight_ref
  69.4 9.1 %shard_map.144 = (bf16[8,512,512]{2,1,0:T(8,128)(2,1)}, bf16[128,512]{1,0:T(8,128)(2,1)}, bf16[128,512]{1,0:T(8,128)(2,1)S(1)}, bf16[128,512]{1,0:T(8,128)(2,1)S...) custom-call(s32[1]{0:T(128)} %bitcast.core_ref, ...), custom_call_target="tpu_custom_call" | custom-call | tf_op jit(solution)/shard_map/pallas_call | solution.py:306
  78.5 0.7 shard_map.148
  79.2 1.9 collective-permute-start.14
  81.2 1.3 collective-permute-start.7
  82.5 11.8 %collective-permute-done.7.four_ref = bf16[272,512]{1,0:T(8,128)(2,1)S(1)} collective-permute-done((bf16[272,512]{1,0:T(8,128)(2,1)S(1)}, bf16[272,512]{1,0:T(8,128)(2,1)S(1)}, u32[]{:S(2)}, u32[]{:S(2)}) %collective-permute-start.7) | collective-permute-done | bytes 278560 | tf_op jit(solution)/shard_map/ppermute | solution.py:20
  94.2 1.3 collective-permute-start.8
  95.6 1.3 collective-permute-start.5
  96.9 1.3 collective-permute-start.10
  98.2 1.3 collective-permute-start.11
  99.5 6.1 %collective-permute-done.5.one_ref = bf16[256,512]{1,0:T(8,128)(2,1)S(1)} collective-permute-done((bf16[256,512]{1,0:T(8,128)(2,1)S(1)}, bf16[256,512]{1,0:T(8,128)(2,1)S(1)}, u32[]{:S(2)}, u32[]{:S(2)}) %collective-permute-start.5) | collective-permute-done | bytes 262176 | tf_op jit(solution)/shard_map/ppermute | solution.py:20
  105.6 1.3 collective-permute-start.12
  106.9 3.3 %collective-permute-done.8.eight_ref = bf16[272,512]{1,0:T(8,128)(2,1)S(1)} collective-permute-done((bf16[272,512]{1,0:T(8,128)(2,1)S(1)}, bf16[272,512]{1,0:T(8,128)(2,1)S(1)}, u32[]{:S(2)}, u32[]{:S(2)}) %collective-permute-start.8) | collective-permute-done | bytes 278560 | tf_op jit(solution)/shard_map/ppermute | solution.py:20
  110.2 1.3 collective-permute-start.9
  111.5 3.5 %shard_map.145 = (bf16[512,512]{1,0:T(8,128)(2,1)S(1)}, bf16[512,512]{1,0:T(8,128)(2,1)S(1)}) custom-call(bf16[128,512]{1,0:T(8,128)(2,1)S(1)} %bitcast.34, bf16[256,512]{1,0:T(8,128)(2,1)S(1)} %collective-permute-done.5.one_ref, bf16[272,512]{1,0:T(8,128)(2,1)S(1)} %collective-permute-done.6.two_ref, bf16[272,512]{1,0:T(8,128)(2,1)S(1)} %collective-permute-done.7.four_ref, ...), custom_call_target="tpu_custom_call" | custom-call | tf_op jit(solution)/shard_map/pallas_call | solution.py:326
  115.0 5.1 %collective-permute-done.11.four_ref = f32[24,128]{1,0:T(8,128)S(1)} collective-permute-done((f32[24,128]{1,0:T(8,128)S(1)}, f32[24,128]{1,0:T(8,128)S(1)}, u32[]{:S(2)}, u32[]{:S(2)}) %collective-permute-start.11) | collective-permute-done | bytes 12320 | tf_op jit(solution)/shard_map/ppermute | solution.py:20
  120.1 6.8 %collective-permute-done.12.eight_ref = f32[24,128]{1,0:T(8,128)S(1)} collective-permute-done((f32[24,128]{1,0:T(8,128)S(1)}, f32[24,128]{1,0:T(8,128)S(1)}, u32[]{:S(2)}, u32[]{:S(2)}) %collective-permute-start.12) | collective-permute-done | bytes 12320 | tf_op jit(solution)/shard_map/ppermute | solution.py:20
  126.9 5.1 %shard_map.146 = (bf16[128,512]{1,0:T(8,128)(2,1)S(1)}, bf16[128,512]{1,0:T(8,128)(2,1)S(1)}, bf16[8,4,32,512]{3,2,1,0:T(8,128)(2,1)S(1)}, bf16[8,4,32,512]{3,2,1,0:T(8,128)(2,1)}) custom-call(s32[1]{0:T(128)} %bitcast.core_ref, bf16[128,512]{1,0:T(8,128)(2,1)S(1)} %get-tuple-element.30.key_ref, bf16[128,512]{1,0:T(8,128)(2,1)S(1)} %get-tuple-element.31.value_ref, ...), custom_call_target="tpu_custom_call" | custom-call | tf_op jit(solution)/shard_map/pallas_call | solution.py:333
  132.0 1.9 collective-permute-start.15
  133.9 1.5 collective-permute-start.13
  135.4 7.4 %collective-permute-done.13.leading_ref = bf16[16,1024]{1,0:T(8,128)(2,1)S(1)} collective-permute-done((bf16[16,1024]{1,0:T(8,128)(2,1)S(1)}, bf16[16,1024]{1,0:T(8,128)(2,1)S(1)}, u32[]{:S(2)}, u32[]{:S(2)}) %collective-permute-start.13) | collective-permute-done | bytes 32800 | tf_op jit(solution)/shard_map/ppermute | solution.py:20
  142.8 4.3 %shard_map.147 = (bf16[128,512]{1,0:T(8,128)(2,1)}, f32[1,512]{1,0:T(1,128)S(1)}) custom-call(bf16[128,512]{1,0:T(8,128)(2,1)S(1)} %get-tuple-element.29.d_query_ref, bf16[128,512]{1,0:T(8,128)(2,1)S(1)} %get-tuple-element.40.d_key_ref, bf16[128,512]{1,0:T(8,128)(2,1)S(1)} %get-tuple-element.41.d_value_ref, ...), custom_call_target="tpu_custom_call" | custom-call | tf_op jit(solution)/shard_map/pallas_call | solution.py:338
  147.1 0.6 broadcast_in_dim.61
  147.7 5.7 %all-to-all-start.3 = ((f32[16,4,128]{2,1,0:T(4,128)}), f32[16,4,128]{2,1,0:T(4,128)S(1)}, u32[]{:S(2)}, u32[]{:S(2)}) async-start(f32[16,4,128]{2,1,0:T(4,128)} %broadcast_in_dim.61), calls=%async_computation.3 | async-start | bytes 65536 | tf_op jit(solution)/shard_map/all_to_all | solution.py:343
  153.4 2.6 add_convert_fusion.1
  156.0 3.1 %all-to-all-done.3 = f32[16,4,128]{2,1,0:T(4,128)S(1)} async-done(((f32[16,4,128]{2,1,0:T(4,128)}), f32[16,4,128]{2,1,0:T(4,128)S(1)}, u32[]{:S(2)}, u32[]{:S(2)}) %all-to-all-start.3) | async-done | bytes 32800 | tf_op jit(solution)/shard_map/all_to_all | solution.py:343
  159.1 5.5 %all-to-all-start.1 = ((bf16[8,4,32,512]{3,2,1,0:T(8,128)(2,1)}), bf16[8,4,32,512]{3,2,1,0:T(8,128)(2,1)S(1)}, u32[]{:S(2)}, u32[]{:S(2)}) async-start(bf16[8,4,32,512]{3,2,1,0:T(8,128)(2,1)} %add_convert_fusion.1), calls=%async_computation.1 | async-start | bytes 2097152 | tf_op jit(solution)/shard_map/all_to_all | solution.py:28
  164.6 2.6 add_convert_fusion
  167.2 12.6 %all-to-all-done.1 = bf16[8,4,32,512]{3,2,1,0:T(8,128)(2,1)S(1)} async-done(((bf16[8,4,32,512]{3,2,1,0:T(8,128)(2,1)}), bf16[8,4,32,512]{3,2,1,0:T(8,128)(2,1)S(1)}, u32[]{:S(2)}, u32[]{:S(2)}) %all-to-all-start.1) | async-done | bytes 1048608 | tf_op jit(solution)/shard_map/all_to_all | solution.py:28
  179.8 5.3 %all-to-all-start.2 = ((bf16[8,4,32,512]{3,2,1,0:T(8,128)(2,1)}), bf16[8,4,32,512]{3,2,1,0:T(8,128)(2,1)S(1)}, u32[]{:S(2)}, u32[]{:S(2)}) async-start(bf16[8,4,32,512]{3,2,1,0:T(8,128)(2,1)} %add_convert_fusion), calls=%async_computation.2 | async-start | bytes 2097152 | tf_op jit(solution)/shard_map/all_to_all | solution.py:28
  185.3 14.6 %all-to-all-done.2 = bf16[8,4,32,512]{3,2,1,0:T(8,128)(2,1)S(1)} async-done(((bf16[8,4,32,512]{3,2,1,0:T(8,128)(2,1)}), bf16[8,4,32,512]{3,2,1,0:T(8,128)(2,1)S(1)}, u32[]{:S(2)}, u32[]{:S(2)}) %all-to-all-start.2) | async-done | bytes 1048608 | tf_op jit(solution)/shard_map/all_to_all | solution.py:28
  200.1 41.3 %all_to_all.31 = bf16[32,8,640]{2,1,0:T(8,128)(2,1)S(1)} all-to-all(bf16[32,8,640]{2,1,0:T(8,128)(2,1)S(1)} %pad_maximum_fusion), channel_id=1, replica_groups=mesh['dp'=16,'ctx'=32] {'ctx'}, dimensions={0} | all-to-all | bytes 655360 | tf_op jit(solution)/shard_map/all_to_all | solution.py:349
  241.5 0.7 broadcast_in_dim.63
  242.2 3.9 %all-to-all-start.5 = ((bf16[32,8,512]{2,1,0:T(8,128)(2,1)}), bf16[32,8,512]{2,1,0:T(8,128)(2,1)S(1)}, u32[]{:S(2)}, u32[]{:S(2)}) async-start(bf16[32,8,512]{2,1,0:T(8,128)(2,1)} %broadcast_in_dim.63), calls=%async_computation.5 | async-start | bytes 524288 | tf_op jit(solution)/shard_map/all_to_all | solution.py:353
  246.7 19.6 %all-to-all-done.5 = bf16[32,8,512]{2,1,0:T(8,128)(2,1)S(1)} async-done(((bf16[32,8,512]{2,1,0:T(8,128)(2,1)}), bf16[32,8,512]{2,1,0:T(8,128)(2,1)S(1)}, u32[]{:S(2)}, u32[]{:S(2)}) %all-to-all-start.5) | async-done | bytes 262176 | tf_op jit(solution)/shard_map/all_to_all | solution.py:353
  266.3 0.7 slice_bitcast_fusion
  266.9 0.8 fusion.1
  (44 shorter events, 1.8 us)
Async XLA Ops:
  1.9 35.1 %copy-start = (bf16[1,128,512]{2,1,0:T(8,128)(2,1)S(1)}, bf16[1,128,512]{2,1,0:T(8,128)(2,1)}, u32[]{:S(2)}) copy-start(bf16[1,128,512]{2,1,0:T(8,128)(2,1)} %param.9) | copy-start | bytes 393220
  1.9 37.9 %copy-start.3 = (s32[1,1,8,4]{2,3,1,0:T(4,128)S(1)}, s32[1,1,8,4]{2,3,1,0:T(4,128)}, u32[]{:S(2)}) copy-start(s32[1,1,8,4]{2,3,1,0:T(4,128)} %param.15) | copy-start | bytes 388
  1.9 47.7 %copy-start.4 = (s32[4]{0:T(128)S(1)}, s32[4]{0:T(128)}, u32[]{:S(2)}) copy-start(s32[4]{0:T(128)} %constant.34.clone) | copy-start | bytes 52
  1.9 55.0 %copy-start.1 = (bf16[1,128,512]{2,1,0:T(8,128)(2,1)S(1)}, bf16[1,128,512]{2,1,0:T(8,128)(2,1)}, u32[]{:S(2)}) copy-start(bf16[1,128,512]{2,1,0:T(8,128)(2,1)} %param.16) | copy-start | bytes 393220
  2.0 67.4 %copy-start.2 = (f32[512]{0:T(512)S(1)}, f32[512]{0:T(512)}, u32[]{:S(2)}) copy-start(f32[512]{0:T(512)} %param.10) | copy-start | bytes 6148
  35.1 34.2 %collective-permute-start = (bf16[8,8,32,512]{3,2,1,0:T(8,128)(2,1)}, bf16[8,8,32,512]{3,2,1,0:T(8,128)(2,1)}, u32[]{:S(2)}, u32[]{:S(2)}) collective-permute-start(bf16[8,8,32,512]{3,2,1,0:T(8,128)(2,1)} %all_to_all.30.mine_ref), channel_id=1, source_target_pairs={{0,32},{32,0},{64,96},{96,64},{128,160},{160,128},{192,224},{224,1... | collective-permute-start | bytes 6291464 | tf_op jit(solution)/shard_map/ppermute | solution.py:24
  37.0 6.2 %collective-permute-start.1 = (bf16[128,512]{1,0:T(8,128)(2,1)S(1)}, bf16[128,512]{1,0:T(8,128)(2,1)S(1)}, u32[]{:S(2)}, u32[]{:S(2)}) collective-permute-start(bf16[128,512]{1,0:T(8,128)(2,1)S(1)} %bitcast.30), channel_id=1, source_target_pairs={{0,1},{1,2},{2,3},{3,4},{4,5},{5,6},{6,7},{7,8},{8,9},{9,10},{10,1... | collective-permute-start | bytes 393224 | tf_op jit(solution)/shard_map/ppermute | solution.py:20
  43.2 9.3 %collective-permute-start.2 = (bf16[144,512]{1,0:T(8,128)(2,1)S(1)}, bf16[144,512]{1,0:T(8,128)(2,1)S(1)}, u32[]{:S(2)}, u32[]{:S(2)}) collective-permute-start(bf16[144,512]{1,0:T(8,128)(2,1)S(1)} %pad_maximum_fusion.5.window_ref), channel_id=1, source_target_pairs={{0,2},{1,3},{2,4},{3,5},{4,6},{5,7},{6,8},{7,9},{8,10},{9,11},{10,... | collective-permute-start | bytes 442376 | tf_op jit(solution)/shard_map/ppermute | solution.py:20
  52.6 7.0 %collective-permute-start.3 = (bf16[144,512]{1,0:T(8,128)(2,1)S(1)}, bf16[144,512]{1,0:T(8,128)(2,1)S(1)}, u32[]{:S(2)}, u32[]{:S(2)}) collective-permute-start(bf16[144,512]{1,0:T(8,128)(2,1)S(1)} %collective-permute-done.2.two_ref), channel_id=1, source_target_pairs={{0,2},{1,3},{2,4},{3,5},{4,6},{5,7},{6,8},{7,9},{8,10},{9,11},{10,... | collective-permute-start | bytes 442376 | tf_op jit(solution)/shard_map/ppermute | solution.py:20
  57.0 24.2 %collective-permute-start.6 = (bf16[272,512]{1,0:T(8,128)(2,1)S(1)}, bf16[272,512]{1,0:T(8,128)(2,1)S(1)}, u32[]{:S(2)}, u32[]{:S(2)}) collective-permute-start(bf16[272,512]{1,0:T(8,128)(2,1)S(1)} %pad_maximum_fusion.1), channel_id=1, source_target_pairs={{2,0},{3,1},{4,2},{5,3},{6,4},{7,5},{8,6},{9,7},{10,8},{11,9},{12,... | collective-permute-start | bytes 835592 | tf_op jit(solution)/shard_map/ppermute | solution.py:20
  59.6 9.7 %collective-permute-start.4 = (bf16[144,512]{1,0:T(8,128)(2,1)S(1)}, bf16[144,512]{1,0:T(8,128)(2,1)S(1)}, u32[]{:S(2)}, u32[]{:S(2)}) collective-permute-start(bf16[144,512]{1,0:T(8,128)(2,1)S(1)} %collective-permute-done.3.four_ref), channel_id=1, source_target_pairs={{0,4},{1,5},{2,6},{3,7},{4,8},{5,9},{6,10},{7,11},{8,12},{9,13},{1... | collective-permute-start | bytes 442376 | tf_op jit(solution)/shard_map/ppermute | solution.py:20
  79.2 74.2 %collective-permute-start.14 = (bf16[8,4,32,512]{3,2,1,0:T(8,128)(2,1)S(1)}, bf16[8,4,32,512]{3,2,1,0:T(8,128)(2,1)}, u32[]{:S(2)}, u32[]{:S(2)}) collective-permute-start(bf16[8,4,32,512]{3,2,1,0:T(8,128)(2,1)S(1)} %get-tuple-element.45), channel_id=1, source_target_pairs={{0,32},{32,0},{64,96},{96,64},{128,160},{160,128},{192,224},{224,1... | collective-permute-start | bytes 3145736 | tf_op jit(solution)/shard_map/ppermute | solution.py:24
  81.2 13.1 %collective-permute-start.7 = (bf16[272,512]{1,0:T(8,128)(2,1)S(1)}, bf16[272,512]{1,0:T(8,128)(2,1)S(1)}, u32[]{:S(2)}, u32[]{:S(2)}) collective-permute-start(bf16[272,512]{1,0:T(8,128)(2,1)S(1)} %collective-permute-done.6.two_ref), channel_id=1, source_target_pairs={{2,0},{3,1},{4,2},{5,3},{6,4},{7,5},{8,6},{9,7},{10,8},{11,9},{12,... | collective-permute-start | bytes 835592 | tf_op jit(solution)/shard_map/ppermute | solution.py:20
  94.2 15.9 %collective-permute-start.8 = (bf16[272,512]{1,0:T(8,128)(2,1)S(1)}, bf16[272,512]{1,0:T(8,128)(2,1)S(1)}, u32[]{:S(2)}, u32[]{:S(2)}) collective-permute-start(bf16[272,512]{1,0:T(8,128)(2,1)S(1)} %collective-permute-done.7.four_ref), channel_id=1, source_target_pairs={{4,0},{5,1},{6,2},{7,3},{8,4},{9,5},{10,6},{11,7},{12,8},{13,9},{1... | collective-permute-start | bytes 835592 | tf_op jit(solution)/shard_map/ppermute | solution.py:20
  95.6 10.0 %collective-permute-start.5 = (bf16[256,512]{1,0:T(8,128)(2,1)S(1)}, bf16[256,512]{1,0:T(8,128)(2,1)S(1)}, u32[]{:S(2)}, u32[]{:S(2)}) collective-permute-start(bf16[256,512]{1,0:T(8,128)(2,1)S(1)} %pad_maximum_fusion.3), channel_id=1, source_target_pairs={{1,0},{2,1},{3,2},{4,3},{5,4},{6,5},{7,6},{8,7},{9,8},{10,9},{11,1... | collective-permute-start | bytes 786440 | tf_op jit(solution)/shard_map/ppermute | solution.py:20
  96.9 18.1 %collective-permute-start.10 = (f32[24,128]{1,0:T(8,128)S(1)}, f32[24,128]{1,0:T(8,128)S(1)}, u32[]{:S(2)}, u32[]{:S(2)}) collective-permute-start(f32[24,128]{1,0:T(8,128)S(1)} %get-tuple-element.57), channel_id=1, source_target_pairs={{2,0},{3,1},{4,2},{5,3},{6,4},{7,5},{8,6},{9,7},{10,8},{11,9},{12,... | collective-permute-start | bytes 36872 | tf_op jit(solution)/shard_map/ppermute | solution.py:20
  98.2 21.9 %collective-permute-start.11 = (f32[24,128]{1,0:T(8,128)S(1)}, f32[24,128]{1,0:T(8,128)S(1)}, u32[]{:S(2)}, u32[]{:S(2)}) collective-permute-start(f32[24,128]{1,0:T(8,128)S(1)} %get-tuple-element.56), channel_id=1, source_target_pairs={{4,0},{5,1},{6,2},{7,3},{8,4},{9,5},{10,6},{11,7},{12,8},{13,9},{1... | collective-permute-start | bytes 36872 | tf_op jit(solution)/shard_map/ppermute | solution.py:20
  105.6 21.3 %collective-permute-start.12 = (f32[24,128]{1,0:T(8,128)S(1)}, f32[24,128]{1,0:T(8,128)S(1)}, u32[]{:S(2)}, u32[]{:S(2)}) collective-permute-start(f32[24,128]{1,0:T(8,128)S(1)} %get-tuple-element.55), channel_id=1, source_target_pairs={{8,0},{9,1},{10,2},{11,3},{12,4},{13,5},{14,6},{15,7},{16,8},{17,9... | collective-permute-start | bytes 36872 | tf_op jit(solution)/shard_map/ppermute | solution.py:20
  110.2 16.8 %collective-permute-start.9 = (f32[24,128]{1,0:T(8,128)S(1)}, f32[24,128]{1,0:T(8,128)S(1)}, u32[]{:S(2)}, u32[]{:S(2)}) collective-permute-start(f32[24,128]{1,0:T(8,128)S(1)} %get-tuple-element.58), channel_id=1, source_target_pairs={{1,0},{2,1},{3,2},{4,3},{5,4},{6,5},{7,6},{8,7},{9,8},{10,9},{11,1... | collective-permute-start | bytes 36872 | tf_op jit(solution)/shard_map/ppermute | solution.py:20
  132.0 32.6 %collective-permute-start.15 = (bf16[8,4,32,512]{3,2,1,0:T(8,128)(2,1)}, bf16[8,4,32,512]{3,2,1,0:T(8,128)(2,1)}, u32[]{:S(2)}, u32[]{:S(2)}) collective-permute-start(bf16[8,4,32,512]{3,2,1,0:T(8,128)(2,1)} %get-tuple-element.47), channel_id=1, source_target_pairs={{0,32},{32,0},{64,96},{96,64},{128,160},{160,128},{192,224},{224,1... | collective-permute-start | bytes 3145736 | tf_op jit(solution)/shard_map/ppermute | solution.py:24
  133.9 8.8 %collective-permute-start.13 = (bf16[16,1024]{1,0:T(8,128)(2,1)S(1)}, bf16[16,1024]{1,0:T(8,128)(2,1)S(1)}, u32[]{:S(2)}, u32[]{:S(2)}) collective-permute-start(bf16[16,1024]{1,0:T(8,128)(2,1)S(1)} %pad_maximum_fusion.6), channel_id=1, source_target_pairs={{1,0},{2,1},{3,2},{4,3},{5,4},{6,5},{7,6},{8,7},{9,8},{10,9},{11,1... | collective-permute-start | bytes 98312 | tf_op jit(solution)/shard_map/ppermute | solution.py:20
  147.7 11.5 %all-to-all-start.3 = ((f32[16,4,128]{2,1,0:T(4,128)}), f32[16,4,128]{2,1,0:T(4,128)S(1)}, u32[]{:S(2)}, u32[]{:S(2)}) async-start(f32[16,4,128]{2,1,0:T(4,128)} %broadcast_in_dim.61), calls=%async_computation.3 | async-start | bytes 65536 | tf_op jit(solution)/shard_map/all_to_all | solution.py:343
  159.1 20.7 %all-to-all-start.1 = ((bf16[8,4,32,512]{3,2,1,0:T(8,128)(2,1)}), bf16[8,4,32,512]{3,2,1,0:T(8,128)(2,1)S(1)}, u32[]{:S(2)}, u32[]{:S(2)}) async-start(bf16[8,4,32,512]{3,2,1,0:T(8,128)(2,1)} %add_convert_fusion.1), calls=%async_computation.1 | async-start | bytes 2097152 | tf_op jit(solution)/shard_map/all_to_all | solution.py:28
  179.8 20.1 %all-to-all-start.2 = ((bf16[8,4,32,512]{3,2,1,0:T(8,128)(2,1)}), bf16[8,4,32,512]{3,2,1,0:T(8,128)(2,1)S(1)}, u32[]{:S(2)}, u32[]{:S(2)}) async-start(bf16[8,4,32,512]{3,2,1,0:T(8,128)(2,1)} %add_convert_fusion), calls=%async_computation.2 | async-start | bytes 2097152 | tf_op jit(solution)/shard_map/all_to_all | solution.py:28
  242.2 24.0 %all-to-all-start.5 = ((bf16[32,8,512]{2,1,0:T(8,128)(2,1)}), bf16[32,8,512]{2,1,0:T(8,128)(2,1)S(1)}, u32[]{:S(2)}, u32[]{:S(2)}) async-start(bf16[32,8,512]{2,1,0:T(8,128)(2,1)} %broadcast_in_dim.63), calls=%async_computation.5 | async-start | bytes 524288 | tf_op jit(solution)/shard_map/all_to_all | solution.py:353

commit v3 on v2

--- a/solution.py
+++ b/solution.py
@@ -38,6 +38,11 @@
 
 def product_left_t(left, right):
     return lax.dot_general(left, right, (((0,), (0,)), ((), ())), preferred_element_type=f32)
+
+
+def in_two(values):
+    top = values.astype(bf16)
+    return top, (values - top.astype(f32)).astype(bf16)
 
 
 def inverse_rms(values):
@@ -258,16 +263,19 @@
             d_normed = d_normed + product_right_t(part, weights_ref[base + tap])
     values = own_ref[...].astype(f32)
     scale = inverse_rms(values)
-    d_gain_ref[...] = jnp.sum(d_normed * values * scale, axis=0, keepdims=True)
+    top, rest = in_two(jnp.sum(d_normed * values * scale, axis=0, keepdims=True))
+    blank = jnp.zeros((d_gain_ref.shape[0] - 2, features), f32)
+    d_gain_ref[...] = jnp.concatenate(
+        [top.astype(f32), rest.astype(f32), blank], axis=0
+    ).astype(bf16)
     slope = d_normed * gain_ref[...]
     along = jnp.mean(slope * values, axis=-1, keepdims=True)
     d_values = scale * slope - values * (scale * scale * scale * along)
     grad_ref[...] = (upstream_ref[...].astype(f32) + d_values).astype(bf16)
 
 
-def reduce_rows(keep, send):
-    half = (keep.astype(f32) + other_core(send).astype(f32)).astype(bf16)
-    return jnp.sum(over_chips(half).astype(f32), axis=0).astype(bf16)
+def halve(keep, send):
+    return (keep.astype(f32) + other_core(send).astype(f32)).astype(bf16)
 
 
 def body(
@@ -279,20 +287,25 @@
     own, cotangent = series[0], grad_out[0]
     count, features = own.shape
     gain = norm_gain.reshape(1, features)
-    shard = jnp.concatenate(
-        [key_kernel, value_weight[None], query_kernel, out_weight[None]], axis=0
-    )
-    mine = over_chips(jnp.broadcast_to(shard[None], (8,) + shard.shape))
 
     before_one = shift_ctx(own, 1)
     after_one = shift_ctx(jnp.concatenate([own, cotangent], axis=0), -1)
     window = jnp.concatenate([before_one[count - edge :], own], axis=0)
-    before_two = shift_ctx(window, 2)
-    after_two = shift_ctx(jnp.concatenate([window, cotangent], axis=0), -2)
-    before_four = shift_ctx(before_two, 2)
-    after_four = shift_ctx(after_two, -2)
-    before_eight = shift_ctx(before_four, 4)
-    after_eight = shift_ctx(after_four, -4)
+    carried = jnp.concatenate([window, cotangent], axis=0)
+    before_four, before_two = shift_ctx(window, 4), shift_ctx(window, 2)
+    after_four, after_two = shift_ctx(carried, -4), shift_ctx(carried, -2)
+    before_eight, after_eight = shift_ctx(before_four, 4), shift_ctx(after_four, -4)
+    shard = jnp.concatenate(
+        [key_kernel, value_weight[None], query_kernel, out_weight[None]], axis=0
+    )
+    mine = lax.all_gather(
+        shard.reshape(256, features), "dp", axis=0, axis_index_groups=chip_groups, tiled=True
+    ).reshape(8, 8, 32, features)
+    (
+        mine, before_two, before_four, before_eight, after_one, after_two, after_four, after_eight
+    ) = lax.optimization_barrier(
+        (mine, before_two, before_four, before_eight, after_one, after_two, after_four, after_eight)
+    )
     other = other_core(mine)
 
     offsets = jnp.array(block_offsets, dtype=jnp.int32)
@@ -329,26 +342,31 @@
         [pltpu.VMEM((3, 4 * count, features), bf16), pltpu.VMEM((4 * count, features), bf16)],
         inputs=7,
     )(own, after_one, after_two, after_four, after_eight, gain, weights)
-    rows_query = reduce_rows(keep, send)
+    partial = halve(keep, send)
+    partial, queries, uppers = lax.optimization_barrier((partial, queries, uppers))
+    rows_query = jnp.sum(over_chips(partial).astype(f32), axis=0).astype(bf16)
+    rows_query, key = lax.optimization_barrier((rows_query, key))
     d_key, d_value, keep, send = call(
         columns_kernel, [half, half, parts, parts], smem=1, inputs=13
     )(core, key, value, query, upper, queries, uppers, taps, own_stats, *returned)
     leading = shift_ctx(jnp.concatenate([d_query[:edge], d_key[:edge]], axis=1), -1)
-    rows_key = reduce_rows(keep, send)
+    partial = halve(keep, send).reshape(8, 128, features)
     grad_series, d_gain = call(
-        series_kernel, [half, ((1, features), f32)], inputs=8
+        series_kernel, [half, ((edge, features), bf16)], inputs=8
     )(d_query, d_key, d_value, leading, weights, own, cotangent, gain)
-
-    d_gain = jnp.broadcast_to(d_gain.reshape(1, 4, 128), (16, 4, 128))
-    d_gain = jnp.sum(lax.all_to_all(d_gain, "dp", 0, 0, tiled=True), axis=0)
-    top = d_gain.astype(bf16)
-    rest = (d_gain - top.astype(f32)).astype(bf16)
+    d_gain = jnp.broadcast_to(d_gain[None], (8, edge, features))
+    arrived = over_chips(jnp.concatenate([partial, d_gain], axis=1))
+    arrived = jnp.sum(arrived.astype(f32), axis=0)
+    rows_key = arrived[:128].astype(bf16).reshape(4, 32, features)
+    chip_gain = jnp.sum(arrived[128:], axis=0).reshape(4, 128)
+    top, rest = in_two(chip_gain)
     extra = jnp.broadcast_to(jnp.concatenate([top, rest], axis=0)[None], (32, 8, 128))
     rows = jnp.concatenate([rows_query, rows_key], axis=0).reshape(32, 8, features)
     payload = jnp.concatenate([rows, extra], axis=2)
     arrived = lax.all_to_all(payload, "ctx", 0, 0, tiled=True).astype(f32)
     summed = jnp.sum(arrived, axis=0)
-    gain_total = (summed[:4, features:] + summed[4:, features:]).reshape(features)
+    core_gain = summed[:4, features:] + summed[4:, features:]
+    gain_total = (core_gain + other_core(core_gain)).reshape(features)
     summed = summed[:, :features].astype(bf16)
     final = lax.all_to_all(
         jnp.broadcast_to(summed[None], (32, 8, features)), "ctx", 0, 0, tiled=True

time: 271 us -> 241 us (0.89)
  waiting for transfers between devices: 100 us -> 79.6 us
  blocking collectives: 74.4 us -> 58.5 us
  between operations: 1.04 us -> 14.5 us
  starting transfers between devices: 58.5 us -> 52.2 us
    ppermute x13, waiting for transfers between devices: 50.5 us -> 18.8 us  [shift_ctx(): return lax.ppermute(shard, 'ctx', pairs)]
    all_gather x0 -> x1, waiting for transfers between devices: none -> 28.6 us  [body(): lax.all_gather(shard.reshape(256, features), 'dp', axis=0, axis_index_gro...]
    all_to_all x2 -> x1, waiting for transfers between devices: 27.2 us -> 10.4 us  [over_chips(): lax.all_to_all(stacked, 'dp', 0, 0, axis_index_groups=chip_groups, tiled=...]
    all_to_all x1, blocking collectives: 33.1 us -> 21 us  [over_chips(): lax.all_to_all(stacked, 'dp', 0, 0, axis_index_groups=chip_groups, tiled=...]
    all_to_all x1 -> x0, starting transfers between devices: 5.75 us -> none  [body(): d_gain = jnp.sum(lax.all_to_all(d_gain, 'dp', 0, 0, tiled=True), axis=0)]
    ppermute x3 -> x4, waiting for transfers between devices: 0.01 us -> 5.36 us  [other_core(): return lax.ppermute(shard, 'dp', [(i, i ^ 1) for i in range(16)])]
    all_to_all x2 -> x1, starting transfers between devices: 10.8 us -> 5.6 us  [over_chips(): lax.all_to_all(stacked, 'dp', 0, 0, axis_index_groups=chip_groups, tiled=...]
    all_to_all x1, blocking collectives: 41.3 us -> 37.5 us  [body(): arrived = lax.all_to_all(payload, 'ctx', 0, 0, tiled=True).astype(f32)]
  transfers between devices with their start and end apart: 20 -> 20, of which waited for: 14 -> 10; matrix products, arithmetic and copies ran while one was open for 3% -> 2% of each run, Pallas kernels for 8% -> 3%
where the time goes in v3:
time: 241 us; the launch traced here: 238 us
  waiting for transfers between devices  79.6 us (33%)
  blocking collectives  58.5 us (24%)
  starting transfers between devices  52.2 us (22%)
  Pallas kernels  22.8 us (9%)
  between operations  14.5 us (6%)
  other arithmetic  8.33 us (3%)
  local copies, waits for them, and re-layouts  2.5 us (1%)
    all_to_all x1, blocking collectives, body(): arrived = lax.all_to_all(payload, 'ctx', 0, 0, tiled=True).astype(f32)  37.5 us
    ppermute x13, starting transfers between devices, shift_ctx(): return lax.ppermute(shard, 'ctx', pairs)  34.7 us
    all_gather x1, waiting for transfers between devices, body(): lax.all_gather(shard.reshape(256, features), 'dp', axis=0, axis_index_gro...  28.6 us
    all_to_all x1, blocking collectives, over_chips(): lax.all_to_all(stacked, 'dp', 0, 0, axis_index_groups=chip_groups, tiled=...  21 us
    ppermute x13, waiting for transfers between devices, shift_ctx(): return lax.ppermute(shard, 'ctx', pairs)  18.8 us
    all_to_all x1, waiting for transfers between devices, body(): lax.all_to_all(jnp.broadcast_to(summed[None], (32, 8, features)), 'ctx',...  16.4 us
    all_to_all x1, waiting for transfers between devices, over_chips(): lax.all_to_all(stacked, 'dp', 0, 0, axis_index_groups=chip_groups, tiled=...  10.4 us
    pallas_call x1, Pallas kernels, body(): call(rows_kernel, [((8, features, features), bf16)] + [half] * 7 + [((3,...  9.14 us
  transfers between devices with their start and end apart: 20, of which 10 were waited for; matrix products, arithmetic and copies ran while one was open for 2% of the time, Pallas kernels for 3%

profile of v3, /device:TPU:24, one launch (start us, length us, event | category | flops | bytes accessed | tf_op | source)
XLA Modules:
  0.0 238.4 jit_solution(16350400429312143332)
XLA Ops:
  7.3 1.7 pad_maximum_fusion.3
  9.0 3.4 %collective-permute-start = (bf16[128,512]{1,0:T(8,128)(2,1)}, bf16[128,512]{1,0:T(8,128)(2,1)S(1)}, u32[]{:S(2)}, u32[]{:S(2)}) collective-permute-start(bf16[128,512]{1,0:T(8,128)(2,1)} %bitcast.39), channel_id=1, source_target_pairs={{0,1},{1,2},{2,3},{3,4},{4,5},{5,6},{6,7},{7,8},{8,9},{9,10},{10,1... | collective-permute-start | bytes 393224 | tf_op jit(solution)/shard_map/ppermute | solution.py:20
  12.4 3.0 %collective-permute-done.one_ref = bf16[128,512]{1,0:T(8,128)(2,1)S(1)} collective-permute-done((bf16[128,512]{1,0:T(8,128)(2,1)}, bf16[128,512]{1,0:T(8,128)(2,1)S(1)}, u32[]{:S(2)}, u32[]{:S(2)}) %collective-permute-start) | collective-permute-done | bytes 131104 | tf_op jit(solution)/shard_map/ppermute | solution.py:20
  15.5 1.0 pad_maximum_fusion.2
  16.5 1.3 collective-permute-start.6
  17.8 1.3 collective-permute-start.5
  19.1 0.9 pad_maximum_fusion.6.window_ref
  20.0 8.2 %collective-permute-start.2 = (bf16[144,512]{1,0:T(8,128)(2,1)S(1)}, bf16[144,512]{1,0:T(8,128)(2,1)S(1)}, u32[]{:S(2)}, u32[]{:S(2)}) collective-permute-start(bf16[144,512]{1,0:T(8,128)(2,1)S(1)} %pad_maximum_fusion.6.window_ref), channel_id=1, source_target_pairs={{0,4},{1,5},{2,6},{3,7},{4,8},{5,9},{6,10},{7,11},{8,12},{9,13},{1... | collective-permute-start | bytes 442376 | tf_op jit(solution)/shard_map/ppermute | solution.py:20
  28.2 8.5 %collective-permute-done.6.four_ref = bf16[272,512]{1,0:T(8,128)(2,1)S(1)} collective-permute-done((bf16[272,512]{1,0:T(8,128)(2,1)S(1)}, bf16[272,512]{1,0:T(8,128)(2,1)S(1)}, u32[]{:S(2)}, u32[]{:S(2)}) %collective-permute-start.6) | collective-permute-done | bytes 278560 | tf_op jit(solution)/shard_map/ppermute | solution.py:20
  36.7 1.3 collective-permute-start.7
  38.0 1.0 pad_maximum_fusion.4
  39.0 1.3 collective-permute-start.4
  40.3 3.9 %collective-permute-start.1 = (bf16[144,512]{1,0:T(8,128)(2,1)S(1)}, bf16[144,512]{1,0:T(8,128)(2,1)S(1)}, u32[]{:S(2)}, u32[]{:S(2)}) collective-permute-start(bf16[144,512]{1,0:T(8,128)(2,1)S(1)} %pad_maximum_fusion.6.window_ref), channel_id=1, source_target_pairs={{0,2},{1,3},{2,4},{3,5},{4,6},{5,7},{6,8},{7,9},{8,10},{9,11},{10,... | collective-permute-start | bytes 442376 | tf_op jit(solution)/shard_map/ppermute | solution.py:20
  44.2 7.6 %collective-permute-start.3 = (bf16[144,512]{1,0:T(8,128)(2,1)S(1)}, bf16[144,512]{1,0:T(8,128)(2,1)S(1)}, u32[]{:S(2)}, u32[]{:S(2)}) collective-permute-start(bf16[144,512]{1,0:T(8,128)(2,1)S(1)} %collective-permute-done.2.four_ref), channel_id=1, source_target_pairs={{0,4},{1,5},{2,6},{3,7},{4,8},{5,9},{6,10},{7,11},{8,12},{9,13},{1... | collective-permute-start | bytes 442376 | tf_op jit(solution)/shard_map/ppermute | solution.py:20
  51.8 2.7 %collective-permute-done.3.eight_ref = bf16[144,512]{1,0:T(8,128)(2,1)S(1)} collective-permute-done((bf16[144,512]{1,0:T(8,128)(2,1)S(1)}, bf16[144,512]{1,0:T(8,128)(2,1)S(1)}, u32[]{:S(2)}, u32[]{:S(2)}) %collective-permute-start.3) | collective-permute-done | bytes 147488 | tf_op jit(solution)/shard_map/ppermute | solution.py:20
  54.6 28.6 %all-gather.2.cloned.1.call-done = bf16[2048,512]{1,0:T(8,128)(2,1)} async-done(((bf16[256,512]{1,0:T(8,128)(2,1)}), bf16[2048,512]{1,0:T(8,128)(2,1)}) %all-gather.2.cloned.1.call-update) | async-done | bytes 2097168 | tf_op jit(solution)/shard_map/all_gather | solution.py:301
  83.2 1.9 collective-permute-start.8
  85.2 0.1 copy.18
  85.4 4.2 %collective-permute-done.8.other_ref = bf16[8,8,32,512]{3,2,1,0:T(8,128)(2,1)} collective-permute-done((bf16[8,8,32,512]{3,2,1,0:T(8,128)(2,1)}, bf16[8,8,32,512]{3,2,1,0:T(8,128)(2,1)}, u32[]{:S(2)}, u32[]{:S(2)}) %collective-permute-start.8) | collective-permute-done | bytes 2097184 | tf_op jit(solution)/shard_map/ppermute | solution.py:24
  89.7 9.1 %shard_map.144 = (bf16[8,512,512]{2,1,0:T(8,128)(2,1)}, bf16[128,512]{1,0:T(8,128)(2,1)}, bf16[128,512]{1,0:T(8,128)(2,1)S(1)}, bf16[128,512]{1,0:T(8,128)(2,1)S...) custom-call(s32[1]{0:T(128)} %bitcast.core_ref, ...), custom_call_target="tpu_custom_call" | custom-call | tf_op jit(solution)/shard_map/pallas_call | solution.py:319
  98.8 0.7 shard_map.145
  99.6 2.0 collective-permute-start.9
  101.6 3.5 %shard_map.146 = (bf16[512,512]{1,0:T(8,128)(2,1)S(1)}, bf16[512,512]{1,0:T(8,128)(2,1)S(1)}) custom-call(bf16[128,512]{1,0:T(8,128)(2,1)S(1)} %bitcast.43, bf16[256,512]{1,0:T(8,128)(2,1)S(1)} %collective-permute-done.4.one_ref, bf16[272,512]{1,0:T(8,128)(2,1)S(1)} %collective-permute-done.5.two_ref, bf16[272,512]{1,0:T(8,128)(2,1)S(1)} %collective-permute-done.6.four_ref, ...), custom_call_target="tpu_custom_call" | custom-call | tf_op jit(solution)/shard_map/pallas_call | solution.py:339
  105.2 1.4 add_convert_fusion.1
  106.6 5.6 %all-to-all-start = ((bf16[8,4,32,512]{3,2,1,0:T(8,128)(2,1)}), bf16[8,4,32,512]{3,2,1,0:T(8,128)(2,1)S(1)}, u32[]{:S(2)}, u32[]{:S(2)}) async-start(bf16[8,4,32,512]{3,2,1,0:T(8,128)(2,1)} %add_convert_fusion.1), calls=%async_computation | async-start | bytes 2097152 | tf_op jit(solution)/shard_map/all_to_all | solution.py:28
  112.2 1.3 collective-permute-start.13
  113.5 1.3 collective-permute-start.12
  114.8 1.3 collective-permute-start.11
  116.1 1.3 collective-permute-start.10
  117.4 10.4 %all-to-all-done = bf16[8,4,32,512]{3,2,1,0:T(8,128)(2,1)S(1)} async-done(((bf16[8,4,32,512]{3,2,1,0:T(8,128)(2,1)}), bf16[8,4,32,512]{3,2,1,0:T(8,128)(2,1)S(1)}, u32[]{:S(2)}, u32[]{:S(2)}) %all-to-all-start) | async-done | bytes 1048608 | tf_op jit(solution)/shard_map/all_to_all | solution.py:28
  127.8 0.8 reduce_sum.39
  128.7 5.1 %shard_map.147 = (bf16[128,512]{1,0:T(8,128)(2,1)S(1)}, bf16[128,512]{1,0:T(8,128)(2,1)S(1)}, bf16[8,4,32,512]{3,2,1,0:T(8,128)(2,1)S(1)}, bf16[8,4,32,512]{3,2,1,0:T(8,128)(2,1)}) custom-call(s32[1]{0:T(128)} %bitcast.core_ref, bf16[128,512]{1,0:T(8,128)(2,1)S(1)} %get-tuple-element.60.key_ref, bf16[128,512]{1,0:T(8,128)(2,1)S(1)} %get-tuple-element.61.value_ref, ...), custom_call_target="tpu_custom_call" | custom-call | tf_op jit(solution)/shard_map/pallas_call | solution.py:349
  133.8 2.1 collective-permute-start.15
  135.9 1.3 collective-permute-start.14
  137.2 4.5 %collective-permute-done.14.leading_ref = bf16[16,1024]{1,0:T(8,128)(2,1)S(1)} collective-permute-done((bf16[16,1024]{1,0:T(8,128)(2,1)S(1)}, bf16[16,1024]{1,0:T(8,128)(2,1)S(1)}, u32[]{:S(2)}, u32[]{:S(2)}) %collective-permute-start.14) | collective-permute-done | bytes 32800 | tf_op jit(solution)/shard_map/ppermute | solution.py:20
  141.7 4.3 %shard_map.148 = (bf16[128,512]{1,0:T(8,128)(2,1)}, bf16[16,512]{1,0:T(8,128)(2,1)S(1)}) custom-call(bf16[128,512]{1,0:T(8,128)(2,1)S(1)} %get-tuple-element.46.d_query_ref, bf16[128,512]{1,0:T(8,128)(2,1)S(1)} %get-tuple-element.68.d_key_ref, bf16[128,512]{1,0:T(8,128)(2,1)S(1)} %get-tuple-element.69.d_value_ref, ...), custom_call_target="tpu_custom_call" | custom-call | tf_op jit(solution)/shard_map/pallas_call | solution.py:354
  146.0 0.4 add_convert_fusion
  146.5 21.0 %all_to_all.20 = bf16[8,144,512]{2,1,0:T(8,128)(2,1)S(1)} all-to-all(bf16[8,144,512]{2,1,0:T(8,128)(2,1)S(1)} %pad_maximum_fusion), channel_id=1, replica_groups={{0,64,128,192,256,320,384,448},{32,96,160,224,288,352,416,480},{1,65,12..., dimensions={0} | all-to-all | bytes 2359296 | tf_op jit(solution)/shard_map/all_to_all | solution.py:28
  167.5 0.2 convert_reduce_fusion
  167.9 37.5 %all_to_all.21 = bf16[32,8,640]{2,1,0:T(8,128)(2,1)S(1)} all-to-all(bf16[32,8,640]{2,1,0:T(8,128)(2,1)S(1)} %pad_maximum_fusion.1), channel_id=1, replica_groups=mesh['dp'=16,'ctx'=32] {'ctx'}, dimensions={0} | all-to-all | bytes 655360 | tf_op jit(solution)/shard_map/all_to_all | solution.py:366
  205.4 0.7 broadcast_in_dim.54
  206.1 3.9 %all-to-all-start.3 = ((bf16[32,8,512]{2,1,0:T(8,128)(2,1)}), bf16[32,8,512]{2,1,0:T(8,128)(2,1)S(1)}, u32[]{:S(2)}, u32[]{:S(2)}) async-start(bf16[32,8,512]{2,1,0:T(8,128)(2,1)} %broadcast_in_dim.54), calls=%async_computation.3 | async-start | bytes 524288 | tf_op jit(solution)/shard_map/all_to_all | solution.py:371
  210.0 1.9 collective-permute-start.16
  211.9 1.1 collective-permute-done.16
  213.1 0.6 add_bitcast_fusion
  213.6 16.4 %all-to-all-done.3 = bf16[32,8,512]{2,1,0:T(8,128)(2,1)S(1)} async-done(((bf16[32,8,512]{2,1,0:T(8,128)(2,1)}), bf16[32,8,512]{2,1,0:T(8,128)(2,1)S(1)}, u32[]{:S(2)}, u32[]{:S(2)}) %all-to-all-start.3) | async-done | bytes 262176 | tf_op jit(solution)/shard_map/all_to_all | solution.py:371
  230.1 0.7 slice_bitcast_fusion
  230.8 0.8 fusion.1
  (49 shorter events, 0.7 us)
Async XLA Ops:
  7.2 78.1 %copy-start.5 = (s32[4]{0:T(128)S(1)}, s32[4]{0:T(128)}, u32[]{:S(2)}) copy-start(s32[4]{0:T(128)} %constant.33.clone) | copy-start | bytes 52
  7.2 82.5 %copy-start.1 = (bf16[1,128,512]{2,1,0:T(8,128)(2,1)S(1)}, bf16[1,128,512]{2,1,0:T(8,128)(2,1)}, u32[]{:S(2)}) copy-start(bf16[1,128,512]{2,1,0:T(8,128)(2,1)} %param.16) | copy-start | bytes 393220
  7.2 78.0 %copy-start.4 = (s32[1,1,8,4]{2,3,1,0:T(4,128)S(1)}, s32[1,1,8,4]{2,3,1,0:T(4,128)}, u32[]{:S(2)}) copy-start(s32[1,1,8,4]{2,3,1,0:T(4,128)} %param.15) | copy-start | bytes 388
  7.2 82.5 %copy-start.2 = (f32[512]{0:T(512)S(1)}, f32[512]{0:T(512)}, u32[]{:S(2)}) copy-start(f32[512]{0:T(512)} %param.10) | copy-start | bytes 6148
  7.2 76.0 %all-gather.2.cloned.1.call-start = ((), (), s32[]{:S(2)}) async-start(), calls=%async_computation.4 | async-start | bytes 2359296 | tf_op jit(solution)/shard_map/all_gather | solution.py:301
  9.0 6.5 %collective-permute-start = (bf16[128,512]{1,0:T(8,128)(2,1)}, bf16[128,512]{1,0:T(8,128)(2,1)S(1)}, u32[]{:S(2)}, u32[]{:S(2)}) collective-permute-start(bf16[128,512]{1,0:T(8,128)(2,1)} %bitcast.39), channel_id=1, source_target_pairs={{0,1},{1,2},{2,3},{3,4},{4,5},{5,6},{6,7},{7,8},{8,9},{9,10},{10,1... | collective-permute-start | bytes 393224 | tf_op jit(solution)/shard_map/ppermute | solution.py:20
  16.5 20.2 %collective-permute-start.6 = (bf16[272,512]{1,0:T(8,128)(2,1)S(1)}, bf16[272,512]{1,0:T(8,128)(2,1)S(1)}, u32[]{:S(2)}, u32[]{:S(2)}) collective-permute-start(bf16[272,512]{1,0:T(8,128)(2,1)S(1)} %pad_maximum_fusion.2), channel_id=1, source_target_pairs={{4,0},{5,1},{6,2},{7,3},{8,4},{9,5},{10,6},{11,7},{12,8},{13,9},{1... | collective-permute-start | bytes 835592 | tf_op jit(solution)/shard_map/ppermute | solution.py:20
  17.8 34.1 %collective-permute-start.5 = (bf16[272,512]{1,0:T(8,128)(2,1)S(1)}, bf16[272,512]{1,0:T(8,128)(2,1)S(1)}, u32[]{:S(2)}, u32[]{:S(2)}) collective-permute-start(bf16[272,512]{1,0:T(8,128)(2,1)S(1)} %pad_maximum_fusion.2), channel_id=1, source_target_pairs={{2,0},{3,1},{4,2},{5,3},{6,4},{7,5},{8,6},{9,7},{10,8},{11,9},{12,... | collective-permute-start | bytes 835592 | tf_op jit(solution)/shard_map/ppermute | solution.py:20
  20.0 24.2 %collective-permute-start.2 = (bf16[144,512]{1,0:T(8,128)(2,1)S(1)}, bf16[144,512]{1,0:T(8,128)(2,1)S(1)}, u32[]{:S(2)}, u32[]{:S(2)}) collective-permute-start(bf16[144,512]{1,0:T(8,128)(2,1)S(1)} %pad_maximum_fusion.6.window_ref), channel_id=1, source_target_pairs={{0,4},{1,5},{2,6},{3,7},{4,8},{5,9},{6,10},{7,11},{8,12},{9,13},{1... | collective-permute-start | bytes 442376 | tf_op jit(solution)/shard_map/ppermute | solution.py:20
  36.7 17.9 %collective-permute-start.7 = (bf16[272,512]{1,0:T(8,128)(2,1)S(1)}, bf16[272,512]{1,0:T(8,128)(2,1)S(1)}, u32[]{:S(2)}, u32[]{:S(2)}) collective-permute-start(bf16[272,512]{1,0:T(8,128)(2,1)S(1)} %collective-permute-done.6.four_ref), channel_id=1, source_target_pairs={{4,0},{5,1},{6,2},{7,3},{8,4},{9,5},{10,6},{11,7},{12,8},{13,9},{1... | collective-permute-start | bytes 835592 | tf_op jit(solution)/shard_map/ppermute | solution.py:20
  39.0 12.8 %collective-permute-start.4 = (bf16[256,512]{1,0:T(8,128)(2,1)S(1)}, bf16[256,512]{1,0:T(8,128)(2,1)S(1)}, u32[]{:S(2)}, u32[]{:S(2)}) collective-permute-start(bf16[256,512]{1,0:T(8,128)(2,1)S(1)} %pad_maximum_fusion.4), channel_id=1, source_target_pairs={{1,0},{2,1},{3,2},{4,3},{5,4},{6,5},{7,6},{8,7},{9,8},{10,9},{11,1... | collective-permute-start | bytes 786440 | tf_op jit(solution)/shard_map/ppermute | solution.py:20
  40.3 11.5 %collective-permute-start.1 = (bf16[144,512]{1,0:T(8,128)(2,1)S(1)}, bf16[144,512]{1,0:T(8,128)(2,1)S(1)}, u32[]{:S(2)}, u32[]{:S(2)}) collective-permute-start(bf16[144,512]{1,0:T(8,128)(2,1)S(1)} %pad_maximum_fusion.6.window_ref), channel_id=1, source_target_pairs={{0,2},{1,3},{2,4},{3,5},{4,6},{5,7},{6,8},{7,9},{8,10},{9,11},{10,... | collective-permute-start | bytes 442376 | tf_op jit(solution)/shard_map/ppermute | solution.py:20
  44.2 10.3 %collective-permute-start.3 = (bf16[144,512]{1,0:T(8,128)(2,1)S(1)}, bf16[144,512]{1,0:T(8,128)(2,1)S(1)}, u32[]{:S(2)}, u32[]{:S(2)}) collective-permute-start(bf16[144,512]{1,0:T(8,128)(2,1)S(1)} %collective-permute-done.2.four_ref), channel_id=1, source_target_pairs={{0,4},{1,5},{2,6},{3,7},{4,8},{5,9},{6,10},{7,11},{8,12},{9,13},{1... | collective-permute-start | bytes 442376 | tf_op jit(solution)/shard_map/ppermute | solution.py:20
  83.2 6.4 %collective-permute-start.8 = (bf16[8,8,32,512]{3,2,1,0:T(8,128)(2,1)}, bf16[8,8,32,512]{3,2,1,0:T(8,128)(2,1)}, u32[]{:S(2)}, u32[]{:S(2)}) collective-permute-start(bf16[8,8,32,512]{3,2,1,0:T(8,128)(2,1)} %bitcast.54), channel_id=1, source_target_pairs={{0,32},{32,0},{64,96},{96,64},{128,160},{160,128},{192,224},{224,1... | collective-permute-start | bytes 6291464 | tf_op jit(solution)/shard_map/ppermute | solution.py:24
  89.7 11.9 %copy-start = (bf16[1,128,512]{2,1,0:T(8,128)(2,1)S(1)}, bf16[1,128,512]{2,1,0:T(8,128)(2,1)}, u32[]{:S(2)}) copy-start(bf16[1,128,512]{2,1,0:T(8,128)(2,1)} %param.9) | copy-start | bytes 393220
  99.6 5.6 %collective-permute-start.9 = (bf16[8,4,32,512]{3,2,1,0:T(8,128)(2,1)S(1)}, bf16[8,4,32,512]{3,2,1,0:T(8,128)(2,1)S(1)}, u32[]{:S(2)}, u32[]{:S(2)}) collective-permute-start(bf16[8,4,32,512]{3,2,1,0:T(8,128)(2,1)S(1)} %get-tuple-element.50), channel_id=1, source_target_pairs={{0,32},{32,0},{64,96},{96,64},{128,160},{160,128},{192,224},{224,1... | collective-permute-start | bytes 3145736 | tf_op jit(solution)/shard_map/ppermute | solution.py:24
  106.6 21.2 %all-to-all-start = ((bf16[8,4,32,512]{3,2,1,0:T(8,128)(2,1)}), bf16[8,4,32,512]{3,2,1,0:T(8,128)(2,1)S(1)}, u32[]{:S(2)}, u32[]{:S(2)}) async-start(bf16[8,4,32,512]{3,2,1,0:T(8,128)(2,1)} %add_convert_fusion.1), calls=%async_computation | async-start | bytes 2097152 | tf_op jit(solution)/shard_map/all_to_all | solution.py:28
  112.2 16.4 %collective-permute-start.13 = (f32[24,128]{1,0:T(8,128)S(1)}, f32[24,128]{1,0:T(8,128)S(1)}, u32[]{:S(2)}, u32[]{:S(2)}) collective-permute-start(f32[24,128]{1,0:T(8,128)S(1)} %get-tuple-element.81), channel_id=1, source_target_pairs={{8,0},{9,1},{10,2},{11,3},{12,4},{13,5},{14,6},{15,7},{16,8},{17,9... | collective-permute-start | bytes 36872 | tf_op jit(solution)/shard_map/ppermute | solution.py:20
  113.5 15.1 %collective-permute-start.12 = (f32[24,128]{1,0:T(8,128)S(1)}, f32[24,128]{1,0:T(8,128)S(1)}, u32[]{:S(2)}, u32[]{:S(2)}) collective-permute-start(f32[24,128]{1,0:T(8,128)S(1)} %get-tuple-element.82), channel_id=1, source_target_pairs={{4,0},{5,1},{6,2},{7,3},{8,4},{9,5},{10,6},{11,7},{12,8},{13,9},{1... | collective-permute-start | bytes 36872 | tf_op jit(solution)/shard_map/ppermute | solution.py:20
  114.8 13.8 %collective-permute-start.11 = (f32[24,128]{1,0:T(8,128)S(1)}, f32[24,128]{1,0:T(8,128)S(1)}, u32[]{:S(2)}, u32[]{:S(2)}) collective-permute-start(f32[24,128]{1,0:T(8,128)S(1)} %get-tuple-element.83), channel_id=1, source_target_pairs={{2,0},{3,1},{4,2},{5,3},{6,4},{7,5},{8,6},{9,7},{10,8},{11,9},{12,... | collective-permute-start | bytes 36872 | tf_op jit(solution)/shard_map/ppermute | solution.py:20
  116.1 12.6 %collective-permute-start.10 = (f32[24,128]{1,0:T(8,128)S(1)}, f32[24,128]{1,0:T(8,128)S(1)}, u32[]{:S(2)}, u32[]{:S(2)}) collective-permute-start(f32[24,128]{1,0:T(8,128)S(1)} %get-tuple-element.84), channel_id=1, source_target_pairs={{1,0},{2,1},{3,2},{4,3},{5,4},{6,5},{7,6},{8,7},{9,8},{10,9},{11,1... | collective-permute-start | bytes 36872 | tf_op jit(solution)/shard_map/ppermute | solution.py:20
  133.8 12.2 %collective-permute-start.15 = (bf16[8,4,32,512]{3,2,1,0:T(8,128)(2,1)}, bf16[8,4,32,512]{3,2,1,0:T(8,128)(2,1)S(1)}, u32[]{:S(2)}, u32[]{:S(2)}) collective-permute-start(bf16[8,4,32,512]{3,2,1,0:T(8,128)(2,1)} %get-tuple-element.73), channel_id=1, source_target_pairs={{0,32},{32,0},{64,96},{96,64},{128,160},{160,128},{192,224},{224,1... | collective-permute-start | bytes 3145736 | tf_op jit(solution)/shard_map/ppermute | solution.py:24
  135.9 5.8 %collective-permute-start.14 = (bf16[16,1024]{1,0:T(8,128)(2,1)S(1)}, bf16[16,1024]{1,0:T(8,128)(2,1)S(1)}, u32[]{:S(2)}, u32[]{:S(2)}) collective-permute-start(bf16[16,1024]{1,0:T(8,128)(2,1)S(1)} %pad_maximum_fusion.7), channel_id=1, source_target_pairs={{1,0},{2,1},{3,2},{4,3},{5,4},{6,5},{7,6},{8,7},{9,8},{10,9},{11,1... | collective-permute-start | bytes 98312 | tf_op jit(solution)/shard_map/ppermute | solution.py:20
  146.5 21.3 %copy-start.3 = (bf16[4,32,512]{2,1,0:T(8,128)(2,1)S(1)}, bf16[4,32,512]{2,1,0:T(8,128)(2,1)}, u32[]{:S(2)}) copy-start(bf16[4,32,512]{2,1,0:T(8,128)(2,1)} %reduce_sum.39) | copy-start | bytes 393220
  206.1 23.9 %all-to-all-start.3 = ((bf16[32,8,512]{2,1,0:T(8,128)(2,1)}), bf16[32,8,512]{2,1,0:T(8,128)(2,1)S(1)}, u32[]{:S(2)}, u32[]{:S(2)}) async-start(bf16[32,8,512]{2,1,0:T(8,128)(2,1)} %broadcast_in_dim.54), calls=%async_computation.3 | async-start | bytes 524288 | tf_op jit(solution)/shard_map/all_to_all | solution.py:371
  210.0 3.1 %collective-permute-start.16 = (f32[4,128]{1,0:T(4,128)S(1)}, f32[4,128]{1,0:T(4,128)S(1)}, u32[]{:S(2)}, u32[]{:S(2)}) collective-permute-start(f32[4,128]{1,0:T(4,128)S(1)} %slice_add_fusion), channel_id=1, source_target_pairs={{0,32},{32,0},{64,96},{96,64},{128,160},{160,128},{192,224},{224,1... | collective-permute-start | bytes 6152 | tf_op jit(solution)/shard_map/ppermute | solution.py:24
Sparse Core Ops, SparseCore 0:
  11.3 71.8 all-gather.1

commit v4 on v3

--- a/solution.py
+++ b/solution.py
@@ -20,8 +20,16 @@
     return lax.ppermute(shard, "ctx", pairs)
 
 
+def dp_to(shard, dx, dy, dc):
+    def target(i):
+        x, y, c = i // 8, (i // 2) % 4, i % 2
+        return ((x + dx) % 2) * 8 + ((y + dy) % 4) * 2 + (c + dc) % 2
+
+    return lax.ppermute(shard, "dp", [(i, target(i)) for i in range(16)])
+
+
 def other_core(shard):
-    return lax.ppermute(shard, "dp", [(i, i ^ 1) for i in range(16)])
+    return dp_to(shard, 0, 0, 1)
 
 
 def over_chips(stacked):
@@ -81,18 +89,22 @@
 
 
 def rows_kernel(
-    core_ref, links_ref, mine_ref, other_ref, window_ref, one_ref, two_ref, four_ref, eight_ref,
-    upstream_ref, gain_ref, barred_ref,
+    place_ref, links_ref, mine_0, mine_1, mine_2, mine_3, other_0, other_1, other_2, other_3,
+    window_ref, one_ref, two_ref, four_ref, eight_ref, upstream_ref, gain_ref, barred_ref,
     weights_ref, mixed_ref, attn_ref, d_query_ref, query_ref, upper_ref, key_ref, value_ref,
     taps_ref, own_stats_ref, stats_ref,
     lines_ref, keys_ref, values_ref,
 ):
-    even = core_ref[0] == 0
-    for chip in range(8):
-        for matrix in range(8):
-            mine, other = mine_ref[chip, matrix], other_ref[chip, matrix]
-            weights_ref[matrix, chip * 64 : chip * 64 + 32] = jnp.where(even, mine, other)
-            weights_ref[matrix, chip * 64 + 32 : chip * 64 + 64] = jnp.where(even, other, mine)
+    x, y, core = place_ref[0], place_ref[1], place_ref[2]
+    pieces = ((mine_0, other_0), (mine_1, other_1), (mine_2, other_2), (mine_3, other_3))
+    for back in range(4):
+        for side in range(2):
+            chip = (x if side == 0 else 1 - x) * 4 + lax.rem(y + 4 - back, 4)
+            for inner in range(2):
+                start = chip * 64 + (core if inner == 0 else 1 - core) * 32
+                rows = pl.ds(pl.multiple_of(start, 32), 32)
+                for matrix in range(8):
+                    weights_ref[matrix, rows] = pieces[back][inner][side, matrix]
     gain = gain_ref[...]
     count = one_ref.shape[0]
     one = jnp.concatenate([two_ref[count:], one_ref[...]], axis=0)
@@ -281,32 +293,37 @@
 def body(
     series, norm_gain, query_kernel, key_kernel, value_weight, out_weight, block_links, grad_out
 ):
-    core = (lax.axis_index("dp") % 2).reshape(1)
+    position = lax.axis_index("dp")
+    place = jnp.stack([position // 8, (position // 2) % 4, position % 2])
+    core = (position % 2).reshape(1)
     block = lax.axis_index("ctx")
     heads = block_links.shape[2]
     own, cotangent = series[0], grad_out[0]
     count, features = own.shape
     gain = norm_gain.reshape(1, features)
 
+    shard = jnp.concatenate(
+        [key_kernel, value_weight[None], query_kernel, out_weight[None]], axis=0
+    )
+    across = dp_to(shard, 1, 0, 0)
     before_one = shift_ctx(own, 1)
     after_one = shift_ctx(jnp.concatenate([own, cotangent], axis=0), -1)
+    across, before_one = lax.optimization_barrier((across, before_one))
+    shards = jnp.stack([shard, across])
+    mine = [shards] + [dp_to(shards, 0, by, 0) for by in (1, 2, 3)]
     window = jnp.concatenate([before_one[count - edge :], own], axis=0)
     carried = jnp.concatenate([window, cotangent], axis=0)
     before_four, before_two = shift_ctx(window, 4), shift_ctx(window, 2)
     after_four, after_two = shift_ctx(carried, -4), shift_ctx(carried, -2)
     before_eight, after_eight = shift_ctx(before_four, 4), shift_ctx(after_four, -4)
-    shard = jnp.concatenate(
-        [key_kernel, value_weight[None], query_kernel, out_weight[None]], axis=0
-    )
-    mine = lax.all_gather(
-        shard.reshape(256, features), "dp", axis=0, axis_index_groups=chip_groups, tiled=True
-    ).reshape(8, 8, 32, features)
-    (
-        mine, before_two, before_four, before_eight, after_one, after_two, after_four, after_eight
-    ) = lax.optimization_barrier(
-        (mine, before_two, before_four, before_eight, after_one, after_two, after_four, after_eight)
-    )
-    other = other_core(mine)
+    other = [other_core(piece) for piece in mine]
+    before, after, other = lax.optimization_barrier(
+        (
+            (before_two, before_four, before_eight),
+            (after_one, after_two, after_four, after_eight),
+            other,
+        )
+    )
 
     offsets = jnp.array(block_offsets, dtype=jnp.int32)
     reach = (block_links[0, 0] > 0) & (block >= offsets)[None, :]
@@ -326,10 +343,10 @@
             pltpu.VMEM((5 * count, features), bf16),
         ],
         smem=2,
-        inputs=12,
+        inputs=18,
     )(
-        core, reach.astype(jnp.int32), mine, other, window, before_one, before_two, before_four,
-        before_eight, cotangent, gain, barred,
+        place, reach.astype(jnp.int32), *mine, *other, window, before_one, *before, cotangent, gain,
+        barred,
     )
     returned = [shift_ctx(stats[i], -block_offsets[i]) for i in range(4)]
     parts = ((8, 4, 32, features), bf16)
@@ -341,11 +358,12 @@
         [((4 * count, features), bf16)] * 2,
         [pltpu.VMEM((3, 4 * count, features), bf16), pltpu.VMEM((4 * count, features), bf16)],
         inputs=7,
-    )(own, after_one, after_two, after_four, after_eight, gain, weights)
+    )(own, *after, gain, weights)
     partial = halve(keep, send)
-    partial, queries, uppers = lax.optimization_barrier((partial, queries, uppers))
+    partial, queries, uppers, returned = lax.optimization_barrier(
+        (partial, queries, uppers, returned)
+    )
     rows_query = jnp.sum(over_chips(partial).astype(f32), axis=0).astype(bf16)
-    rows_query, key = lax.optimization_barrier((rows_query, key))
     d_key, d_value, keep, send = call(
         columns_kernel, [half, half, parts, parts], smem=1, inputs=13
     )(core, key, value, query, upper, queries, uppers, taps, own_stats, *returned)
@@ -355,11 +373,12 @@
         series_kernel, [half, ((edge, features), bf16)], inputs=8
     )(d_query, d_key, d_value, leading, weights, own, cotangent, gain)
     d_gain = jnp.broadcast_to(d_gain[None], (8, edge, features))
-    arrived = over_chips(jnp.concatenate([partial, d_gain], axis=1))
-    arrived = jnp.sum(arrived.astype(f32), axis=0)
+    partial, rows_query = lax.optimization_barrier(
+        (jnp.concatenate([partial, d_gain], axis=1), rows_query)
+    )
+    arrived = jnp.sum(over_chips(partial).astype(f32), axis=0)
     rows_key = arrived[:128].astype(bf16).reshape(4, 32, features)
-    chip_gain = jnp.sum(arrived[128:], axis=0).reshape(4, 128)
-    top, rest = in_two(chip_gain)
+    top, rest = in_two(jnp.sum(arrived[128:], axis=0).reshape(4, 128))
     extra = jnp.broadcast_to(jnp.concatenate([top, rest], axis=0)[None], (32, 8, 128))
     rows = jnp.concatenate([rows_query, rows_key], axis=0).reshape(32, 8, features)
     payload = jnp.concatenate([rows, extra], axis=2)

time: 241 us -> 240 us (level)
  starting transfers between devices: 52.2 us -> 67.5 us
  between operations: 14.5 us -> 1.24 us
  waiting for transfers between devices: 79.6 us -> 68.7 us
  blocking collectives: 58.5 us -> 63.2 us
  local copies, waits for them, and re-layouts: 2.5 us -> 7.17 us
    ppermute x13, waiting for transfers between devices: 18.8 us -> 51.1 us  [shift_ctx(): return lax.ppermute(shard, 'ctx', pairs)]
    all_gather x1 -> x0, waiting for transfers between devices: 28.6 us -> none  [body(): lax.all_gather(shard.reshape(256, features), 'dp', axis=0, axis_index_gro...]
    ppermute x4 -> x11, starting transfers between devices: 7.96 us -> 28.9 us  [dp_to(): return lax.ppermute(shard, 'dp', [(i, target(i)) for i in range(16)])]
    all_to_all x1, waiting for transfers between devices: 10.4 us -> 0.01 us  [over_chips(): lax.all_to_all(stacked, 'dp', 0, 0, axis_index_groups=chip_groups, tiled=...]
    unnamed x12 -> x22, local copies, waits for them, and re-layouts: 0.03 us -> 4.72 us
    ppermute x13, starting transfers between devices: 34.7 us -> 30.2 us  [shift_ctx(): return lax.ppermute(shard, 'ctx', pairs)]
    ppermute x4 -> x11, waiting for transfers between devices: 5.36 us -> 1.15 us  [dp_to(): return lax.ppermute(shard, 'dp', [(i, target(i)) for i in range(16)])]
    all_to_all x1, blocking collectives: 37.5 us -> 40 us  [body(): arrived = lax.all_to_all(payload, 'ctx', 0, 0, tiled=True).astype(f32)]
  transfers between devices with their start and end apart: 20 -> 26, of which waited for: 10 -> 6; matrix products, arithmetic and copies ran while one was open for 2% -> 2% of each run, Pallas kernels for 3% -> 3%
where the time goes in v4:
time: 240 us; the launch traced here: 238 us
  waiting for transfers between devices  68.7 us (29%)
  starting transfers between devices  67.5 us (28%)
  blocking collectives  63.2 us (26%)
  Pallas kernels  22.4 us (9%)
  other arithmetic  7.34 us (3%)
  local copies, waits for them, and re-layouts  7.17 us (3%)
    ppermute x13, waiting for transfers between devices, shift_ctx(): return lax.ppermute(shard, 'ctx', pairs)  51.1 us
    all_to_all x1, blocking collectives, body(): arrived = lax.all_to_all(payload, 'ctx', 0, 0, tiled=True).astype(f32)  40 us
    ppermute x13, starting transfers between devices, shift_ctx(): return lax.ppermute(shard, 'ctx', pairs)  30.2 us
    ppermute x11, starting transfers between devices, dp_to(): return lax.ppermute(shard, 'dp', [(i, target(i)) for i in range(16)])  28.9 us
    all_to_all x1, blocking collectives, over_chips(): lax.all_to_all(stacked, 'dp', 0, 0, axis_index_groups=chip_groups, tiled=...  23.2 us
    all_to_all x1, waiting for transfers between devices, body(): lax.all_to_all(jnp.broadcast_to(summed[None], (32, 8, features)), 'ctx',...  16.4 us
    pallas_call x1, Pallas kernels, body(): call(rows_kernel, [((8, features, features), bf16)] + [half] * 7 + [((3,...  8.72 us
    pallas_call x1, Pallas kernels, body(): call(columns_kernel, [half, half, parts, parts], smem=1, inputs=13)  5.14 us
  transfers between devices with their start and end apart: 26, of which 6 were waited for; matrix products, arithmetic and copies ran while one was open for 2% of the time, Pallas kernels for 3%

profile of v4, /device:TPU:24, one launch (start us, length us, event | category | flops | bytes accessed | tf_op | source)
XLA Modules:
  0.0 237.5 jit_solution(5144395415613280112)
XLA Ops:
  0.7 1.1 fusion.1
  1.8 4.9 %collective-permute-start = (bf16[8,32,512]{2,1,0:T(8,128)(2,1)S(1)}, bf16[8,32,512]{2,1,0:T(8,128)(2,1)S(1)}, u32[]{:S(2)}, u32[]{:S(2)}) collective-permute-start(bf16[8,32,512]{2,1,0:T(8,128)(2,1)S(1)} %get-tuple-element.100), channel_id=1, source_target_pairs={{0,256},{32,288},{64,320},{96,352},{128,384},{160,416},{192,448},{... | collective-permute-start | bytes 786440 | tf_op jit(solution)/shard_map/ppermute | solution.py:28
  6.7 2.5 %collective-permute-start.1 = (bf16[128,512]{1,0:T(8,128)(2,1)}, bf16[128,512]{1,0:T(8,128)(2,1)S(1)}, u32[]{:S(2)}, u32[]{:S(2)}) collective-permute-start(bf16[128,512]{1,0:T(8,128)(2,1)} %bitcast.42), channel_id=1, source_target_pairs={{0,1},{1,2},{2,3},{3,4},{4,5},{5,6},{6,7},{7,8},{8,9},{9,10},{10,1... | collective-permute-start | bytes 393224 | tf_op jit(solution)/shard_map/ppermute | solution.py:20
  9.2 1.0 pad_maximum_fusion.5
  10.2 1.3 collective-permute-start.8
  11.5 3.7 %collective-permute-done.1.one_ref = bf16[128,512]{1,0:T(8,128)(2,1)S(1)} collective-permute-done((bf16[128,512]{1,0:T(8,128)(2,1)}, bf16[128,512]{1,0:T(8,128)(2,1)S(1)}, u32[]{:S(2)}, u32[]{:S(2)}) %collective-permute-start.1) | collective-permute-done | bytes 131104 | tf_op jit(solution)/shard_map/ppermute | solution.py:20
  15.2 0.9 pad_maximum_fusion.7.window_ref
  16.1 5.2 %collective-permute-start.6 = (bf16[144,512]{1,0:T(8,128)(2,1)S(1)}, bf16[144,512]{1,0:T(8,128)(2,1)S(1)}, u32[]{:S(2)}, u32[]{:S(2)}) collective-permute-start(bf16[144,512]{1,0:T(8,128)(2,1)S(1)} %pad_maximum_fusion.7.window_ref), channel_id=1, source_target_pairs={{0,4},{1,5},{2,6},{3,7},{4,8},{5,9},{6,10},{7,11},{8,12},{9,13},{1... | collective-permute-start | bytes 442376 | tf_op jit(solution)/shard_map/ppermute | solution.py:20
  21.3 3.8 %collective-permute-start.5 = (bf16[144,512]{1,0:T(8,128)(2,1)S(1)}, bf16[144,512]{1,0:T(8,128)(2,1)S(1)}, u32[]{:S(2)}, u32[]{:S(2)}) collective-permute-start(bf16[144,512]{1,0:T(8,128)(2,1)S(1)} %pad_maximum_fusion.7.window_ref), channel_id=1, source_target_pairs={{0,2},{1,3},{2,4},{3,5},{4,6},{5,7},{6,8},{7,9},{8,10},{9,11},{10,... | collective-permute-start | bytes 442376 | tf_op jit(solution)/shard_map/ppermute | solution.py:20
  25.2 2.7 %collective-permute-start.4 = (bf16[2,8,32,512]{3,2,1,0:T(8,128)(2,1)S(1)}, bf16[2,8,32,512]{3,2,1,0:T(8,128)(2,1)}, u32[]{:S(2)}, u32[]{:S(2)}) collective-permute-start(bf16[2,8,32,512]{3,2,1,0:T(8,128)(2,1)S(1)} %pad_maximum_fusion.1.mine_0), channel_id=1, source_target_pairs={{0,192},{32,224},{64,0},{96,32},{128,64},{160,96},{192,128},{224,1... | collective-permute-start | bytes 1572872 | tf_op jit(solution)/shard_map/ppermute | solution.py:28
  27.9 3.8 %collective-permute-start.3 = (bf16[2,8,32,512]{3,2,1,0:T(8,128)(2,1)S(1)}, bf16[2,8,32,512]{3,2,1,0:T(8,128)(2,1)S(1)}, u32[]{:S(2)}, u32[]{:S(2)}) collective-permute-start(bf16[2,8,32,512]{3,2,1,0:T(8,128)(2,1)S(1)} %pad_maximum_fusion.1.mine_0), channel_id=1, source_target_pairs={{0,128},{32,160},{64,192},{96,224},{128,0},{160,32},{192,64},{224,... | collective-permute-start | bytes 1572872 | tf_op jit(solution)/shard_map/ppermute | solution.py:28
  31.7 3.1 %collective-permute-start.2 = (bf16[2,8,32,512]{3,2,1,0:T(8,128)(2,1)S(1)}, bf16[2,8,32,512]{3,2,1,0:T(8,128)(2,1)S(1)}, u32[]{:S(2)}, u32[]{:S(2)}) collective-permute-start(bf16[2,8,32,512]{3,2,1,0:T(8,128)(2,1)S(1)} %pad_maximum_fusion.1.mine_0), channel_id=1, source_target_pairs={{0,64},{32,96},{64,128},{96,160},{128,192},{160,224},{192,0},{224,... | collective-permute-start | bytes 1572872 | tf_op jit(solution)/shard_map/ppermute | solution.py:28
  34.9 1.3 collective-permute-start.10
  36.9 1.3 collective-permute-start.9
  38.3 14.3 %collective-permute-done.10.four_ref = bf16[272,512]{1,0:T(8,128)(2,1)S(1)} collective-permute-done((bf16[272,512]{1,0:T(8,128)(2,1)S(1)}, bf16[272,512]{1,0:T(8,128)(2,1)S(1)}, u32[]{:S(2)}, u32[]{:S(2)}) %collective-permute-start.10) | collective-permute-done | bytes 278560 | tf_op jit(solution)/shard_map/ppermute | solution.py:20
  52.6 1.9 collective-permute-start.12
  54.5 6.9 %collective-permute-start.7 = (bf16[144,512]{1,0:T(8,128)(2,1)S(1)}, bf16[144,512]{1,0:T(8,128)(2,1)S(1)}, u32[]{:S(2)}, u32[]{:S(2)}) collective-permute-start(bf16[144,512]{1,0:T(8,128)(2,1)S(1)} %collective-permute-done.6.four_ref), channel_id=1, source_target_pairs={{0,4},{1,5},{2,6},{3,7},{4,8},{5,9},{6,10},{7,11},{8,12},{9,13},{1... | collective-permute-start | bytes 442376 | tf_op jit(solution)/shard_map/ppermute | solution.py:20
  62.1 1.9 collective-permute-start.15
  64.0 2.4 %collective-permute-start.14 = (bf16[2,8,32,512]{3,2,1,0:T(8,128)(2,1)S(1)}, bf16[2,8,32,512]{3,2,1,0:T(8,128)(2,1)}, u32[]{:S(2)}, u32[]{:S(2)}) collective-permute-start(bf16[2,8,32,512]{3,2,1,0:T(8,128)(2,1)S(1)} %collective-permute-done.3.mine_2), channel_id=1, source_target_pairs={{0,32},{32,0},{64,96},{96,64},{128,160},{160,128},{192,224},{224,1... | collective-permute-start | bytes 1572872 | tf_op jit(solution)/shard_map/ppermute | solution.py:28
  66.5 1.9 collective-permute-start.13
  69.1 1.3 collective-permute-start.11
  70.5 18.7 %collective-permute-done.11.eight_ref = bf16[272,512]{1,0:T(8,128)(2,1)S(1)} collective-permute-done((bf16[272,512]{1,0:T(8,128)(2,1)S(1)}, bf16[272,512]{1,0:T(8,128)(2,1)S(1)}, u32[]{:S(2)}, u32[]{:S(2)}) %collective-permute-start.11) | collective-permute-done | bytes 278560 | tf_op jit(solution)/shard_map/ppermute | solution.py:20
  89.3 0.9 copy-done.3
  90.2 0.9 copy-done.5
  91.1 0.9 copy-done.7
  92.0 8.7 %shard_map.144 = (bf16[8,512,512]{2,1,0:T(8,128)(2,1)}, bf16[128,512]{1,0:T(8,128)(2,1)}, bf16[128,512]{1,0:T(8,128)(2,1)S(1)}, bf16[128,512]{1,0:T(8,128)(2,1)S...) custom-call(s32[3]{0:T(128)S(1)} %pad_add_fusion.place_ref, ...), custom_call_target="tpu_custom_call" | custom-call | tf_op jit(solution)/shard_map/pallas_call | solution.py:336
  100.7 0.7 shard_map.145
  101.5 1.9 collective-permute-start.16
  103.4 1.3 collective-permute-start.20
  104.7 1.3 collective-permute-start.19
  106.0 1.3 collective-permute-start.18
  107.3 1.5 collective-permute-start.17
  108.8 3.5 %shard_map.146 = (bf16[512,512]{1,0:T(8,128)(2,1)S(1)}, bf16[512,512]{1,0:T(8,128)(2,1)S(1)}) custom-call(bf16[128,512]{1,0:T(8,128)(2,1)S(1)} %bitcast.46, bf16[256,512]{1,0:T(8,128)(2,1)S(1)} %collective-permute-done.8.one_ref, bf16[272,512]{1,0:T(8,128)(2,1)S(1)} %collective-permute-done.9.two_ref, bf16[272,512]{1,0:T(8,128)(2,1)S(1)} %collective-permute-done.10.four_ref, ...), custom_call_target="tpu_custom_call" | custom-call | tf_op jit(solution)/shard_map/pallas_call | solution.py:356
  112.3 1.4 add_convert_fusion.1
  113.8 5.1 %shard_map.147 = (bf16[128,512]{1,0:T(8,128)(2,1)S(1)}, bf16[128,512]{1,0:T(8,128)(2,1)S(1)}, bf16[8,4,32,512]{3,2,1,0:T(8,128)(2,1)S(1)}, bf16[8,4,32,512]{3,2,1,0:T(8,128)(2,1)}) custom-call(s32[1]{0:T(128)} %bitcast.2.core_ref, bf16[128,512]{1,0:T(8,128)(2,1)S(1)} %get-tuple-element.61.key_ref, bf16[128,512]{1,0:T(8,128)(2,1)S(1)} %get-tuple-element.62.value_ref, ...), custom_call_target="tpu_custom_call" | custom-call | tf_op jit(solution)/shard_map/pallas_call | solution.py:367
  118.9 2.4 collective-permute-start.22
  121.3 4.6 %all-to-all-start = ((bf16[8,4,32,512]{3,2,1,0:T(8,128)(2,1)}), bf16[8,4,32,512]{3,2,1,0:T(8,128)(2,1)S(1)}, u32[]{:S(2)}, u32[]{:S(2)}) async-start(bf16[8,4,32,512]{3,2,1,0:T(8,128)(2,1)} %add_convert_fusion.1), calls=%async_computation | async-start | bytes 2097152 | tf_op jit(solution)/shard_map/all_to_all | solution.py:36
  125.9 1.3 collective-permute-start.21
  127.2 14.5 %collective-permute-done.21.leading_ref = bf16[16,1024]{1,0:T(8,128)(2,1)S(1)} collective-permute-done((bf16[16,1024]{1,0:T(8,128)(2,1)S(1)}, bf16[16,1024]{1,0:T(8,128)(2,1)S(1)}, u32[]{:S(2)}, u32[]{:S(2)}) %collective-permute-start.21) | collective-permute-done | bytes 32800 | tf_op jit(solution)/shard_map/ppermute | solution.py:20
  141.7 4.3 %shard_map.148 = (bf16[128,512]{1,0:T(8,128)(2,1)}, bf16[16,512]{1,0:T(8,128)(2,1)S(1)}) custom-call(bf16[128,512]{1,0:T(8,128)(2,1)S(1)} %get-tuple-element.60.d_query_ref, bf16[128,512]{1,0:T(8,128)(2,1)S(1)} %get-tuple-element.84.d_key_ref, bf16[128,512]{1,0:T(8,128)(2,1)S(1)} %get-tuple-element.85.d_value_ref, ...), custom_call_target="tpu_custom_call" | custom-call | tf_op jit(solution)/shard_map/pallas_call | solution.py:372
  146.1 1.6 add_convert_fusion
  147.9 23.2 %all_to_all.20 = bf16[8,144,512]{2,1,0:T(8,128)(2,1)S(1)} all-to-all(bf16[8,144,512]{2,1,0:T(8,128)(2,1)S(1)} %pad_maximum_fusion), channel_id=1, replica_groups={{0,64,128,192,256,320,384,448},{32,96,160,224,288,352,416,480},{1,65,12..., dimensions={0} | all-to-all | bytes 2359296 | tf_op jit(solution)/shard_map/all_to_all | solution.py:36
  171.3 40.0 %all_to_all.21 = bf16[32,8,640]{2,1,0:T(8,128)(2,1)S(1)} all-to-all(bf16[32,8,640]{2,1,0:T(8,128)(2,1)S(1)} %pad_maximum_fusion.2), channel_id=1, replica_groups=mesh['dp'=16,'ctx'=32] {'ctx'}, dimensions={0} | all-to-all | bytes 655360 | tf_op jit(solution)/shard_map/all_to_all | solution.py:385
  212.1 3.9 %all-to-all-start.3 = ((bf16[32,8,512]{2,1,0:T(8,128)(2,1)}), bf16[32,8,512]{2,1,0:T(8,128)(2,1)S(1)}, u32[]{:S(2)}, u32[]{:S(2)}) async-start(bf16[32,8,512]{2,1,0:T(8,128)(2,1)} %broadcast_in_dim.54), calls=%async_computation.3 | async-start | bytes 524288 | tf_op jit(solution)/shard_map/all_to_all | solution.py:390
  216.0 1.9 collective-permute-start.23
  217.9 1.1 collective-permute-done.23
  219.7 16.4 %all-to-all-done.3 = bf16[32,8,512]{2,1,0:T(8,128)(2,1)S(1)} async-done(((bf16[32,8,512]{2,1,0:T(8,128)(2,1)}), bf16[32,8,512]{2,1,0:T(8,128)(2,1)S(1)}, u32[]{:S(2)}, u32[]{:S(2)}) %all-to-all-start.3) | async-done | bytes 262176 | tf_op jit(solution)/shard_map/all_to_all | solution.py:390
  236.7 0.8 fusion.2
  (72 shorter events, 5.1 us)
Async XLA Ops:
  0.6 37.7 %copy-start.10 = (s32[4]{0:T(128)S(1)}, s32[4]{0:T(128)}, u32[]{:S(2)}) copy-start(s32[4]{0:T(128)} %constant.66.clone) | copy-start | bytes 52
  0.6 34.2 %copy-start = (bf16[1,128,512]{2,1,0:T(8,128)(2,1)S(1)}, bf16[1,128,512]{2,1,0:T(8,128)(2,1)}, u32[]{:S(2)}) copy-start(bf16[1,128,512]{2,1,0:T(8,128)(2,1)} %param.9) | copy-start | bytes 393220
  0.7 34.2 %copy-start.1 = (bf16[1,128,512]{2,1,0:T(8,128)(2,1)S(1)}, bf16[1,128,512]{2,1,0:T(8,128)(2,1)}, u32[]{:S(2)}) copy-start(bf16[1,128,512]{2,1,0:T(8,128)(2,1)} %param.16) | copy-start | bytes 393220
  0.7 37.5 %copy-start.9 = (s32[1,1,8,4]{2,3,1,0:T(4,128)S(1)}, s32[1,1,8,4]{2,3,1,0:T(4,128)}, u32[]{:S(2)}) copy-start(s32[1,1,8,4]{2,3,1,0:T(4,128)} %param.15) | copy-start | bytes 388
  0.7 88.6 %copy-start.8 = (f32[512]{0:T(512)S(1)}, f32[512]{0:T(512)}, u32[]{:S(2)}) copy-start(f32[512]{0:T(512)} %param.10) | copy-start | bytes 6148
  1.8 13.4 %collective-permute-start = (bf16[8,32,512]{2,1,0:T(8,128)(2,1)S(1)}, bf16[8,32,512]{2,1,0:T(8,128)(2,1)S(1)}, u32[]{:S(2)}, u32[]{:S(2)}) collective-permute-start(bf16[8,32,512]{2,1,0:T(8,128)(2,1)S(1)} %get-tuple-element.100), channel_id=1, source_target_pairs={{0,256},{32,288},{64,320},{96,352},{128,384},{160,416},{192,448},{... | collective-permute-start | bytes 786440 | tf_op jit(solution)/shard_map/ppermute | solution.py:28
  6.7 8.5 %collective-permute-start.1 = (bf16[128,512]{1,0:T(8,128)(2,1)}, bf16[128,512]{1,0:T(8,128)(2,1)S(1)}, u32[]{:S(2)}, u32[]{:S(2)}) collective-permute-start(bf16[128,512]{1,0:T(8,128)(2,1)} %bitcast.42), channel_id=1, source_target_pairs={{0,1},{1,2},{2,3},{3,4},{4,5},{5,6},{6,7},{7,8},{8,9},{9,10},{10,1... | collective-permute-start | bytes 393224 | tf_op jit(solution)/shard_map/ppermute | solution.py:20
  10.2 21.4 %collective-permute-start.8 = (bf16[256,512]{1,0:T(8,128)(2,1)S(1)}, bf16[256,512]{1,0:T(8,128)(2,1)S(1)}, u32[]{:S(2)}, u32[]{:S(2)}) collective-permute-start(bf16[256,512]{1,0:T(8,128)(2,1)S(1)} %pad_maximum_fusion.5), channel_id=1, source_target_pairs={{1,0},{2,1},{3,2},{4,3},{5,4},{6,5},{7,6},{8,7},{9,8},{10,9},{11,1... | collective-permute-start | bytes 786440 | tf_op jit(solution)/shard_map/ppermute | solution.py:20
  16.1 18.8 %collective-permute-start.6 = (bf16[144,512]{1,0:T(8,128)(2,1)S(1)}, bf16[144,512]{1,0:T(8,128)(2,1)S(1)}, u32[]{:S(2)}, u32[]{:S(2)}) collective-permute-start(bf16[144,512]{1,0:T(8,128)(2,1)S(1)} %pad_maximum_fusion.7.window_ref), channel_id=1, source_target_pairs={{0,4},{1,5},{2,6},{3,7},{4,8},{5,9},{6,10},{7,11},{8,12},{9,13},{1... | collective-permute-start | bytes 442376 | tf_op jit(solution)/shard_map/ppermute | solution.py:20
  21.3 14.9 %collective-permute-start.5 = (bf16[144,512]{1,0:T(8,128)(2,1)S(1)}, bf16[144,512]{1,0:T(8,128)(2,1)S(1)}, u32[]{:S(2)}, u32[]{:S(2)}) collective-permute-start(bf16[144,512]{1,0:T(8,128)(2,1)S(1)} %pad_maximum_fusion.7.window_ref), channel_id=1, source_target_pairs={{0,2},{1,3},{2,4},{3,5},{4,6},{5,7},{6,8},{7,9},{8,10},{9,11},{10,... | collective-permute-start | bytes 442376 | tf_op jit(solution)/shard_map/ppermute | solution.py:20
  25.2 36.9 %collective-permute-start.4 = (bf16[2,8,32,512]{3,2,1,0:T(8,128)(2,1)S(1)}, bf16[2,8,32,512]{3,2,1,0:T(8,128)(2,1)}, u32[]{:S(2)}, u32[]{:S(2)}) collective-permute-start(bf16[2,8,32,512]{3,2,1,0:T(8,128)(2,1)S(1)} %pad_maximum_fusion.1.mine_0), channel_id=1, source_target_pairs={{0,192},{32,224},{64,0},{96,32},{128,64},{160,96},{192,128},{224,1... | collective-permute-start | bytes 1572872 | tf_op jit(solution)/shard_map/ppermute | solution.py:28
  27.9 36.2 %collective-permute-start.3 = (bf16[2,8,32,512]{3,2,1,0:T(8,128)(2,1)S(1)}, bf16[2,8,32,512]{3,2,1,0:T(8,128)(2,1)S(1)}, u32[]{:S(2)}, u32[]{:S(2)}) collective-permute-start(bf16[2,8,32,512]{3,2,1,0:T(8,128)(2,1)S(1)} %pad_maximum_fusion.1.mine_0), channel_id=1, source_target_pairs={{0,128},{32,160},{64,192},{96,224},{128,0},{160,32},{192,64},{224,... | collective-permute-start | bytes 1572872 | tf_op jit(solution)/shard_map/ppermute | solution.py:28
  31.7 34.8 %collective-permute-start.2 = (bf16[2,8,32,512]{3,2,1,0:T(8,128)(2,1)S(1)}, bf16[2,8,32,512]{3,2,1,0:T(8,128)(2,1)S(1)}, u32[]{:S(2)}, u32[]{:S(2)}) collective-permute-start(bf16[2,8,32,512]{3,2,1,0:T(8,128)(2,1)S(1)} %pad_maximum_fusion.1.mine_0), channel_id=1, source_target_pairs={{0,64},{32,96},{64,128},{96,160},{128,192},{160,224},{192,0},{224,... | collective-permute-start | bytes 1572872 | tf_op jit(solution)/shard_map/ppermute | solution.py:28
  34.9 17.7 %collective-permute-start.10 = (bf16[272,512]{1,0:T(8,128)(2,1)S(1)}, bf16[272,512]{1,0:T(8,128)(2,1)S(1)}, u32[]{:S(2)}, u32[]{:S(2)}) collective-permute-start(bf16[272,512]{1,0:T(8,128)(2,1)S(1)} %pad_maximum_fusion.3), channel_id=1, source_target_pairs={{4,0},{5,1},{6,2},{7,3},{8,4},{9,5},{10,6},{11,7},{12,8},{13,9},{1... | collective-permute-start | bytes 835592 | tf_op jit(solution)/shard_map/ppermute | solution.py:20
  36.2 0.7 copy-start.4
  36.9 17.7 %collective-permute-start.9 = (bf16[272,512]{1,0:T(8,128)(2,1)S(1)}, bf16[272,512]{1,0:T(8,128)(2,1)S(1)}, u32[]{:S(2)}, u32[]{:S(2)}) collective-permute-start(bf16[272,512]{1,0:T(8,128)(2,1)S(1)} %pad_maximum_fusion.3), channel_id=1, source_target_pairs={{2,0},{3,1},{4,2},{5,3},{6,4},{7,5},{8,6},{9,7},{10,8},{11,9},{12,... | collective-permute-start | bytes 835592 | tf_op jit(solution)/shard_map/ppermute | solution.py:20
  52.6 17.9 %collective-permute-start.12 = (bf16[2,8,32,512]{3,2,1,0:T(8,128)(2,1)S(1)}, bf16[2,8,32,512]{3,2,1,0:T(8,128)(2,1)}, u32[]{:S(2)}, u32[]{:S(2)}) collective-permute-start(bf16[2,8,32,512]{3,2,1,0:T(8,128)(2,1)S(1)} %pad_maximum_fusion.1.mine_0), channel_id=1, source_target_pairs={{0,32},{32,0},{64,96},{96,64},{128,160},{160,128},{192,224},{224,1... | collective-permute-start | bytes 1572872 | tf_op jit(solution)/shard_map/ppermute | solution.py:28
  54.5 13.9 %collective-permute-start.7 = (bf16[144,512]{1,0:T(8,128)(2,1)S(1)}, bf16[144,512]{1,0:T(8,128)(2,1)S(1)}, u32[]{:S(2)}, u32[]{:S(2)}) collective-permute-start(bf16[144,512]{1,0:T(8,128)(2,1)S(1)} %collective-permute-done.6.four_ref), channel_id=1, source_target_pairs={{0,4},{1,5},{2,6},{3,7},{4,8},{5,9},{6,10},{7,11},{8,12},{9,13},{1... | collective-permute-start | bytes 442376 | tf_op jit(solution)/shard_map/ppermute | solution.py:20
  61.4 0.7 copy-start.2
  62.1 27.1 %collective-permute-start.15 = (bf16[2,8,32,512]{3,2,1,0:T(8,128)(2,1)}, bf16[2,8,32,512]{3,2,1,0:T(8,128)(2,1)}, u32[]{:S(2)}, u32[]{:S(2)}) collective-permute-start(bf16[2,8,32,512]{3,2,1,0:T(8,128)(2,1)} %collective-permute-done.4.mine_3), channel_id=1, source_target_pairs={{0,32},{32,0},{64,96},{96,64},{128,160},{160,128},{192,224},{224,1... | collective-permute-start | bytes 1572872 | tf_op jit(solution)/shard_map/ppermute | solution.py:28
  64.0 25.2 %collective-permute-start.14 = (bf16[2,8,32,512]{3,2,1,0:T(8,128)(2,1)S(1)}, bf16[2,8,32,512]{3,2,1,0:T(8,128)(2,1)}, u32[]{:S(2)}, u32[]{:S(2)}) collective-permute-start(bf16[2,8,32,512]{3,2,1,0:T(8,128)(2,1)S(1)} %collective-permute-done.3.mine_2), channel_id=1, source_target_pairs={{0,32},{32,0},{64,96},{96,64},{128,160},{160,128},{192,224},{224,1... | collective-permute-start | bytes 1572872 | tf_op jit(solution)/shard_map/ppermute | solution.py:28
  66.5 22.7 %collective-permute-start.13 = (bf16[2,8,32,512]{3,2,1,0:T(8,128)(2,1)S(1)}, bf16[2,8,32,512]{3,2,1,0:T(8,128)(2,1)}, u32[]{:S(2)}, u32[]{:S(2)}) collective-permute-start(bf16[2,8,32,512]{3,2,1,0:T(8,128)(2,1)S(1)} %collective-permute-done.2.mine_1), channel_id=1, source_target_pairs={{0,32},{32,0},{64,96},{96,64},{128,160},{160,128},{192,224},{224,1... | collective-permute-start | bytes 1572872 | tf_op jit(solution)/shard_map/ppermute | solution.py:28
  68.4 0.7 copy-start.6
  69.1 20.1 %collective-permute-start.11 = (bf16[272,512]{1,0:T(8,128)(2,1)S(1)}, bf16[272,512]{1,0:T(8,128)(2,1)S(1)}, u32[]{:S(2)}, u32[]{:S(2)}) collective-permute-start(bf16[272,512]{1,0:T(8,128)(2,1)S(1)} %collective-permute-done.10.four_ref), channel_id=1, source_target_pairs={{4,0},{5,1},{6,2},{7,3},{8,4},{9,5},{10,6},{11,7},{12,8},{13,9},{1... | collective-permute-start | bytes 835592 | tf_op jit(solution)/shard_map/ppermute | solution.py:20
  89.3 0.9 copy-start.3
  90.2 0.9 copy-start.5
  91.1 0.9 copy-start.7
  101.5 10.9 %collective-permute-start.16 = (bf16[8,4,32,512]{3,2,1,0:T(8,128)(2,1)S(1)}, bf16[8,4,32,512]{3,2,1,0:T(8,128)(2,1)S(1)}, u32[]{:S(2)}, u32[]{:S(2)}) collective-permute-start(bf16[8,4,32,512]{3,2,1,0:T(8,128)(2,1)S(1)} %get-tuple-element.68), channel_id=1, source_target_pairs={{0,32},{32,0},{64,96},{96,64},{128,160},{160,128},{192,224},{224,1... | collective-permute-start | bytes 3145736 | tf_op jit(solution)/shard_map/ppermute | solution.py:28
  103.4 10.3 %collective-permute-start.20 = (f32[24,128]{1,0:T(8,128)S(1)}, f32[24,128]{1,0:T(8,128)S(1)}, u32[]{:S(2)}, u32[]{:S(2)}) collective-permute-start(f32[24,128]{1,0:T(8,128)S(1)} %get-tuple-element.101), channel_id=1, source_target_pairs={{8,0},{9,1},{10,2},{11,3},{12,4},{13,5},{14,6},{15,7},{16,8},{17,9... | collective-permute-start | bytes 36872 | tf_op jit(solution)/shard_map/ppermute | solution.py:20
  104.7 9.0 %collective-permute-start.19 = (f32[24,128]{1,0:T(8,128)S(1)}, f32[24,128]{1,0:T(8,128)S(1)}, u32[]{:S(2)}, u32[]{:S(2)}) collective-permute-start(f32[24,128]{1,0:T(8,128)S(1)} %get-tuple-element.102), channel_id=1, source_target_pairs={{4,0},{5,1},{6,2},{7,3},{8,4},{9,5},{10,6},{11,7},{12,8},{13,9},{1... | collective-permute-start | bytes 36872 | tf_op jit(solution)/shard_map/ppermute | solution.py:20
  106.0 7.7 %collective-permute-start.18 = (f32[24,128]{1,0:T(8,128)S(1)}, f32[24,128]{1,0:T(8,128)S(1)}, u32[]{:S(2)}, u32[]{:S(2)}) collective-permute-start(f32[24,128]{1,0:T(8,128)S(1)} %get-tuple-element.103), channel_id=1, source_target_pairs={{2,0},{3,1},{4,2},{5,3},{6,4},{7,5},{8,6},{9,7},{10,8},{11,9},{12,... | collective-permute-start | bytes 36872 | tf_op jit(solution)/shard_map/ppermute | solution.py:20
  107.3 6.4 %collective-permute-start.17 = (f32[24,128]{1,0:T(8,128)S(1)}, f32[24,128]{1,0:T(8,128)S(1)}, u32[]{:S(2)}, u32[]{:S(2)}) collective-permute-start(f32[24,128]{1,0:T(8,128)S(1)} %get-tuple-element.104), channel_id=1, source_target_pairs={{1,0},{2,1},{3,2},{4,3},{5,4},{6,5},{7,6},{8,7},{9,8},{10,9},{11,1... | collective-permute-start | bytes 36872 | tf_op jit(solution)/shard_map/ppermute | solution.py:20
  118.9 27.2 %collective-permute-start.22 = (bf16[8,4,32,512]{3,2,1,0:T(8,128)(2,1)}, bf16[8,4,32,512]{3,2,1,0:T(8,128)(2,1)}, u32[]{:S(2)}, u32[]{:S(2)}) collective-permute-start(bf16[8,4,32,512]{3,2,1,0:T(8,128)(2,1)} %get-tuple-element.88), channel_id=1, source_target_pairs={{0,32},{32,0},{64,96},{96,64},{128,160},{160,128},{192,224},{224,1... | collective-permute-start | bytes 3145736 | tf_op jit(solution)/shard_map/ppermute | solution.py:28
  121.3 24.7 %all-to-all-start = ((bf16[8,4,32,512]{3,2,1,0:T(8,128)(2,1)}), bf16[8,4,32,512]{3,2,1,0:T(8,128)(2,1)S(1)}, u32[]{:S(2)}, u32[]{:S(2)}) async-start(bf16[8,4,32,512]{3,2,1,0:T(8,128)(2,1)} %add_convert_fusion.1), calls=%async_computation | async-start | bytes 2097152 | tf_op jit(solution)/shard_map/all_to_all | solution.py:36
  125.9 15.8 %collective-permute-start.21 = (bf16[16,1024]{1,0:T(8,128)(2,1)S(1)}, bf16[16,1024]{1,0:T(8,128)(2,1)S(1)}, u32[]{:S(2)}, u32[]{:S(2)}) collective-permute-start(bf16[16,1024]{1,0:T(8,128)(2,1)S(1)} %pad_maximum_fusion.8), channel_id=1, source_target_pairs={{1,0},{2,1},{3,2},{4,3},{5,4},{6,5},{7,6},{8,7},{9,8},{10,9},{11,1... | collective-permute-start | bytes 98312 | tf_op jit(solution)/shard_map/ppermute | solution.py:20
  212.1 23.9 %all-to-all-start.3 = ((bf16[32,8,512]{2,1,0:T(8,128)(2,1)}), bf16[32,8,512]{2,1,0:T(8,128)(2,1)S(1)}, u32[]{:S(2)}, u32[]{:S(2)}) async-start(bf16[32,8,512]{2,1,0:T(8,128)(2,1)} %broadcast_in_dim.54), calls=%async_computation.3 | async-start | bytes 524288 | tf_op jit(solution)/shard_map/all_to_all | solution.py:390
  216.0 3.1 %collective-permute-start.23 = (f32[4,128]{1,0:T(4,128)S(1)}, f32[4,128]{1,0:T(4,128)S(1)}, u32[]{:S(2)}, u32[]{:S(2)}) collective-permute-start(f32[4,128]{1,0:T(4,128)S(1)} %slice_add_fusion), channel_id=1, source_target_pairs={{0,32},{32,0},{64,96},{96,64},{128,160},{160,128},{192,224},{224,1... | collective-permute-start | bytes 6152 | tf_op jit(solution)/shard_map/ppermute | solution.py:28

commit v5 on v4

--- a/solution.py
+++ b/solution.py
@@ -11,7 +11,12 @@
 f32 = jnp.float32
 bf16 = jnp.bfloat16
 edge = 16
-chip_groups = [[2 * i + c for i in range(8)] for c in range(2)]
+plane_groups = [
+    [(2 * chip + core) * 32 + 2 * z + side for chip in range(8) for side in range(2)]
+    for core in range(2)
+    for z in range(16)
+]
+z_groups = [[2 * z + side for z in range(16)] for side in range(2)]
 
 
 def shift_ctx(shard, by):
@@ -32,8 +37,18 @@
     return dp_to(shard, 0, 0, 1)
 
 
-def over_chips(stacked):
-    return lax.all_to_all(stacked, "dp", 0, 0, axis_index_groups=chip_groups, tiled=True)
+def over_plane(stacked):
+    return lax.all_to_all(
+        stacked, ("dp", "ctx"), 0, 0, axis_index_groups=plane_groups, tiled=True
+    )
+
+
+def over_z(stacked):
+    return lax.all_to_all(stacked, "ctx", 0, 0, axis_index_groups=z_groups, tiled=True)
+
+
+def other_side(shard):
+    return lax.ppermute(shard, "ctx", [(i, i ^ 1) for i in range(32)])
 
 
 def product(left, right):
@@ -313,17 +328,13 @@
     mine = [shards] + [dp_to(shards, 0, by, 0) for by in (1, 2, 3)]
     window = jnp.concatenate([before_one[count - edge :], own], axis=0)
     carried = jnp.concatenate([window, cotangent], axis=0)
-    before_four, before_two = shift_ctx(window, 4), shift_ctx(window, 2)
+    before = [shift_ctx(window, by) for by in (2, 4, 8)]
     after_four, after_two = shift_ctx(carried, -4), shift_ctx(carried, -2)
-    before_eight, after_eight = shift_ctx(before_four, 4), shift_ctx(after_four, -4)
     other = [other_core(piece) for piece in mine]
-    before, after, other = lax.optimization_barrier(
-        (
-            (before_two, before_four, before_eight),
-            (after_one, after_two, after_four, after_eight),
-            other,
-        )
-    )
+    before, after_one, after_two, after_four, other = lax.optimization_barrier(
+        (before, after_one, after_two, after_four, other)
+    )
+    after = (after_one, after_two, after_four, shift_ctx(after_four, -4))
 
     offsets = jnp.array(block_offsets, dtype=jnp.int32)
     reach = (block_links[0, 0] > 0) & (block >= offsets)[None, :]
@@ -359,39 +370,41 @@
         [pltpu.VMEM((3, 4 * count, features), bf16), pltpu.VMEM((4 * count, features), bf16)],
         inputs=7,
     )(own, *after, gain, weights)
-    partial = halve(keep, send)
-    partial, queries, uppers, returned = lax.optimization_barrier(
-        (partial, queries, uppers, returned)
-    )
-    rows_query = jnp.sum(over_chips(partial).astype(f32), axis=0).astype(bf16)
+    query_half = halve(keep, send)
     d_key, d_value, keep, send = call(
         columns_kernel, [half, half, parts, parts], smem=1, inputs=13
     )(core, key, value, query, upper, queries, uppers, taps, own_stats, *returned)
     leading = shift_ctx(jnp.concatenate([d_query[:edge], d_key[:edge]], axis=1), -1)
-    partial = halve(keep, send).reshape(8, 128, features)
+    key_half = halve(keep, send)
     grad_series, d_gain = call(
         series_kernel, [half, ((edge, features), bf16)], inputs=8
     )(d_query, d_key, d_value, leading, weights, own, cotangent, gain)
-    d_gain = jnp.broadcast_to(d_gain[None], (8, edge, features))
-    partial, rows_query = lax.optimization_barrier(
-        (jnp.concatenate([partial, d_gain], axis=1), rows_query)
-    )
-    arrived = jnp.sum(over_chips(partial).astype(f32), axis=0)
-    rows_key = arrived[:128].astype(bf16).reshape(4, 32, features)
+    terms = jnp.stack([query_half, key_half], axis=1).reshape(16, 128, features)
+    d_gain = jnp.broadcast_to(d_gain[None], (16, edge, features))
+    arrived = over_plane(jnp.concatenate([terms, d_gain], axis=1))
+    arrived = jnp.sum(arrived.astype(f32), axis=0)
+    rows = arrived[:128].astype(bf16).reshape(16, 8, features)
     top, rest = in_two(jnp.sum(arrived[128:], axis=0).reshape(4, 128))
-    extra = jnp.broadcast_to(jnp.concatenate([top, rest], axis=0)[None], (32, 8, 128))
-    rows = jnp.concatenate([rows_query, rows_key], axis=0).reshape(32, 8, features)
-    payload = jnp.concatenate([rows, extra], axis=2)
-    arrived = lax.all_to_all(payload, "ctx", 0, 0, tiled=True).astype(f32)
+    extra = jnp.broadcast_to(jnp.concatenate([top, rest], axis=0)[None], (16, 8, 128))
+    arrived = over_z(jnp.concatenate([rows, extra], axis=2)).astype(f32)
     summed = jnp.sum(arrived, axis=0)
     core_gain = summed[:4, features:] + summed[4:, features:]
     gain_total = (core_gain + other_core(core_gain)).reshape(features)
     summed = summed[:, :features].astype(bf16)
-    final = lax.all_to_all(
-        jnp.broadcast_to(summed[None], (32, 8, features)), "ctx", 0, 0, tiled=True
-    )
-    final = final.reshape(8, 32, features).astype(f32)
-    return (mixed[None], grad_series[None], gain_total, final[:3], final[4:7], final[7], final[3])
+    mine = over_z(jnp.broadcast_to(summed[None], (16, 8, features)))
+    other = other_side(mine)
+    first = block % 2 == 0
+    for_query = jnp.where(first, mine, other).reshape(4, 32, features).astype(f32)
+    for_key = jnp.where(first, other, mine).reshape(4, 32, features).astype(f32)
+    return (
+        mixed[None],
+        grad_series[None],
+        gain_total,
+        for_query[:3],
+        for_key[:3],
+        for_key[3],
+        for_query[3],
+    )
 
 
 def solution(mesh):

time: 240 us -> 228 us (0.950)
  waiting for transfers between devices: 68.7 us -> 63.1 us
  local copies, waits for them, and re-layouts: 7.17 us -> 3.29 us
    ppermute x13, waiting for transfers between devices: 51.1 us -> 44.6 us  [shift_ctx(): return lax.ppermute(shard, 'ctx', pairs)]
    unnamed x22 -> x12, local copies, waits for them, and re-layouts: 4.72 us -> 0.03 us
    all_to_all x2 -> x1, waiting for transfers between devices: 16.4 us -> 12 us  [over_z(): lax.all_to_all(stacked, 'ctx', 0, 0, axis_index_groups=z_groups, tiled=True)]
    ppermute x0 -> x1, waiting for transfers between devices: none -> 4.34 us  [other_side(): return lax.ppermute(shard, 'ctx', [(i, i ^ 1) for i in range(32)])]
    all_to_all x2 -> x1, starting transfers between devices: 8.46 us -> 4.57 us  [over_z(): lax.all_to_all(stacked, 'ctx', 0, 0, axis_index_groups=z_groups, tiled=True)]
    convert_element_type x3 -> x1, other arithmetic: 3.02 us -> 0.04 us  [body(): for_key = jnp.where(first, other, mine).reshape(4, 32, features).astype(f32)]
  transfers between devices with their start and end apart: 26 -> 26, of which waited for: 6 -> 10; matrix products, arithmetic and copies ran while one was open for 2% -> 1% of each run, Pallas kernels for 3% -> 6%
where the time goes in v5:
time: 228 us; the launch traced here: 227 us
  starting transfers between devices  66.3 us (29%)
  blocking collectives  64.7 us (28%)
  waiting for transfers between devices  63.1 us (28%)
  Pallas kernels  22.5 us (10%)
  other arithmetic  5.43 us (2%)
  local copies, waits for them, and re-layouts  3.29 us (1%)
    ppermute x13, waiting for transfers between devices, shift_ctx(): return lax.ppermute(shard, 'ctx', pairs)  44.6 us
    all_to_all x1, blocking collectives, over_plane(): lax.all_to_all(stacked, ('dp', 'ctx'), 0, 0, axis_index_groups=plane_grou...  35.7 us
    ppermute x13, starting transfers between devices, shift_ctx(): return lax.ppermute(shard, 'ctx', pairs)  32.2 us
    all_to_all x1, blocking collectives, over_z(): lax.all_to_all(stacked, 'ctx', 0, 0, axis_index_groups=z_groups, tiled=True)  29.1 us
    ppermute x11, starting transfers between devices, dp_to(): return lax.ppermute(shard, 'dp', [(i, target(i)) for i in range(16)])  27.6 us
    all_to_all x1, waiting for transfers between devices, over_z(): lax.all_to_all(stacked, 'ctx', 0, 0, axis_index_groups=z_groups, tiled=True)  12 us
    pallas_call x1, Pallas kernels, body(): call(rows_kernel, [((8, features, features), bf16)] + [half] * 7 + [((3,...  8.76 us
    pallas_call x1, Pallas kernels, body(): call(columns_kernel, [half, half, parts, parts], smem=1, inputs=13)  5.15 us
  transfers between devices with their start and end apart: 26, of which 10 were waited for; matrix products, arithmetic and copies ran while one was open for 1% of the time, Pallas kernels for 6%

profile of v5, /device:TPU:24, one launch (start us, length us, event | category | flops | bytes accessed | tf_op | source)
XLA Modules:
  0.0 226.5 jit_solution(15527720085718519702)
XLA Ops:
  0.7 1.1 fusion.4
  1.8 4.9 %collective-permute-start = (bf16[8,32,512]{2,1,0:T(8,128)(2,1)S(1)}, bf16[8,32,512]{2,1,0:T(8,128)(2,1)S(1)}, u32[]{:S(2)}, u32[]{:S(2)}) collective-permute-start(bf16[8,32,512]{2,1,0:T(8,128)(2,1)S(1)} %get-tuple-element.78), channel_id=1, source_target_pairs={{0,256},{32,288},{64,320},{96,352},{128,384},{160,416},{192,448},{... | collective-permute-start | bytes 786440 | tf_op jit(solution)/shard_map/ppermute | solution.py:33
  6.7 2.5 %collective-permute-start.1 = (bf16[128,512]{1,0:T(8,128)(2,1)}, bf16[128,512]{1,0:T(8,128)(2,1)S(1)}, u32[]{:S(2)}, u32[]{:S(2)}) collective-permute-start(bf16[128,512]{1,0:T(8,128)(2,1)} %bitcast.46), channel_id=1, source_target_pairs={{0,1},{1,2},{2,3},{3,4},{4,5},{5,6},{6,7},{7,8},{8,9},{9,10},{10,1... | collective-permute-start | bytes 393224 | tf_op jit(solution)/shard_map/ppermute | solution.py:25
  9.2 1.0 pad_maximum_fusion.5
  10.2 1.3 collective-permute-start.8
  11.5 3.7 %collective-permute-done.1.one_ref = bf16[128,512]{1,0:T(8,128)(2,1)S(1)} collective-permute-done((bf16[128,512]{1,0:T(8,128)(2,1)}, bf16[128,512]{1,0:T(8,128)(2,1)S(1)}, u32[]{:S(2)}, u32[]{:S(2)}) %collective-permute-start.1) | collective-permute-done | bytes 131104 | tf_op jit(solution)/shard_map/ppermute | solution.py:25
  15.2 0.9 pad_maximum_fusion.7.window_ref
  16.1 3.8 %collective-permute-start.5 = (bf16[144,512]{1,0:T(8,128)(2,1)S(1)}, bf16[144,512]{1,0:T(8,128)(2,1)S(1)}, u32[]{:S(2)}, u32[]{:S(2)}) collective-permute-start(bf16[144,512]{1,0:T(8,128)(2,1)S(1)} %pad_maximum_fusion.7.window_ref), channel_id=1, source_target_pairs={{0,2},{1,3},{2,4},{3,5},{4,6},{5,7},{6,8},{7,9},{8,10},{9,11},{10,... | collective-permute-start | bytes 442376 | tf_op jit(solution)/shard_map/ppermute | solution.py:25
  20.0 5.2 %collective-permute-start.6 = (bf16[144,512]{1,0:T(8,128)(2,1)S(1)}, bf16[144,512]{1,0:T(8,128)(2,1)S(1)}, u32[]{:S(2)}, u32[]{:S(2)}) collective-permute-start(bf16[144,512]{1,0:T(8,128)(2,1)S(1)} %pad_maximum_fusion.7.window_ref), channel_id=1, source_target_pairs={{0,4},{1,5},{2,6},{3,7},{4,8},{5,9},{6,10},{7,11},{8,12},{9,13},{1... | collective-permute-start | bytes 442376 | tf_op jit(solution)/shard_map/ppermute | solution.py:25
  25.2 3.1 %collective-permute-start.2 = (bf16[2,8,32,512]{3,2,1,0:T(8,128)(2,1)S(1)}, bf16[2,8,32,512]{3,2,1,0:T(8,128)(2,1)S(1)}, u32[]{:S(2)}, u32[]{:S(2)}) collective-permute-start(bf16[2,8,32,512]{3,2,1,0:T(8,128)(2,1)S(1)} %pad_maximum_fusion.2.mine_0), channel_id=1, source_target_pairs={{0,64},{32,96},{64,128},{96,160},{128,192},{160,224},{192,0},{224,... | collective-permute-start | bytes 1572872 | tf_op jit(solution)/shard_map/ppermute | solution.py:33
  28.3 3.5 %collective-permute-start.3 = (bf16[2,8,32,512]{3,2,1,0:T(8,128)(2,1)S(1)}, bf16[2,8,32,512]{3,2,1,0:T(8,128)(2,1)S(1)}, u32[]{:S(2)}, u32[]{:S(2)}) collective-permute-start(bf16[2,8,32,512]{3,2,1,0:T(8,128)(2,1)S(1)} %pad_maximum_fusion.2.mine_0), channel_id=1, source_target_pairs={{0,128},{32,160},{64,192},{96,224},{128,0},{160,32},{192,64},{224,... | collective-permute-start | bytes 1572872 | tf_op jit(solution)/shard_map/ppermute | solution.py:33
  31.9 1.9 collective-permute-start.4
  33.9 9.1 %collective-permute-start.7 = (bf16[144,512]{1,0:T(8,128)(2,1)S(1)}, bf16[144,512]{1,0:T(8,128)(2,1)S(1)}, u32[]{:S(2)}, u32[]{:S(2)}) collective-permute-start(bf16[144,512]{1,0:T(8,128)(2,1)S(1)} %pad_maximum_fusion.7.window_ref), channel_id=1, source_target_pairs={{0,8},{1,9},{2,10},{3,11},{4,12},{5,13},{6,14},{7,15},{8,16},{9,17... | collective-permute-start | bytes 442376 | tf_op jit(solution)/shard_map/ppermute | solution.py:25
  43.0 1.3 collective-permute-start.10
  44.5 1.3 collective-permute-done.7.eight_ref
  45.8 1.9 collective-permute-start.11
  47.7 2.4 %collective-permute-start.12 = (bf16[2,8,32,512]{3,2,1,0:T(8,128)(2,1)S(1)}, bf16[2,8,32,512]{3,2,1,0:T(8,128)(2,1)}, u32[]{:S(2)}, u32[]{:S(2)}) collective-permute-start(bf16[2,8,32,512]{3,2,1,0:T(8,128)(2,1)S(1)} %collective-permute-done.2.mine_1), channel_id=1, source_target_pairs={{0,32},{32,0},{64,96},{96,64},{128,160},{160,128},{192,224},{224,1... | collective-permute-start | bytes 1572872 | tf_op jit(solution)/shard_map/ppermute | solution.py:33
  50.1 1.9 collective-permute-start.13
  52.0 2.1 collective-permute-done.4.mine_3
  54.1 1.9 collective-permute-start.14
  56.0 5.6 %collective-permute-done.10.four_ref = bf16[272,512]{1,0:T(8,128)(2,1)S(1)} collective-permute-done((bf16[272,512]{1,0:T(8,128)(2,1)S(1)}, bf16[272,512]{1,0:T(8,128)(2,1)S(1)}, u32[]{:S(2)}, u32[]{:S(2)}) %collective-permute-start.10) | collective-permute-done | bytes 278560 | tf_op jit(solution)/shard_map/ppermute | solution.py:25
  61.6 1.3 collective-permute-start.9
  63.1 9.1 %collective-permute-done.9.two_ref = bf16[272,512]{1,0:T(8,128)(2,1)S(1)} collective-permute-done((bf16[272,512]{1,0:T(8,128)(2,1)}, bf16[272,512]{1,0:T(8,128)(2,1)S(1)}, u32[]{:S(2)}, u32[]{:S(2)}) %collective-permute-start.9) | collective-permute-done | bytes 278560 | tf_op jit(solution)/shard_map/ppermute | solution.py:25
  72.2 8.8 %shard_map.144 = (bf16[8,512,512]{2,1,0:T(8,128)(2,1)}, bf16[128,512]{1,0:T(8,128)(2,1)}, bf16[128,512]{1,0:T(8,128)(2,1)S(1)}, bf16[128,512]{1,0:T(8,128)(2,1)S...) custom-call(s32[3]{0:T(128)S(1)} %pad_add_fusion.place_ref, ...), custom_call_target="tpu_custom_call" | custom-call | tf_op jit(solution)/shard_map/pallas_call | solution.py:347
  81.0 0.7 shard_map.148
  81.7 1.9 collective-permute-start.21
  83.7 1.3 collective-permute-start.15
  85.0 1.3 collective-permute-start.16
  86.3 1.3 collective-permute-start.17
  87.6 1.3 collective-permute-start.18
  88.9 10.0 %collective-permute-done.15.eight_ref = bf16[272,512]{1,0:T(8,128)(2,1)S(1)} collective-permute-done((bf16[272,512]{1,0:T(8,128)(2,1)S(1)}, bf16[272,512]{1,0:T(8,128)(2,1)S(1)}, u32[]{:S(2)}, u32[]{:S(2)}) %collective-permute-start.15) | collective-permute-done | bytes 278560 | tf_op jit(solution)/shard_map/ppermute | solution.py:25
  98.9 1.3 collective-permute-start.19
  100.2 3.5 %shard_map.145 = (bf16[512,512]{1,0:T(8,128)(2,1)S(1)}, bf16[512,512]{1,0:T(8,128)(2,1)S(1)}) custom-call(bf16[128,512]{1,0:T(8,128)(2,1)S(1)} %bitcast.50, bf16[256,512]{1,0:T(8,128)(2,1)S(1)} %collective-permute-done.8.one_ref, bf16[272,512]{1,0:T(8,128)(2,1)S(1)} %collective-permute-done.9.two_ref, bf16[272,512]{1,0:T(8,128)(2,1)S(1)} %collective-permute-done.10.four_ref, ...), custom_call_target="tpu_custom_call" | custom-call | tf_op jit(solution)/shard_map/pallas_call | solution.py:367
  103.8 9.9 %collective-permute-done.19.eight_ref = f32[24,128]{1,0:T(8,128)S(1)} collective-permute-done((f32[24,128]{1,0:T(8,128)S(1)}, f32[24,128]{1,0:T(8,128)S(1)}, u32[]{:S(2)}, u32[]{:S(2)}) %collective-permute-start.19) | collective-permute-done | bytes 12320 | tf_op jit(solution)/shard_map/ppermute | solution.py:25
  113.7 5.1 %shard_map.146 = (bf16[128,512]{1,0:T(8,128)(2,1)S(1)}, bf16[128,512]{1,0:T(8,128)(2,1)S(1)}, bf16[8,4,32,512]{3,2,1,0:T(8,128)(2,1)S(1)}, bf16[8,4,32,512]{3,2,1,0:T(8,128)(2,1)}) custom-call(s32[1]{0:T(128)} %bitcast.2.core_ref, bf16[128,512]{1,0:T(8,128)(2,1)S(1)} %get-tuple-element.51.key_ref, bf16[128,512]{1,0:T(8,128)(2,1)S(1)} %get-tuple-element.52.value_ref, ...), custom_call_target="tpu_custom_call" | custom-call | tf_op jit(solution)/shard_map/pallas_call | solution.py:374
  118.8 2.1 collective-permute-start.22
  121.0 1.3 collective-permute-start.20
  122.3 5.1 %collective-permute-done.20.leading_ref = bf16[16,1024]{1,0:T(8,128)(2,1)S(1)} collective-permute-done((bf16[16,1024]{1,0:T(8,128)(2,1)S(1)}, bf16[16,1024]{1,0:T(8,128)(2,1)S(1)}, u32[]{:S(2)}, u32[]{:S(2)}) %collective-permute-start.20) | collective-permute-done | bytes 32800 | tf_op jit(solution)/shard_map/ppermute | solution.py:25
  127.4 4.3 %shard_map.147 = (bf16[128,512]{1,0:T(8,128)(2,1)}, bf16[16,512]{1,0:T(8,128)(2,1)S(1)}) custom-call(bf16[128,512]{1,0:T(8,128)(2,1)S(1)} %get-tuple-element.50.d_query_ref, bf16[128,512]{1,0:T(8,128)(2,1)S(1)} %get-tuple-element.64.d_key_ref, bf16[128,512]{1,0:T(8,128)(2,1)S(1)} %get-tuple-element.65.d_value_ref, ...), custom_call_target="tpu_custom_call" | custom-call | tf_op jit(solution)/shard_map/pallas_call | solution.py:379
  133.2 35.7 %all_to_all.15 = bf16[16,144,512]{2,1,0:T(8,128)(2,1)S(1)} all-to-all(bf16[16,144,512]{2,1,0:T(8,128)(2,1)S(1)} %pad_maximum_fusion), channel_id=1, replica_groups={{0,1,64,65,128,129,192,193,256,257,320,321,384,385,448,449},{2,3,66,67,..., dimensions={0} | all-to-all | bytes 4718592 | tf_op jit(solution)/shard_map/all_to_all | solution.py:41
  169.3 29.1 %all_to_all.16 = bf16[16,8,640]{2,1,0:T(8,128)(2,1)S(1)} all-to-all(bf16[16,8,640]{2,1,0:T(8,128)(2,1)S(1)} %pad_maximum_fusion.6), channel_id=1, replica_groups={{0,2,4,6,8,10,12,14,16,18,20,22,24,26,28,30},{1,3,5,7,9,11,13,15,17,19,..., dimensions={0} | all-to-all | bytes 327680 | tf_op jit(solution)/shard_map/all_to_all | solution.py:47
  199.1 4.6 %all-to-all-start.2 = ((bf16[16,8,512]{2,1,0:T(8,128)(2,1)}), bf16[16,8,512]{2,1,0:T(8,128)(2,1)S(1)}, u32[]{:S(2)}, u32[]{:S(2)}) async-start(bf16[16,8,512]{2,1,0:T(8,128)(2,1)} %broadcast_in_dim.54), calls=%async_computation.2 | async-start | bytes 262144 | tf_op jit(solution)/shard_map/all_to_all | solution.py:47
  203.6 1.9 collective-permute-start.23
  205.6 12.0 %all-to-all-done.2 = bf16[16,8,512]{2,1,0:T(8,128)(2,1)S(1)} async-done(((bf16[16,8,512]{2,1,0:T(8,128)(2,1)}), bf16[16,8,512]{2,1,0:T(8,128)(2,1)S(1)}, u32[]{:S(2)}, u32[]{:S(2)}) %all-to-all-start.2) | async-done | bytes 131104 | tf_op jit(solution)/shard_map/all_to_all | solution.py:47
  217.6 1.9 collective-permute-start.24
  220.1 4.3 %collective-permute-done.24 = bf16[16,8,512]{2,1,0:T(8,128)(2,1)S(1)} collective-permute-done((bf16[16,8,512]{2,1,0:T(8,128)(2,1)S(1)}, bf16[16,8,512]{2,1,0:T(8,128)(2,1)S(1)}, u32[]{:S(2)}, u32[]{:S(2)}) %collective-permute-start.24) | collective-permute-done | bytes 131104 | tf_op jit(solution)/shard_map/ppermute | solution.py:51
  224.5 0.7 slice.81
  225.9 0.7 slice.82
  (63 shorter events, 4.4 us)
Async XLA Ops:
  0.6 43.7 %copy-start.5 = (s32[4]{0:T(128)S(1)}, s32[4]{0:T(128)}, u32[]{:S(2)}) copy-start(s32[4]{0:T(128)} %constant.69.clone) | copy-start | bytes 52
  0.6 33.2 %copy-start = (bf16[1,128,512]{2,1,0:T(8,128)(2,1)S(1)}, bf16[1,128,512]{2,1,0:T(8,128)(2,1)}, u32[]{:S(2)}) copy-start(bf16[1,128,512]{2,1,0:T(8,128)(2,1)} %param.9) | copy-start | bytes 393220
  0.7 33.2 %copy-start.1 = (bf16[1,128,512]{2,1,0:T(8,128)(2,1)S(1)}, bf16[1,128,512]{2,1,0:T(8,128)(2,1)}, u32[]{:S(2)}) copy-start(bf16[1,128,512]{2,1,0:T(8,128)(2,1)} %param.16) | copy-start | bytes 393220
  0.7 33.1 %copy-start.4 = (s32[1,1,8,4]{2,3,1,0:T(4,128)S(1)}, s32[1,1,8,4]{2,3,1,0:T(4,128)}, u32[]{:S(2)}) copy-start(s32[1,1,8,4]{2,3,1,0:T(4,128)} %param.15) | copy-start | bytes 388
  0.7 71.6 %copy-start.2 = (f32[512]{0:T(512)S(1)}, f32[512]{0:T(512)}, u32[]{:S(2)}) copy-start(f32[512]{0:T(512)} %param.10) | copy-start | bytes 6148
  1.8 13.4 %collective-permute-start = (bf16[8,32,512]{2,1,0:T(8,128)(2,1)S(1)}, bf16[8,32,512]{2,1,0:T(8,128)(2,1)S(1)}, u32[]{:S(2)}, u32[]{:S(2)}) collective-permute-start(bf16[8,32,512]{2,1,0:T(8,128)(2,1)S(1)} %get-tuple-element.78), channel_id=1, source_target_pairs={{0,256},{32,288},{64,320},{96,352},{128,384},{160,416},{192,448},{... | collective-permute-start | bytes 786440 | tf_op jit(solution)/shard_map/ppermute | solution.py:33
  6.7 8.5 %collective-permute-start.1 = (bf16[128,512]{1,0:T(8,128)(2,1)}, bf16[128,512]{1,0:T(8,128)(2,1)S(1)}, u32[]{:S(2)}, u32[]{:S(2)}) collective-permute-start(bf16[128,512]{1,0:T(8,128)(2,1)} %bitcast.46), channel_id=1, source_target_pairs={{0,1},{1,2},{2,3},{3,4},{4,5},{5,6},{6,7},{7,8},{8,9},{9,10},{10,1... | collective-permute-start | bytes 393224 | tf_op jit(solution)/shard_map/ppermute | solution.py:25
  10.2 21.6 %collective-permute-start.8 = (bf16[256,512]{1,0:T(8,128)(2,1)S(1)}, bf16[256,512]{1,0:T(8,128)(2,1)S(1)}, u32[]{:S(2)}, u32[]{:S(2)}) collective-permute-start(bf16[256,512]{1,0:T(8,128)(2,1)S(1)} %pad_maximum_fusion.5), channel_id=1, source_target_pairs={{1,0},{2,1},{3,2},{4,3},{5,4},{6,5},{7,6},{8,7},{9,8},{10,9},{11,1... | collective-permute-start | bytes 786440 | tf_op jit(solution)/shard_map/ppermute | solution.py:25
  16.1 17.8 %collective-permute-start.5 = (bf16[144,512]{1,0:T(8,128)(2,1)S(1)}, bf16[144,512]{1,0:T(8,128)(2,1)S(1)}, u32[]{:S(2)}, u32[]{:S(2)}) collective-permute-start(bf16[144,512]{1,0:T(8,128)(2,1)S(1)} %pad_maximum_fusion.7.window_ref), channel_id=1, source_target_pairs={{0,2},{1,3},{2,4},{3,5},{4,6},{5,7},{6,8},{7,9},{8,10},{9,11},{10,... | collective-permute-start | bytes 442376 | tf_op jit(solution)/shard_map/ppermute | solution.py:25
  20.0 23.0 %collective-permute-start.6 = (bf16[144,512]{1,0:T(8,128)(2,1)S(1)}, bf16[144,512]{1,0:T(8,128)(2,1)S(1)}, u32[]{:S(2)}, u32[]{:S(2)}) collective-permute-start(bf16[144,512]{1,0:T(8,128)(2,1)S(1)} %pad_maximum_fusion.7.window_ref), channel_id=1, source_target_pairs={{0,4},{1,5},{2,6},{3,7},{4,8},{5,9},{6,10},{7,11},{8,12},{9,13},{1... | collective-permute-start | bytes 442376 | tf_op jit(solution)/shard_map/ppermute | solution.py:25
  25.2 22.5 %collective-permute-start.2 = (bf16[2,8,32,512]{3,2,1,0:T(8,128)(2,1)S(1)}, bf16[2,8,32,512]{3,2,1,0:T(8,128)(2,1)S(1)}, u32[]{:S(2)}, u32[]{:S(2)}) collective-permute-start(bf16[2,8,32,512]{3,2,1,0:T(8,128)(2,1)S(1)} %pad_maximum_fusion.2.mine_0), channel_id=1, source_target_pairs={{0,64},{32,96},{64,128},{96,160},{128,192},{160,224},{192,0},{224,... | collective-permute-start | bytes 1572872 | tf_op jit(solution)/shard_map/ppermute | solution.py:33
  28.3 21.8 %collective-permute-start.3 = (bf16[2,8,32,512]{3,2,1,0:T(8,128)(2,1)S(1)}, bf16[2,8,32,512]{3,2,1,0:T(8,128)(2,1)S(1)}, u32[]{:S(2)}, u32[]{:S(2)}) collective-permute-start(bf16[2,8,32,512]{3,2,1,0:T(8,128)(2,1)S(1)} %pad_maximum_fusion.2.mine_0), channel_id=1, source_target_pairs={{0,128},{32,160},{64,192},{96,224},{128,0},{160,32},{192,64},{224,... | collective-permute-start | bytes 1572872 | tf_op jit(solution)/shard_map/ppermute | solution.py:33
  31.9 22.2 %collective-permute-start.4 = (bf16[2,8,32,512]{3,2,1,0:T(8,128)(2,1)S(1)}, bf16[2,8,32,512]{3,2,1,0:T(8,128)(2,1)}, u32[]{:S(2)}, u32[]{:S(2)}) collective-permute-start(bf16[2,8,32,512]{3,2,1,0:T(8,128)(2,1)S(1)} %pad_maximum_fusion.2.mine_0), channel_id=1, source_target_pairs={{0,192},{32,224},{64,0},{96,32},{128,64},{160,96},{192,128},{224,1... | collective-permute-start | bytes 1572872 | tf_op jit(solution)/shard_map/ppermute | solution.py:33
  33.9 22.2 %copy-start.3 = (bf16[272,512]{1,0:T(8,128)(2,1)}, bf16[272,512]{1,0:T(8,128)(2,1)S(1)}, u32[]{:S(2)}) copy-start(bf16[272,512]{1,0:T(8,128)(2,1)S(1)} %pad_maximum_fusion.3) | copy-start | bytes 835588
  33.9 11.9 %collective-permute-start.7 = (bf16[144,512]{1,0:T(8,128)(2,1)S(1)}, bf16[144,512]{1,0:T(8,128)(2,1)S(1)}, u32[]{:S(2)}, u32[]{:S(2)}) collective-permute-start(bf16[144,512]{1,0:T(8,128)(2,1)S(1)} %pad_maximum_fusion.7.window_ref), channel_id=1, source_target_pairs={{0,8},{1,9},{2,10},{3,11},{4,12},{5,13},{6,14},{7,15},{8,16},{9,17... | collective-permute-start | bytes 442376 | tf_op jit(solution)/shard_map/ppermute | solution.py:25
  43.0 18.6 %collective-permute-start.10 = (bf16[272,512]{1,0:T(8,128)(2,1)S(1)}, bf16[272,512]{1,0:T(8,128)(2,1)S(1)}, u32[]{:S(2)}, u32[]{:S(2)}) collective-permute-start(bf16[272,512]{1,0:T(8,128)(2,1)S(1)} %pad_maximum_fusion.3), channel_id=1, source_target_pairs={{4,0},{5,1},{6,2},{7,3},{8,4},{9,5},{10,6},{11,7},{12,8},{13,9},{1... | collective-permute-start | bytes 835592 | tf_op jit(solution)/shard_map/ppermute | solution.py:25
  45.8 26.4 %collective-permute-start.11 = (bf16[2,8,32,512]{3,2,1,0:T(8,128)(2,1)S(1)}, bf16[2,8,32,512]{3,2,1,0:T(8,128)(2,1)}, u32[]{:S(2)}, u32[]{:S(2)}) collective-permute-start(bf16[2,8,32,512]{3,2,1,0:T(8,128)(2,1)S(1)} %pad_maximum_fusion.2.mine_0), channel_id=1, source_target_pairs={{0,32},{32,0},{64,96},{96,64},{128,160},{160,128},{192,224},{224,1... | collective-permute-start | bytes 1572872 | tf_op jit(solution)/shard_map/ppermute | solution.py:33
  47.7 24.5 %collective-permute-start.12 = (bf16[2,8,32,512]{3,2,1,0:T(8,128)(2,1)S(1)}, bf16[2,8,32,512]{3,2,1,0:T(8,128)(2,1)}, u32[]{:S(2)}, u32[]{:S(2)}) collective-permute-start(bf16[2,8,32,512]{3,2,1,0:T(8,128)(2,1)S(1)} %collective-permute-done.2.mine_1), channel_id=1, source_target_pairs={{0,32},{32,0},{64,96},{96,64},{128,160},{160,128},{192,224},{224,1... | collective-permute-start | bytes 1572872 | tf_op jit(solution)/shard_map/ppermute | solution.py:33
  50.1 22.0 %collective-permute-start.13 = (bf16[2,8,32,512]{3,2,1,0:T(8,128)(2,1)S(1)}, bf16[2,8,32,512]{3,2,1,0:T(8,128)(2,1)}, u32[]{:S(2)}, u32[]{:S(2)}) collective-permute-start(bf16[2,8,32,512]{3,2,1,0:T(8,128)(2,1)S(1)} %collective-permute-done.3.mine_2), channel_id=1, source_target_pairs={{0,32},{32,0},{64,96},{96,64},{128,160},{160,128},{192,224},{224,1... | collective-permute-start | bytes 1572872 | tf_op jit(solution)/shard_map/ppermute | solution.py:33
  54.1 18.1 %collective-permute-start.14 = (bf16[2,8,32,512]{3,2,1,0:T(8,128)(2,1)}, bf16[2,8,32,512]{3,2,1,0:T(8,128)(2,1)}, u32[]{:S(2)}, u32[]{:S(2)}) collective-permute-start(bf16[2,8,32,512]{3,2,1,0:T(8,128)(2,1)} %collective-permute-done.4.mine_3), channel_id=1, source_target_pairs={{0,32},{32,0},{64,96},{96,64},{128,160},{160,128},{192,224},{224,1... | collective-permute-start | bytes 1572872 | tf_op jit(solution)/shard_map/ppermute | solution.py:33
  61.6 10.5 %collective-permute-start.9 = (bf16[272,512]{1,0:T(8,128)(2,1)}, bf16[272,512]{1,0:T(8,128)(2,1)S(1)}, u32[]{:S(2)}, u32[]{:S(2)}) collective-permute-start(bf16[272,512]{1,0:T(8,128)(2,1)} %copy-done.3), channel_id=1, source_target_pairs={{2,0},{3,1},{4,2},{5,3},{6,4},{7,5},{8,6},{9,7},{10,8},{11,9},{12,... | collective-permute-start | bytes 835592 | tf_op jit(solution)/shard_map/ppermute | solution.py:25
  81.7 49.9 %collective-permute-start.21 = (bf16[8,4,32,512]{3,2,1,0:T(8,128)(2,1)S(1)}, bf16[8,4,32,512]{3,2,1,0:T(8,128)(2,1)S(1)}, u32[]{:S(2)}, u32[]{:S(2)}) collective-permute-start(bf16[8,4,32,512]{3,2,1,0:T(8,128)(2,1)S(1)} %get-tuple-element.69), channel_id=1, source_target_pairs={{0,32},{32,0},{64,96},{96,64},{128,160},{160,128},{192,224},{224,1... | collective-permute-start | bytes 3145736 | tf_op jit(solution)/shard_map/ppermute | solution.py:33
  83.7 15.2 %collective-permute-start.15 = (bf16[272,512]{1,0:T(8,128)(2,1)S(1)}, bf16[272,512]{1,0:T(8,128)(2,1)S(1)}, u32[]{:S(2)}, u32[]{:S(2)}) collective-permute-start(bf16[272,512]{1,0:T(8,128)(2,1)S(1)} %collective-permute-done.10.four_ref), channel_id=1, source_target_pairs={{4,0},{5,1},{6,2},{7,3},{8,4},{9,5},{10,6},{11,7},{12,8},{13,9},{1... | collective-permute-start | bytes 835592 | tf_op jit(solution)/shard_map/ppermute | solution.py:25
  85.0 18.8 %collective-permute-start.16 = (f32[24,128]{1,0:T(8,128)S(1)}, f32[24,128]{1,0:T(8,128)S(1)}, u32[]{:S(2)}, u32[]{:S(2)}) collective-permute-start(f32[24,128]{1,0:T(8,128)S(1)} %get-tuple-element.82), channel_id=1, source_target_pairs={{1,0},{2,1},{3,2},{4,3},{5,4},{6,5},{7,6},{8,7},{9,8},{10,9},{11,1... | collective-permute-start | bytes 36872 | tf_op jit(solution)/shard_map/ppermute | solution.py:25
  86.3 17.5 %collective-permute-start.17 = (f32[24,128]{1,0:T(8,128)S(1)}, f32[24,128]{1,0:T(8,128)S(1)}, u32[]{:S(2)}, u32[]{:S(2)}) collective-permute-start(f32[24,128]{1,0:T(8,128)S(1)} %get-tuple-element.81), channel_id=1, source_target_pairs={{2,0},{3,1},{4,2},{5,3},{6,4},{7,5},{8,6},{9,7},{10,8},{11,9},{12,... | collective-permute-start | bytes 36872 | tf_op jit(solution)/shard_map/ppermute | solution.py:25
  87.6 16.2 %collective-permute-start.18 = (f32[24,128]{1,0:T(8,128)S(1)}, f32[24,128]{1,0:T(8,128)S(1)}, u32[]{:S(2)}, u32[]{:S(2)}) collective-permute-start(f32[24,128]{1,0:T(8,128)S(1)} %get-tuple-element.80), channel_id=1, source_target_pairs={{4,0},{5,1},{6,2},{7,3},{8,4},{9,5},{10,6},{11,7},{12,8},{13,9},{1... | collective-permute-start | bytes 36872 | tf_op jit(solution)/shard_map/ppermute | solution.py:25
  98.9 14.8 %collective-permute-start.19 = (f32[24,128]{1,0:T(8,128)S(1)}, f32[24,128]{1,0:T(8,128)S(1)}, u32[]{:S(2)}, u32[]{:S(2)}) collective-permute-start(f32[24,128]{1,0:T(8,128)S(1)} %get-tuple-element.79), channel_id=1, source_target_pairs={{8,0},{9,1},{10,2},{11,3},{12,4},{13,5},{14,6},{15,7},{16,8},{17,9... | collective-permute-start | bytes 36872 | tf_op jit(solution)/shard_map/ppermute | solution.py:25
  118.8 13.3 %collective-permute-start.22 = (bf16[8,4,32,512]{3,2,1,0:T(8,128)(2,1)}, bf16[8,4,32,512]{3,2,1,0:T(8,128)(2,1)S(1)}, u32[]{:S(2)}, u32[]{:S(2)}) collective-permute-start(bf16[8,4,32,512]{3,2,1,0:T(8,128)(2,1)} %get-tuple-element.71), channel_id=1, source_target_pairs={{0,32},{32,0},{64,96},{96,64},{128,160},{160,128},{192,224},{224,1... | collective-permute-start | bytes 3145736 | tf_op jit(solution)/shard_map/ppermute | solution.py:33
  121.0 6.4 %collective-permute-start.20 = (bf16[16,1024]{1,0:T(8,128)(2,1)S(1)}, bf16[16,1024]{1,0:T(8,128)(2,1)S(1)}, u32[]{:S(2)}, u32[]{:S(2)}) collective-permute-start(bf16[16,1024]{1,0:T(8,128)(2,1)S(1)} %pad_maximum_fusion.8), channel_id=1, source_target_pairs={{1,0},{2,1},{3,2},{4,3},{5,4},{6,5},{7,6},{8,7},{9,8},{10,9},{11,1... | collective-permute-start | bytes 98312 | tf_op jit(solution)/shard_map/ppermute | solution.py:25
  199.1 18.6 %all-to-all-start.2 = ((bf16[16,8,512]{2,1,0:T(8,128)(2,1)}), bf16[16,8,512]{2,1,0:T(8,128)(2,1)S(1)}, u32[]{:S(2)}, u32[]{:S(2)}) async-start(bf16[16,8,512]{2,1,0:T(8,128)(2,1)} %broadcast_in_dim.54), calls=%async_computation.2 | async-start | bytes 262144 | tf_op jit(solution)/shard_map/all_to_all | solution.py:47
  203.6 15.9 %collective-permute-start.23 = (f32[4,128]{1,0:T(4,128)S(1)}, f32[4,128]{1,0:T(4,128)S(1)}, u32[]{:S(2)}, u32[]{:S(2)}) collective-permute-start(f32[4,128]{1,0:T(4,128)S(1)} %slice_add_fusion), channel_id=1, source_target_pairs={{0,32},{32,0},{64,96},{96,64},{128,160},{160,128},{192,224},{224,1... | collective-permute-start | bytes 6152 | tf_op jit(solution)/shard_map/ppermute | solution.py:33
  217.6 6.8 %collective-permute-start.24 = (bf16[16,8,512]{2,1,0:T(8,128)(2,1)S(1)}, bf16[16,8,512]{2,1,0:T(8,128)(2,1)S(1)}, u32[]{:S(2)}, u32[]{:S(2)}) collective-permute-start(bf16[16,8,512]{2,1,0:T(8,128)(2,1)S(1)} %all-to-all-done.2), channel_id=1, source_target_pairs={{0,1},{1,0},{2,3},{3,2},{4,5},{5,4},{6,7},{7,6},{8,9},{9,8},{10,11... | collective-permute-start | bytes 393224 | tf_op jit(solution)/shard_map/ppermute | solution.py:51

commit v6 on v5

--- a/solution.py
+++ b/solution.py
@@ -16,6 +16,7 @@
     for core in range(2)
     for z in range(16)
 ]
+chip_groups = [[2 * chip + core for chip in range(8)] for core in range(2)]
 z_groups = [[2 * z + side for z in range(16)] for side in range(2)]
 
 
@@ -35,6 +36,10 @@
 
 def other_core(shard):
     return dp_to(shard, 0, 0, 1)
+
+
+def over_chips(stacked):
+    return lax.all_to_all(stacked, "dp", 0, 0, axis_index_groups=chip_groups, tiled=True)
 
 
 def over_plane(stacked):
@@ -104,22 +109,17 @@
 
 
 def rows_kernel(
-    place_ref, links_ref, mine_0, mine_1, mine_2, mine_3, other_0, other_1, other_2, other_3,
-    window_ref, one_ref, two_ref, four_ref, eight_ref, upstream_ref, gain_ref, barred_ref,
+    core_ref, links_ref, mine_ref, other_ref, window_ref, one_ref, two_ref, four_ref, eight_ref, upstream_ref, gain_ref, barred_ref,
     weights_ref, mixed_ref, attn_ref, d_query_ref, query_ref, upper_ref, key_ref, value_ref,
     taps_ref, own_stats_ref, stats_ref,
     lines_ref, keys_ref, values_ref,
 ):
-    x, y, core = place_ref[0], place_ref[1], place_ref[2]
-    pieces = ((mine_0, other_0), (mine_1, other_1), (mine_2, other_2), (mine_3, other_3))
-    for back in range(4):
-        for side in range(2):
-            chip = (x if side == 0 else 1 - x) * 4 + lax.rem(y + 4 - back, 4)
-            for inner in range(2):
-                start = chip * 64 + (core if inner == 0 else 1 - core) * 32
-                rows = pl.ds(pl.multiple_of(start, 32), 32)
-                for matrix in range(8):
-                    weights_ref[matrix, rows] = pieces[back][inner][side, matrix]
+    even = core_ref[0] == 0
+    for chip in range(8):
+        for matrix in range(8):
+            mine, other = mine_ref[chip, matrix], other_ref[chip, matrix]
+            weights_ref[matrix, chip * 64 : chip * 64 + 32] = jnp.where(even, mine, other)
+            weights_ref[matrix, chip * 64 + 32 : chip * 64 + 64] = jnp.where(even, other, mine)
     gain = gain_ref[...]
     count = one_ref.shape[0]
     one = jnp.concatenate([two_ref[count:], one_ref[...]], axis=0)
@@ -308,9 +308,7 @@
 def body(
     series, norm_gain, query_kernel, key_kernel, value_weight, out_weight, block_links, grad_out
 ):
-    position = lax.axis_index("dp")
-    place = jnp.stack([position // 8, (position // 2) % 4, position % 2])
-    core = (position % 2).reshape(1)
+    core = (lax.axis_index("dp") % 2).reshape(1)
     block = lax.axis_index("ctx")
     heads = block_links.shape[2]
     own, cotangent = series[0], grad_out[0]
@@ -320,21 +318,23 @@
     shard = jnp.concatenate(
         [key_kernel, value_weight[None], query_kernel, out_weight[None]], axis=0
     )
-    across = dp_to(shard, 1, 0, 0)
+    mine = over_chips(jnp.broadcast_to(shard[None], (8,) + shard.shape))
     before_one = shift_ctx(own, 1)
     after_one = shift_ctx(jnp.concatenate([own, cotangent], axis=0), -1)
-    across, before_one = lax.optimization_barrier((across, before_one))
-    shards = jnp.stack([shard, across])
-    mine = [shards] + [dp_to(shards, 0, by, 0) for by in (1, 2, 3)]
+    before_one, after_one = lax.optimization_barrier((before_one, after_one))
     window = jnp.concatenate([before_one[count - edge :], own], axis=0)
     carried = jnp.concatenate([window, cotangent], axis=0)
-    before = [shift_ctx(window, by) for by in (2, 4, 8)]
-    after_four, after_two = shift_ctx(carried, -4), shift_ctx(carried, -2)
-    other = [other_core(piece) for piece in mine]
-    before, after_one, after_two, after_four, other = lax.optimization_barrier(
-        (before, after_one, after_two, after_four, other)
-    )
-    after = (after_one, after_two, after_four, shift_ctx(after_four, -4))
+    before_two, before_four = shift_ctx(window, 2), shift_ctx(window, 4)
+    after_two, after_four = shift_ctx(carried, -2), shift_ctx(carried, -4)
+    mine, before_two, before_four, after_two, after_four = lax.optimization_barrier(
+        (mine, before_two, before_four, after_two, after_four)
+    )
+    other = other_core(mine)
+    other, before_eight, after_eight = lax.optimization_barrier(
+        (other, shift_ctx(before_four, 4), shift_ctx(after_four, -4))
+    )
+    before = (before_two, before_four, before_eight)
+    after = (after_one, after_two, after_four, after_eight)
 
     offsets = jnp.array(block_offsets, dtype=jnp.int32)
     reach = (block_links[0, 0] > 0) & (block >= offsets)[None, :]
@@ -354,9 +354,9 @@
             pltpu.VMEM((5 * count, features), bf16),
         ],
         smem=2,
-        inputs=18,
+        inputs=12,
     )(
-        place, reach.astype(jnp.int32), *mine, *other, window, before_one, *before, cotangent, gain,
+        core, reach.astype(jnp.int32), mine, other, window, before_one, *before, cotangent, gain,
         barred,
     )
     returned = [shift_ctx(stats[i], -block_offsets[i]) for i in range(4)]

time: 228 us -> 226 us (level)
  blocking collectives: 64.7 us -> 70.3 us
  starting transfers between devices: 66.3 us -> 61.4 us
    ppermute x11 -> x4, starting transfers between devices: 27.6 us -> 7.66 us  [dp_to(): return lax.ppermute(shard, 'dp', [(i, target(i)) for i in range(16)])]
    all_to_all x0 -> x1, starting transfers between devices: none -> 9.98 us  [over_chips(): lax.all_to_all(stacked, 'dp', 0, 0, axis_index_groups=chip_groups, tiled=...]
    ppermute x13, starting transfers between devices: 32.2 us -> 37.2 us  [shift_ctx(): return lax.ppermute(shard, 'ctx', pairs)]
    all_to_all x1, blocking collectives: 29.1 us -> 33.2 us  [over_z(): lax.all_to_all(stacked, 'ctx', 0, 0, axis_index_groups=z_groups, tiled=True)]
  transfers between devices with their start and end apart: 26 -> 20, of which waited for: 10 -> 10; matrix products, arithmetic and copies ran while one was open for 1% -> 1% of each run, Pallas kernels for 6% -> 6%
where the time goes in v6:
time: 226 us; the launch traced here: 225 us
  blocking collectives  70.3 us (31%)
  starting transfers between devices  61.4 us (27%)
  waiting for transfers between devices  61.2 us (27%)
  Pallas kernels  22.8 us (10%)
  local copies, waits for them, and re-layouts  4.86 us (2%)
  other arithmetic  3.33 us (1%)
    ppermute x13, waiting for transfers between devices, shift_ctx(): return lax.ppermute(shard, 'ctx', pairs)  44.8 us
    ppermute x13, starting transfers between devices, shift_ctx(): return lax.ppermute(shard, 'ctx', pairs)  37.2 us
    all_to_all x1, blocking collectives, over_plane(): lax.all_to_all(stacked, ('dp', 'ctx'), 0, 0, axis_index_groups=plane_grou...  37.2 us
    all_to_all x1, blocking collectives, over_z(): lax.all_to_all(stacked, 'ctx', 0, 0, axis_index_groups=z_groups, tiled=True)  33.2 us
    all_to_all x1, waiting for transfers between devices, over_z(): lax.all_to_all(stacked, 'ctx', 0, 0, axis_index_groups=z_groups, tiled=True)  12 us
    all_to_all x1, starting transfers between devices, over_chips(): lax.all_to_all(stacked, 'dp', 0, 0, axis_index_groups=chip_groups, tiled=...  9.98 us
    pallas_call x1, Pallas kernels, body(): call(rows_kernel, [((8, features, features), bf16)] + [half] * 7 + [((3,...  9.1 us
    ppermute x4, starting transfers between devices, dp_to(): return lax.ppermute(shard, 'dp', [(i, target(i)) for i in range(16)])  7.66 us
  transfers between devices with their start and end apart: 20, of which 10 were waited for; matrix products, arithmetic and copies ran while one was open for 1% of the time, Pallas kernels for 6%

profile of v6, /device:TPU:24, one launch (start us, length us, event | category | flops | bytes accessed | tf_op | source)
XLA Modules:
  0.0 224.9 jit_solution(17787674875149887750)
XLA Ops:
  0.6 1.0 pad_maximum_fusion.3
  1.7 1.6 broadcast_in_dim.28
  3.3 10.0 %all-to-all-start = ((bf16[8,8,32,512]{3,2,1,0:T(8,128)(2,1)}), bf16[8,8,32,512]{3,2,1,0:T(8,128)(2,1)}, u32[]{:S(2)}, u32[]{:S(2)}) async-start(bf16[8,8,32,512]{3,2,1,0:T(8,128)(2,1)} %broadcast_in_dim.28), calls=%async_computation | async-start | bytes 4194304 | tf_op jit(solution)/shard_map/all_to_all | solution.py:42
  13.3 1.3 collective-permute-start.1
  14.6 4.6 %collective-permute-start = (bf16[128,512]{1,0:T(8,128)(2,1)S(1)}, bf16[128,512]{1,0:T(8,128)(2,1)S(1)}, u32[]{:S(2)}, u32[]{:S(2)}) collective-permute-start(bf16[128,512]{1,0:T(8,128)(2,1)S(1)} %bitcast.42), channel_id=1, source_target_pairs={{0,1},{1,2},{2,3},{3,4},{4,5},{5,6},{6,7},{7,8},{8,9},{9,10},{10,1... | collective-permute-start | bytes 393224 | tf_op jit(solution)/shard_map/ppermute | solution.py:26
  19.1 22.2 %collective-permute-done.one_ref = bf16[128,512]{1,0:T(8,128)(2,1)S(1)} collective-permute-done((bf16[128,512]{1,0:T(8,128)(2,1)S(1)}, bf16[128,512]{1,0:T(8,128)(2,1)S(1)}, u32[]{:S(2)}, u32[]{:S(2)}) %collective-permute-start) | collective-permute-done | bytes 131104 | tf_op jit(solution)/shard_map/ppermute | solution.py:26
  41.4 1.3 collective-permute-start.5
  42.7 1.3 collective-permute-start.4
  44.0 7.8 %collective-permute-start.3 = (bf16[144,512]{1,0:T(8,128)(2,1)S(1)}, bf16[144,512]{1,0:T(8,128)(2,1)S(1)}, u32[]{:S(2)}, u32[]{:S(2)}) collective-permute-start(bf16[144,512]{1,0:T(8,128)(2,1)S(1)} %pad_maximum_fusion.6.window_ref), channel_id=1, source_target_pairs={{0,4},{1,5},{2,6},{3,7},{4,8},{5,9},{6,10},{7,11},{8,12},{9,13},{1... | collective-permute-start | bytes 442376 | tf_op jit(solution)/shard_map/ppermute | solution.py:26
  51.8 3.9 %collective-permute-start.2 = (bf16[144,512]{1,0:T(8,128)(2,1)S(1)}, bf16[144,512]{1,0:T(8,128)(2,1)S(1)}, u32[]{:S(2)}, u32[]{:S(2)}) collective-permute-start(bf16[144,512]{1,0:T(8,128)(2,1)S(1)} %pad_maximum_fusion.6.window_ref), channel_id=1, source_target_pairs={{0,2},{1,3},{2,4},{3,5},{4,6},{5,7},{6,8},{7,9},{8,10},{9,11},{10,... | collective-permute-start | bytes 442376 | tf_op jit(solution)/shard_map/ppermute | solution.py:26
  55.7 2.6 %collective-permute-done.2.two_ref = bf16[144,512]{1,0:T(8,128)(2,1)S(1)} collective-permute-done((bf16[144,512]{1,0:T(8,128)(2,1)S(1)}, bf16[144,512]{1,0:T(8,128)(2,1)S(1)}, u32[]{:S(2)}, u32[]{:S(2)}) %collective-permute-start.2) | collective-permute-done | bytes 147488 | tf_op jit(solution)/shard_map/ppermute | solution.py:26
  58.4 2.4 %collective-permute-done.5.four_ref = bf16[272,512]{1,0:T(8,128)(2,1)S(1)} collective-permute-done((bf16[272,512]{1,0:T(8,128)(2,1)S(1)}, bf16[272,512]{1,0:T(8,128)(2,1)S(1)}, u32[]{:S(2)}, u32[]{:S(2)}) %collective-permute-start.5) | collective-permute-done | bytes 278560 | tf_op jit(solution)/shard_map/ppermute | solution.py:26
  60.8 1.9 collective-permute-start.6
  62.9 1.3 collective-permute-start.8
  64.3 9.2 %collective-permute-start.7 = (bf16[144,512]{1,0:T(8,128)(2,1)S(1)}, bf16[144,512]{1,0:T(8,128)(2,1)S(1)}, u32[]{:S(2)}, u32[]{:S(2)}) collective-permute-start(bf16[144,512]{1,0:T(8,128)(2,1)S(1)} %collective-permute-done.3.four_ref), channel_id=1, source_target_pairs={{0,4},{1,5},{2,6},{3,7},{4,8},{5,9},{6,10},{7,11},{8,12},{9,13},{1... | collective-permute-start | bytes 442376 | tf_op jit(solution)/shard_map/ppermute | solution.py:26
  73.4 3.7 %collective-permute-done.7.eight_ref = bf16[144,512]{1,0:T(8,128)(2,1)S(1)} collective-permute-done((bf16[144,512]{1,0:T(8,128)(2,1)S(1)}, bf16[144,512]{1,0:T(8,128)(2,1)S(1)}, u32[]{:S(2)}, u32[]{:S(2)}) %collective-permute-start.7) | collective-permute-done | bytes 147488 | tf_op jit(solution)/shard_map/ppermute | solution.py:26
  77.2 4.0 %collective-permute-done.8.eight_ref = bf16[272,512]{1,0:T(8,128)(2,1)S(1)} collective-permute-done((bf16[272,512]{1,0:T(8,128)(2,1)S(1)}, bf16[272,512]{1,0:T(8,128)(2,1)S(1)}, u32[]{:S(2)}, u32[]{:S(2)}) %collective-permute-start.8) | collective-permute-done | bytes 278560 | tf_op jit(solution)/shard_map/ppermute | solution.py:26
  81.2 9.1 %shard_map.144 = (bf16[8,512,512]{2,1,0:T(8,128)(2,1)}, bf16[128,512]{1,0:T(8,128)(2,1)}, bf16[128,512]{1,0:T(8,128)(2,1)S(1)}, bf16[128,512]{1,0:T(8,128)(2,1)S...) custom-call(s32[1]{0:T(128)} %bitcast.core_ref, ...), custom_call_target="tpu_custom_call" | custom-call | tf_op jit(solution)/shard_map/pallas_call | solution.py:347
  90.3 0.7 shard_map.148
  91.1 1.9 collective-permute-start.14
  93.0 1.3 collective-permute-start.12
  94.3 1.3 collective-permute-start.11
  95.6 1.3 collective-permute-start.10
  96.9 1.3 collective-permute-start.9
  98.2 3.5 %shard_map.145 = (bf16[512,512]{1,0:T(8,128)(2,1)S(1)}, bf16[512,512]{1,0:T(8,128)(2,1)S(1)}) custom-call(bf16[128,512]{1,0:T(8,128)(2,1)S(1)} %bitcast.45, bf16[256,512]{1,0:T(8,128)(2,1)S(1)} %collective-permute-done.1.one_ref, bf16[272,512]{1,0:T(8,128)(2,1)S(1)} %collective-permute-done.4.two_ref, bf16[272,512]{1,0:T(8,128)(2,1)S(1)} %collective-permute-done.5.four_ref, ...), custom_call_target="tpu_custom_call" | custom-call | tf_op jit(solution)/shard_map/pallas_call | solution.py:367
  101.8 2.5 %collective-permute-done.12.eight_ref = f32[24,128]{1,0:T(8,128)S(1)} collective-permute-done((f32[24,128]{1,0:T(8,128)S(1)}, f32[24,128]{1,0:T(8,128)S(1)}, u32[]{:S(2)}, u32[]{:S(2)}) %collective-permute-start.12) | collective-permute-done | bytes 12320 | tf_op jit(solution)/shard_map/ppermute | solution.py:26
  104.3 1.5 collective-permute-done.10.two_ref
  105.8 5.1 %shard_map.146 = (bf16[128,512]{1,0:T(8,128)(2,1)S(1)}, bf16[128,512]{1,0:T(8,128)(2,1)S(1)}, bf16[8,4,32,512]{3,2,1,0:T(8,128)(2,1)S(1)}, bf16[8,4,32,512]{3,2,1,0:T(8,128)(2,1)}) custom-call(s32[1]{0:T(128)} %bitcast.core_ref, bf16[128,512]{1,0:T(8,128)(2,1)S(1)} %get-tuple-element.47.key_ref, bf16[128,512]{1,0:T(8,128)(2,1)S(1)} %get-tuple-element.48.value_ref, ...), custom_call_target="tpu_custom_call" | custom-call | tf_op jit(solution)/shard_map/pallas_call | solution.py:374
  110.9 1.9 collective-permute-start.15
  112.8 1.5 collective-permute-start.13
  114.3 5.9 %collective-permute-done.13.leading_ref = bf16[16,1024]{1,0:T(8,128)(2,1)S(1)} collective-permute-done((bf16[16,1024]{1,0:T(8,128)(2,1)S(1)}, bf16[16,1024]{1,0:T(8,128)(2,1)S(1)}, u32[]{:S(2)}, u32[]{:S(2)}) %collective-permute-start.13) | collective-permute-done | bytes 32800 | tf_op jit(solution)/shard_map/ppermute | solution.py:26
  120.2 4.3 %shard_map.147 = (bf16[128,512]{1,0:T(8,128)(2,1)}, bf16[16,512]{1,0:T(8,128)(2,1)S(1)}) custom-call(bf16[128,512]{1,0:T(8,128)(2,1)S(1)} %get-tuple-element.46.d_query_ref, bf16[128,512]{1,0:T(8,128)(2,1)S(1)} %get-tuple-element.60.d_key_ref, bf16[128,512]{1,0:T(8,128)(2,1)S(1)} %get-tuple-element.61.d_value_ref, ...), custom_call_target="tpu_custom_call" | custom-call | tf_op jit(solution)/shard_map/pallas_call | solution.py:379
  124.5 0.4 fusion
  124.9 0.4 fusion.1
  125.5 0.2 copy.23
  126.0 37.2 %all_to_all.20 = bf16[16,144,512]{2,1,0:T(8,128)(2,1)S(1)} all-to-all(bf16[16,144,512]{2,1,0:T(8,128)(2,1)S(1)} %pad_maximum_fusion), channel_id=1, replica_groups={{0,1,64,65,128,129,192,193,256,257,320,321,384,385,448,449},{2,3,66,67,..., dimensions={0} | all-to-all | bytes 4718592 | tf_op jit(solution)/shard_map/all_to_all | solution.py:46
  163.1 0.3 convert_reduce_fusion
  163.6 33.2 %all_to_all.21 = bf16[16,8,640]{2,1,0:T(8,128)(2,1)S(1)} all-to-all(bf16[16,8,640]{2,1,0:T(8,128)(2,1)S(1)} %pad_maximum_fusion.5), channel_id=1, replica_groups={{0,2,4,6,8,10,12,14,16,18,20,22,24,26,28,30},{1,3,5,7,9,11,13,15,17,19,..., dimensions={0} | all-to-all | bytes 327680 | tf_op jit(solution)/shard_map/all_to_all | solution.py:52
  196.8 0.7 broadcast_in_dim.61
  197.5 4.6 %all-to-all-start.3 = ((bf16[16,8,512]{2,1,0:T(8,128)(2,1)}), bf16[16,8,512]{2,1,0:T(8,128)(2,1)S(1)}, u32[]{:S(2)}, u32[]{:S(2)}) async-start(bf16[16,8,512]{2,1,0:T(8,128)(2,1)} %broadcast_in_dim.61), calls=%async_computation.3 | async-start | bytes 262144 | tf_op jit(solution)/shard_map/all_to_all | solution.py:52
  202.1 1.9 collective-permute-start.16
  204.0 12.0 %all-to-all-done.3 = bf16[16,8,512]{2,1,0:T(8,128)(2,1)S(1)} async-done(((bf16[16,8,512]{2,1,0:T(8,128)(2,1)}), bf16[16,8,512]{2,1,0:T(8,128)(2,1)S(1)}, u32[]{:S(2)}, u32[]{:S(2)}) %all-to-all-start.3) | async-done | bytes 131104 | tf_op jit(solution)/shard_map/all_to_all | solution.py:52
  216.0 1.9 collective-permute-start.17
  217.9 0.6 add_bitcast_fusion
  218.5 4.3 %collective-permute-done.17 = bf16[16,8,512]{2,1,0:T(8,128)(2,1)S(1)} collective-permute-done((bf16[16,8,512]{2,1,0:T(8,128)(2,1)S(1)}, bf16[16,8,512]{2,1,0:T(8,128)(2,1)S(1)}, u32[]{:S(2)}, u32[]{:S(2)}) %collective-permute-start.17) | collective-permute-done | bytes 131104 | tf_op jit(solution)/shard_map/ppermute | solution.py:56
  222.9 0.7 slice.82
  223.6 0.7 slice_bitcast_fusion
  224.3 0.7 slice.81
  (48 shorter events, 1.0 us)
Async XLA Ops:
  3.2 10.0 %copy-start = (bf16[1,128,512]{2,1,0:T(8,128)(2,1)S(1)}, bf16[1,128,512]{2,1,0:T(8,128)(2,1)}, u32[]{:S(2)}) copy-start(bf16[1,128,512]{2,1,0:T(8,128)(2,1)} %param.9) | copy-start | bytes 393220
  3.2 10.0 %copy-start.1 = (bf16[1,128,512]{2,1,0:T(8,128)(2,1)S(1)}, bf16[1,128,512]{2,1,0:T(8,128)(2,1)}, u32[]{:S(2)}) copy-start(bf16[1,128,512]{2,1,0:T(8,128)(2,1)} %param.16) | copy-start | bytes 393220
  3.2 59.5 %copy-start.3 = (s32[1,1,8,4]{2,3,1,0:T(4,128)S(1)}, s32[1,1,8,4]{2,3,1,0:T(4,128)}, u32[]{:S(2)}) copy-start(s32[1,1,8,4]{2,3,1,0:T(4,128)} %param.15) | copy-start | bytes 388
  3.2 59.6 %copy-start.4 = (s32[4]{0:T(128)S(1)}, s32[4]{0:T(128)}, u32[]{:S(2)}) copy-start(s32[4]{0:T(128)} %constant.36.clone) | copy-start | bytes 52
  3.3 78.0 %copy-start.2 = (f32[512]{0:T(512)S(1)}, f32[512]{0:T(512)}, u32[]{:S(2)}) copy-start(f32[512]{0:T(512)} %param.10) | copy-start | bytes 6148
  3.3 57.5 %all-to-all-start = ((bf16[8,8,32,512]{3,2,1,0:T(8,128)(2,1)}), bf16[8,8,32,512]{3,2,1,0:T(8,128)(2,1)}, u32[]{:S(2)}, u32[]{:S(2)}) async-start(bf16[8,8,32,512]{3,2,1,0:T(8,128)(2,1)} %broadcast_in_dim.28), calls=%async_computation | async-start | bytes 4194304 | tf_op jit(solution)/shard_map/all_to_all | solution.py:42
  13.3 28.1 %collective-permute-start.1 = (bf16[256,512]{1,0:T(8,128)(2,1)S(1)}, bf16[256,512]{1,0:T(8,128)(2,1)S(1)}, u32[]{:S(2)}, u32[]{:S(2)}) collective-permute-start(bf16[256,512]{1,0:T(8,128)(2,1)S(1)} %pad_maximum_fusion.4), channel_id=1, source_target_pairs={{1,0},{2,1},{3,2},{4,3},{5,4},{6,5},{7,6},{8,7},{9,8},{10,9},{11,1... | collective-permute-start | bytes 786440 | tf_op jit(solution)/shard_map/ppermute | solution.py:26
  14.6 26.7 %collective-permute-start = (bf16[128,512]{1,0:T(8,128)(2,1)S(1)}, bf16[128,512]{1,0:T(8,128)(2,1)S(1)}, u32[]{:S(2)}, u32[]{:S(2)}) collective-permute-start(bf16[128,512]{1,0:T(8,128)(2,1)S(1)} %bitcast.42), channel_id=1, source_target_pairs={{0,1},{1,2},{2,3},{3,4},{4,5},{5,6},{6,7},{7,8},{8,9},{9,10},{10,1... | collective-permute-start | bytes 393224 | tf_op jit(solution)/shard_map/ppermute | solution.py:26
  41.4 19.4 %collective-permute-start.5 = (bf16[272,512]{1,0:T(8,128)(2,1)S(1)}, bf16[272,512]{1,0:T(8,128)(2,1)S(1)}, u32[]{:S(2)}, u32[]{:S(2)}) collective-permute-start(bf16[272,512]{1,0:T(8,128)(2,1)S(1)} %pad_maximum_fusion.2), channel_id=1, source_target_pairs={{4,0},{5,1},{6,2},{7,3},{8,4},{9,5},{10,6},{11,7},{12,8},{13,9},{1... | collective-permute-start | bytes 835592 | tf_op jit(solution)/shard_map/ppermute | solution.py:26
  42.7 18.1 %collective-permute-start.4 = (bf16[272,512]{1,0:T(8,128)(2,1)S(1)}, bf16[272,512]{1,0:T(8,128)(2,1)S(1)}, u32[]{:S(2)}, u32[]{:S(2)}) collective-permute-start(bf16[272,512]{1,0:T(8,128)(2,1)S(1)} %pad_maximum_fusion.2), channel_id=1, source_target_pairs={{2,0},{3,1},{4,2},{5,3},{6,4},{7,5},{8,6},{9,7},{10,8},{11,9},{12,... | collective-permute-start | bytes 835592 | tf_op jit(solution)/shard_map/ppermute | solution.py:26
  44.0 11.8 %collective-permute-start.3 = (bf16[144,512]{1,0:T(8,128)(2,1)S(1)}, bf16[144,512]{1,0:T(8,128)(2,1)S(1)}, u32[]{:S(2)}, u32[]{:S(2)}) collective-permute-start(bf16[144,512]{1,0:T(8,128)(2,1)S(1)} %pad_maximum_fusion.6.window_ref), channel_id=1, source_target_pairs={{0,4},{1,5},{2,6},{3,7},{4,8},{5,9},{6,10},{7,11},{8,12},{9,13},{1... | collective-permute-start | bytes 442376 | tf_op jit(solution)/shard_map/ppermute | solution.py:26
  51.8 6.6 %collective-permute-start.2 = (bf16[144,512]{1,0:T(8,128)(2,1)S(1)}, bf16[144,512]{1,0:T(8,128)(2,1)S(1)}, u32[]{:S(2)}, u32[]{:S(2)}) collective-permute-start(bf16[144,512]{1,0:T(8,128)(2,1)S(1)} %pad_maximum_fusion.6.window_ref), channel_id=1, source_target_pairs={{0,2},{1,3},{2,4},{3,5},{4,6},{5,7},{6,8},{7,9},{8,10},{9,11},{10,... | collective-permute-start | bytes 442376 | tf_op jit(solution)/shard_map/ppermute | solution.py:26
  60.8 20.4 %collective-permute-start.6 = (bf16[8,8,32,512]{3,2,1,0:T(8,128)(2,1)}, bf16[8,8,32,512]{3,2,1,0:T(8,128)(2,1)}, u32[]{:S(2)}, u32[]{:S(2)}) collective-permute-start(bf16[8,8,32,512]{3,2,1,0:T(8,128)(2,1)} %all-to-all-done.mine_ref), channel_id=1, source_target_pairs={{0,32},{32,0},{64,96},{96,64},{128,160},{160,128},{192,224},{224,1... | collective-permute-start | bytes 6291464 | tf_op jit(solution)/shard_map/ppermute | solution.py:34
  62.9 18.3 %collective-permute-start.8 = (bf16[272,512]{1,0:T(8,128)(2,1)S(1)}, bf16[272,512]{1,0:T(8,128)(2,1)S(1)}, u32[]{:S(2)}, u32[]{:S(2)}) collective-permute-start(bf16[272,512]{1,0:T(8,128)(2,1)S(1)} %collective-permute-done.5.four_ref), channel_id=1, source_target_pairs={{4,0},{5,1},{6,2},{7,3},{8,4},{9,5},{10,6},{11,7},{12,8},{13,9},{1... | collective-permute-start | bytes 835592 | tf_op jit(solution)/shard_map/ppermute | solution.py:26
  64.3 12.9 %collective-permute-start.7 = (bf16[144,512]{1,0:T(8,128)(2,1)S(1)}, bf16[144,512]{1,0:T(8,128)(2,1)S(1)}, u32[]{:S(2)}, u32[]{:S(2)}) collective-permute-start(bf16[144,512]{1,0:T(8,128)(2,1)S(1)} %collective-permute-done.3.four_ref), channel_id=1, source_target_pairs={{0,4},{1,5},{2,6},{3,7},{4,8},{5,9},{6,10},{7,11},{8,12},{9,13},{1... | collective-permute-start | bytes 442376 | tf_op jit(solution)/shard_map/ppermute | solution.py:26
  91.1 33.4 %collective-permute-start.14 = (bf16[8,4,32,512]{3,2,1,0:T(8,128)(2,1)S(1)}, bf16[8,4,32,512]{3,2,1,0:T(8,128)(2,1)S(1)}, u32[]{:S(2)}, u32[]{:S(2)}) collective-permute-start(bf16[8,4,32,512]{3,2,1,0:T(8,128)(2,1)S(1)} %get-tuple-element.65), channel_id=1, source_target_pairs={{0,32},{32,0},{64,96},{96,64},{128,160},{160,128},{192,224},{224,1... | collective-permute-start | bytes 3145736 | tf_op jit(solution)/shard_map/ppermute | solution.py:34
  93.0 11.3 %collective-permute-start.12 = (f32[24,128]{1,0:T(8,128)S(1)}, f32[24,128]{1,0:T(8,128)S(1)}, u32[]{:S(2)}, u32[]{:S(2)}) collective-permute-start(f32[24,128]{1,0:T(8,128)S(1)} %get-tuple-element.73), channel_id=1, source_target_pairs={{8,0},{9,1},{10,2},{11,3},{12,4},{13,5},{14,6},{15,7},{16,8},{17,9... | collective-permute-start | bytes 36872 | tf_op jit(solution)/shard_map/ppermute | solution.py:26
  94.3 10.0 %collective-permute-start.11 = (f32[24,128]{1,0:T(8,128)S(1)}, f32[24,128]{1,0:T(8,128)S(1)}, u32[]{:S(2)}, u32[]{:S(2)}) collective-permute-start(f32[24,128]{1,0:T(8,128)S(1)} %get-tuple-element.74), channel_id=1, source_target_pairs={{4,0},{5,1},{6,2},{7,3},{8,4},{9,5},{10,6},{11,7},{12,8},{13,9},{1... | collective-permute-start | bytes 36872 | tf_op jit(solution)/shard_map/ppermute | solution.py:26
  95.6 10.2 %collective-permute-start.10 = (f32[24,128]{1,0:T(8,128)S(1)}, f32[24,128]{1,0:T(8,128)S(1)}, u32[]{:S(2)}, u32[]{:S(2)}) collective-permute-start(f32[24,128]{1,0:T(8,128)S(1)} %get-tuple-element.75), channel_id=1, source_target_pairs={{2,0},{3,1},{4,2},{5,3},{6,4},{7,5},{8,6},{9,7},{10,8},{11,9},{12,... | collective-permute-start | bytes 36872 | tf_op jit(solution)/shard_map/ppermute | solution.py:26
  96.9 8.9 %collective-permute-start.9 = (f32[24,128]{1,0:T(8,128)S(1)}, f32[24,128]{1,0:T(8,128)S(1)}, u32[]{:S(2)}, u32[]{:S(2)}) collective-permute-start(f32[24,128]{1,0:T(8,128)S(1)} %get-tuple-element.76), channel_id=1, source_target_pairs={{1,0},{2,1},{3,2},{4,3},{5,4},{6,5},{7,6},{8,7},{9,8},{10,9},{11,1... | collective-permute-start | bytes 36872 | tf_op jit(solution)/shard_map/ppermute | solution.py:26
  110.9 14.0 %collective-permute-start.15 = (bf16[8,4,32,512]{3,2,1,0:T(8,128)(2,1)}, bf16[8,4,32,512]{3,2,1,0:T(8,128)(2,1)S(1)}, u32[]{:S(2)}, u32[]{:S(2)}) collective-permute-start(bf16[8,4,32,512]{3,2,1,0:T(8,128)(2,1)} %get-tuple-element.67), channel_id=1, source_target_pairs={{0,32},{32,0},{64,96},{96,64},{128,160},{160,128},{192,224},{224,1... | collective-permute-start | bytes 3145736 | tf_op jit(solution)/shard_map/ppermute | solution.py:34
  112.8 7.3 %collective-permute-start.13 = (bf16[16,1024]{1,0:T(8,128)(2,1)S(1)}, bf16[16,1024]{1,0:T(8,128)(2,1)S(1)}, u32[]{:S(2)}, u32[]{:S(2)}) collective-permute-start(bf16[16,1024]{1,0:T(8,128)(2,1)S(1)} %pad_maximum_fusion.7), channel_id=1, source_target_pairs={{1,0},{2,1},{3,2},{4,3},{5,4},{6,5},{7,6},{8,7},{9,8},{10,9},{11,1... | collective-permute-start | bytes 98312 | tf_op jit(solution)/shard_map/ppermute | solution.py:26
  197.5 18.6 %all-to-all-start.3 = ((bf16[16,8,512]{2,1,0:T(8,128)(2,1)}), bf16[16,8,512]{2,1,0:T(8,128)(2,1)S(1)}, u32[]{:S(2)}, u32[]{:S(2)}) async-start(bf16[16,8,512]{2,1,0:T(8,128)(2,1)} %broadcast_in_dim.61), calls=%async_computation.3 | async-start | bytes 262144 | tf_op jit(solution)/shard_map/all_to_all | solution.py:52
  202.1 15.9 %collective-permute-start.16 = (f32[4,128]{1,0:T(4,128)S(1)}, f32[4,128]{1,0:T(4,128)S(1)}, u32[]{:S(2)}, u32[]{:S(2)}) collective-permute-start(f32[4,128]{1,0:T(4,128)S(1)} %slice_add_fusion), channel_id=1, source_target_pairs={{0,32},{32,0},{64,96},{96,64},{128,160},{160,128},{192,224},{224,1... | collective-permute-start | bytes 6152 | tf_op jit(solution)/shard_map/ppermute | solution.py:34
  216.0 6.8 %collective-permute-start.17 = (bf16[16,8,512]{2,1,0:T(8,128)(2,1)S(1)}, bf16[16,8,512]{2,1,0:T(8,128)(2,1)S(1)}, u32[]{:S(2)}, u32[]{:S(2)}) collective-permute-start(bf16[16,8,512]{2,1,0:T(8,128)(2,1)S(1)} %all-to-all-done.3), channel_id=1, source_target_pairs={{0,1},{1,0},{2,3},{3,2},{4,5},{5,4},{6,7},{7,6},{8,9},{9,8},{10,11... | collective-permute-start | bytes 393224 | tf_op jit(solution)/shard_map/ppermute | solution.py:56

commit v7 on v6

--- a/solution.py
+++ b/solution.py
@@ -318,21 +318,18 @@
     shard = jnp.concatenate(
         [key_kernel, value_weight[None], query_kernel, out_weight[None]], axis=0
     )
-    mine = over_chips(jnp.broadcast_to(shard[None], (8,) + shard.shape))
     before_one = shift_ctx(own, 1)
     after_one = shift_ctx(jnp.concatenate([own, cotangent], axis=0), -1)
-    before_one, after_one = lax.optimization_barrier((before_one, after_one))
+    shard, before_one, after_one = lax.optimization_barrier((shard, before_one, after_one))
     window = jnp.concatenate([before_one[count - edge :], own], axis=0)
     carried = jnp.concatenate([window, cotangent], axis=0)
-    before_two, before_four = shift_ctx(window, 2), shift_ctx(window, 4)
-    after_two, after_four = shift_ctx(carried, -2), shift_ctx(carried, -4)
-    mine, before_two, before_four, after_two, after_four = lax.optimization_barrier(
-        (mine, before_two, before_four, after_two, after_four)
-    )
-    other = other_core(mine)
-    other, before_eight, after_eight = lax.optimization_barrier(
-        (other, shift_ctx(before_four, 4), shift_ctx(after_four, -4))
-    )
+    after_eight, after_four, after_two = [shift_ctx(carried, -by) for by in (8, 4, 2)]
+    before_four, before_two = shift_ctx(window, 4), shift_ctx(window, 2)
+    mine = over_chips(jnp.broadcast_to(shard[None], (8,) + shard.shape))
+    mine, before_two, before_four, after_two, after_four, after_eight = lax.optimization_barrier(
+        (mine, before_two, before_four, after_two, after_four, after_eight)
+    )
+    other, before_eight = lax.optimization_barrier((other_core(mine), shift_ctx(before_four, 4)))
     before = (before_two, before_four, before_eight)
     after = (after_one, after_two, after_four, after_eight)
 

time: 226 us -> 227 us (level)
  starting transfers between devices: 61.4 us -> 58.1 us
    all_to_all x1, starting transfers between devices: 9.98 us -> 7 us  [over_chips(): lax.all_to_all(stacked, 'dp', 0, 0, axis_index_groups=chip_groups, tiled=...]
  transfers between devices with their start and end apart: 20 -> 20, of which waited for: 10 -> 8; matrix products, arithmetic and copies ran while one was open for 1% -> 1% of each run, Pallas kernels for 6% -> 6%
where the time goes in v7:
time: 227 us; the launch traced here: 226 us
  blocking collectives  71.8 us (32%)
  waiting for transfers between devices  63.2 us (28%)
  starting transfers between devices  58.1 us (26%)
  Pallas kernels  22.8 us (10%)
  local copies, waits for them, and re-layouts  4.86 us (2%)
  other arithmetic  4.27 us (2%)
    ppermute x13, waiting for transfers between devices, shift_ctx(): return lax.ppermute(shard, 'ctx', pairs)  46.8 us
    all_to_all x1, blocking collectives, over_plane(): lax.all_to_all(stacked, ('dp', 'ctx'), 0, 0, axis_index_groups=plane_grou...  37.5 us
    ppermute x13, starting transfers between devices, shift_ctx(): return lax.ppermute(shard, 'ctx', pairs)  36.9 us
    all_to_all x1, blocking collectives, over_z(): lax.all_to_all(stacked, 'ctx', 0, 0, axis_index_groups=z_groups, tiled=True)  34.2 us
    all_to_all x1, waiting for transfers between devices, over_z(): lax.all_to_all(stacked, 'ctx', 0, 0, axis_index_groups=z_groups, tiled=True)  12 us
    pallas_call x1, Pallas kernels, body(): call(rows_kernel, [((8, features, features), bf16)] + [half] * 7 + [((3,...  9.1 us
    ppermute x4, starting transfers between devices, dp_to(): return lax.ppermute(shard, 'dp', [(i, target(i)) for i in range(16)])  7.67 us
    all_to_all x1, starting transfers between devices, over_chips(): lax.all_to_all(stacked, 'dp', 0, 0, axis_index_groups=chip_groups, tiled=...  7 us
  transfers between devices with their start and end apart: 20, of which 8 were waited for; matrix products, arithmetic and copies ran while one was open for 1% of the time, Pallas kernels for 6%

profile of v7, /device:TPU:24, one launch (start us, length us, event | category | flops | bytes accessed | tf_op | source)
XLA Modules:
  0.0 226.0 jit_solution(8836968356626888367)
XLA Ops:
  0.6 1.0 pad_maximum_fusion.4
  1.6 1.3 collective-permute-start.1
  2.9 4.6 %collective-permute-start = (bf16[128,512]{1,0:T(8,128)(2,1)}, bf16[128,512]{1,0:T(8,128)(2,1)S(1)}, u32[]{:S(2)}, u32[]{:S(2)}) collective-permute-start(bf16[128,512]{1,0:T(8,128)(2,1)} %bitcast.42), channel_id=1, source_target_pairs={{0,1},{1,2},{2,3},{3,4},{4,5},{5,6},{6,7},{7,8},{8,9},{9,10},{10,1... | collective-permute-start | bytes 393224 | tf_op jit(solution)/shard_map/ppermute | solution.py:26
  7.5 1.0 pad_maximum_fusion.3
  8.5 5.9 %collective-permute-done.one_ref = bf16[128,512]{1,0:T(8,128)(2,1)S(1)} collective-permute-done((bf16[128,512]{1,0:T(8,128)(2,1)}, bf16[128,512]{1,0:T(8,128)(2,1)S(1)}, u32[]{:S(2)}, u32[]{:S(2)}) %collective-permute-start) | collective-permute-done | bytes 131104 | tf_op jit(solution)/shard_map/ppermute | solution.py:26
  14.4 1.6 broadcast_in_dim.28
  16.0 7.0 %all-to-all-start = ((bf16[8,8,32,512]{3,2,1,0:T(8,128)(2,1)}), bf16[8,8,32,512]{3,2,1,0:T(8,128)(2,1)}, u32[]{:S(2)}, u32[]{:S(2)}) async-start(bf16[8,8,32,512]{3,2,1,0:T(8,128)(2,1)} %broadcast_in_dim.28), calls=%async_computation | async-start | bytes 4194304 | tf_op jit(solution)/shard_map/all_to_all | solution.py:42
  23.0 1.3 collective-permute-start.6
  24.3 1.3 collective-permute-start.5
  25.6 1.3 collective-permute-start.4
  27.0 6.7 %collective-permute-start.3 = (bf16[144,512]{1,0:T(8,128)(2,1)S(1)}, bf16[144,512]{1,0:T(8,128)(2,1)S(1)}, u32[]{:S(2)}, u32[]{:S(2)}) collective-permute-start(bf16[144,512]{1,0:T(8,128)(2,1)S(1)} %pad_maximum_fusion.6.window_ref), channel_id=1, source_target_pairs={{0,4},{1,5},{2,6},{3,7},{4,8},{5,9},{6,10},{7,11},{8,12},{9,13},{1... | collective-permute-start | bytes 442376 | tf_op jit(solution)/shard_map/ppermute | solution.py:26
  33.7 4.8 %collective-permute-start.2 = (bf16[144,512]{1,0:T(8,128)(2,1)S(1)}, bf16[144,512]{1,0:T(8,128)(2,1)S(1)}, u32[]{:S(2)}, u32[]{:S(2)}) collective-permute-start(bf16[144,512]{1,0:T(8,128)(2,1)S(1)} %pad_maximum_fusion.6.window_ref), channel_id=1, source_target_pairs={{0,2},{1,3},{2,4},{3,5},{4,6},{5,7},{6,8},{7,9},{8,10},{9,11},{10,... | collective-permute-start | bytes 442376 | tf_op jit(solution)/shard_map/ppermute | solution.py:26
  38.5 2.6 %collective-permute-done.2.two_ref = bf16[144,512]{1,0:T(8,128)(2,1)S(1)} collective-permute-done((bf16[144,512]{1,0:T(8,128)(2,1)S(1)}, bf16[144,512]{1,0:T(8,128)(2,1)S(1)}, u32[]{:S(2)}, u32[]{:S(2)}) %collective-permute-start.2) | collective-permute-done | bytes 147488 | tf_op jit(solution)/shard_map/ppermute | solution.py:26
  41.1 21.9 %collective-permute-done.6.eight_ref = bf16[272,512]{1,0:T(8,128)(2,1)S(1)} collective-permute-done((bf16[272,512]{1,0:T(8,128)(2,1)S(1)}, bf16[272,512]{1,0:T(8,128)(2,1)S(1)}, u32[]{:S(2)}, u32[]{:S(2)}) %collective-permute-start.6) | collective-permute-done | bytes 278560 | tf_op jit(solution)/shard_map/ppermute | solution.py:26
  63.0 1.9 collective-permute-start.7
  65.2 9.1 %collective-permute-start.8 = (bf16[144,512]{1,0:T(8,128)(2,1)S(1)}, bf16[144,512]{1,0:T(8,128)(2,1)S(1)}, u32[]{:S(2)}, u32[]{:S(2)}) collective-permute-start(bf16[144,512]{1,0:T(8,128)(2,1)S(1)} %collective-permute-done.3.four_ref), channel_id=1, source_target_pairs={{0,4},{1,5},{2,6},{3,7},{4,8},{5,9},{6,10},{7,11},{8,12},{9,13},{1... | collective-permute-start | bytes 442376 | tf_op jit(solution)/shard_map/ppermute | solution.py:26
  74.2 3.7 %collective-permute-done.8.eight_ref = bf16[144,512]{1,0:T(8,128)(2,1)S(1)} collective-permute-done((bf16[144,512]{1,0:T(8,128)(2,1)S(1)}, bf16[144,512]{1,0:T(8,128)(2,1)S(1)}, u32[]{:S(2)}, u32[]{:S(2)}) %collective-permute-start.8) | collective-permute-done | bytes 147488 | tf_op jit(solution)/shard_map/ppermute | solution.py:26
  78.0 9.1 %shard_map.144 = (bf16[8,512,512]{2,1,0:T(8,128)(2,1)}, bf16[128,512]{1,0:T(8,128)(2,1)}, bf16[128,512]{1,0:T(8,128)(2,1)S(1)}, bf16[128,512]{1,0:T(8,128)(2,1)S...) custom-call(s32[1]{0:T(128)} %bitcast.core_ref, ...), custom_call_target="tpu_custom_call" | custom-call | tf_op jit(solution)/shard_map/pallas_call | solution.py:344
  87.1 0.7 shard_map.148
  87.9 1.9 collective-permute-start.14
  89.8 1.3 collective-permute-start.12
  91.1 1.3 collective-permute-start.11
  92.4 1.3 collective-permute-start.10
  93.7 1.3 collective-permute-start.9
  95.0 3.5 %shard_map.145 = (bf16[512,512]{1,0:T(8,128)(2,1)S(1)}, bf16[512,512]{1,0:T(8,128)(2,1)S(1)}) custom-call(bf16[128,512]{1,0:T(8,128)(2,1)S(1)} %bitcast.45, bf16[256,512]{1,0:T(8,128)(2,1)S(1)} %collective-permute-done.1.one_ref, bf16[272,512]{1,0:T(8,128)(2,1)S(1)} %collective-permute-done.4.two_ref, bf16[272,512]{1,0:T(8,128)(2,1)S(1)} %collective-permute-done.5.four_ref, ...), custom_call_target="tpu_custom_call" | custom-call | tf_op jit(solution)/shard_map/pallas_call | solution.py:364
  98.6 8.3 %collective-permute-done.12.eight_ref = f32[24,128]{1,0:T(8,128)S(1)} collective-permute-done((f32[24,128]{1,0:T(8,128)S(1)}, f32[24,128]{1,0:T(8,128)S(1)}, u32[]{:S(2)}, u32[]{:S(2)}) %collective-permute-start.12) | collective-permute-done | bytes 12320 | tf_op jit(solution)/shard_map/ppermute | solution.py:26
  106.9 5.1 %shard_map.146 = (bf16[128,512]{1,0:T(8,128)(2,1)S(1)}, bf16[128,512]{1,0:T(8,128)(2,1)S(1)}, bf16[8,4,32,512]{3,2,1,0:T(8,128)(2,1)S(1)}, bf16[8,4,32,512]{3,2,1,0:T(8,128)(2,1)}) custom-call(s32[1]{0:T(128)} %bitcast.core_ref, bf16[128,512]{1,0:T(8,128)(2,1)S(1)} %get-tuple-element.48.key_ref, bf16[128,512]{1,0:T(8,128)(2,1)S(1)} %get-tuple-element.49.value_ref, ...), custom_call_target="tpu_custom_call" | custom-call | tf_op jit(solution)/shard_map/pallas_call | solution.py:371
  112.0 1.9 collective-permute-start.15
  114.0 1.5 collective-permute-start.13
  115.5 4.3 %collective-permute-done.13.leading_ref = bf16[16,1024]{1,0:T(8,128)(2,1)S(1)} collective-permute-done((bf16[16,1024]{1,0:T(8,128)(2,1)S(1)}, bf16[16,1024]{1,0:T(8,128)(2,1)S(1)}, u32[]{:S(2)}, u32[]{:S(2)}) %collective-permute-start.13) | collective-permute-done | bytes 32800 | tf_op jit(solution)/shard_map/ppermute | solution.py:26
  119.8 4.3 %shard_map.147 = (bf16[128,512]{1,0:T(8,128)(2,1)}, bf16[16,512]{1,0:T(8,128)(2,1)S(1)}) custom-call(bf16[128,512]{1,0:T(8,128)(2,1)S(1)} %get-tuple-element.47.d_query_ref, bf16[128,512]{1,0:T(8,128)(2,1)S(1)} %get-tuple-element.62.d_key_ref, bf16[128,512]{1,0:T(8,128)(2,1)S(1)} %get-tuple-element.63.d_value_ref, ...), custom_call_target="tpu_custom_call" | custom-call | tf_op jit(solution)/shard_map/pallas_call | solution.py:376
  124.1 0.4 fusion
  124.5 0.4 fusion.1
  125.1 0.2 copy.23
  125.3 0.2 pad_maximum_fusion
  125.6 37.5 %all_to_all.20 = bf16[16,144,512]{2,1,0:T(8,128)(2,1)S(1)} all-to-all(bf16[16,144,512]{2,1,0:T(8,128)(2,1)S(1)} %pad_maximum_fusion), channel_id=1, replica_groups={{0,1,64,65,128,129,192,193,256,257,320,321,384,385,448,449},{2,3,66,67,..., dimensions={0} | all-to-all | bytes 4718592 | tf_op jit(solution)/shard_map/all_to_all | solution.py:46
  163.1 0.3 convert_reduce_fusion
  163.5 34.2 %all_to_all.21 = bf16[16,8,640]{2,1,0:T(8,128)(2,1)S(1)} all-to-all(bf16[16,8,640]{2,1,0:T(8,128)(2,1)S(1)} %pad_maximum_fusion.5), channel_id=1, replica_groups={{0,2,4,6,8,10,12,14,16,18,20,22,24,26,28,30},{1,3,5,7,9,11,13,15,17,19,..., dimensions={0} | all-to-all | bytes 327680 | tf_op jit(solution)/shard_map/all_to_all | solution.py:52
  197.8 0.7 broadcast_in_dim.61
  198.5 4.6 %all-to-all-start.3 = ((bf16[16,8,512]{2,1,0:T(8,128)(2,1)}), bf16[16,8,512]{2,1,0:T(8,128)(2,1)S(1)}, u32[]{:S(2)}, u32[]{:S(2)}) async-start(bf16[16,8,512]{2,1,0:T(8,128)(2,1)} %broadcast_in_dim.61), calls=%async_computation.3 | async-start | bytes 262144 | tf_op jit(solution)/shard_map/all_to_all | solution.py:52
  203.1 1.9 collective-permute-start.16
  205.0 12.0 %all-to-all-done.3 = bf16[16,8,512]{2,1,0:T(8,128)(2,1)S(1)} async-done(((bf16[16,8,512]{2,1,0:T(8,128)(2,1)}), bf16[16,8,512]{2,1,0:T(8,128)(2,1)S(1)}, u32[]{:S(2)}, u32[]{:S(2)}) %all-to-all-start.3) | async-done | bytes 131104 | tf_op jit(solution)/shard_map/all_to_all | solution.py:52
  217.0 1.9 collective-permute-start.17
  218.9 0.6 add_bitcast_fusion
  219.5 4.3 %collective-permute-done.17 = bf16[16,8,512]{2,1,0:T(8,128)(2,1)S(1)} collective-permute-done((bf16[16,8,512]{2,1,0:T(8,128)(2,1)S(1)}, bf16[16,8,512]{2,1,0:T(8,128)(2,1)S(1)}, u32[]{:S(2)}, u32[]{:S(2)}) %collective-permute-start.17) | collective-permute-done | bytes 131104 | tf_op jit(solution)/shard_map/ppermute | solution.py:56
  223.9 0.7 slice.82
  224.6 0.7 slice_bitcast_fusion
  225.3 0.7 slice.81
  (48 shorter events, 0.8 us)
Async XLA Ops:
  1.6 12.8 %collective-permute-start.1 = (bf16[256,512]{1,0:T(8,128)(2,1)S(1)}, bf16[256,512]{1,0:T(8,128)(2,1)S(1)}, u32[]{:S(2)}, u32[]{:S(2)}) collective-permute-start(bf16[256,512]{1,0:T(8,128)(2,1)S(1)} %pad_maximum_fusion.4), channel_id=1, source_target_pairs={{1,0},{2,1},{3,2},{4,3},{5,4},{6,5},{7,6},{8,7},{9,8},{10,9},{11,1... | collective-permute-start | bytes 786440 | tf_op jit(solution)/shard_map/ppermute | solution.py:26
  2.9 11.5 %collective-permute-start = (bf16[128,512]{1,0:T(8,128)(2,1)}, bf16[128,512]{1,0:T(8,128)(2,1)S(1)}, u32[]{:S(2)}, u32[]{:S(2)}) collective-permute-start(bf16[128,512]{1,0:T(8,128)(2,1)} %bitcast.42), channel_id=1, source_target_pairs={{0,1},{1,2},{2,3},{3,4},{4,5},{5,6},{6,7},{7,8},{8,9},{9,10},{10,1... | collective-permute-start | bytes 393224 | tf_op jit(solution)/shard_map/ppermute | solution.py:26
  16.0 7.0 %copy-start = (bf16[1,128,512]{2,1,0:T(8,128)(2,1)S(1)}, bf16[1,128,512]{2,1,0:T(8,128)(2,1)}, u32[]{:S(2)}) copy-start(bf16[1,128,512]{2,1,0:T(8,128)(2,1)} %param.9) | copy-start | bytes 393220
  16.0 7.0 %copy-start.1 = (bf16[1,128,512]{2,1,0:T(8,128)(2,1)S(1)}, bf16[1,128,512]{2,1,0:T(8,128)(2,1)}, u32[]{:S(2)}) copy-start(bf16[1,128,512]{2,1,0:T(8,128)(2,1)} %param.16) | copy-start | bytes 393220
  16.0 49.0 %copy-start.3 = (s32[1,1,8,4]{2,3,1,0:T(4,128)S(1)}, s32[1,1,8,4]{2,3,1,0:T(4,128)}, u32[]{:S(2)}) copy-start(s32[1,1,8,4]{2,3,1,0:T(4,128)} %param.15) | copy-start | bytes 388
  16.0 49.1 %copy-start.4 = (s32[4]{0:T(128)S(1)}, s32[4]{0:T(128)}, u32[]{:S(2)}) copy-start(s32[4]{0:T(128)} %constant.36.clone) | copy-start | bytes 52
  16.0 62.1 %copy-start.2 = (f32[512]{0:T(512)S(1)}, f32[512]{0:T(512)}, u32[]{:S(2)}) copy-start(f32[512]{0:T(512)} %param.10) | copy-start | bytes 6148
  16.0 47.0 %all-to-all-start = ((bf16[8,8,32,512]{3,2,1,0:T(8,128)(2,1)}), bf16[8,8,32,512]{3,2,1,0:T(8,128)(2,1)}, u32[]{:S(2)}, u32[]{:S(2)}) async-start(bf16[8,8,32,512]{3,2,1,0:T(8,128)(2,1)} %broadcast_in_dim.28), calls=%async_computation | async-start | bytes 4194304 | tf_op jit(solution)/shard_map/all_to_all | solution.py:42
  23.0 39.9 %collective-permute-start.6 = (bf16[272,512]{1,0:T(8,128)(2,1)S(1)}, bf16[272,512]{1,0:T(8,128)(2,1)S(1)}, u32[]{:S(2)}, u32[]{:S(2)}) collective-permute-start(bf16[272,512]{1,0:T(8,128)(2,1)S(1)} %pad_maximum_fusion.2), channel_id=1, source_target_pairs={{8,0},{9,1},{10,2},{11,3},{12,4},{13,5},{14,6},{15,7},{16,8},{17,9... | collective-permute-start | bytes 835592 | tf_op jit(solution)/shard_map/ppermute | solution.py:26
  24.3 38.6 %collective-permute-start.5 = (bf16[272,512]{1,0:T(8,128)(2,1)S(1)}, bf16[272,512]{1,0:T(8,128)(2,1)S(1)}, u32[]{:S(2)}, u32[]{:S(2)}) collective-permute-start(bf16[272,512]{1,0:T(8,128)(2,1)S(1)} %pad_maximum_fusion.2), channel_id=1, source_target_pairs={{4,0},{5,1},{6,2},{7,3},{8,4},{9,5},{10,6},{11,7},{12,8},{13,9},{1... | collective-permute-start | bytes 835592 | tf_op jit(solution)/shard_map/ppermute | solution.py:26
  25.6 37.3 %collective-permute-start.4 = (bf16[272,512]{1,0:T(8,128)(2,1)S(1)}, bf16[272,512]{1,0:T(8,128)(2,1)S(1)}, u32[]{:S(2)}, u32[]{:S(2)}) collective-permute-start(bf16[272,512]{1,0:T(8,128)(2,1)S(1)} %pad_maximum_fusion.2), channel_id=1, source_target_pairs={{2,0},{3,1},{4,2},{5,3},{6,4},{7,5},{8,6},{9,7},{10,8},{11,9},{12,... | collective-permute-start | bytes 835592 | tf_op jit(solution)/shard_map/ppermute | solution.py:26
  27.0 11.5 %collective-permute-start.3 = (bf16[144,512]{1,0:T(8,128)(2,1)S(1)}, bf16[144,512]{1,0:T(8,128)(2,1)S(1)}, u32[]{:S(2)}, u32[]{:S(2)}) collective-permute-start(bf16[144,512]{1,0:T(8,128)(2,1)S(1)} %pad_maximum_fusion.6.window_ref), channel_id=1, source_target_pairs={{0,4},{1,5},{2,6},{3,7},{4,8},{5,9},{6,10},{7,11},{8,12},{9,13},{1... | collective-permute-start | bytes 442376 | tf_op jit(solution)/shard_map/ppermute | solution.py:26
  33.7 7.4 %collective-permute-start.2 = (bf16[144,512]{1,0:T(8,128)(2,1)S(1)}, bf16[144,512]{1,0:T(8,128)(2,1)S(1)}, u32[]{:S(2)}, u32[]{:S(2)}) collective-permute-start(bf16[144,512]{1,0:T(8,128)(2,1)S(1)} %pad_maximum_fusion.6.window_ref), channel_id=1, source_target_pairs={{0,2},{1,3},{2,4},{3,5},{4,6},{5,7},{6,8},{7,9},{8,10},{9,11},{10,... | collective-permute-start | bytes 442376 | tf_op jit(solution)/shard_map/ppermute | solution.py:26
  63.0 15.0 %collective-permute-start.7 = (bf16[8,8,32,512]{3,2,1,0:T(8,128)(2,1)}, bf16[8,8,32,512]{3,2,1,0:T(8,128)(2,1)}, u32[]{:S(2)}, u32[]{:S(2)}) collective-permute-start(bf16[8,8,32,512]{3,2,1,0:T(8,128)(2,1)} %all-to-all-done.mine_ref), channel_id=1, source_target_pairs={{0,32},{32,0},{64,96},{96,64},{128,160},{160,128},{192,224},{224,1... | collective-permute-start | bytes 6291464 | tf_op jit(solution)/shard_map/ppermute | solution.py:34
  65.2 12.8 %collective-permute-start.8 = (bf16[144,512]{1,0:T(8,128)(2,1)S(1)}, bf16[144,512]{1,0:T(8,128)(2,1)S(1)}, u32[]{:S(2)}, u32[]{:S(2)}) collective-permute-start(bf16[144,512]{1,0:T(8,128)(2,1)S(1)} %collective-permute-done.3.four_ref), channel_id=1, source_target_pairs={{0,4},{1,5},{2,6},{3,7},{4,8},{5,9},{6,10},{7,11},{8,12},{9,13},{1... | collective-permute-start | bytes 442376 | tf_op jit(solution)/shard_map/ppermute | solution.py:26
  87.9 36.2 %collective-permute-start.14 = (bf16[8,4,32,512]{3,2,1,0:T(8,128)(2,1)S(1)}, bf16[8,4,32,512]{3,2,1,0:T(8,128)(2,1)S(1)}, u32[]{:S(2)}, u32[]{:S(2)}) collective-permute-start(bf16[8,4,32,512]{3,2,1,0:T(8,128)(2,1)S(1)} %get-tuple-element.67), channel_id=1, source_target_pairs={{0,32},{32,0},{64,96},{96,64},{128,160},{160,128},{192,224},{224,1... | collective-permute-start | bytes 3145736 | tf_op jit(solution)/shard_map/ppermute | solution.py:34
  89.8 17.1 %collective-permute-start.12 = (f32[24,128]{1,0:T(8,128)S(1)}, f32[24,128]{1,0:T(8,128)S(1)}, u32[]{:S(2)}, u32[]{:S(2)}) collective-permute-start(f32[24,128]{1,0:T(8,128)S(1)} %get-tuple-element.75), channel_id=1, source_target_pairs={{8,0},{9,1},{10,2},{11,3},{12,4},{13,5},{14,6},{15,7},{16,8},{17,9... | collective-permute-start | bytes 36872 | tf_op jit(solution)/shard_map/ppermute | solution.py:26
  91.1 15.8 %collective-permute-start.11 = (f32[24,128]{1,0:T(8,128)S(1)}, f32[24,128]{1,0:T(8,128)S(1)}, u32[]{:S(2)}, u32[]{:S(2)}) collective-permute-start(f32[24,128]{1,0:T(8,128)S(1)} %get-tuple-element.76), channel_id=1, source_target_pairs={{4,0},{5,1},{6,2},{7,3},{8,4},{9,5},{10,6},{11,7},{12,8},{13,9},{1... | collective-permute-start | bytes 36872 | tf_op jit(solution)/shard_map/ppermute | solution.py:26
  92.4 14.5 %collective-permute-start.10 = (f32[24,128]{1,0:T(8,128)S(1)}, f32[24,128]{1,0:T(8,128)S(1)}, u32[]{:S(2)}, u32[]{:S(2)}) collective-permute-start(f32[24,128]{1,0:T(8,128)S(1)} %get-tuple-element.77), channel_id=1, source_target_pairs={{2,0},{3,1},{4,2},{5,3},{6,4},{7,5},{8,6},{9,7},{10,8},{11,9},{12,... | collective-permute-start | bytes 36872 | tf_op jit(solution)/shard_map/ppermute | solution.py:26
  93.7 13.2 %collective-permute-start.9 = (f32[24,128]{1,0:T(8,128)S(1)}, f32[24,128]{1,0:T(8,128)S(1)}, u32[]{:S(2)}, u32[]{:S(2)}) collective-permute-start(f32[24,128]{1,0:T(8,128)S(1)} %get-tuple-element.78), channel_id=1, source_target_pairs={{1,0},{2,1},{3,2},{4,3},{5,4},{6,5},{7,6},{8,7},{9,8},{10,9},{11,1... | collective-permute-start | bytes 36872 | tf_op jit(solution)/shard_map/ppermute | solution.py:26
  112.0 12.4 %collective-permute-start.15 = (bf16[8,4,32,512]{3,2,1,0:T(8,128)(2,1)}, bf16[8,4,32,512]{3,2,1,0:T(8,128)(2,1)S(1)}, u32[]{:S(2)}, u32[]{:S(2)}) collective-permute-start(bf16[8,4,32,512]{3,2,1,0:T(8,128)(2,1)} %get-tuple-element.69), channel_id=1, source_target_pairs={{0,32},{32,0},{64,96},{96,64},{128,160},{160,128},{192,224},{224,1... | collective-permute-start | bytes 3145736 | tf_op jit(solution)/shard_map/ppermute | solution.py:34
  114.0 5.8 %collective-permute-start.13 = (bf16[16,1024]{1,0:T(8,128)(2,1)S(1)}, bf16[16,1024]{1,0:T(8,128)(2,1)S(1)}, u32[]{:S(2)}, u32[]{:S(2)}) collective-permute-start(bf16[16,1024]{1,0:T(8,128)(2,1)S(1)} %pad_maximum_fusion.7), channel_id=1, source_target_pairs={{1,0},{2,1},{3,2},{4,3},{5,4},{6,5},{7,6},{8,7},{9,8},{10,9},{11,1... | collective-permute-start | bytes 98312 | tf_op jit(solution)/shard_map/ppermute | solution.py:26
  198.5 18.6 %all-to-all-start.3 = ((bf16[16,8,512]{2,1,0:T(8,128)(2,1)}), bf16[16,8,512]{2,1,0:T(8,128)(2,1)S(1)}, u32[]{:S(2)}, u32[]{:S(2)}) async-start(bf16[16,8,512]{2,1,0:T(8,128)(2,1)} %broadcast_in_dim.61), calls=%async_computation.3 | async-start | bytes 262144 | tf_op jit(solution)/shard_map/all_to_all | solution.py:52
  203.1 15.9 %collective-permute-start.16 = (f32[4,128]{1,0:T(4,128)S(1)}, f32[4,128]{1,0:T(4,128)S(1)}, u32[]{:S(2)}, u32[]{:S(2)}) collective-permute-start(f32[4,128]{1,0:T(4,128)S(1)} %slice_add_fusion), channel_id=1, source_target_pairs={{0,32},{32,0},{64,96},{96,64},{128,160},{160,128},{192,224},{224,1... | collective-permute-start | bytes 6152 | tf_op jit(solution)/shard_map/ppermute | solution.py:34
  217.0 6.8 %collective-permute-start.17 = (bf16[16,8,512]{2,1,0:T(8,128)(2,1)S(1)}, bf16[16,8,512]{2,1,0:T(8,128)(2,1)S(1)}, u32[]{:S(2)}, u32[]{:S(2)}) collective-permute-start(bf16[16,8,512]{2,1,0:T(8,128)(2,1)S(1)} %all-to-all-done.3), channel_id=1, source_target_pairs={{0,1},{1,0},{2,3},{3,2},{4,5},{5,4},{6,7},{7,6},{8,9},{9,8},{10,11... | collective-permute-start | bytes 393224 | tf_op jit(solution)/shard_map/ppermute | solution.py:56

commit v8 on v7

--- a/solution.py
+++ b/solution.py
@@ -323,13 +323,15 @@
     shard, before_one, after_one = lax.optimization_barrier((shard, before_one, after_one))
     window = jnp.concatenate([before_one[count - edge :], own], axis=0)
     carried = jnp.concatenate([window, cotangent], axis=0)
-    after_eight, after_four, after_two = [shift_ctx(carried, -by) for by in (8, 4, 2)]
+    after_four, after_two = shift_ctx(carried, -4), shift_ctx(carried, -2)
     before_four, before_two = shift_ctx(window, 4), shift_ctx(window, 2)
     mine = over_chips(jnp.broadcast_to(shard[None], (8,) + shard.shape))
-    mine, before_two, before_four, after_two, after_four, after_eight = lax.optimization_barrier(
-        (mine, before_two, before_four, after_two, after_four, after_eight)
-    )
-    other, before_eight = lax.optimization_barrier((other_core(mine), shift_ctx(before_four, 4)))
+    mine, before_two, before_four, after_two, after_four = lax.optimization_barrier(
+        (mine, before_two, before_four, after_two, after_four)
+    )
+    other, before_eight, after_eight = lax.optimization_barrier(
+        (other_core(mine), shift_ctx(before_four, 4), shift_ctx(after_four, -4))
+    )
     before = (before_two, before_four, before_eight)
     after = (after_one, after_two, after_four, after_eight)
 

time: 227 us -> 211 us (0.930)
  waiting for transfers between devices: 63.2 us -> 52.3 us
  starting transfers between devices: 58.1 us -> 54.7 us
    ppermute x13, waiting for transfers between devices: 46.8 us -> 26.8 us  [shift_ctx(): return lax.ppermute(shard, 'ctx', pairs)]
    all_to_all x1, waiting for transfers between devices: 0.01 us -> 9.07 us  [over_chips(): lax.all_to_all(stacked, 'dp', 0, 0, axis_index_groups=chip_groups, tiled=...]
    ppermute x13, starting transfers between devices: 36.9 us -> 33.6 us  [shift_ctx(): return lax.ppermute(shard, 'ctx', pairs)]
    all_to_all x1, blocking collectives: 37.5 us -> 35.2 us  [over_plane(): lax.all_to_all(stacked, ('dp', 'ctx'), 0, 0, axis_index_groups=plane_grou...]
  transfers between devices with their start and end apart: 20 -> 20, of which waited for: 8 -> 12; matrix products, arithmetic and copies ran while one was open for 1% -> 1% of each run, Pallas kernels for 6% -> 6%
where the time goes in v8:
time: 211 us; the launch traced here: 210 us
  blocking collectives  70.3 us (33%)
  starting transfers between devices  54.7 us (26%)
  waiting for transfers between devices  52.3 us (25%)
  Pallas kernels  22.8 us (11%)
  local copies, waits for them, and re-layouts  4.86 us (2%)
  other arithmetic  4.3 us (2%)
    all_to_all x1, blocking collectives, over_plane(): lax.all_to_all(stacked, ('dp', 'ctx'), 0, 0, axis_index_groups=plane_grou...  35.2 us
    all_to_all x1, blocking collectives, over_z(): lax.all_to_all(stacked, 'ctx', 0, 0, axis_index_groups=z_groups, tiled=True)  35.1 us
    ppermute x13, starting transfers between devices, shift_ctx(): return lax.ppermute(shard, 'ctx', pairs)  33.6 us
    ppermute x13, waiting for transfers between devices, shift_ctx(): return lax.ppermute(shard, 'ctx', pairs)  26.8 us
    all_to_all x1, waiting for transfers between devices, over_z(): lax.all_to_all(stacked, 'ctx', 0, 0, axis_index_groups=z_groups, tiled=True)  12 us
    pallas_call x1, Pallas kernels, body(): call(rows_kernel, [((8, features, features), bf16)] + [half] * 7 + [((3,...  9.1 us
    all_to_all x1, waiting for transfers between devices, over_chips(): lax.all_to_all(stacked, 'dp', 0, 0, axis_index_groups=chip_groups, tiled=...  9.07 us
    ppermute x4, starting transfers between devices, dp_to(): return lax.ppermute(shard, 'dp', [(i, target(i)) for i in range(16)])  7.66 us
  transfers between devices with their start and end apart: 20, of which 12 were waited for; matrix products, arithmetic and copies ran while one was open for 1% of the time, Pallas kernels for 6%

profile of v8, /device:TPU:24, one launch (start us, length us, event | category | flops | bytes accessed | tf_op | source)
XLA Modules:
  0.0 210.3 jit_solution(17135792702989266092)
XLA Ops:
  0.6 1.0 pad_maximum_fusion.4
  1.6 1.3 collective-permute-start.1
  2.9 4.6 %collective-permute-start = (bf16[128,512]{1,0:T(8,128)(2,1)}, bf16[128,512]{1,0:T(8,128)(2,1)S(1)}, u32[]{:S(2)}, u32[]{:S(2)}) collective-permute-start(bf16[128,512]{1,0:T(8,128)(2,1)} %bitcast.42), channel_id=1, source_target_pairs={{0,1},{1,2},{2,3},{3,4},{4,5},{5,6},{6,7},{7,8},{8,9},{9,10},{10,1... | collective-permute-start | bytes 393224 | tf_op jit(solution)/shard_map/ppermute | solution.py:26
  7.5 1.0 pad_maximum_fusion.3
  8.5 5.9 %collective-permute-done.one_ref = bf16[128,512]{1,0:T(8,128)(2,1)S(1)} collective-permute-done((bf16[128,512]{1,0:T(8,128)(2,1)}, bf16[128,512]{1,0:T(8,128)(2,1)S(1)}, u32[]{:S(2)}, u32[]{:S(2)}) %collective-permute-start) | collective-permute-done | bytes 131104 | tf_op jit(solution)/shard_map/ppermute | solution.py:26
  14.4 1.6 broadcast_in_dim.28
  16.0 7.0 %all-to-all-start = ((bf16[8,8,32,512]{3,2,1,0:T(8,128)(2,1)}), bf16[8,8,32,512]{3,2,1,0:T(8,128)(2,1)}, u32[]{:S(2)}, u32[]{:S(2)}) async-start(bf16[8,8,32,512]{3,2,1,0:T(8,128)(2,1)} %broadcast_in_dim.28), calls=%async_computation | async-start | bytes 4194304 | tf_op jit(solution)/shard_map/all_to_all | solution.py:42
  23.0 1.3 collective-permute-start.5
  24.3 1.3 collective-permute-start.4
  25.7 6.7 %collective-permute-start.3 = (bf16[144,512]{1,0:T(8,128)(2,1)S(1)}, bf16[144,512]{1,0:T(8,128)(2,1)S(1)}, u32[]{:S(2)}, u32[]{:S(2)}) collective-permute-start(bf16[144,512]{1,0:T(8,128)(2,1)S(1)} %pad_maximum_fusion.6.window_ref), channel_id=1, source_target_pairs={{0,4},{1,5},{2,6},{3,7},{4,8},{5,9},{6,10},{7,11},{8,12},{9,13},{1... | collective-permute-start | bytes 442376 | tf_op jit(solution)/shard_map/ppermute | solution.py:26
  32.4 4.8 %collective-permute-start.2 = (bf16[144,512]{1,0:T(8,128)(2,1)S(1)}, bf16[144,512]{1,0:T(8,128)(2,1)S(1)}, u32[]{:S(2)}, u32[]{:S(2)}) collective-permute-start(bf16[144,512]{1,0:T(8,128)(2,1)S(1)} %pad_maximum_fusion.6.window_ref), channel_id=1, source_target_pairs={{0,2},{1,3},{2,4},{3,5},{4,6},{5,7},{6,8},{7,9},{8,10},{9,11},{10,... | collective-permute-start | bytes 442376 | tf_op jit(solution)/shard_map/ppermute | solution.py:26
  37.2 2.6 %collective-permute-done.2.two_ref = bf16[144,512]{1,0:T(8,128)(2,1)S(1)} collective-permute-done((bf16[144,512]{1,0:T(8,128)(2,1)S(1)}, bf16[144,512]{1,0:T(8,128)(2,1)S(1)}, u32[]{:S(2)}, u32[]{:S(2)}) %collective-permute-start.2) | collective-permute-done | bytes 147488 | tf_op jit(solution)/shard_map/ppermute | solution.py:26
  39.8 0.5 collective-permute-done.5.four_ref
  40.4 9.1 %all-to-all-done.mine_ref = bf16[8,8,32,512]{3,2,1,0:T(8,128)(2,1)} async-done(((bf16[8,8,32,512]{3,2,1,0:T(8,128)(2,1)}), bf16[8,8,32,512]{3,2,1,0:T(8,128)(2,1)}, u32[]{:S(2)}, u32[]{:S(2)}) %all-to-all-start) | async-done | bytes 2097184 | tf_op jit(solution)/shard_map/all_to_all | solution.py:42
  49.5 1.9 collective-permute-start.6
  51.5 1.3 collective-permute-start.8
  52.9 5.8 %collective-permute-start.7 = (bf16[144,512]{1,0:T(8,128)(2,1)S(1)}, bf16[144,512]{1,0:T(8,128)(2,1)S(1)}, u32[]{:S(2)}, u32[]{:S(2)}) collective-permute-start(bf16[144,512]{1,0:T(8,128)(2,1)S(1)} %collective-permute-done.3.four_ref), channel_id=1, source_target_pairs={{0,4},{1,5},{2,6},{3,7},{4,8},{5,9},{6,10},{7,11},{8,12},{9,13},{1... | collective-permute-start | bytes 442376 | tf_op jit(solution)/shard_map/ppermute | solution.py:26
  58.7 3.7 %collective-permute-done.7.eight_ref = bf16[144,512]{1,0:T(8,128)(2,1)S(1)} collective-permute-done((bf16[144,512]{1,0:T(8,128)(2,1)S(1)}, bf16[144,512]{1,0:T(8,128)(2,1)S(1)}, u32[]{:S(2)}, u32[]{:S(2)}) %collective-permute-start.7) | collective-permute-done | bytes 147488 | tf_op jit(solution)/shard_map/ppermute | solution.py:26
  62.5 3.8 %collective-permute-done.8.eight_ref = bf16[272,512]{1,0:T(8,128)(2,1)S(1)} collective-permute-done((bf16[272,512]{1,0:T(8,128)(2,1)S(1)}, bf16[272,512]{1,0:T(8,128)(2,1)S(1)}, u32[]{:S(2)}, u32[]{:S(2)}) %collective-permute-start.8) | collective-permute-done | bytes 278560 | tf_op jit(solution)/shard_map/ppermute | solution.py:26
  66.3 9.1 %shard_map.144 = (bf16[8,512,512]{2,1,0:T(8,128)(2,1)}, bf16[128,512]{1,0:T(8,128)(2,1)}, bf16[128,512]{1,0:T(8,128)(2,1)S(1)}, bf16[128,512]{1,0:T(8,128)(2,1)S...) custom-call(s32[1]{0:T(128)} %bitcast.core_ref, ...), custom_call_target="tpu_custom_call" | custom-call | tf_op jit(solution)/shard_map/pallas_call | solution.py:346
  75.4 0.7 shard_map.148
  76.1 1.9 collective-permute-start.14
  78.1 1.3 collective-permute-start.12
  79.4 1.3 collective-permute-start.11
  80.7 1.3 collective-permute-start.10
  82.0 1.3 collective-permute-start.9
  83.3 3.6 %shard_map.145 = (bf16[512,512]{1,0:T(8,128)(2,1)S(1)}, bf16[512,512]{1,0:T(8,128)(2,1)S(1)}) custom-call(bf16[128,512]{1,0:T(8,128)(2,1)S(1)} %bitcast.45, bf16[256,512]{1,0:T(8,128)(2,1)S(1)} %collective-permute-done.1.one_ref, bf16[272,512]{1,0:T(8,128)(2,1)S(1)} %collective-permute-done.4.two_ref, bf16[272,512]{1,0:T(8,128)(2,1)S(1)} %collective-permute-done.5.four_ref, ...), custom_call_target="tpu_custom_call" | custom-call | tf_op jit(solution)/shard_map/pallas_call | solution.py:366
  86.8 3.0 %collective-permute-done.12.eight_ref = f32[24,128]{1,0:T(8,128)S(1)} collective-permute-done((f32[24,128]{1,0:T(8,128)S(1)}, f32[24,128]{1,0:T(8,128)S(1)}, u32[]{:S(2)}, u32[]{:S(2)}) %collective-permute-start.12) | collective-permute-done | bytes 12320 | tf_op jit(solution)/shard_map/ppermute | solution.py:26
  89.8 1.4 collective-permute-done.10.two_ref
  91.2 5.1 %shard_map.146 = (bf16[128,512]{1,0:T(8,128)(2,1)S(1)}, bf16[128,512]{1,0:T(8,128)(2,1)S(1)}, bf16[8,4,32,512]{3,2,1,0:T(8,128)(2,1)S(1)}, bf16[8,4,32,512]{3,2,1,0:T(8,128)(2,1)}) custom-call(s32[1]{0:T(128)} %bitcast.core_ref, bf16[128,512]{1,0:T(8,128)(2,1)S(1)} %get-tuple-element.49.key_ref, bf16[128,512]{1,0:T(8,128)(2,1)S(1)} %get-tuple-element.50.value_ref, ...), custom_call_target="tpu_custom_call" | custom-call | tf_op jit(solution)/shard_map/pallas_call | solution.py:373
  96.3 1.9 collective-permute-start.15
  98.3 1.5 collective-permute-start.13
  99.7 5.9 %collective-permute-done.13.leading_ref = bf16[16,1024]{1,0:T(8,128)(2,1)S(1)} collective-permute-done((bf16[16,1024]{1,0:T(8,128)(2,1)S(1)}, bf16[16,1024]{1,0:T(8,128)(2,1)S(1)}, u32[]{:S(2)}, u32[]{:S(2)}) %collective-permute-start.13) | collective-permute-done | bytes 32800 | tf_op jit(solution)/shard_map/ppermute | solution.py:26
  105.6 4.3 %shard_map.147 = (bf16[128,512]{1,0:T(8,128)(2,1)}, bf16[16,512]{1,0:T(8,128)(2,1)S(1)}) custom-call(bf16[128,512]{1,0:T(8,128)(2,1)S(1)} %get-tuple-element.48.d_query_ref, bf16[128,512]{1,0:T(8,128)(2,1)S(1)} %get-tuple-element.62.d_key_ref, bf16[128,512]{1,0:T(8,128)(2,1)S(1)} %get-tuple-element.63.d_value_ref, ...), custom_call_target="tpu_custom_call" | custom-call | tf_op jit(solution)/shard_map/pallas_call | solution.py:378
  109.9 0.4 fusion
  110.3 0.4 fusion.1
  111.4 35.2 %all_to_all.20 = bf16[16,144,512]{2,1,0:T(8,128)(2,1)S(1)} all-to-all(bf16[16,144,512]{2,1,0:T(8,128)(2,1)S(1)} %pad_maximum_fusion), channel_id=1, replica_groups={{0,1,64,65,128,129,192,193,256,257,320,321,384,385,448,449},{2,3,66,67,..., dimensions={0} | all-to-all | bytes 4718592 | tf_op jit(solution)/shard_map/all_to_all | solution.py:46
  147.0 35.1 %all_to_all.21 = bf16[16,8,640]{2,1,0:T(8,128)(2,1)S(1)} all-to-all(bf16[16,8,640]{2,1,0:T(8,128)(2,1)S(1)} %pad_maximum_fusion.5), channel_id=1, replica_groups={{0,2,4,6,8,10,12,14,16,18,20,22,24,26,28,30},{1,3,5,7,9,11,13,15,17,19,..., dimensions={0} | all-to-all | bytes 327680 | tf_op jit(solution)/shard_map/all_to_all | solution.py:52
  182.2 0.7 broadcast_in_dim.61
  182.8 4.6 %all-to-all-start.3 = ((bf16[16,8,512]{2,1,0:T(8,128)(2,1)}), bf16[16,8,512]{2,1,0:T(8,128)(2,1)S(1)}, u32[]{:S(2)}, u32[]{:S(2)}) async-start(bf16[16,8,512]{2,1,0:T(8,128)(2,1)} %broadcast_in_dim.61), calls=%async_computation.3 | async-start | bytes 262144 | tf_op jit(solution)/shard_map/all_to_all | solution.py:52
  187.4 1.9 collective-permute-start.16
  189.4 12.0 %all-to-all-done.3 = bf16[16,8,512]{2,1,0:T(8,128)(2,1)S(1)} async-done(((bf16[16,8,512]{2,1,0:T(8,128)(2,1)}), bf16[16,8,512]{2,1,0:T(8,128)(2,1)S(1)}, u32[]{:S(2)}, u32[]{:S(2)}) %all-to-all-start.3) | async-done | bytes 131104 | tf_op jit(solution)/shard_map/all_to_all | solution.py:52
  201.4 1.9 collective-permute-start.17
  203.3 0.6 add_bitcast_fusion
  203.9 4.3 %collective-permute-done.17 = bf16[16,8,512]{2,1,0:T(8,128)(2,1)S(1)} collective-permute-done((bf16[16,8,512]{2,1,0:T(8,128)(2,1)S(1)}, bf16[16,8,512]{2,1,0:T(8,128)(2,1)S(1)}, u32[]{:S(2)}, u32[]{:S(2)}) %collective-permute-start.17) | collective-permute-done | bytes 131104 | tf_op jit(solution)/shard_map/ppermute | solution.py:56
  208.3 0.7 slice.82
  209.0 0.7 slice_bitcast_fusion
  209.6 0.7 slice.81
  (48 shorter events, 1.6 us)
Async XLA Ops:
  1.6 12.8 %collective-permute-start.1 = (bf16[256,512]{1,0:T(8,128)(2,1)S(1)}, bf16[256,512]{1,0:T(8,128)(2,1)S(1)}, u32[]{:S(2)}, u32[]{:S(2)}) collective-permute-start(bf16[256,512]{1,0:T(8,128)(2,1)S(1)} %pad_maximum_fusion.4), channel_id=1, source_target_pairs={{1,0},{2,1},{3,2},{4,3},{5,4},{6,5},{7,6},{8,7},{9,8},{10,9},{11,1... | collective-permute-start | bytes 786440 | tf_op jit(solution)/shard_map/ppermute | solution.py:26
  2.9 11.5 %collective-permute-start = (bf16[128,512]{1,0:T(8,128)(2,1)}, bf16[128,512]{1,0:T(8,128)(2,1)S(1)}, u32[]{:S(2)}, u32[]{:S(2)}) collective-permute-start(bf16[128,512]{1,0:T(8,128)(2,1)} %bitcast.42), channel_id=1, source_target_pairs={{0,1},{1,2},{2,3},{3,4},{4,5},{5,6},{6,7},{7,8},{8,9},{9,10},{10,1... | collective-permute-start | bytes 393224 | tf_op jit(solution)/shard_map/ppermute | solution.py:26
  16.0 7.0 %copy-start = (bf16[1,128,512]{2,1,0:T(8,128)(2,1)S(1)}, bf16[1,128,512]{2,1,0:T(8,128)(2,1)}, u32[]{:S(2)}) copy-start(bf16[1,128,512]{2,1,0:T(8,128)(2,1)} %param.9) | copy-start | bytes 393220
  16.0 7.0 %copy-start.1 = (bf16[1,128,512]{2,1,0:T(8,128)(2,1)S(1)}, bf16[1,128,512]{2,1,0:T(8,128)(2,1)}, u32[]{:S(2)}) copy-start(bf16[1,128,512]{2,1,0:T(8,128)(2,1)} %param.16) | copy-start | bytes 393220
  16.0 35.4 %copy-start.3 = (s32[1,1,8,4]{2,3,1,0:T(4,128)S(1)}, s32[1,1,8,4]{2,3,1,0:T(4,128)}, u32[]{:S(2)}) copy-start(s32[1,1,8,4]{2,3,1,0:T(4,128)} %param.15) | copy-start | bytes 388
  16.0 35.5 %copy-start.4 = (s32[4]{0:T(128)S(1)}, s32[4]{0:T(128)}, u32[]{:S(2)}) copy-start(s32[4]{0:T(128)} %constant.36.clone) | copy-start | bytes 52
  16.0 50.3 %copy-start.2 = (f32[512]{0:T(512)S(1)}, f32[512]{0:T(512)}, u32[]{:S(2)}) copy-start(f32[512]{0:T(512)} %param.10) | copy-start | bytes 6148
  16.0 33.5 %all-to-all-start = ((bf16[8,8,32,512]{3,2,1,0:T(8,128)(2,1)}), bf16[8,8,32,512]{3,2,1,0:T(8,128)(2,1)}, u32[]{:S(2)}, u32[]{:S(2)}) async-start(bf16[8,8,32,512]{3,2,1,0:T(8,128)(2,1)} %broadcast_in_dim.28), calls=%async_computation | async-start | bytes 4194304 | tf_op jit(solution)/shard_map/all_to_all | solution.py:42
  23.0 17.3 %collective-permute-start.5 = (bf16[272,512]{1,0:T(8,128)(2,1)S(1)}, bf16[272,512]{1,0:T(8,128)(2,1)S(1)}, u32[]{:S(2)}, u32[]{:S(2)}) collective-permute-start(bf16[272,512]{1,0:T(8,128)(2,1)S(1)} %pad_maximum_fusion.2), channel_id=1, source_target_pairs={{4,0},{5,1},{6,2},{7,3},{8,4},{9,5},{10,6},{11,7},{12,8},{13,9},{1... | collective-permute-start | bytes 835592 | tf_op jit(solution)/shard_map/ppermute | solution.py:26
  24.3 16.1 %collective-permute-start.4 = (bf16[272,512]{1,0:T(8,128)(2,1)S(1)}, bf16[272,512]{1,0:T(8,128)(2,1)S(1)}, u32[]{:S(2)}, u32[]{:S(2)}) collective-permute-start(bf16[272,512]{1,0:T(8,128)(2,1)S(1)} %pad_maximum_fusion.2), channel_id=1, source_target_pairs={{2,0},{3,1},{4,2},{5,3},{6,4},{7,5},{8,6},{9,7},{10,8},{11,9},{12,... | collective-permute-start | bytes 835592 | tf_op jit(solution)/shard_map/ppermute | solution.py:26
  25.7 11.5 %collective-permute-start.3 = (bf16[144,512]{1,0:T(8,128)(2,1)S(1)}, bf16[144,512]{1,0:T(8,128)(2,1)S(1)}, u32[]{:S(2)}, u32[]{:S(2)}) collective-permute-start(bf16[144,512]{1,0:T(8,128)(2,1)S(1)} %pad_maximum_fusion.6.window_ref), channel_id=1, source_target_pairs={{0,4},{1,5},{2,6},{3,7},{4,8},{5,9},{6,10},{7,11},{8,12},{9,13},{1... | collective-permute-start | bytes 442376 | tf_op jit(solution)/shard_map/ppermute | solution.py:26
  32.4 7.4 %collective-permute-start.2 = (bf16[144,512]{1,0:T(8,128)(2,1)S(1)}, bf16[144,512]{1,0:T(8,128)(2,1)S(1)}, u32[]{:S(2)}, u32[]{:S(2)}) collective-permute-start(bf16[144,512]{1,0:T(8,128)(2,1)S(1)} %pad_maximum_fusion.6.window_ref), channel_id=1, source_target_pairs={{0,2},{1,3},{2,4},{3,5},{4,6},{5,7},{6,8},{7,9},{8,10},{9,11},{10,... | collective-permute-start | bytes 442376 | tf_op jit(solution)/shard_map/ppermute | solution.py:26
  49.5 16.7 %collective-permute-start.6 = (bf16[8,8,32,512]{3,2,1,0:T(8,128)(2,1)}, bf16[8,8,32,512]{3,2,1,0:T(8,128)(2,1)}, u32[]{:S(2)}, u32[]{:S(2)}) collective-permute-start(bf16[8,8,32,512]{3,2,1,0:T(8,128)(2,1)} %all-to-all-done.mine_ref), channel_id=1, source_target_pairs={{0,32},{32,0},{64,96},{96,64},{128,160},{160,128},{192,224},{224,1... | collective-permute-start | bytes 6291464 | tf_op jit(solution)/shard_map/ppermute | solution.py:34
  51.5 14.7 %collective-permute-start.8 = (bf16[272,512]{1,0:T(8,128)(2,1)S(1)}, bf16[272,512]{1,0:T(8,128)(2,1)S(1)}, u32[]{:S(2)}, u32[]{:S(2)}) collective-permute-start(bf16[272,512]{1,0:T(8,128)(2,1)S(1)} %collective-permute-done.5.four_ref), channel_id=1, source_target_pairs={{4,0},{5,1},{6,2},{7,3},{8,4},{9,5},{10,6},{11,7},{12,8},{13,9},{1... | collective-permute-start | bytes 835592 | tf_op jit(solution)/shard_map/ppermute | solution.py:26
  52.9 9.5 %collective-permute-start.7 = (bf16[144,512]{1,0:T(8,128)(2,1)S(1)}, bf16[144,512]{1,0:T(8,128)(2,1)S(1)}, u32[]{:S(2)}, u32[]{:S(2)}) collective-permute-start(bf16[144,512]{1,0:T(8,128)(2,1)S(1)} %collective-permute-done.3.four_ref), channel_id=1, source_target_pairs={{0,4},{1,5},{2,6},{3,7},{4,8},{5,9},{6,10},{7,11},{8,12},{9,13},{1... | collective-permute-start | bytes 442376 | tf_op jit(solution)/shard_map/ppermute | solution.py:26
  76.1 33.8 %collective-permute-start.14 = (bf16[8,4,32,512]{3,2,1,0:T(8,128)(2,1)S(1)}, bf16[8,4,32,512]{3,2,1,0:T(8,128)(2,1)S(1)}, u32[]{:S(2)}, u32[]{:S(2)}) collective-permute-start(bf16[8,4,32,512]{3,2,1,0:T(8,128)(2,1)S(1)} %get-tuple-element.67), channel_id=1, source_target_pairs={{0,32},{32,0},{64,96},{96,64},{128,160},{160,128},{192,224},{224,1... | collective-permute-start | bytes 3145736 | tf_op jit(solution)/shard_map/ppermute | solution.py:34
  78.1 11.7 %collective-permute-start.12 = (f32[24,128]{1,0:T(8,128)S(1)}, f32[24,128]{1,0:T(8,128)S(1)}, u32[]{:S(2)}, u32[]{:S(2)}) collective-permute-start(f32[24,128]{1,0:T(8,128)S(1)} %get-tuple-element.75), channel_id=1, source_target_pairs={{8,0},{9,1},{10,2},{11,3},{12,4},{13,5},{14,6},{15,7},{16,8},{17,9... | collective-permute-start | bytes 36872 | tf_op jit(solution)/shard_map/ppermute | solution.py:26
  79.4 10.5 %collective-permute-start.11 = (f32[24,128]{1,0:T(8,128)S(1)}, f32[24,128]{1,0:T(8,128)S(1)}, u32[]{:S(2)}, u32[]{:S(2)}) collective-permute-start(f32[24,128]{1,0:T(8,128)S(1)} %get-tuple-element.76), channel_id=1, source_target_pairs={{4,0},{5,1},{6,2},{7,3},{8,4},{9,5},{10,6},{11,7},{12,8},{13,9},{1... | collective-permute-start | bytes 36872 | tf_op jit(solution)/shard_map/ppermute | solution.py:26
  80.7 10.5 %collective-permute-start.10 = (f32[24,128]{1,0:T(8,128)S(1)}, f32[24,128]{1,0:T(8,128)S(1)}, u32[]{:S(2)}, u32[]{:S(2)}) collective-permute-start(f32[24,128]{1,0:T(8,128)S(1)} %get-tuple-element.77), channel_id=1, source_target_pairs={{2,0},{3,1},{4,2},{5,3},{6,4},{7,5},{8,6},{9,7},{10,8},{11,9},{12,... | collective-permute-start | bytes 36872 | tf_op jit(solution)/shard_map/ppermute | solution.py:26
  82.0 9.2 %collective-permute-start.9 = (f32[24,128]{1,0:T(8,128)S(1)}, f32[24,128]{1,0:T(8,128)S(1)}, u32[]{:S(2)}, u32[]{:S(2)}) collective-permute-start(f32[24,128]{1,0:T(8,128)S(1)} %get-tuple-element.78), channel_id=1, source_target_pairs={{1,0},{2,1},{3,2},{4,3},{5,4},{6,5},{7,6},{8,7},{9,8},{10,9},{11,1... | collective-permute-start | bytes 36872 | tf_op jit(solution)/shard_map/ppermute | solution.py:26
  96.3 14.0 %collective-permute-start.15 = (bf16[8,4,32,512]{3,2,1,0:T(8,128)(2,1)}, bf16[8,4,32,512]{3,2,1,0:T(8,128)(2,1)S(1)}, u32[]{:S(2)}, u32[]{:S(2)}) collective-permute-start(bf16[8,4,32,512]{3,2,1,0:T(8,128)(2,1)} %get-tuple-element.69), channel_id=1, source_target_pairs={{0,32},{32,0},{64,96},{96,64},{128,160},{160,128},{192,224},{224,1... | collective-permute-start | bytes 3145736 | tf_op jit(solution)/shard_map/ppermute | solution.py:34
  98.3 7.3 %collective-permute-start.13 = (bf16[16,1024]{1,0:T(8,128)(2,1)S(1)}, bf16[16,1024]{1,0:T(8,128)(2,1)S(1)}, u32[]{:S(2)}, u32[]{:S(2)}) collective-permute-start(bf16[16,1024]{1,0:T(8,128)(2,1)S(1)} %pad_maximum_fusion.7), channel_id=1, source_target_pairs={{1,0},{2,1},{3,2},{4,3},{5,4},{6,5},{7,6},{8,7},{9,8},{10,9},{11,1... | collective-permute-start | bytes 98312 | tf_op jit(solution)/shard_map/ppermute | solution.py:26
  182.8 18.6 %all-to-all-start.3 = ((bf16[16,8,512]{2,1,0:T(8,128)(2,1)}), bf16[16,8,512]{2,1,0:T(8,128)(2,1)S(1)}, u32[]{:S(2)}, u32[]{:S(2)}) async-start(bf16[16,8,512]{2,1,0:T(8,128)(2,1)} %broadcast_in_dim.61), calls=%async_computation.3 | async-start | bytes 262144 | tf_op jit(solution)/shard_map/all_to_all | solution.py:52
  187.4 15.9 %collective-permute-start.16 = (f32[4,128]{1,0:T(4,128)S(1)}, f32[4,128]{1,0:T(4,128)S(1)}, u32[]{:S(2)}, u32[]{:S(2)}) collective-permute-start(f32[4,128]{1,0:T(4,128)S(1)} %slice_add_fusion), channel_id=1, source_target_pairs={{0,32},{32,0},{64,96},{96,64},{128,160},{160,128},{192,224},{224,1... | collective-permute-start | bytes 6152 | tf_op jit(solution)/shard_map/ppermute | solution.py:34
  201.4 6.8 %collective-permute-start.17 = (bf16[16,8,512]{2,1,0:T(8,128)(2,1)S(1)}, bf16[16,8,512]{2,1,0:T(8,128)(2,1)S(1)}, u32[]{:S(2)}, u32[]{:S(2)}) collective-permute-start(bf16[16,8,512]{2,1,0:T(8,128)(2,1)S(1)} %all-to-all-done.3), channel_id=1, source_target_pairs={{0,1},{1,0},{2,3},{3,2},{4,5},{5,4},{6,7},{7,6},{8,9},{9,8},{10,11... | collective-permute-start | bytes 393224 | tf_op jit(solution)/shard_map/ppermute | solution.py:56

commit v9 on v8

--- a/solution.py
+++ b/solution.py
@@ -276,25 +276,35 @@
     store_partials(even, product_left_t(taps_ref[0], d_value_ref[...]), keep_ref, send_ref, 3)
 
 
-def series_kernel(
-    d_query_ref, d_key_ref, d_value_ref, leading_ref, weights_ref, own_ref, upstream_ref, gain_ref,
-    grad_ref, d_gain_ref,
+def normed_kernel(
+    d_query_ref, d_key_ref, d_value_ref, weights_ref, window_ref, d_normed_ref, back_ref, d_gain_ref
 ):
-    count, features = own_ref.shape
-    d_normed = product_right_t(d_value_ref[...], weights_ref[3])
-    for which, (ref, base) in enumerate(((d_query_ref, 4), (d_key_ref, 0))):
-        after = leading_ref[:, which * features : (which + 1) * features]
-        window = jnp.concatenate([ref[...], after], axis=0).astype(f32)
+    count, features = d_query_ref.shape
+    blank = jnp.zeros((edge, features), f32)
+    own = product_right_t(d_value_ref[...], weights_ref[3])
+    d_normed = jnp.concatenate([blank, own], axis=0)
+    for ref, base in ((d_query_ref, 4), (d_key_ref, 0)):
+        rows = jnp.concatenate([blank, ref[...].astype(f32), blank], axis=0)
         for tap in range(3):
-            part = window[tap : tap + count].astype(bf16)
+            part = rows[tap : tap + count + edge].astype(bf16)
             d_normed = d_normed + product_right_t(part, weights_ref[base + tap])
-    values = own_ref[...].astype(f32)
+    values = window_ref[...].astype(f32)
+    top, rest = in_two(jnp.sum(d_normed * values * inverse_rms(values), axis=0, keepdims=True))
+    unused = jnp.zeros((d_gain_ref.shape[0] - 2, features), f32)
+    d_gain_ref[...] = jnp.concatenate(
+        [top.astype(f32), rest.astype(f32), unused], axis=0
+    ).astype(bf16)
+    back_ref[...] = d_normed[:edge]
+    d_normed_ref[...] = d_normed[edge:]
+
+
+def series_kernel(d_normed_ref, later_ref, window_ref, upstream_ref, gain_ref, grad_ref):
+    count = d_normed_ref.shape[0]
+    d_normed = jnp.concatenate(
+        [d_normed_ref[: count - edge], d_normed_ref[count - edge :] + later_ref[...]], axis=0
+    )
+    values = window_ref[edge:].astype(f32)
     scale = inverse_rms(values)
-    top, rest = in_two(jnp.sum(d_normed * values * scale, axis=0, keepdims=True))
-    blank = jnp.zeros((d_gain_ref.shape[0] - 2, features), f32)
-    d_gain_ref[...] = jnp.concatenate(
-        [top.astype(f32), rest.astype(f32), blank], axis=0
-    ).astype(bf16)
     slope = d_normed * gain_ref[...]
     along = jnp.mean(slope * values, axis=-1, keepdims=True)
     d_values = scale * slope - values * (scale * scale * scale * along)
@@ -326,11 +336,12 @@
     after_four, after_two = shift_ctx(carried, -4), shift_ctx(carried, -2)
     before_four, before_two = shift_ctx(window, 4), shift_ctx(window, 2)
     mine = over_chips(jnp.broadcast_to(shard[None], (8,) + shard.shape))
+    before_eight, after_eight = shift_ctx(before_four, 4), shift_ctx(after_four, -4)
     mine, before_two, before_four, after_two, after_four = lax.optimization_barrier(
         (mine, before_two, before_four, after_two, after_four)
     )
     other, before_eight, after_eight = lax.optimization_barrier(
-        (other_core(mine), shift_ctx(before_four, 4), shift_ctx(after_four, -4))
+        (other_core(mine), before_eight, after_eight)
     )
     before = (before_two, before_four, before_eight)
     after = (after_one, after_two, after_four, after_eight)
@@ -373,11 +384,13 @@
     d_key, d_value, keep, send = call(
         columns_kernel, [half, half, parts, parts], smem=1, inputs=13
     )(core, key, value, query, upper, queries, uppers, taps, own_stats, *returned)
-    leading = shift_ctx(jnp.concatenate([d_query[:edge], d_key[:edge]], axis=1), -1)
     key_half = halve(keep, send)
-    grad_series, d_gain = call(
-        series_kernel, [half, ((edge, features), bf16)], inputs=8
-    )(d_query, d_key, d_value, leading, weights, own, cotangent, gain)
+    d_normed, back, d_gain = call(
+        normed_kernel,
+        [((count, features), f32), ((edge, features), f32), ((edge, features), bf16)],
+        inputs=5,
+    )(d_query, d_key, d_value, weights, window)
+    later = shift_ctx(back, -1)
     terms = jnp.stack([query_half, key_half], axis=1).reshape(16, 128, features)
     d_gain = jnp.broadcast_to(d_gain[None], (16, edge, features))
     arrived = over_plane(jnp.concatenate([terms, d_gain], axis=1))
@@ -387,6 +400,10 @@
     extra = jnp.broadcast_to(jnp.concatenate([top, rest], axis=0)[None], (16, 8, 128))
     arrived = over_z(jnp.concatenate([rows, extra], axis=2)).astype(f32)
     summed = jnp.sum(arrived, axis=0)
+    d_normed, summed = lax.optimization_barrier((d_normed, summed))
+    (grad_series,) = call(series_kernel, [half], inputs=5)(
+        d_normed, later, window, cotangent, gain
+    )
     core_gain = summed[:4, features:] + summed[4:, features:]
     gain_total = (core_gain + other_core(core_gain)).reshape(features)
     summed = summed[:, :features].astype(bf16)

time: 211 us -> 205 us (0.972)
  waiting for transfers between devices: 52.3 us -> 44.8 us
    all_to_all x1, waiting for transfers between devices: 12 us -> 7.81 us  [over_z(): lax.all_to_all(stacked, 'ctx', 0, 0, axis_index_groups=z_groups, tiled=True)]
    ppermute x13, waiting for transfers between devices: 26.8 us -> 23.5 us  [shift_ctx(): return lax.ppermute(shard, 'ctx', pairs)]
    pallas_call x1 -> x2, Pallas kernels: 4.28 us -> 4.35 us  [the longest x1 3.54 us: body(): call(normed_kernel, [((count, features), f32), ((edge, features), f32), (...]
where the time goes in v9:
time: 205 us; the launch traced here: 204 us
  blocking collectives  71.5 us (35%)
  starting transfers between devices  54.5 us (27%)
  waiting for transfers between devices  44.8 us (22%)
  Pallas kernels  22.9 us (11%)
  local copies, waits for them, and re-layouts  4.85 us (2%)
  other arithmetic  4.26 us (2%)
    all_to_all x1, blocking collectives, over_plane(): lax.all_to_all(stacked, ('dp', 'ctx'), 0, 0, axis_index_groups=plane_grou...  37 us
    all_to_all x1, blocking collectives, over_z(): lax.all_to_all(stacked, 'ctx', 0, 0, axis_index_groups=z_groups, tiled=True)  34.5 us
    ppermute x13, starting transfers between devices, shift_ctx(): return lax.ppermute(shard, 'ctx', pairs)  33.4 us
    ppermute x13, waiting for transfers between devices, shift_ctx(): return lax.ppermute(shard, 'ctx', pairs)  23.5 us
    pallas_call x1, Pallas kernels, body(): call(rows_kernel, [((8, features, features), bf16)] + [half] * 7 + [((3,...  9.14 us
    all_to_all x1, waiting for transfers between devices, over_chips(): lax.all_to_all(stacked, 'dp', 0, 0, axis_index_groups=chip_groups, tiled=...  9.07 us
    ppermute x4, starting transfers between devices, dp_to(): return lax.ppermute(shard, 'dp', [(i, target(i)) for i in range(16)])  7.84 us
    all_to_all x1, waiting for transfers between devices, over_z(): lax.all_to_all(stacked, 'ctx', 0, 0, axis_index_groups=z_groups, tiled=True)  7.81 us
  transfers between devices with their start and end apart: 20, of which 12 were waited for; matrix products, arithmetic and copies ran while one was open for 1% of the time, Pallas kernels for 6%

profile of v9, /device:TPU:24, one launch (start us, length us, event | category | flops | bytes accessed | tf_op | source)
XLA Modules:
  0.0 203.8 jit_solution(3053996444448519133)
XLA Ops:
  0.6 1.0 pad_maximum_fusion.4
  1.6 1.3 collective-permute-start.1
  2.9 4.6 %collective-permute-start = (bf16[128,512]{1,0:T(8,128)(2,1)}, bf16[128,512]{1,0:T(8,128)(2,1)S(1)}, u32[]{:S(2)}, u32[]{:S(2)}) collective-permute-start(bf16[128,512]{1,0:T(8,128)(2,1)} %bitcast.47), channel_id=1, source_target_pairs={{0,1},{1,2},{2,3},{3,4},{4,5},{5,6},{6,7},{7,8},{8,9},{9,10},{10,1... | collective-permute-start | bytes 393224 | tf_op jit(solution)/shard_map/ppermute | solution.py:26
  7.5 1.0 pad_maximum_fusion.3
  8.5 5.9 %collective-permute-done.one_ref = bf16[128,512]{1,0:T(8,128)(2,1)S(1)} collective-permute-done((bf16[128,512]{1,0:T(8,128)(2,1)}, bf16[128,512]{1,0:T(8,128)(2,1)S(1)}, u32[]{:S(2)}, u32[]{:S(2)}) %collective-permute-start) | collective-permute-done | bytes 131104 | tf_op jit(solution)/shard_map/ppermute | solution.py:26
  14.4 1.6 broadcast_in_dim.28
  16.0 7.0 %all-to-all-start = ((bf16[8,8,32,512]{3,2,1,0:T(8,128)(2,1)}), bf16[8,8,32,512]{3,2,1,0:T(8,128)(2,1)}, u32[]{:S(2)}, u32[]{:S(2)}) async-start(bf16[8,8,32,512]{3,2,1,0:T(8,128)(2,1)} %broadcast_in_dim.28), calls=%async_computation | async-start | bytes 4194304 | tf_op jit(solution)/shard_map/all_to_all | solution.py:42
  23.0 1.3 collective-permute-start.5
  24.3 1.3 collective-permute-start.4
  25.7 6.7 %collective-permute-start.3 = (bf16[144,512]{1,0:T(8,128)(2,1)S(1)}, bf16[144,512]{1,0:T(8,128)(2,1)S(1)}, u32[]{:S(2)}, u32[]{:S(2)}) collective-permute-start(bf16[144,512]{1,0:T(8,128)(2,1)S(1)} %pad_maximum_fusion.6.window_ref), channel_id=1, source_target_pairs={{0,4},{1,5},{2,6},{3,7},{4,8},{5,9},{6,10},{7,11},{8,12},{9,13},{1... | collective-permute-start | bytes 442376 | tf_op jit(solution)/shard_map/ppermute | solution.py:26
  32.4 4.8 %collective-permute-start.2 = (bf16[144,512]{1,0:T(8,128)(2,1)S(1)}, bf16[144,512]{1,0:T(8,128)(2,1)S(1)}, u32[]{:S(2)}, u32[]{:S(2)}) collective-permute-start(bf16[144,512]{1,0:T(8,128)(2,1)S(1)} %pad_maximum_fusion.6.window_ref), channel_id=1, source_target_pairs={{0,2},{1,3},{2,4},{3,5},{4,6},{5,7},{6,8},{7,9},{8,10},{9,11},{10,... | collective-permute-start | bytes 442376 | tf_op jit(solution)/shard_map/ppermute | solution.py:26
  37.2 2.6 %collective-permute-done.2.two_ref = bf16[144,512]{1,0:T(8,128)(2,1)S(1)} collective-permute-done((bf16[144,512]{1,0:T(8,128)(2,1)S(1)}, bf16[144,512]{1,0:T(8,128)(2,1)S(1)}, u32[]{:S(2)}, u32[]{:S(2)}) %collective-permute-start.2) | collective-permute-done | bytes 147488 | tf_op jit(solution)/shard_map/ppermute | solution.py:26
  39.8 0.5 collective-permute-done.5.four_ref
  40.4 9.1 %all-to-all-done.mine_ref = bf16[8,8,32,512]{3,2,1,0:T(8,128)(2,1)} async-done(((bf16[8,8,32,512]{3,2,1,0:T(8,128)(2,1)}), bf16[8,8,32,512]{3,2,1,0:T(8,128)(2,1)}, u32[]{:S(2)}, u32[]{:S(2)}) %all-to-all-start) | async-done | bytes 2097184 | tf_op jit(solution)/shard_map/all_to_all | solution.py:42
  49.5 1.9 collective-permute-start.6
  51.5 1.3 collective-permute-start.8
  52.9 5.8 %collective-permute-start.7 = (bf16[144,512]{1,0:T(8,128)(2,1)S(1)}, bf16[144,512]{1,0:T(8,128)(2,1)S(1)}, u32[]{:S(2)}, u32[]{:S(2)}) collective-permute-start(bf16[144,512]{1,0:T(8,128)(2,1)S(1)} %collective-permute-done.3.four_ref), channel_id=1, source_target_pairs={{0,4},{1,5},{2,6},{3,7},{4,8},{5,9},{6,10},{7,11},{8,12},{9,13},{1... | collective-permute-start | bytes 442376 | tf_op jit(solution)/shard_map/ppermute | solution.py:26
  58.7 3.7 %collective-permute-done.7.eight_ref = bf16[144,512]{1,0:T(8,128)(2,1)S(1)} collective-permute-done((bf16[144,512]{1,0:T(8,128)(2,1)S(1)}, bf16[144,512]{1,0:T(8,128)(2,1)S(1)}, u32[]{:S(2)}, u32[]{:S(2)}) %collective-permute-start.7) | collective-permute-done | bytes 147488 | tf_op jit(solution)/shard_map/ppermute | solution.py:26
  62.5 3.8 %collective-permute-done.8.eight_ref = bf16[272,512]{1,0:T(8,128)(2,1)S(1)} collective-permute-done((bf16[272,512]{1,0:T(8,128)(2,1)S(1)}, bf16[272,512]{1,0:T(8,128)(2,1)S(1)}, u32[]{:S(2)}, u32[]{:S(2)}) %collective-permute-start.8) | collective-permute-done | bytes 278560 | tf_op jit(solution)/shard_map/ppermute | solution.py:26
  66.3 9.1 %shard_map.144 = (bf16[8,512,512]{2,1,0:T(8,128)(2,1)}, bf16[128,512]{1,0:T(8,128)(2,1)}, bf16[128,512]{1,0:T(8,128)(2,1)S(1)}, bf16[128,512]{1,0:T(8,128)(2,1)S...) custom-call(s32[1]{0:T(128)} %bitcast.core_ref, ...), custom_call_target="tpu_custom_call" | custom-call | tf_op jit(solution)/shard_map/pallas_call | solution.py:357
  75.4 0.7 shard_map.148
  76.2 1.9 collective-permute-start.13
  78.1 1.3 collective-permute-start.12
  79.4 1.3 collective-permute-start.11
  80.7 1.3 collective-permute-start.10
  82.0 1.3 collective-permute-start.9
  83.3 3.5 %shard_map.145 = (bf16[512,512]{1,0:T(8,128)(2,1)S(1)}, bf16[512,512]{1,0:T(8,128)(2,1)S(1)}) custom-call(bf16[128,512]{1,0:T(8,128)(2,1)S(1)} %bitcast.50, bf16[256,512]{1,0:T(8,128)(2,1)S(1)} %collective-permute-done.1.one_ref, bf16[272,512]{1,0:T(8,128)(2,1)S(1)} %collective-permute-done.4.two_ref, bf16[272,512]{1,0:T(8,128)(2,1)S(1)} %collective-permute-done.5.four_ref, ...), custom_call_target="tpu_custom_call" | custom-call | tf_op jit(solution)/shard_map/pallas_call | solution.py:377
  86.9 3.0 %collective-permute-done.12.eight_ref = f32[24,128]{1,0:T(8,128)S(1)} collective-permute-done((f32[24,128]{1,0:T(8,128)S(1)}, f32[24,128]{1,0:T(8,128)S(1)}, u32[]{:S(2)}, u32[]{:S(2)}) %collective-permute-start.12) | collective-permute-done | bytes 12320 | tf_op jit(solution)/shard_map/ppermute | solution.py:26
  89.9 1.4 collective-permute-done.10.two_ref
  91.2 5.1 %shard_map.146 = (bf16[128,512]{1,0:T(8,128)(2,1)S(1)}, bf16[128,512]{1,0:T(8,128)(2,1)S(1)}, bf16[8,4,32,512]{3,2,1,0:T(8,128)(2,1)S(1)}, bf16[8,4,32,512]{3,2,1,0:T(8,128)(2,1)}) custom-call(s32[1]{0:T(128)} %bitcast.core_ref, bf16[128,512]{1,0:T(8,128)(2,1)S(1)} %get-tuple-element.51.key_ref, bf16[128,512]{1,0:T(8,128)(2,1)S(1)} %get-tuple-element.52.value_ref, ...), custom_call_target="tpu_custom_call" | custom-call | tf_op jit(solution)/shard_map/pallas_call | solution.py:384
  96.3 2.1 %collective-permute-start.14 = (bf16[8,4,32,512]{3,2,1,0:T(8,128)(2,1)}, bf16[8,4,32,512]{3,2,1,0:T(8,128)(2,1)S(1)}, u32[]{:S(2)}, u32[]{:S(2)}) collective-permute-start(bf16[8,4,32,512]{3,2,1,0:T(8,128)(2,1)} %get-tuple-element.72), channel_id=1, source_target_pairs={{0,32},{32,0},{64,96},{96,64},{128,160},{160,128},{192,224},{224,1... | collective-permute-start | bytes 3145736 | tf_op jit(solution)/shard_map/ppermute | solution.py:34
  98.4 3.5 %shard_map.147 = (f32[128,512]{1,0:T(8,128)S(1)}, f32[16,512]{1,0:T(8,128)S(1)}, bf16[16,512]{1,0:T(8,128)(2,1)S(1)}) custom-call(bf16[128,512]{1,0:T(8,128)(2,1)S(1)} %get-tuple-element.50.d_query_ref, bf16[128,512]{1,0:T(8,128)(2,1)S(1)} %get-tuple-element.65.d_key_ref, bf16[128,512]{1,0:T(8,128)(2,1)S(1)} %get-tuple-element.66.d_value_ref, ...), custom_call_target="tpu_custom_call" | custom-call | tf_op jit(solution)/shard_map/pallas_call | solution.py:388
  102.0 0.4 fusion
  103.5 37.0 %all_to_all.20 = bf16[16,144,512]{2,1,0:T(8,128)(2,1)S(1)} all-to-all(bf16[16,144,512]{2,1,0:T(8,128)(2,1)S(1)} %pad_maximum_fusion), channel_id=1, replica_groups={{0,1,64,65,128,129,192,193,256,257,320,321,384,385,448,449},{2,3,66,67,..., dimensions={0} | all-to-all | bytes 4718592 | tf_op jit(solution)/shard_map/all_to_all | solution.py:46
  140.9 34.5 %all_to_all.21 = bf16[16,8,640]{2,1,0:T(8,128)(2,1)S(1)} all-to-all(bf16[16,8,640]{2,1,0:T(8,128)(2,1)S(1)} %pad_maximum_fusion.5), channel_id=1, replica_groups={{0,2,4,6,8,10,12,14,16,18,20,22,24,26,28,30},{1,3,5,7,9,11,13,15,17,19,..., dimensions={0} | all-to-all | bytes 327680 | tf_op jit(solution)/shard_map/all_to_all | solution.py:52
  175.5 0.7 broadcast_in_dim.61
  176.1 4.3 %all-to-all-start.3 = ((bf16[16,8,512]{2,1,0:T(8,128)(2,1)}), bf16[16,8,512]{2,1,0:T(8,128)(2,1)S(1)}, u32[]{:S(2)}, u32[]{:S(2)}) async-start(bf16[16,8,512]{2,1,0:T(8,128)(2,1)} %broadcast_in_dim.61), calls=%async_computation.3 | async-start | bytes 262144 | tf_op jit(solution)/shard_map/all_to_all | solution.py:52
  180.4 1.3 collective-permute-start.15
  181.7 1.9 collective-permute-start.16
  183.7 2.6 %collective-permute-done.15.later_ref = f32[16,512]{1,0:T(8,128)S(1)} collective-permute-done((f32[16,512]{1,0:T(8,128)S(1)}, f32[16,512]{1,0:T(8,128)S(1)}, u32[]{:S(2)}, u32[]{:S(2)}) %collective-permute-start.15) | collective-permute-done | bytes 32800 | tf_op jit(solution)/shard_map/ppermute | solution.py:26
  186.2 0.8 shard_map.149
  187.1 7.8 %all-to-all-done.3 = bf16[16,8,512]{2,1,0:T(8,128)(2,1)S(1)} async-done(((bf16[16,8,512]{2,1,0:T(8,128)(2,1)}), bf16[16,8,512]{2,1,0:T(8,128)(2,1)S(1)}, u32[]{:S(2)}, u32[]{:S(2)}) %all-to-all-start.3) | async-done | bytes 131104 | tf_op jit(solution)/shard_map/all_to_all | solution.py:52
  194.9 1.9 collective-permute-start.17
  196.8 0.6 add_bitcast_fusion
  197.4 4.3 %collective-permute-done.17 = bf16[16,8,512]{2,1,0:T(8,128)(2,1)S(1)} collective-permute-done((bf16[16,8,512]{2,1,0:T(8,128)(2,1)S(1)}, bf16[16,8,512]{2,1,0:T(8,128)(2,1)S(1)}, u32[]{:S(2)}, u32[]{:S(2)}) %collective-permute-start.17) | collective-permute-done | bytes 131104 | tf_op jit(solution)/shard_map/ppermute | solution.py:56
  201.8 0.7 slice.72
  202.5 0.7 slice_bitcast_fusion
  203.1 0.7 slice.71
  (46 shorter events, 2.0 us)
Async XLA Ops:
  1.6 12.8 %collective-permute-start.1 = (bf16[256,512]{1,0:T(8,128)(2,1)S(1)}, bf16[256,512]{1,0:T(8,128)(2,1)S(1)}, u32[]{:S(2)}, u32[]{:S(2)}) collective-permute-start(bf16[256,512]{1,0:T(8,128)(2,1)S(1)} %pad_maximum_fusion.4), channel_id=1, source_target_pairs={{1,0},{2,1},{3,2},{4,3},{5,4},{6,5},{7,6},{8,7},{9,8},{10,9},{11,1... | collective-permute-start | bytes 786440 | tf_op jit(solution)/shard_map/ppermute | solution.py:26
  2.9 11.5 %collective-permute-start = (bf16[128,512]{1,0:T(8,128)(2,1)}, bf16[128,512]{1,0:T(8,128)(2,1)S(1)}, u32[]{:S(2)}, u32[]{:S(2)}) collective-permute-start(bf16[128,512]{1,0:T(8,128)(2,1)} %bitcast.47), channel_id=1, source_target_pairs={{0,1},{1,2},{2,3},{3,4},{4,5},{5,6},{6,7},{7,8},{8,9},{9,10},{10,1... | collective-permute-start | bytes 393224 | tf_op jit(solution)/shard_map/ppermute | solution.py:26
  16.0 7.0 %copy-start = (bf16[1,128,512]{2,1,0:T(8,128)(2,1)S(1)}, bf16[1,128,512]{2,1,0:T(8,128)(2,1)}, u32[]{:S(2)}) copy-start(bf16[1,128,512]{2,1,0:T(8,128)(2,1)} %param.16) | copy-start | bytes 393220
  16.0 7.0 %copy-start.1 = (bf16[1,128,512]{2,1,0:T(8,128)(2,1)S(1)}, bf16[1,128,512]{2,1,0:T(8,128)(2,1)}, u32[]{:S(2)}) copy-start(bf16[1,128,512]{2,1,0:T(8,128)(2,1)} %param.9) | copy-start | bytes 393220
  16.0 35.4 %copy-start.3 = (s32[1,1,8,4]{2,3,1,0:T(4,128)S(1)}, s32[1,1,8,4]{2,3,1,0:T(4,128)}, u32[]{:S(2)}) copy-start(s32[1,1,8,4]{2,3,1,0:T(4,128)} %param.15) | copy-start | bytes 388
  16.0 35.5 %copy-start.4 = (s32[4]{0:T(128)S(1)}, s32[4]{0:T(128)}, u32[]{:S(2)}) copy-start(s32[4]{0:T(128)} %constant.36.clone) | copy-start | bytes 52
  16.0 50.3 %copy-start.2 = (f32[512]{0:T(512)S(1)}, f32[512]{0:T(512)}, u32[]{:S(2)}) copy-start(f32[512]{0:T(512)} %param.10) | copy-start | bytes 6148
  16.0 33.5 %all-to-all-start = ((bf16[8,8,32,512]{3,2,1,0:T(8,128)(2,1)}), bf16[8,8,32,512]{3,2,1,0:T(8,128)(2,1)}, u32[]{:S(2)}, u32[]{:S(2)}) async-start(bf16[8,8,32,512]{3,2,1,0:T(8,128)(2,1)} %broadcast_in_dim.28), calls=%async_computation | async-start | bytes 4194304 | tf_op jit(solution)/shard_map/all_to_all | solution.py:42
  23.0 17.3 %collective-permute-start.5 = (bf16[272,512]{1,0:T(8,128)(2,1)S(1)}, bf16[272,512]{1,0:T(8,128)(2,1)S(1)}, u32[]{:S(2)}, u32[]{:S(2)}) collective-permute-start(bf16[272,512]{1,0:T(8,128)(2,1)S(1)} %pad_maximum_fusion.2), channel_id=1, source_target_pairs={{4,0},{5,1},{6,2},{7,3},{8,4},{9,5},{10,6},{11,7},{12,8},{13,9},{1... | collective-permute-start | bytes 835592 | tf_op jit(solution)/shard_map/ppermute | solution.py:26
  24.3 16.1 %collective-permute-start.4 = (bf16[272,512]{1,0:T(8,128)(2,1)S(1)}, bf16[272,512]{1,0:T(8,128)(2,1)S(1)}, u32[]{:S(2)}, u32[]{:S(2)}) collective-permute-start(bf16[272,512]{1,0:T(8,128)(2,1)S(1)} %pad_maximum_fusion.2), channel_id=1, source_target_pairs={{2,0},{3,1},{4,2},{5,3},{6,4},{7,5},{8,6},{9,7},{10,8},{11,9},{12,... | collective-permute-start | bytes 835592 | tf_op jit(solution)/shard_map/ppermute | solution.py:26
  25.7 11.5 %collective-permute-start.3 = (bf16[144,512]{1,0:T(8,128)(2,1)S(1)}, bf16[144,512]{1,0:T(8,128)(2,1)S(1)}, u32[]{:S(2)}, u32[]{:S(2)}) collective-permute-start(bf16[144,512]{1,0:T(8,128)(2,1)S(1)} %pad_maximum_fusion.6.window_ref), channel_id=1, source_target_pairs={{0,4},{1,5},{2,6},{3,7},{4,8},{5,9},{6,10},{7,11},{8,12},{9,13},{1... | collective-permute-start | bytes 442376 | tf_op jit(solution)/shard_map/ppermute | solution.py:26
  32.4 7.4 %collective-permute-start.2 = (bf16[144,512]{1,0:T(8,128)(2,1)S(1)}, bf16[144,512]{1,0:T(8,128)(2,1)S(1)}, u32[]{:S(2)}, u32[]{:S(2)}) collective-permute-start(bf16[144,512]{1,0:T(8,128)(2,1)S(1)} %pad_maximum_fusion.6.window_ref), channel_id=1, source_target_pairs={{0,2},{1,3},{2,4},{3,5},{4,6},{5,7},{6,8},{7,9},{8,10},{9,11},{10,... | collective-permute-start | bytes 442376 | tf_op jit(solution)/shard_map/ppermute | solution.py:26
  49.5 16.7 %collective-permute-start.6 = (bf16[8,8,32,512]{3,2,1,0:T(8,128)(2,1)}, bf16[8,8,32,512]{3,2,1,0:T(8,128)(2,1)}, u32[]{:S(2)}, u32[]{:S(2)}) collective-permute-start(bf16[8,8,32,512]{3,2,1,0:T(8,128)(2,1)} %all-to-all-done.mine_ref), channel_id=1, source_target_pairs={{0,32},{32,0},{64,96},{96,64},{128,160},{160,128},{192,224},{224,1... | collective-permute-start | bytes 6291464 | tf_op jit(solution)/shard_map/ppermute | solution.py:34
  51.5 14.7 %collective-permute-start.8 = (bf16[272,512]{1,0:T(8,128)(2,1)S(1)}, bf16[272,512]{1,0:T(8,128)(2,1)S(1)}, u32[]{:S(2)}, u32[]{:S(2)}) collective-permute-start(bf16[272,512]{1,0:T(8,128)(2,1)S(1)} %collective-permute-done.5.four_ref), channel_id=1, source_target_pairs={{4,0},{5,1},{6,2},{7,3},{8,4},{9,5},{10,6},{11,7},{12,8},{13,9},{1... | collective-permute-start | bytes 835592 | tf_op jit(solution)/shard_map/ppermute | solution.py:26
  52.9 9.5 %collective-permute-start.7 = (bf16[144,512]{1,0:T(8,128)(2,1)S(1)}, bf16[144,512]{1,0:T(8,128)(2,1)S(1)}, u32[]{:S(2)}, u32[]{:S(2)}) collective-permute-start(bf16[144,512]{1,0:T(8,128)(2,1)S(1)} %collective-permute-done.3.four_ref), channel_id=1, source_target_pairs={{0,4},{1,5},{2,6},{3,7},{4,8},{5,9},{6,10},{7,11},{8,12},{9,13},{1... | collective-permute-start | bytes 442376 | tf_op jit(solution)/shard_map/ppermute | solution.py:26
  76.2 25.8 %collective-permute-start.13 = (bf16[8,4,32,512]{3,2,1,0:T(8,128)(2,1)S(1)}, bf16[8,4,32,512]{3,2,1,0:T(8,128)(2,1)S(1)}, u32[]{:S(2)}, u32[]{:S(2)}) collective-permute-start(bf16[8,4,32,512]{3,2,1,0:T(8,128)(2,1)S(1)} %get-tuple-element.70), channel_id=1, source_target_pairs={{0,32},{32,0},{64,96},{96,64},{128,160},{160,128},{192,224},{224,1... | collective-permute-start | bytes 3145736 | tf_op jit(solution)/shard_map/ppermute | solution.py:34
  78.1 11.7 %collective-permute-start.12 = (f32[24,128]{1,0:T(8,128)S(1)}, f32[24,128]{1,0:T(8,128)S(1)}, u32[]{:S(2)}, u32[]{:S(2)}) collective-permute-start(f32[24,128]{1,0:T(8,128)S(1)} %get-tuple-element.81), channel_id=1, source_target_pairs={{8,0},{9,1},{10,2},{11,3},{12,4},{13,5},{14,6},{15,7},{16,8},{17,9... | collective-permute-start | bytes 36872 | tf_op jit(solution)/shard_map/ppermute | solution.py:26
  79.4 10.4 %collective-permute-start.11 = (f32[24,128]{1,0:T(8,128)S(1)}, f32[24,128]{1,0:T(8,128)S(1)}, u32[]{:S(2)}, u32[]{:S(2)}) collective-permute-start(f32[24,128]{1,0:T(8,128)S(1)} %get-tuple-element.82), channel_id=1, source_target_pairs={{4,0},{5,1},{6,2},{7,3},{8,4},{9,5},{10,6},{11,7},{12,8},{13,9},{1... | collective-permute-start | bytes 36872 | tf_op jit(solution)/shard_map/ppermute | solution.py:26
  80.7 10.5 %collective-permute-start.10 = (f32[24,128]{1,0:T(8,128)S(1)}, f32[24,128]{1,0:T(8,128)S(1)}, u32[]{:S(2)}, u32[]{:S(2)}) collective-permute-start(f32[24,128]{1,0:T(8,128)S(1)} %get-tuple-element.83), channel_id=1, source_target_pairs={{2,0},{3,1},{4,2},{5,3},{6,4},{7,5},{8,6},{9,7},{10,8},{11,9},{12,... | collective-permute-start | bytes 36872 | tf_op jit(solution)/shard_map/ppermute | solution.py:26
  82.0 9.2 %collective-permute-start.9 = (f32[24,128]{1,0:T(8,128)S(1)}, f32[24,128]{1,0:T(8,128)S(1)}, u32[]{:S(2)}, u32[]{:S(2)}) collective-permute-start(f32[24,128]{1,0:T(8,128)S(1)} %get-tuple-element.84), channel_id=1, source_target_pairs={{1,0},{2,1},{3,2},{4,3},{5,4},{6,5},{7,6},{8,7},{9,8},{10,9},{11,1... | collective-permute-start | bytes 36872 | tf_op jit(solution)/shard_map/ppermute | solution.py:26
  96.3 6.0 %collective-permute-start.14 = (bf16[8,4,32,512]{3,2,1,0:T(8,128)(2,1)}, bf16[8,4,32,512]{3,2,1,0:T(8,128)(2,1)S(1)}, u32[]{:S(2)}, u32[]{:S(2)}) collective-permute-start(bf16[8,4,32,512]{3,2,1,0:T(8,128)(2,1)} %get-tuple-element.72), channel_id=1, source_target_pairs={{0,32},{32,0},{64,96},{96,64},{128,160},{160,128},{192,224},{224,1... | collective-permute-start | bytes 3145736 | tf_op jit(solution)/shard_map/ppermute | solution.py:34
  176.1 18.8 %all-to-all-start.3 = ((bf16[16,8,512]{2,1,0:T(8,128)(2,1)}), bf16[16,8,512]{2,1,0:T(8,128)(2,1)S(1)}, u32[]{:S(2)}, u32[]{:S(2)}) async-start(bf16[16,8,512]{2,1,0:T(8,128)(2,1)} %broadcast_in_dim.61), calls=%async_computation.3 | async-start | bytes 262144 | tf_op jit(solution)/shard_map/all_to_all | solution.py:52
  180.4 5.8 %collective-permute-start.15 = (f32[16,512]{1,0:T(8,128)S(1)}, f32[16,512]{1,0:T(8,128)S(1)}, u32[]{:S(2)}, u32[]{:S(2)}) collective-permute-start(f32[16,512]{1,0:T(8,128)S(1)} %get-tuple-element.75), channel_id=1, source_target_pairs={{1,0},{2,1},{3,2},{4,3},{5,4},{6,5},{7,6},{8,7},{9,8},{10,9},{11,1... | collective-permute-start | bytes 98312 | tf_op jit(solution)/shard_map/ppermute | solution.py:26
  181.7 15.0 %collective-permute-start.16 = (f32[4,128]{1,0:T(4,128)S(1)}, f32[4,128]{1,0:T(4,128)S(1)}, u32[]{:S(2)}, u32[]{:S(2)}) collective-permute-start(f32[4,128]{1,0:T(4,128)S(1)} %slice_add_fusion), channel_id=1, source_target_pairs={{0,32},{32,0},{64,96},{96,64},{128,160},{160,128},{192,224},{224,1... | collective-permute-start | bytes 6152 | tf_op jit(solution)/shard_map/ppermute | solution.py:34
  194.9 6.8 %collective-permute-start.17 = (bf16[16,8,512]{2,1,0:T(8,128)(2,1)S(1)}, bf16[16,8,512]{2,1,0:T(8,128)(2,1)S(1)}, u32[]{:S(2)}, u32[]{:S(2)}) collective-permute-start(bf16[16,8,512]{2,1,0:T(8,128)(2,1)S(1)} %all-to-all-done.3), channel_id=1, source_target_pairs={{0,1},{1,0},{2,3},{3,2},{4,5},{5,4},{6,7},{7,6},{8,9},{9,8},{10,11... | collective-permute-start | bytes 393224 | tf_op jit(solution)/shard_map/ppermute | solution.py:56

commit v10 on v9

--- a/solution.py
+++ b/solution.py
@@ -340,11 +340,8 @@
     mine, before_two, before_four, after_two, after_four = lax.optimization_barrier(
         (mine, before_two, before_four, after_two, after_four)
     )
-    other, before_eight, after_eight = lax.optimization_barrier(
-        (other_core(mine), before_eight, after_eight)
-    )
+    other, before_eight = lax.optimization_barrier((other_core(mine), before_eight))
     before = (before_two, before_four, before_eight)
-    after = (after_one, after_two, after_four, after_eight)
 
     offsets = jnp.array(block_offsets, dtype=jnp.int32)
     reach = (block_links[0, 0] > 0) & (block >= offsets)[None, :]
@@ -369,6 +366,8 @@
         core, reach.astype(jnp.int32), mine, other, window, before_one, *before, cotangent, gain,
         barred,
     )
+    attn, stats, after_eight = lax.optimization_barrier((attn, stats, after_eight))
+    after = (after_one, after_two, after_four, after_eight)
     returned = [shift_ctx(stats[i], -block_offsets[i]) for i in range(4)]
     parts = ((8, 4, 32, features), bf16)
     keep, send = call(partials_kernel, [parts, parts], smem=1, inputs=5)(

time: 205 us -> 202 us (0.985)
  blocking collectives: 71.5 us -> 66.3 us
  waiting for transfers between devices: 44.8 us -> 47.1 us
    all_to_all x1, blocking collectives: 34.5 us -> 30.7 us  [over_z(): lax.all_to_all(stacked, 'ctx', 0, 0, axis_index_groups=z_groups, tiled=True)]
    ppermute x13, waiting for transfers between devices: 23.5 us -> 25.8 us  [shift_ctx(): return lax.ppermute(shard, 'ctx', pairs)]
  transfers between devices with their start and end apart: 20 -> 20, of which waited for: 12 -> 11; matrix products, arithmetic and copies ran while one was open for 1% -> 1% of each run, Pallas kernels for 6% -> 11%
where the time goes in v10:
time: 202 us; the launch traced here: 201 us
  blocking collectives  66.3 us (33%)
  starting transfers between devices  54.5 us (27%)
  waiting for transfers between devices  47.1 us (23%)
  Pallas kernels  22.9 us (11%)
  local copies, waits for them, and re-layouts  4.86 us (2%)
  other arithmetic  4.26 us (2%)
    all_to_all x1, blocking collectives, over_plane(): lax.all_to_all(stacked, ('dp', 'ctx'), 0, 0, axis_index_groups=plane_grou...  35.5 us
    ppermute x13, starting transfers between devices, shift_ctx(): return lax.ppermute(shard, 'ctx', pairs)  33.4 us
    all_to_all x1, blocking collectives, over_z(): lax.all_to_all(stacked, 'ctx', 0, 0, axis_index_groups=z_groups, tiled=True)  30.7 us
    ppermute x13, waiting for transfers between devices, shift_ctx(): return lax.ppermute(shard, 'ctx', pairs)  25.8 us
    pallas_call x1, Pallas kernels, body(): call(rows_kernel, [((8, features, features), bf16)] + [half] * 7 + [((3,...  9.14 us
    all_to_all x1, waiting for transfers between devices, over_chips(): lax.all_to_all(stacked, 'dp', 0, 0, axis_index_groups=chip_groups, tiled=...  9.07 us
    ppermute x4, starting transfers between devices, dp_to(): return lax.ppermute(shard, 'dp', [(i, target(i)) for i in range(16)])  7.84 us
    all_to_all x1, waiting for transfers between devices, over_z(): lax.all_to_all(stacked, 'ctx', 0, 0, axis_index_groups=z_groups, tiled=True)  7.81 us
  transfers between devices with their start and end apart: 20, of which 11 were waited for; matrix products, arithmetic and copies ran while one was open for 1% of the time, Pallas kernels for 11%

profile of v10, /device:TPU:24, one launch (start us, length us, event | category | flops | bytes accessed | tf_op | source)
XLA Modules:
  0.0 200.9 jit_solution(15842401032985276141)
XLA Ops:
  0.6 1.0 pad_maximum_fusion.4
  1.6 1.3 collective-permute-start.1
  2.9 4.6 %collective-permute-start = (bf16[128,512]{1,0:T(8,128)(2,1)}, bf16[128,512]{1,0:T(8,128)(2,1)S(1)}, u32[]{:S(2)}, u32[]{:S(2)}) collective-permute-start(bf16[128,512]{1,0:T(8,128)(2,1)} %bitcast.47), channel_id=1, source_target_pairs={{0,1},{1,2},{2,3},{3,4},{4,5},{5,6},{6,7},{7,8},{8,9},{9,10},{10,1... | collective-permute-start | bytes 393224 | tf_op jit(solution)/shard_map/ppermute | solution.py:26
  7.5 1.0 pad_maximum_fusion.3
  8.5 5.9 %collective-permute-done.one_ref = bf16[128,512]{1,0:T(8,128)(2,1)S(1)} collective-permute-done((bf16[128,512]{1,0:T(8,128)(2,1)}, bf16[128,512]{1,0:T(8,128)(2,1)S(1)}, u32[]{:S(2)}, u32[]{:S(2)}) %collective-permute-start) | collective-permute-done | bytes 131104 | tf_op jit(solution)/shard_map/ppermute | solution.py:26
  14.4 1.6 broadcast_in_dim.28
  16.0 7.0 %all-to-all-start = ((bf16[8,8,32,512]{3,2,1,0:T(8,128)(2,1)}), bf16[8,8,32,512]{3,2,1,0:T(8,128)(2,1)}, u32[]{:S(2)}, u32[]{:S(2)}) async-start(bf16[8,8,32,512]{3,2,1,0:T(8,128)(2,1)} %broadcast_in_dim.28), calls=%async_computation | async-start | bytes 4194304 | tf_op jit(solution)/shard_map/all_to_all | solution.py:42
  23.0 1.3 collective-permute-start.5
  24.3 1.3 collective-permute-start.4
  25.7 6.7 %collective-permute-start.3 = (bf16[144,512]{1,0:T(8,128)(2,1)S(1)}, bf16[144,512]{1,0:T(8,128)(2,1)S(1)}, u32[]{:S(2)}, u32[]{:S(2)}) collective-permute-start(bf16[144,512]{1,0:T(8,128)(2,1)S(1)} %pad_maximum_fusion.6.window_ref), channel_id=1, source_target_pairs={{0,4},{1,5},{2,6},{3,7},{4,8},{5,9},{6,10},{7,11},{8,12},{9,13},{1... | collective-permute-start | bytes 442376 | tf_op jit(solution)/shard_map/ppermute | solution.py:26
  32.4 4.8 %collective-permute-start.2 = (bf16[144,512]{1,0:T(8,128)(2,1)S(1)}, bf16[144,512]{1,0:T(8,128)(2,1)S(1)}, u32[]{:S(2)}, u32[]{:S(2)}) collective-permute-start(bf16[144,512]{1,0:T(8,128)(2,1)S(1)} %pad_maximum_fusion.6.window_ref), channel_id=1, source_target_pairs={{0,2},{1,3},{2,4},{3,5},{4,6},{5,7},{6,8},{7,9},{8,10},{9,11},{10,... | collective-permute-start | bytes 442376 | tf_op jit(solution)/shard_map/ppermute | solution.py:26
  37.2 2.6 %collective-permute-done.2.two_ref = bf16[144,512]{1,0:T(8,128)(2,1)S(1)} collective-permute-done((bf16[144,512]{1,0:T(8,128)(2,1)S(1)}, bf16[144,512]{1,0:T(8,128)(2,1)S(1)}, u32[]{:S(2)}, u32[]{:S(2)}) %collective-permute-start.2) | collective-permute-done | bytes 147488 | tf_op jit(solution)/shard_map/ppermute | solution.py:26
  39.8 0.5 collective-permute-done.5.four_ref
  40.4 9.1 %all-to-all-done.mine_ref = bf16[8,8,32,512]{3,2,1,0:T(8,128)(2,1)} async-done(((bf16[8,8,32,512]{3,2,1,0:T(8,128)(2,1)}), bf16[8,8,32,512]{3,2,1,0:T(8,128)(2,1)}, u32[]{:S(2)}, u32[]{:S(2)}) %all-to-all-start) | async-done | bytes 2097184 | tf_op jit(solution)/shard_map/all_to_all | solution.py:42
  49.5 1.9 collective-permute-start.6
  51.5 1.3 collective-permute-start.8
  52.9 5.8 %collective-permute-start.7 = (bf16[144,512]{1,0:T(8,128)(2,1)S(1)}, bf16[144,512]{1,0:T(8,128)(2,1)S(1)}, u32[]{:S(2)}, u32[]{:S(2)}) collective-permute-start(bf16[144,512]{1,0:T(8,128)(2,1)S(1)} %collective-permute-done.3.four_ref), channel_id=1, source_target_pairs={{0,4},{1,5},{2,6},{3,7},{4,8},{5,9},{6,10},{7,11},{8,12},{9,13},{1... | collective-permute-start | bytes 442376 | tf_op jit(solution)/shard_map/ppermute | solution.py:26
  58.7 3.7 %collective-permute-done.7.eight_ref = bf16[144,512]{1,0:T(8,128)(2,1)S(1)} collective-permute-done((bf16[144,512]{1,0:T(8,128)(2,1)S(1)}, bf16[144,512]{1,0:T(8,128)(2,1)S(1)}, u32[]{:S(2)}, u32[]{:S(2)}) %collective-permute-start.7) | collective-permute-done | bytes 147488 | tf_op jit(solution)/shard_map/ppermute | solution.py:26
  62.5 9.1 %shard_map.144 = (bf16[8,512,512]{2,1,0:T(8,128)(2,1)}, bf16[128,512]{1,0:T(8,128)(2,1)}, bf16[128,512]{1,0:T(8,128)(2,1)S(1)}, bf16[128,512]{1,0:T(8,128)(2,1)S...) custom-call(s32[1]{0:T(128)} %bitcast.core_ref, ...), custom_call_target="tpu_custom_call" | custom-call | tf_op jit(solution)/shard_map/pallas_call | solution.py:354
  71.7 0.7 shard_map.148
  72.4 1.9 collective-permute-start.13
  74.4 1.3 collective-permute-start.10
  75.7 1.3 collective-permute-start.11
  77.0 1.3 collective-permute-start.12
  78.3 1.3 collective-permute-start.9
  79.6 3.5 %shard_map.145 = (bf16[512,512]{1,0:T(8,128)(2,1)S(1)}, bf16[512,512]{1,0:T(8,128)(2,1)S(1)}) custom-call(bf16[128,512]{1,0:T(8,128)(2,1)S(1)} %bitcast.50, bf16[256,512]{1,0:T(8,128)(2,1)S(1)} %collective-permute-done.1.one_ref, bf16[272,512]{1,0:T(8,128)(2,1)S(1)} %collective-permute-done.4.two_ref, bf16[272,512]{1,0:T(8,128)(2,1)S(1)} %collective-permute-done.5.four_ref, ...), custom_call_target="tpu_custom_call" | custom-call | tf_op jit(solution)/shard_map/pallas_call | solution.py:376
  83.1 4.4 %collective-permute-done.11.four_ref = f32[24,128]{1,0:T(8,128)S(1)} collective-permute-done((f32[24,128]{1,0:T(8,128)S(1)}, f32[24,128]{1,0:T(8,128)S(1)}, u32[]{:S(2)}, u32[]{:S(2)}) %collective-permute-start.11) | collective-permute-done | bytes 12320 | tf_op jit(solution)/shard_map/ppermute | solution.py:26
  87.5 6.0 %collective-permute-done.12.eight_ref = f32[24,128]{1,0:T(8,128)S(1)} collective-permute-done((f32[24,128]{1,0:T(8,128)S(1)}, f32[24,128]{1,0:T(8,128)S(1)}, u32[]{:S(2)}, u32[]{:S(2)}) %collective-permute-start.12) | collective-permute-done | bytes 12320 | tf_op jit(solution)/shard_map/ppermute | solution.py:26
  93.5 5.1 %shard_map.146 = (bf16[128,512]{1,0:T(8,128)(2,1)S(1)}, bf16[128,512]{1,0:T(8,128)(2,1)S(1)}, bf16[8,4,32,512]{3,2,1,0:T(8,128)(2,1)S(1)}, bf16[8,4,32,512]{3,2,1,0:T(8,128)(2,1)}) custom-call(s32[1]{0:T(128)} %bitcast.core_ref, bf16[128,512]{1,0:T(8,128)(2,1)S(1)} %get-tuple-element.53.key_ref, bf16[128,512]{1,0:T(8,128)(2,1)S(1)} %get-tuple-element.54.value_ref, ...), custom_call_target="tpu_custom_call" | custom-call | tf_op jit(solution)/shard_map/pallas_call | solution.py:383
  98.6 2.1 %collective-permute-start.14 = (bf16[8,4,32,512]{3,2,1,0:T(8,128)(2,1)}, bf16[8,4,32,512]{3,2,1,0:T(8,128)(2,1)S(1)}, u32[]{:S(2)}, u32[]{:S(2)}) collective-permute-start(bf16[8,4,32,512]{3,2,1,0:T(8,128)(2,1)} %get-tuple-element.76), channel_id=1, source_target_pairs={{0,32},{32,0},{64,96},{96,64},{128,160},{160,128},{192,224},{224,1... | collective-permute-start | bytes 3145736 | tf_op jit(solution)/shard_map/ppermute | solution.py:34
  100.7 3.5 %shard_map.147 = (f32[128,512]{1,0:T(8,128)S(1)}, f32[16,512]{1,0:T(8,128)S(1)}, bf16[16,512]{1,0:T(8,128)(2,1)S(1)}) custom-call(bf16[128,512]{1,0:T(8,128)(2,1)S(1)} %get-tuple-element.52.d_query_ref, bf16[128,512]{1,0:T(8,128)(2,1)S(1)} %get-tuple-element.69.d_key_ref, bf16[128,512]{1,0:T(8,128)(2,1)S(1)} %get-tuple-element.70.d_value_ref, ...), custom_call_target="tpu_custom_call" | custom-call | tf_op jit(solution)/shard_map/pallas_call | solution.py:387
  104.3 0.4 fusion
  104.7 0.4 fusion.1
  105.8 35.5 %all_to_all.20 = bf16[16,144,512]{2,1,0:T(8,128)(2,1)S(1)} all-to-all(bf16[16,144,512]{2,1,0:T(8,128)(2,1)S(1)} %pad_maximum_fusion), channel_id=1, replica_groups={{0,1,64,65,128,129,192,193,256,257,320,321,384,385,448,449},{2,3,66,67,..., dimensions={0} | all-to-all | bytes 4718592 | tf_op jit(solution)/shard_map/all_to_all | solution.py:46
  141.8 30.7 %all_to_all.21 = bf16[16,8,640]{2,1,0:T(8,128)(2,1)S(1)} all-to-all(bf16[16,8,640]{2,1,0:T(8,128)(2,1)S(1)} %pad_maximum_fusion.5), channel_id=1, replica_groups={{0,2,4,6,8,10,12,14,16,18,20,22,24,26,28,30},{1,3,5,7,9,11,13,15,17,19,..., dimensions={0} | all-to-all | bytes 327680 | tf_op jit(solution)/shard_map/all_to_all | solution.py:52
  172.5 0.7 broadcast_in_dim.61
  173.2 4.3 %all-to-all-start.3 = ((bf16[16,8,512]{2,1,0:T(8,128)(2,1)}), bf16[16,8,512]{2,1,0:T(8,128)(2,1)S(1)}, u32[]{:S(2)}, u32[]{:S(2)}) async-start(bf16[16,8,512]{2,1,0:T(8,128)(2,1)} %broadcast_in_dim.61), calls=%async_computation.3 | async-start | bytes 262144 | tf_op jit(solution)/shard_map/all_to_all | solution.py:52
  177.5 1.3 collective-permute-start.15
  178.8 1.9 collective-permute-start.16
  180.7 2.6 %collective-permute-done.15.later_ref = f32[16,512]{1,0:T(8,128)S(1)} collective-permute-done((f32[16,512]{1,0:T(8,128)S(1)}, f32[16,512]{1,0:T(8,128)S(1)}, u32[]{:S(2)}, u32[]{:S(2)}) %collective-permute-start.15) | collective-permute-done | bytes 32800 | tf_op jit(solution)/shard_map/ppermute | solution.py:26
  183.3 0.8 shard_map.149
  184.1 7.8 %all-to-all-done.3 = bf16[16,8,512]{2,1,0:T(8,128)(2,1)S(1)} async-done(((bf16[16,8,512]{2,1,0:T(8,128)(2,1)}), bf16[16,8,512]{2,1,0:T(8,128)(2,1)S(1)}, u32[]{:S(2)}, u32[]{:S(2)}) %all-to-all-start.3) | async-done | bytes 131104 | tf_op jit(solution)/shard_map/all_to_all | solution.py:52
  191.9 1.9 collective-permute-start.17
  193.9 0.6 add_bitcast_fusion
  194.4 4.3 %collective-permute-done.17 = bf16[16,8,512]{2,1,0:T(8,128)(2,1)S(1)} collective-permute-done((bf16[16,8,512]{2,1,0:T(8,128)(2,1)S(1)}, bf16[16,8,512]{2,1,0:T(8,128)(2,1)S(1)}, u32[]{:S(2)}, u32[]{:S(2)}) %collective-permute-start.17) | collective-permute-done | bytes 131104 | tf_op jit(solution)/shard_map/ppermute | solution.py:56
  198.8 0.7 slice.71
  199.5 0.7 slice_bitcast_fusion
  200.2 0.7 slice.72
  (46 shorter events, 1.6 us)
Async XLA Ops:
  1.6 12.8 %collective-permute-start.1 = (bf16[256,512]{1,0:T(8,128)(2,1)S(1)}, bf16[256,512]{1,0:T(8,128)(2,1)S(1)}, u32[]{:S(2)}, u32[]{:S(2)}) collective-permute-start(bf16[256,512]{1,0:T(8,128)(2,1)S(1)} %pad_maximum_fusion.4), channel_id=1, source_target_pairs={{1,0},{2,1},{3,2},{4,3},{5,4},{6,5},{7,6},{8,7},{9,8},{10,9},{11,1... | collective-permute-start | bytes 786440 | tf_op jit(solution)/shard_map/ppermute | solution.py:26
  2.9 11.5 %collective-permute-start = (bf16[128,512]{1,0:T(8,128)(2,1)}, bf16[128,512]{1,0:T(8,128)(2,1)S(1)}, u32[]{:S(2)}, u32[]{:S(2)}) collective-permute-start(bf16[128,512]{1,0:T(8,128)(2,1)} %bitcast.47), channel_id=1, source_target_pairs={{0,1},{1,2},{2,3},{3,4},{4,5},{5,6},{6,7},{7,8},{8,9},{9,10},{10,1... | collective-permute-start | bytes 393224 | tf_op jit(solution)/shard_map/ppermute | solution.py:26
  16.0 7.0 %copy-start = (bf16[1,128,512]{2,1,0:T(8,128)(2,1)S(1)}, bf16[1,128,512]{2,1,0:T(8,128)(2,1)}, u32[]{:S(2)}) copy-start(bf16[1,128,512]{2,1,0:T(8,128)(2,1)} %param.16) | copy-start | bytes 393220
  16.0 7.0 %copy-start.1 = (bf16[1,128,512]{2,1,0:T(8,128)(2,1)S(1)}, bf16[1,128,512]{2,1,0:T(8,128)(2,1)}, u32[]{:S(2)}) copy-start(bf16[1,128,512]{2,1,0:T(8,128)(2,1)} %param.9) | copy-start | bytes 393220
  16.0 35.4 %copy-start.3 = (s32[1,1,8,4]{2,3,1,0:T(4,128)S(1)}, s32[1,1,8,4]{2,3,1,0:T(4,128)}, u32[]{:S(2)}) copy-start(s32[1,1,8,4]{2,3,1,0:T(4,128)} %param.15) | copy-start | bytes 388
  16.0 35.5 %copy-start.4 = (s32[4]{0:T(128)S(1)}, s32[4]{0:T(128)}, u32[]{:S(2)}) copy-start(s32[4]{0:T(128)} %constant.36.clone) | copy-start | bytes 52
  16.0 46.5 %copy-start.2 = (f32[512]{0:T(512)S(1)}, f32[512]{0:T(512)}, u32[]{:S(2)}) copy-start(f32[512]{0:T(512)} %param.10) | copy-start | bytes 6148
  16.0 33.5 %all-to-all-start = ((bf16[8,8,32,512]{3,2,1,0:T(8,128)(2,1)}), bf16[8,8,32,512]{3,2,1,0:T(8,128)(2,1)}, u32[]{:S(2)}, u32[]{:S(2)}) async-start(bf16[8,8,32,512]{3,2,1,0:T(8,128)(2,1)} %broadcast_in_dim.28), calls=%async_computation | async-start | bytes 4194304 | tf_op jit(solution)/shard_map/all_to_all | solution.py:42
  23.0 17.3 %collective-permute-start.5 = (bf16[272,512]{1,0:T(8,128)(2,1)S(1)}, bf16[272,512]{1,0:T(8,128)(2,1)S(1)}, u32[]{:S(2)}, u32[]{:S(2)}) collective-permute-start(bf16[272,512]{1,0:T(8,128)(2,1)S(1)} %pad_maximum_fusion.2), channel_id=1, source_target_pairs={{4,0},{5,1},{6,2},{7,3},{8,4},{9,5},{10,6},{11,7},{12,8},{13,9},{1... | collective-permute-start | bytes 835592 | tf_op jit(solution)/shard_map/ppermute | solution.py:26
  24.3 16.1 %collective-permute-start.4 = (bf16[272,512]{1,0:T(8,128)(2,1)S(1)}, bf16[272,512]{1,0:T(8,128)(2,1)S(1)}, u32[]{:S(2)}, u32[]{:S(2)}) collective-permute-start(bf16[272,512]{1,0:T(8,128)(2,1)S(1)} %pad_maximum_fusion.2), channel_id=1, source_target_pairs={{2,0},{3,1},{4,2},{5,3},{6,4},{7,5},{8,6},{9,7},{10,8},{11,9},{12,... | collective-permute-start | bytes 835592 | tf_op jit(solution)/shard_map/ppermute | solution.py:26
  25.7 11.5 %collective-permute-start.3 = (bf16[144,512]{1,0:T(8,128)(2,1)S(1)}, bf16[144,512]{1,0:T(8,128)(2,1)S(1)}, u32[]{:S(2)}, u32[]{:S(2)}) collective-permute-start(bf16[144,512]{1,0:T(8,128)(2,1)S(1)} %pad_maximum_fusion.6.window_ref), channel_id=1, source_target_pairs={{0,4},{1,5},{2,6},{3,7},{4,8},{5,9},{6,10},{7,11},{8,12},{9,13},{1... | collective-permute-start | bytes 442376 | tf_op jit(solution)/shard_map/ppermute | solution.py:26
  32.4 7.4 %collective-permute-start.2 = (bf16[144,512]{1,0:T(8,128)(2,1)S(1)}, bf16[144,512]{1,0:T(8,128)(2,1)S(1)}, u32[]{:S(2)}, u32[]{:S(2)}) collective-permute-start(bf16[144,512]{1,0:T(8,128)(2,1)S(1)} %pad_maximum_fusion.6.window_ref), channel_id=1, source_target_pairs={{0,2},{1,3},{2,4},{3,5},{4,6},{5,7},{6,8},{7,9},{8,10},{9,11},{10,... | collective-permute-start | bytes 442376 | tf_op jit(solution)/shard_map/ppermute | solution.py:26
  49.5 13.0 %collective-permute-start.6 = (bf16[8,8,32,512]{3,2,1,0:T(8,128)(2,1)}, bf16[8,8,32,512]{3,2,1,0:T(8,128)(2,1)}, u32[]{:S(2)}, u32[]{:S(2)}) collective-permute-start(bf16[8,8,32,512]{3,2,1,0:T(8,128)(2,1)} %all-to-all-done.mine_ref), channel_id=1, source_target_pairs={{0,32},{32,0},{64,96},{96,64},{128,160},{160,128},{192,224},{224,1... | collective-permute-start | bytes 6291464 | tf_op jit(solution)/shard_map/ppermute | solution.py:34
  51.5 20.1 %collective-permute-start.8 = (bf16[272,512]{1,0:T(8,128)(2,1)S(1)}, bf16[272,512]{1,0:T(8,128)(2,1)S(1)}, u32[]{:S(2)}, u32[]{:S(2)}) collective-permute-start(bf16[272,512]{1,0:T(8,128)(2,1)S(1)} %collective-permute-done.5.four_ref), channel_id=1, source_target_pairs={{4,0},{5,1},{6,2},{7,3},{8,4},{9,5},{10,6},{11,7},{12,8},{13,9},{1... | collective-permute-start | bytes 835592 | tf_op jit(solution)/shard_map/ppermute | solution.py:26
  52.9 9.5 %collective-permute-start.7 = (bf16[144,512]{1,0:T(8,128)(2,1)S(1)}, bf16[144,512]{1,0:T(8,128)(2,1)S(1)}, u32[]{:S(2)}, u32[]{:S(2)}) collective-permute-start(bf16[144,512]{1,0:T(8,128)(2,1)S(1)} %collective-permute-done.3.four_ref), channel_id=1, source_target_pairs={{0,4},{1,5},{2,6},{3,7},{4,8},{5,9},{6,10},{7,11},{8,12},{9,13},{1... | collective-permute-start | bytes 442376 | tf_op jit(solution)/shard_map/ppermute | solution.py:26
  72.4 31.9 %collective-permute-start.13 = (bf16[8,4,32,512]{3,2,1,0:T(8,128)(2,1)S(1)}, bf16[8,4,32,512]{3,2,1,0:T(8,128)(2,1)S(1)}, u32[]{:S(2)}, u32[]{:S(2)}) collective-permute-start(bf16[8,4,32,512]{3,2,1,0:T(8,128)(2,1)S(1)} %get-tuple-element.74), channel_id=1, source_target_pairs={{0,32},{32,0},{64,96},{96,64},{128,160},{160,128},{192,224},{224,1... | collective-permute-start | bytes 3145736 | tf_op jit(solution)/shard_map/ppermute | solution.py:34
  74.4 8.8 %collective-permute-start.10 = (f32[24,128]{1,0:T(8,128)S(1)}, f32[24,128]{1,0:T(8,128)S(1)}, u32[]{:S(2)}, u32[]{:S(2)}) collective-permute-start(f32[24,128]{1,0:T(8,128)S(1)} %get-tuple-element.87), channel_id=1, source_target_pairs={{2,0},{3,1},{4,2},{5,3},{6,4},{7,5},{8,6},{9,7},{10,8},{11,9},{12,... | collective-permute-start | bytes 36872 | tf_op jit(solution)/shard_map/ppermute | solution.py:26
  75.7 11.8 %collective-permute-start.11 = (f32[24,128]{1,0:T(8,128)S(1)}, f32[24,128]{1,0:T(8,128)S(1)}, u32[]{:S(2)}, u32[]{:S(2)}) collective-permute-start(f32[24,128]{1,0:T(8,128)S(1)} %get-tuple-element.86), channel_id=1, source_target_pairs={{4,0},{5,1},{6,2},{7,3},{8,4},{9,5},{10,6},{11,7},{12,8},{13,9},{1... | collective-permute-start | bytes 36872 | tf_op jit(solution)/shard_map/ppermute | solution.py:26
  77.0 16.6 %collective-permute-start.12 = (f32[24,128]{1,0:T(8,128)S(1)}, f32[24,128]{1,0:T(8,128)S(1)}, u32[]{:S(2)}, u32[]{:S(2)}) collective-permute-start(f32[24,128]{1,0:T(8,128)S(1)} %get-tuple-element.85), channel_id=1, source_target_pairs={{8,0},{9,1},{10,2},{11,3},{12,4},{13,5},{14,6},{15,7},{16,8},{17,9... | collective-permute-start | bytes 36872 | tf_op jit(solution)/shard_map/ppermute | solution.py:26
  78.3 15.3 %collective-permute-start.9 = (f32[24,128]{1,0:T(8,128)S(1)}, f32[24,128]{1,0:T(8,128)S(1)}, u32[]{:S(2)}, u32[]{:S(2)}) collective-permute-start(f32[24,128]{1,0:T(8,128)S(1)} %get-tuple-element.88), channel_id=1, source_target_pairs={{1,0},{2,1},{3,2},{4,3},{5,4},{6,5},{7,6},{8,7},{9,8},{10,9},{11,1... | collective-permute-start | bytes 36872 | tf_op jit(solution)/shard_map/ppermute | solution.py:26
  98.6 6.0 %collective-permute-start.14 = (bf16[8,4,32,512]{3,2,1,0:T(8,128)(2,1)}, bf16[8,4,32,512]{3,2,1,0:T(8,128)(2,1)S(1)}, u32[]{:S(2)}, u32[]{:S(2)}) collective-permute-start(bf16[8,4,32,512]{3,2,1,0:T(8,128)(2,1)} %get-tuple-element.76), channel_id=1, source_target_pairs={{0,32},{32,0},{64,96},{96,64},{128,160},{160,128},{192,224},{224,1... | collective-permute-start | bytes 3145736 | tf_op jit(solution)/shard_map/ppermute | solution.py:34
  173.2 18.8 %all-to-all-start.3 = ((bf16[16,8,512]{2,1,0:T(8,128)(2,1)}), bf16[16,8,512]{2,1,0:T(8,128)(2,1)S(1)}, u32[]{:S(2)}, u32[]{:S(2)}) async-start(bf16[16,8,512]{2,1,0:T(8,128)(2,1)} %broadcast_in_dim.61), calls=%async_computation.3 | async-start | bytes 262144 | tf_op jit(solution)/shard_map/all_to_all | solution.py:52
  177.5 5.8 %collective-permute-start.15 = (f32[16,512]{1,0:T(8,128)S(1)}, f32[16,512]{1,0:T(8,128)S(1)}, u32[]{:S(2)}, u32[]{:S(2)}) collective-permute-start(f32[16,512]{1,0:T(8,128)S(1)} %get-tuple-element.79), channel_id=1, source_target_pairs={{1,0},{2,1},{3,2},{4,3},{5,4},{6,5},{7,6},{8,7},{9,8},{10,9},{11,1... | collective-permute-start | bytes 98312 | tf_op jit(solution)/shard_map/ppermute | solution.py:26
  178.8 15.0 %collective-permute-start.16 = (f32[4,128]{1,0:T(4,128)S(1)}, f32[4,128]{1,0:T(4,128)S(1)}, u32[]{:S(2)}, u32[]{:S(2)}) collective-permute-start(f32[4,128]{1,0:T(4,128)S(1)} %slice_add_fusion), channel_id=1, source_target_pairs={{0,32},{32,0},{64,96},{96,64},{128,160},{160,128},{192,224},{224,1... | collective-permute-start | bytes 6152 | tf_op jit(solution)/shard_map/ppermute | solution.py:34
  191.9 6.8 %collective-permute-start.17 = (bf16[16,8,512]{2,1,0:T(8,128)(2,1)S(1)}, bf16[16,8,512]{2,1,0:T(8,128)(2,1)S(1)}, u32[]{:S(2)}, u32[]{:S(2)}) collective-permute-start(bf16[16,8,512]{2,1,0:T(8,128)(2,1)S(1)} %all-to-all-done.3), channel_id=1, source_target_pairs={{0,1},{1,0},{2,3},{3,2},{4,5},{5,4},{6,7},{7,6},{8,9},{9,8},{10,11... | collective-permute-start | bytes 393224 | tf_op jit(solution)/shard_map/ppermute | solution.py:56

commit v11 on v10

--- a/solution.py
+++ b/solution.py
@@ -391,7 +391,7 @@
     )(d_query, d_key, d_value, weights, window)
     later = shift_ctx(back, -1)
     terms = jnp.stack([query_half, key_half], axis=1).reshape(16, 128, features)
-    d_gain = jnp.broadcast_to(d_gain[None], (16, edge, features))
+    d_gain = jnp.broadcast_to(d_gain[None, :8], (16, 8, features))
     arrived = over_plane(jnp.concatenate([terms, d_gain], axis=1))
     arrived = jnp.sum(arrived.astype(f32), axis=0)
     rows = arrived[:128].astype(bf16).reshape(16, 8, features)

time: 202 us -> 201 us (level)
  no operation moved by 1% of the time
where the time goes in v11:
time: 201 us; the launch traced here: 199 us
  blocking collectives  64.4 us (32%)
  starting transfers between devices  55.8 us (28%)
  waiting for transfers between devices  45.6 us (23%)
  Pallas kernels  22.9 us (11%)
  local copies, waits for them, and re-layouts  4.75 us (2%)
  other arithmetic  4.3 us (2%)
    all_to_all x1, blocking collectives, over_plane(): lax.all_to_all(stacked, ('dp', 'ctx'), 0, 0, axis_index_groups=plane_grou...  34.3 us
    ppermute x13, starting transfers between devices, shift_ctx(): return lax.ppermute(shard, 'ctx', pairs)  33.4 us
    all_to_all x1, blocking collectives, over_z(): lax.all_to_all(stacked, 'ctx', 0, 0, axis_index_groups=z_groups, tiled=True)  30.1 us
    ppermute x13, waiting for transfers between devices, shift_ctx(): return lax.ppermute(shard, 'ctx', pairs)  25.8 us
    pallas_call x1, Pallas kernels, body(): call(rows_kernel, [((8, features, features), bf16)] + [half] * 7 + [((3,...  9.14 us
    all_to_all x1, waiting for transfers between devices, over_chips(): lax.all_to_all(stacked, 'dp', 0, 0, axis_index_groups=chip_groups, tiled=...  9.07 us
    ppermute x4, starting transfers between devices, dp_to(): return lax.ppermute(shard, 'dp', [(i, target(i)) for i in range(16)])  7.84 us
    all_to_all x1, waiting for transfers between devices, over_z(): lax.all_to_all(stacked, 'ctx', 0, 0, axis_index_groups=z_groups, tiled=True)  7.35 us
  transfers between devices with their start and end apart: 20, of which 11 were waited for; matrix products, arithmetic and copies ran while one was open for 1% of the time, Pallas kernels for 11%

profile of v11, /device:TPU:24, one launch (start us, length us, event | category | flops | bytes accessed | tf_op | source)
XLA Modules:
  0.0 198.7 jit_solution(16607478187108427991)
XLA Ops:
  0.6 1.0 pad_maximum_fusion.4
  1.6 1.3 collective-permute-start.1
  2.9 4.6 %collective-permute-start = (bf16[128,512]{1,0:T(8,128)(2,1)}, bf16[128,512]{1,0:T(8,128)(2,1)S(1)}, u32[]{:S(2)}, u32[]{:S(2)}) collective-permute-start(bf16[128,512]{1,0:T(8,128)(2,1)} %bitcast.47), channel_id=1, source_target_pairs={{0,1},{1,2},{2,3},{3,4},{4,5},{5,6},{6,7},{7,8},{8,9},{9,10},{10,1... | collective-permute-start | bytes 393224 | tf_op jit(solution)/shard_map/ppermute | solution.py:26
  7.5 1.0 pad_maximum_fusion.3
  8.5 5.9 %collective-permute-done.one_ref = bf16[128,512]{1,0:T(8,128)(2,1)S(1)} collective-permute-done((bf16[128,512]{1,0:T(8,128)(2,1)}, bf16[128,512]{1,0:T(8,128)(2,1)S(1)}, u32[]{:S(2)}, u32[]{:S(2)}) %collective-permute-start) | collective-permute-done | bytes 131104 | tf_op jit(solution)/shard_map/ppermute | solution.py:26
  14.4 1.6 broadcast_in_dim.28
  16.0 7.0 %all-to-all-start = ((bf16[8,8,32,512]{3,2,1,0:T(8,128)(2,1)}), bf16[8,8,32,512]{3,2,1,0:T(8,128)(2,1)}, u32[]{:S(2)}, u32[]{:S(2)}) async-start(bf16[8,8,32,512]{3,2,1,0:T(8,128)(2,1)} %broadcast_in_dim.28), calls=%async_computation | async-start | bytes 4194304 | tf_op jit(solution)/shard_map/all_to_all | solution.py:42
  23.0 1.3 collective-permute-start.5
  24.3 1.3 collective-permute-start.4
  25.7 6.7 %collective-permute-start.3 = (bf16[144,512]{1,0:T(8,128)(2,1)S(1)}, bf16[144,512]{1,0:T(8,128)(2,1)S(1)}, u32[]{:S(2)}, u32[]{:S(2)}) collective-permute-start(bf16[144,512]{1,0:T(8,128)(2,1)S(1)} %pad_maximum_fusion.6.window_ref), channel_id=1, source_target_pairs={{0,4},{1,5},{2,6},{3,7},{4,8},{5,9},{6,10},{7,11},{8,12},{9,13},{1... | collective-permute-start | bytes 442376 | tf_op jit(solution)/shard_map/ppermute | solution.py:26
  32.4 4.8 %collective-permute-start.2 = (bf16[144,512]{1,0:T(8,128)(2,1)S(1)}, bf16[144,512]{1,0:T(8,128)(2,1)S(1)}, u32[]{:S(2)}, u32[]{:S(2)}) collective-permute-start(bf16[144,512]{1,0:T(8,128)(2,1)S(1)} %pad_maximum_fusion.6.window_ref), channel_id=1, source_target_pairs={{0,2},{1,3},{2,4},{3,5},{4,6},{5,7},{6,8},{7,9},{8,10},{9,11},{10,... | collective-permute-start | bytes 442376 | tf_op jit(solution)/shard_map/ppermute | solution.py:26
  37.2 2.6 %collective-permute-done.2.two_ref = bf16[144,512]{1,0:T(8,128)(2,1)S(1)} collective-permute-done((bf16[144,512]{1,0:T(8,128)(2,1)S(1)}, bf16[144,512]{1,0:T(8,128)(2,1)S(1)}, u32[]{:S(2)}, u32[]{:S(2)}) %collective-permute-start.2) | collective-permute-done | bytes 147488 | tf_op jit(solution)/shard_map/ppermute | solution.py:26
  39.8 0.5 collective-permute-done.5.four_ref
  40.4 9.1 %all-to-all-done.mine_ref = bf16[8,8,32,512]{3,2,1,0:T(8,128)(2,1)} async-done(((bf16[8,8,32,512]{3,2,1,0:T(8,128)(2,1)}), bf16[8,8,32,512]{3,2,1,0:T(8,128)(2,1)}, u32[]{:S(2)}, u32[]{:S(2)}) %all-to-all-start) | async-done | bytes 2097184 | tf_op jit(solution)/shard_map/all_to_all | solution.py:42
  49.5 1.9 collective-permute-start.6
  51.5 1.3 collective-permute-start.8
  52.9 5.8 %collective-permute-start.7 = (bf16[144,512]{1,0:T(8,128)(2,1)S(1)}, bf16[144,512]{1,0:T(8,128)(2,1)S(1)}, u32[]{:S(2)}, u32[]{:S(2)}) collective-permute-start(bf16[144,512]{1,0:T(8,128)(2,1)S(1)} %collective-permute-done.3.four_ref), channel_id=1, source_target_pairs={{0,4},{1,5},{2,6},{3,7},{4,8},{5,9},{6,10},{7,11},{8,12},{9,13},{1... | collective-permute-start | bytes 442376 | tf_op jit(solution)/shard_map/ppermute | solution.py:26
  58.7 3.7 %collective-permute-done.7.eight_ref = bf16[144,512]{1,0:T(8,128)(2,1)S(1)} collective-permute-done((bf16[144,512]{1,0:T(8,128)(2,1)S(1)}, bf16[144,512]{1,0:T(8,128)(2,1)S(1)}, u32[]{:S(2)}, u32[]{:S(2)}) %collective-permute-start.7) | collective-permute-done | bytes 147488 | tf_op jit(solution)/shard_map/ppermute | solution.py:26
  62.5 9.1 %shard_map.144 = (bf16[8,512,512]{2,1,0:T(8,128)(2,1)}, bf16[128,512]{1,0:T(8,128)(2,1)}, bf16[128,512]{1,0:T(8,128)(2,1)S(1)}, bf16[128,512]{1,0:T(8,128)(2,1)S...) custom-call(s32[1]{0:T(128)} %bitcast.core_ref, ...), custom_call_target="tpu_custom_call" | custom-call | tf_op jit(solution)/shard_map/pallas_call | solution.py:354
  71.7 0.7 shard_map.148
  72.4 1.9 collective-permute-start.13
  74.4 1.3 collective-permute-start.10
  75.7 1.3 collective-permute-start.11
  77.0 1.3 collective-permute-start.12
  78.3 1.3 collective-permute-start.9
  79.6 3.5 %shard_map.145 = (bf16[512,512]{1,0:T(8,128)(2,1)S(1)}, bf16[512,512]{1,0:T(8,128)(2,1)S(1)}) custom-call(bf16[128,512]{1,0:T(8,128)(2,1)S(1)} %bitcast.50, bf16[256,512]{1,0:T(8,128)(2,1)S(1)} %collective-permute-done.1.one_ref, bf16[272,512]{1,0:T(8,128)(2,1)S(1)} %collective-permute-done.4.two_ref, bf16[272,512]{1,0:T(8,128)(2,1)S(1)} %collective-permute-done.5.four_ref, ...), custom_call_target="tpu_custom_call" | custom-call | tf_op jit(solution)/shard_map/pallas_call | solution.py:376
  83.1 4.4 %collective-permute-done.11.four_ref = f32[24,128]{1,0:T(8,128)S(1)} collective-permute-done((f32[24,128]{1,0:T(8,128)S(1)}, f32[24,128]{1,0:T(8,128)S(1)}, u32[]{:S(2)}, u32[]{:S(2)}) %collective-permute-start.11) | collective-permute-done | bytes 12320 | tf_op jit(solution)/shard_map/ppermute | solution.py:26
  87.5 6.0 %collective-permute-done.12.eight_ref = f32[24,128]{1,0:T(8,128)S(1)} collective-permute-done((f32[24,128]{1,0:T(8,128)S(1)}, f32[24,128]{1,0:T(8,128)S(1)}, u32[]{:S(2)}, u32[]{:S(2)}) %collective-permute-start.12) | collective-permute-done | bytes 12320 | tf_op jit(solution)/shard_map/ppermute | solution.py:26
  93.5 5.1 %shard_map.146 = (bf16[128,512]{1,0:T(8,128)(2,1)S(1)}, bf16[128,512]{1,0:T(8,128)(2,1)S(1)}, bf16[8,4,32,512]{3,2,1,0:T(8,128)(2,1)S(1)}, bf16[8,4,32,512]{3,2,1,0:T(8,128)(2,1)}) custom-call(s32[1]{0:T(128)} %bitcast.core_ref, bf16[128,512]{1,0:T(8,128)(2,1)S(1)} %get-tuple-element.53.key_ref, bf16[128,512]{1,0:T(8,128)(2,1)S(1)} %get-tuple-element.54.value_ref, ...), custom_call_target="tpu_custom_call" | custom-call | tf_op jit(solution)/shard_map/pallas_call | solution.py:383
  98.6 2.1 %collective-permute-start.14 = (bf16[8,4,32,512]{3,2,1,0:T(8,128)(2,1)}, bf16[8,4,32,512]{3,2,1,0:T(8,128)(2,1)S(1)}, u32[]{:S(2)}, u32[]{:S(2)}) collective-permute-start(bf16[8,4,32,512]{3,2,1,0:T(8,128)(2,1)} %get-tuple-element.76), channel_id=1, source_target_pairs={{0,32},{32,0},{64,96},{96,64},{128,160},{160,128},{192,224},{224,1... | collective-permute-start | bytes 3145736 | tf_op jit(solution)/shard_map/ppermute | solution.py:34
  100.7 3.5 %shard_map.147 = (f32[128,512]{1,0:T(8,128)S(1)}, f32[16,512]{1,0:T(8,128)S(1)}, bf16[16,512]{1,0:T(8,128)(2,1)S(1)}) custom-call(bf16[128,512]{1,0:T(8,128)(2,1)S(1)} %get-tuple-element.52.d_query_ref, bf16[128,512]{1,0:T(8,128)(2,1)S(1)} %get-tuple-element.69.d_key_ref, bf16[128,512]{1,0:T(8,128)(2,1)S(1)} %get-tuple-element.70.d_value_ref, ...), custom_call_target="tpu_custom_call" | custom-call | tf_op jit(solution)/shard_map/pallas_call | solution.py:387
  104.3 0.4 fusion
  104.7 0.4 fusion.1
  105.7 34.3 %all_to_all.20 = bf16[16,136,512]{2,1,0:T(8,128)(2,1)S(1)} all-to-all(bf16[16,136,512]{2,1,0:T(8,128)(2,1)S(1)} %pad_maximum_fusion), channel_id=1, replica_groups={{0,1,64,65,128,129,192,193,256,257,320,321,384,385,448,449},{2,3,66,67,..., dimensions={0} | all-to-all | bytes 4456448 | tf_op jit(solution)/shard_map/all_to_all | solution.py:46
  140.4 30.1 %all_to_all.21 = bf16[16,8,640]{2,1,0:T(8,128)(2,1)S(1)} all-to-all(bf16[16,8,640]{2,1,0:T(8,128)(2,1)S(1)} %pad_maximum_fusion.5), channel_id=1, replica_groups={{0,2,4,6,8,10,12,14,16,18,20,22,24,26,28,30},{1,3,5,7,9,11,13,15,17,19,..., dimensions={0} | all-to-all | bytes 327680 | tf_op jit(solution)/shard_map/all_to_all | solution.py:52
  170.6 0.7 broadcast_in_dim.61
  171.2 4.6 %all-to-all-start.3 = ((bf16[16,8,512]{2,1,0:T(8,128)(2,1)}), bf16[16,8,512]{2,1,0:T(8,128)(2,1)S(1)}, u32[]{:S(2)}, u32[]{:S(2)}) async-start(bf16[16,8,512]{2,1,0:T(8,128)(2,1)} %broadcast_in_dim.61), calls=%async_computation.3 | async-start | bytes 262144 | tf_op jit(solution)/shard_map/all_to_all | solution.py:52
  175.8 1.3 collective-permute-start.15
  177.1 1.9 collective-permute-start.16
  179.0 2.6 %collective-permute-done.15.later_ref = f32[16,512]{1,0:T(8,128)S(1)} collective-permute-done((f32[16,512]{1,0:T(8,128)S(1)}, f32[16,512]{1,0:T(8,128)S(1)}, u32[]{:S(2)}, u32[]{:S(2)}) %collective-permute-start.15) | collective-permute-done | bytes 32800 | tf_op jit(solution)/shard_map/ppermute | solution.py:26
  181.6 0.8 shard_map.149
  182.4 7.3 %all-to-all-done.3 = bf16[16,8,512]{2,1,0:T(8,128)(2,1)S(1)} async-done(((bf16[16,8,512]{2,1,0:T(8,128)(2,1)}), bf16[16,8,512]{2,1,0:T(8,128)(2,1)S(1)}, u32[]{:S(2)}, u32[]{:S(2)}) %all-to-all-start.3) | async-done | bytes 131104 | tf_op jit(solution)/shard_map/all_to_all | solution.py:52
  189.8 3.0 %collective-permute-start.17 = (bf16[16,8,512]{2,1,0:T(8,128)(2,1)S(1)}, bf16[16,8,512]{2,1,0:T(8,128)(2,1)S(1)}, u32[]{:S(2)}, u32[]{:S(2)}) collective-permute-start(bf16[16,8,512]{2,1,0:T(8,128)(2,1)S(1)} %all-to-all-done.3), channel_id=1, source_target_pairs={{0,1},{1,0},{2,3},{3,2},{4,5},{5,4},{6,7},{7,6},{8,9},{9,8},{10,11... | collective-permute-start | bytes 393224 | tf_op jit(solution)/shard_map/ppermute | solution.py:56
  192.7 0.6 add_bitcast_fusion
  193.3 3.3 %collective-permute-done.17 = bf16[16,8,512]{2,1,0:T(8,128)(2,1)S(1)} collective-permute-done((bf16[16,8,512]{2,1,0:T(8,128)(2,1)S(1)}, bf16[16,8,512]{2,1,0:T(8,128)(2,1)S(1)}, u32[]{:S(2)}, u32[]{:S(2)}) %collective-permute-start.17) | collective-permute-done | bytes 131104 | tf_op jit(solution)/shard_map/ppermute | solution.py:56
  196.7 0.7 slice.75
  197.4 0.7 slice_bitcast_fusion
  198.0 0.7 slice.76
  (47 shorter events, 1.5 us)
Async XLA Ops:
  1.6 12.8 %collective-permute-start.1 = (bf16[256,512]{1,0:T(8,128)(2,1)S(1)}, bf16[256,512]{1,0:T(8,128)(2,1)S(1)}, u32[]{:S(2)}, u32[]{:S(2)}) collective-permute-start(bf16[256,512]{1,0:T(8,128)(2,1)S(1)} %pad_maximum_fusion.4), channel_id=1, source_target_pairs={{1,0},{2,1},{3,2},{4,3},{5,4},{6,5},{7,6},{8,7},{9,8},{10,9},{11,1... | collective-permute-start | bytes 786440 | tf_op jit(solution)/shard_map/ppermute | solution.py:26
  2.9 11.5 %collective-permute-start = (bf16[128,512]{1,0:T(8,128)(2,1)}, bf16[128,512]{1,0:T(8,128)(2,1)S(1)}, u32[]{:S(2)}, u32[]{:S(2)}) collective-permute-start(bf16[128,512]{1,0:T(8,128)(2,1)} %bitcast.47), channel_id=1, source_target_pairs={{0,1},{1,2},{2,3},{3,4},{4,5},{5,6},{6,7},{7,8},{8,9},{9,10},{10,1... | collective-permute-start | bytes 393224 | tf_op jit(solution)/shard_map/ppermute | solution.py:26
  16.0 7.0 %copy-start = (bf16[1,128,512]{2,1,0:T(8,128)(2,1)S(1)}, bf16[1,128,512]{2,1,0:T(8,128)(2,1)}, u32[]{:S(2)}) copy-start(bf16[1,128,512]{2,1,0:T(8,128)(2,1)} %param.16) | copy-start | bytes 393220
  16.0 7.0 %copy-start.1 = (bf16[1,128,512]{2,1,0:T(8,128)(2,1)S(1)}, bf16[1,128,512]{2,1,0:T(8,128)(2,1)}, u32[]{:S(2)}) copy-start(bf16[1,128,512]{2,1,0:T(8,128)(2,1)} %param.9) | copy-start | bytes 393220
  16.0 35.4 %copy-start.3 = (s32[1,1,8,4]{2,3,1,0:T(4,128)S(1)}, s32[1,1,8,4]{2,3,1,0:T(4,128)}, u32[]{:S(2)}) copy-start(s32[1,1,8,4]{2,3,1,0:T(4,128)} %param.15) | copy-start | bytes 388
  16.0 35.5 %copy-start.4 = (s32[4]{0:T(128)S(1)}, s32[4]{0:T(128)}, u32[]{:S(2)}) copy-start(s32[4]{0:T(128)} %constant.36.clone) | copy-start | bytes 52
  16.0 46.5 %copy-start.2 = (f32[512]{0:T(512)S(1)}, f32[512]{0:T(512)}, u32[]{:S(2)}) copy-start(f32[512]{0:T(512)} %param.10) | copy-start | bytes 6148
  16.0 33.5 %all-to-all-start = ((bf16[8,8,32,512]{3,2,1,0:T(8,128)(2,1)}), bf16[8,8,32,512]{3,2,1,0:T(8,128)(2,1)}, u32[]{:S(2)}, u32[]{:S(2)}) async-start(bf16[8,8,32,512]{3,2,1,0:T(8,128)(2,1)} %broadcast_in_dim.28), calls=%async_computation | async-start | bytes 4194304 | tf_op jit(solution)/shard_map/all_to_all | solution.py:42
  23.0 17.3 %collective-permute-start.5 = (bf16[272,512]{1,0:T(8,128)(2,1)S(1)}, bf16[272,512]{1,0:T(8,128)(2,1)S(1)}, u32[]{:S(2)}, u32[]{:S(2)}) collective-permute-start(bf16[272,512]{1,0:T(8,128)(2,1)S(1)} %pad_maximum_fusion.2), channel_id=1, source_target_pairs={{4,0},{5,1},{6,2},{7,3},{8,4},{9,5},{10,6},{11,7},{12,8},{13,9},{1... | collective-permute-start | bytes 835592 | tf_op jit(solution)/shard_map/ppermute | solution.py:26
  24.3 16.1 %collective-permute-start.4 = (bf16[272,512]{1,0:T(8,128)(2,1)S(1)}, bf16[272,512]{1,0:T(8,128)(2,1)S(1)}, u32[]{:S(2)}, u32[]{:S(2)}) collective-permute-start(bf16[272,512]{1,0:T(8,128)(2,1)S(1)} %pad_maximum_fusion.2), channel_id=1, source_target_pairs={{2,0},{3,1},{4,2},{5,3},{6,4},{7,5},{8,6},{9,7},{10,8},{11,9},{12,... | collective-permute-start | bytes 835592 | tf_op jit(solution)/shard_map/ppermute | solution.py:26
  25.7 11.5 %collective-permute-start.3 = (bf16[144,512]{1,0:T(8,128)(2,1)S(1)}, bf16[144,512]{1,0:T(8,128)(2,1)S(1)}, u32[]{:S(2)}, u32[]{:S(2)}) collective-permute-start(bf16[144,512]{1,0:T(8,128)(2,1)S(1)} %pad_maximum_fusion.6.window_ref), channel_id=1, source_target_pairs={{0,4},{1,5},{2,6},{3,7},{4,8},{5,9},{6,10},{7,11},{8,12},{9,13},{1... | collective-permute-start | bytes 442376 | tf_op jit(solution)/shard_map/ppermute | solution.py:26
  32.4 7.4 %collective-permute-start.2 = (bf16[144,512]{1,0:T(8,128)(2,1)S(1)}, bf16[144,512]{1,0:T(8,128)(2,1)S(1)}, u32[]{:S(2)}, u32[]{:S(2)}) collective-permute-start(bf16[144,512]{1,0:T(8,128)(2,1)S(1)} %pad_maximum_fusion.6.window_ref), channel_id=1, source_target_pairs={{0,2},{1,3},{2,4},{3,5},{4,6},{5,7},{6,8},{7,9},{8,10},{9,11},{10,... | collective-permute-start | bytes 442376 | tf_op jit(solution)/shard_map/ppermute | solution.py:26
  49.5 13.0 %collective-permute-start.6 = (bf16[8,8,32,512]{3,2,1,0:T(8,128)(2,1)}, bf16[8,8,32,512]{3,2,1,0:T(8,128)(2,1)}, u32[]{:S(2)}, u32[]{:S(2)}) collective-permute-start(bf16[8,8,32,512]{3,2,1,0:T(8,128)(2,1)} %all-to-all-done.mine_ref), channel_id=1, source_target_pairs={{0,32},{32,0},{64,96},{96,64},{128,160},{160,128},{192,224},{224,1... | collective-permute-start | bytes 6291464 | tf_op jit(solution)/shard_map/ppermute | solution.py:34
  51.5 20.1 %collective-permute-start.8 = (bf16[272,512]{1,0:T(8,128)(2,1)S(1)}, bf16[272,512]{1,0:T(8,128)(2,1)S(1)}, u32[]{:S(2)}, u32[]{:S(2)}) collective-permute-start(bf16[272,512]{1,0:T(8,128)(2,1)S(1)} %collective-permute-done.5.four_ref), channel_id=1, source_target_pairs={{4,0},{5,1},{6,2},{7,3},{8,4},{9,5},{10,6},{11,7},{12,8},{13,9},{1... | collective-permute-start | bytes 835592 | tf_op jit(solution)/shard_map/ppermute | solution.py:26
  52.9 9.5 %collective-permute-start.7 = (bf16[144,512]{1,0:T(8,128)(2,1)S(1)}, bf16[144,512]{1,0:T(8,128)(2,1)S(1)}, u32[]{:S(2)}, u32[]{:S(2)}) collective-permute-start(bf16[144,512]{1,0:T(8,128)(2,1)S(1)} %collective-permute-done.3.four_ref), channel_id=1, source_target_pairs={{0,4},{1,5},{2,6},{3,7},{4,8},{5,9},{6,10},{7,11},{8,12},{9,13},{1... | collective-permute-start | bytes 442376 | tf_op jit(solution)/shard_map/ppermute | solution.py:26
  72.4 31.9 %collective-permute-start.13 = (bf16[8,4,32,512]{3,2,1,0:T(8,128)(2,1)S(1)}, bf16[8,4,32,512]{3,2,1,0:T(8,128)(2,1)S(1)}, u32[]{:S(2)}, u32[]{:S(2)}) collective-permute-start(bf16[8,4,32,512]{3,2,1,0:T(8,128)(2,1)S(1)} %get-tuple-element.74), channel_id=1, source_target_pairs={{0,32},{32,0},{64,96},{96,64},{128,160},{160,128},{192,224},{224,1... | collective-permute-start | bytes 3145736 | tf_op jit(solution)/shard_map/ppermute | solution.py:34
  74.4 8.8 %collective-permute-start.10 = (f32[24,128]{1,0:T(8,128)S(1)}, f32[24,128]{1,0:T(8,128)S(1)}, u32[]{:S(2)}, u32[]{:S(2)}) collective-permute-start(f32[24,128]{1,0:T(8,128)S(1)} %get-tuple-element.87), channel_id=1, source_target_pairs={{2,0},{3,1},{4,2},{5,3},{6,4},{7,5},{8,6},{9,7},{10,8},{11,9},{12,... | collective-permute-start | bytes 36872 | tf_op jit(solution)/shard_map/ppermute | solution.py:26
  75.7 11.8 %collective-permute-start.11 = (f32[24,128]{1,0:T(8,128)S(1)}, f32[24,128]{1,0:T(8,128)S(1)}, u32[]{:S(2)}, u32[]{:S(2)}) collective-permute-start(f32[24,128]{1,0:T(8,128)S(1)} %get-tuple-element.86), channel_id=1, source_target_pairs={{4,0},{5,1},{6,2},{7,3},{8,4},{9,5},{10,6},{11,7},{12,8},{13,9},{1... | collective-permute-start | bytes 36872 | tf_op jit(solution)/shard_map/ppermute | solution.py:26
  77.0 16.6 %collective-permute-start.12 = (f32[24,128]{1,0:T(8,128)S(1)}, f32[24,128]{1,0:T(8,128)S(1)}, u32[]{:S(2)}, u32[]{:S(2)}) collective-permute-start(f32[24,128]{1,0:T(8,128)S(1)} %get-tuple-element.85), channel_id=1, source_target_pairs={{8,0},{9,1},{10,2},{11,3},{12,4},{13,5},{14,6},{15,7},{16,8},{17,9... | collective-permute-start | bytes 36872 | tf_op jit(solution)/shard_map/ppermute | solution.py:26
  78.3 15.3 %collective-permute-start.9 = (f32[24,128]{1,0:T(8,128)S(1)}, f32[24,128]{1,0:T(8,128)S(1)}, u32[]{:S(2)}, u32[]{:S(2)}) collective-permute-start(f32[24,128]{1,0:T(8,128)S(1)} %get-tuple-element.88), channel_id=1, source_target_pairs={{1,0},{2,1},{3,2},{4,3},{5,4},{6,5},{7,6},{8,7},{9,8},{10,9},{11,1... | collective-permute-start | bytes 36872 | tf_op jit(solution)/shard_map/ppermute | solution.py:26
  98.6 6.1 %collective-permute-start.14 = (bf16[8,4,32,512]{3,2,1,0:T(8,128)(2,1)}, bf16[8,4,32,512]{3,2,1,0:T(8,128)(2,1)S(1)}, u32[]{:S(2)}, u32[]{:S(2)}) collective-permute-start(bf16[8,4,32,512]{3,2,1,0:T(8,128)(2,1)} %get-tuple-element.76), channel_id=1, source_target_pairs={{0,32},{32,0},{64,96},{96,64},{128,160},{160,128},{192,224},{224,1... | collective-permute-start | bytes 3145736 | tf_op jit(solution)/shard_map/ppermute | solution.py:34
  171.2 18.5 %all-to-all-start.3 = ((bf16[16,8,512]{2,1,0:T(8,128)(2,1)}), bf16[16,8,512]{2,1,0:T(8,128)(2,1)S(1)}, u32[]{:S(2)}, u32[]{:S(2)}) async-start(bf16[16,8,512]{2,1,0:T(8,128)(2,1)} %broadcast_in_dim.61), calls=%async_computation.3 | async-start | bytes 262144 | tf_op jit(solution)/shard_map/all_to_all | solution.py:52
  175.8 5.8 %collective-permute-start.15 = (f32[16,512]{1,0:T(8,128)S(1)}, f32[16,512]{1,0:T(8,128)S(1)}, u32[]{:S(2)}, u32[]{:S(2)}) collective-permute-start(f32[16,512]{1,0:T(8,128)S(1)} %get-tuple-element.79), channel_id=1, source_target_pairs={{1,0},{2,1},{3,2},{4,3},{5,4},{6,5},{7,6},{8,7},{9,8},{10,9},{11,1... | collective-permute-start | bytes 98312 | tf_op jit(solution)/shard_map/ppermute | solution.py:26
  177.1 15.6 %collective-permute-start.16 = (f32[4,128]{1,0:T(4,128)S(1)}, f32[4,128]{1,0:T(4,128)S(1)}, u32[]{:S(2)}, u32[]{:S(2)}) collective-permute-start(f32[4,128]{1,0:T(4,128)S(1)} %slice_add_fusion), channel_id=1, source_target_pairs={{0,32},{32,0},{64,96},{96,64},{128,160},{160,128},{192,224},{224,1... | collective-permute-start | bytes 6152 | tf_op jit(solution)/shard_map/ppermute | solution.py:34
  189.8 6.8 %collective-permute-start.17 = (bf16[16,8,512]{2,1,0:T(8,128)(2,1)S(1)}, bf16[16,8,512]{2,1,0:T(8,128)(2,1)S(1)}, u32[]{:S(2)}, u32[]{:S(2)}) collective-permute-start(bf16[16,8,512]{2,1,0:T(8,128)(2,1)S(1)} %all-to-all-done.3), channel_id=1, source_target_pairs={{0,1},{1,0},{2,3},{3,2},{4,5},{5,4},{6,7},{7,6},{8,9},{9,8},{10,11... | collective-permute-start | bytes 393224 | tf_op jit(solution)/shard_map/ppermute | solution.py:56
